TPU v7x, 768 devices: a whole 4x8x12 slice. The times are simulated.
768 devices in a mesh: tile: 12 (over z), group: 64 (over y, x, core).
Axes of the slice: x: 4, y: 8, z: 12, core: 2. Of those that a mesh axis runs over, the one named last changes fastest.
Arguments:
- pressure_head: float32 [96, 1024, 128], P('tile', 'group'), may hold values from -2.1 to -0.018, as said below
- old_head: float32 [96, 1024, 128], P('tile', 'group'), may hold values from -3 to -1.5
- soil_type: int32 [96, 1024, 128], P('tile', 'group'), may hold values from 0 to 11
- conduct_sat: float32 [12], replicated, may hold values from 0.1 to 2
- alpha_param: float32 [12], replicated, may hold values from 0.5 to 3
- shape_param: float32 [12], replicated, may hold values from 1.3 to 2.8
- water_span: float32 [12], replicated, may hold values from 0.25 to 0.5
Outputs:
- update: float32 [96, 1024, 128], P('tile', 'group')
- remainder: float32 [96, 1024, 128], P('tile', 'group')
Inputs may be any that keep to these rules, and one draw needn't show every extreme that they name: `pressure_head`: the head is negative in every cell.
All inputs are finite; a program needn't handle non-finite values.
Results may differ from a plain program's by a relative error of at most 0.0003.
Values sent between devices are 32-bit elements; how exact they have to be, the bound alone decides.
No kernel may reach another device: no remote copies, remote signals or barrier semaphores. Data moves between devices by JAX's collectives and lax.ppermute only.
A program may use at most 128 MiB of HBM per device.

v0:
```python
import jax
import jax.numpy as jnp
from jax import lax
from jax.sharding import PartitionSpec as P

LEVELS = 4
COARSE_SWEEPS = 4


OMEGA = 2.0 / 3.0
STORAGE = 0.01


def with_halo(cells, sides, width):
    for axis, dim in sides:
        count = lax.axis_size(axis)
        ends = count - 1
        head = lax.slice_in_dim(cells, 0, width, axis=dim)
        tail = lax.slice_in_dim(cells, cells.shape[dim] - width, cells.shape[dim], axis=dim)
        cells = jnp.concatenate(
            [
                lax.ppermute(tail, axis, [(i, (i + 1) % count) for i in range(ends)]),
                cells,
                lax.ppermute(head, axis, [((i + 1) % count, i) for i in range(ends)]),
            ],
            axis=dim,
        )
    return cells


def lookup(soil_type, entries):
    classes = jnp.arange(entries.shape[0], dtype=jnp.int32)
    chosen = soil_type[None] == classes[:, None, None, None]
    return jnp.sum(jnp.where(chosen, entries[:, None, None, None], 0.0), axis=0)


def hydraulics(head_vals, conduct, alpha_cells, shape_cells, spread_cells):
    shape_m = 1.0 - 1.0 / shape_cells
    power = jnp.exp(shape_cells * jnp.log(alpha_cells * -head_vals))
    saturation = jnp.exp(-shape_m * jnp.log1p(power))
    fraction = power / (1.0 + power)
    factor = 1.0 - jnp.exp(shape_m * jnp.log(fraction))
    conductivity = conduct * jnp.sqrt(saturation) * factor * factor
    capacity = (
        spread_cells * shape_m * shape_cells * power / -head_vals * saturation / (1.0 + power)
    )
    return (saturation, conductivity, capacity)


def harmonic(first, second):
    return 2.0 * first * second / (first + second)


def assemble(
    padded_head,
    padded_cond,
    pressure_head,
    old_head,
    saturation,
    old_saturation,
    spread_cells,
    capacity,
):
    center = padded_cond[1:-1, 1:-1, 1:-1]
    x_low = harmonic(center, padded_cond[:-2, 1:-1, 1:-1])
    x_high = harmonic(center, padded_cond[2:, 1:-1, 1:-1])
    y_low = harmonic(center, padded_cond[1:-1, :-2, 1:-1])
    y_high = harmonic(center, padded_cond[1:-1, 2:, 1:-1])
    z_low = harmonic(center, padded_cond[1:-1, 1:-1, :-2])
    z_high = harmonic(center, padded_cond[1:-1, 1:-1, 2:])
    flux = x_low * (pressure_head - padded_head[:-2, 1:-1, 1:-1]) + x_high * (
        pressure_head - padded_head[2:, 1:-1, 1:-1]
    )
    flux = (
        flux
        + y_low * (pressure_head - padded_head[1:-1, :-2, 1:-1])
        + y_high * (pressure_head - padded_head[1:-1, 2:, 1:-1])
    )
    flux = (
        flux
        + z_low * (pressure_head - padded_head[1:-1, 1:-1, :-2] + 1.0)
        + z_high * (pressure_head - padded_head[1:-1, 1:-1, 2:] - 1.0)
    )
    misfit = (
        spread_cells * (saturation - old_saturation) + STORAGE * (pressure_head - old_head) + flux
    )
    band_set = jnp.stack([capacity + STORAGE, x_low, x_high, y_low, y_high, z_low, z_high])
    return (-misfit, band_set)


def diagonal_of(band_set):
    return (
        band_set[0]
        + band_set[1]
        + band_set[2]
        + band_set[3]
        + band_set[4]
        + band_set[5]
        + band_set[6]
    )


def apply_operator(band_set, diagonal, padded):
    center = padded[1:-1, 1:-1, :]
    vertical = jnp.pad(center, ((0, 0), (0, 0), (1, 1)))
    beside = band_set[1] * padded[:-2, 1:-1, :] + band_set[2] * padded[2:, 1:-1, :]
    beside = beside + band_set[3] * padded[1:-1, :-2, :] + band_set[4] * padded[1:-1, 2:, :]
    beside = beside + band_set[5] * vertical[:, :, :-2] + band_set[6] * vertical[:, :, 2:]
    return diagonal * center - beside


def coarsen_bands(band_set):
    seven, size_x, size_y, size_z = band_set.shape
    split = band_set.reshape(seven, size_x // 2, 2, size_y // 2, 2, size_z // 2, 2)
    storage = jnp.sum(split[0], axis=(1, 3, 5))
    x_low = jnp.sum(split[1][:, 0], axis=(2, 4))
    x_high = jnp.sum(split[2][:, 1], axis=(2, 4))
    y_low = jnp.sum(split[3][:, :, :, 0], axis=(1, 4))
    y_high = jnp.sum(split[4][:, :, :, 1], axis=(1, 4))
    z_low = jnp.sum(split[5][:, :, :, :, :, 0], axis=(1, 3))
    z_high = jnp.sum(split[6][:, :, :, :, :, 1], axis=(1, 3))
    return jnp.stack([storage, x_low, x_high, y_low, y_high, z_low, z_high])


def restrict(values):
    size_x, size_y, size_z = values.shape
    return jnp.sum(values.reshape(size_x // 2, 2, size_y // 2, 2, size_z // 2, 2), axis=(1, 3, 5))


def prolong(values):
    return jnp.repeat(jnp.repeat(jnp.repeat(values, 2, axis=0), 2, axis=1), 2, axis=2)


def line_start(band_set, diagonal, remain):
    inner = diagonal - band_set[3] - band_set[4]
    line_value = jnp.sum(remain, axis=1, keepdims=True) / jnp.sum(inner, axis=1, keepdims=True)
    return jnp.broadcast_to(line_value, remain.shape)


def level_pad(values):
    return with_halo(values, (("tile", 0), ("group", 1)), 1)


def group_pad(values):
    rimmed = with_halo(values, (("tile", 0),), 1)
    return jnp.pad(rimmed, ((0, 0), (1, 1), (0, 0)))


def collect(values):
    return lax.all_gather(values, "group", axis=1, tiled=True)


def descend(level_at, remain, band_sets, diagonals, padders, switch_at):
    band_set = band_sets[level_at]
    diagonal = diagonals[level_at]
    padder = padders[level_at]
    if level_at == len(band_sets) - 1:
        update = line_start(band_set, diagonal, remain)
        for sweep_no in range(COARSE_SWEEPS):
            update = (
                update
                + OMEGA * (remain - apply_operator(band_set, diagonal, padder(update))) / diagonal
            )
        return update
    update = OMEGA * remain / diagonal
    update = (
        update + OMEGA * (remain - apply_operator(band_set, diagonal, padder(update))) / diagonal
    )
    defect = remain - apply_operator(band_set, diagonal, padder(update))
    coarse_remain = restrict(defect)
    if level_at + 1 == switch_at:
        whole = descend(
            level_at + 1, collect(coarse_remain), band_sets, diagonals, padders, switch_at
        )
        row_count = coarse_remain.shape[1]
        coarse = lax.dynamic_slice_in_dim(whole, lax.axis_index("group") * row_count, row_count, 1)
    else:
        coarse = descend(level_at + 1, coarse_remain, band_sets, diagonals, padders, switch_at)
    update = update + prolong(coarse)
    update = (
        update + OMEGA * (remain - apply_operator(band_set, diagonal, padder(update))) / diagonal
    )
    return update


def shards(pressure_head, old_head, soil_type, conduct_sat, alpha_param, shape_param, water_span):
    conduct = lookup(soil_type, conduct_sat)
    alpha_cells = lookup(soil_type, alpha_param)
    shape_cells = lookup(soil_type, shape_param)
    spread_cells = lookup(soil_type, water_span)
    saturation, conductivity, capacity = hydraulics(
        pressure_head, conduct, alpha_cells, shape_cells, spread_cells
    )
    old_saturation = hydraulics(old_head, conduct, alpha_cells, shape_cells, spread_cells)[0]
    rimmed = with_halo(jnp.stack([pressure_head, conductivity]), (("tile", 1), ("group", 2)), 1)
    rimmed = jnp.pad(rimmed, ((0, 0), (0, 0), (0, 0), (1, 1)))
    rhs, band_set = assemble(
        rimmed[0],
        rimmed[1],
        pressure_head,
        old_head,
        saturation,
        old_saturation,
        spread_cells,
        capacity,
    )
    switch_at = LEVELS - 1
    band_sets = [band_set]
    for level_at in range(1, switch_at):
        band_sets.append(coarsen_bands(band_sets[-1]))
    band_sets.append(lax.all_gather(coarsen_bands(band_sets[-1]), "group", axis=2, tiled=True))
    diagonals = [diagonal_of(entry) for entry in band_sets]
    padders = [level_pad if level_at < switch_at else group_pad for level_at in range(LEVELS)]
    update = descend(0, rhs, band_sets, diagonals, padders, switch_at)
    remain = rhs - apply_operator(band_sets[0], diagonals[0], level_pad(update))
    update = update + descend(0, remain, band_sets, diagonals, padders, switch_at)
    remainder = rhs - apply_operator(band_sets[0], diagonals[0], level_pad(update))
    return (update, remainder)


def solution(mesh):
    return jax.shard_map(
        shards,
        mesh=mesh,
        in_specs=(
            P("tile", "group", None),
            P("tile", "group", None),
            P("tile", "group", None),
            P(),
            P(),
            P(),
            P(),
        ),
        out_specs=(P("tile", "group", None), P("tile", "group", None)),
        check_vma=False,
    )
```

profile of v0, /device:TPU:31, one launch (start us, length us, event | category | flops | bytes accessed | tf_op | source)
XLA Modules:
  0.0 685.0 jit_solution(17530918746616553464)
XLA Ops:
  13.5 6.0 collective-permute-start.2
  84.1 7.7 %collective-permute-start.6 = (f32[10,1,128]{2,1,0:T(1,128)S(1)}, f32[10,1,128]{2,1,0:T(1,128)S(1)}, u32[]{:S(2)}, u32[]{:S(2)}) collective-permute-start(f32[10,1,128]{2,1,0:T(1,128)S(1)} %get-tuple-element.56), channel_id=1, source_target_pairs={{0,1},{1,2},{2,3},{3,4},{4,5},{5,6},{6,7},{7,8},{8,9},{9,10},{10,1... | collective-permute-start | bytes 15368 | tf_op jit(solution)/shard_map/ppermute | solution.py:22
  116.6 6.2 collective-permute-done.11
  166.1 6.3 collective-permute-done.19
  178.1 47.1 %all_gather.10 = f32[7,1,128,16]{3,1,0,2:T(1,128)S(1)} all-gather(f32[7,1,2,16]{3,1,0,2:T(1,128)S(1)} %copy.360), channel_id=1, replica_groups=mesh['tile'=12,'group'=64] {'group'}, dimensions={2}, use_global_device_ids=true | all-gather | bytes 58240 | tf_op jit(solution)/shard_map/all_gather | solution.py:211
  251.8 6.2 collective-permute-done.27
  258.2 35.4 %all-gather.2 = f32[64,2,16]{2,1,0:T(2,128)S(1)} all-gather(f32[1,2,16]{2,1,0:T(2,128)S(1)} %bitcast.237), channel_id=2, replica_groups=mesh['tile'=12,'group'=64] {'group'}, dimensions={0}, use_global_device_ids=true | all-gather | bytes 8320 | tf_op jit(solution)/shard_map/all_gather | solution.py:150
  335.6 9.6 %collective-permute-start.38 = (f32[4,1,32]{2,1,0:T(1,128)S(1)}, f32[4,1,32]{2,1,0:T(1,128)S(1)}, u32[]{:S(2)}, u32[]{:S(2)}) collective-permute-start(f32[4,1,32]{2,1,0:T(1,128)S(1)} %get-tuple-element.106), channel_id=1, source_target_pairs={{0,1},{1,2},{2,3},{3,4},{4,5},{5,6},{6,7},{7,8},{8,9},{9,10},{10,1... | collective-permute-start | bytes 1544 | tf_op jit(solution)/shard_map/ppermute | solution.py:22
  347.2 6.3 collective-permute-done.39
  366.8 6.3 collective-permute-done.43
  386.9 6.3 collective-permute-done.47
  405.9 6.3 collective-permute-done.51
  424.9 6.3 collective-permute-done.55
  444.0 6.3 collective-permute-done.59
  471.1 6.3 collective-permute-done.63
  490.0 6.3 collective-permute-done.67
  509.6 6.3 collective-permute-done.71
  528.5 6.3 collective-permute-done.75
  535.1 35.4 %all-gather.3 = f32[64,2,16]{2,1,0:T(2,128)S(1)} all-gather(f32[1,2,16]{2,1,0:T(2,128)S(1)} %bitcast.238), channel_id=3, replica_groups=mesh['tile'=12,'group'=64] {'group'}, dimensions={0}, use_global_device_ids=true | all-gather | bytes 8320 | tf_op jit(solution)/shard_map/all_gather | solution.py:150
  608.6 9.6 %collective-permute-start.86 = (f32[4,1,32]{2,1,0:T(1,128)S(1)}, f32[4,1,32]{2,1,0:T(1,128)S(1)}, u32[]{:S(2)}, u32[]{:S(2)}) collective-permute-start(f32[4,1,32]{2,1,0:T(1,128)S(1)} %get-tuple-element.98), channel_id=1, source_target_pairs={{0,1},{1,2},{2,3},{3,4},{4,5},{5,6},{6,7},{7,8},{8,9},{9,10},{10,1... | collective-permute-start | bytes 1544 | tf_op jit(solution)/shard_map/ppermute | solution.py:22
  620.2 6.3 collective-permute-done.87
  639.4 6.3 collective-permute-done.91
  658.8 6.3 collective-permute-done.95
  677.9 6.3 collective-permute-done.99
  (398 shorter events, 424.5 us)
Async XLA Ops:
  13.5 16.8 %collective-permute-start.2 = (f32[2,10,1,128]{3,0,2,1:T(2,128)S(1)}, f32[2,10,1,128]{3,0,2,1:T(2,128)S(1)}, u32[]{:S(2)}, u32[]{:S(2)}) collective-permute-start(f32[2,10,1,128]{3,0,2,1:T(2,128)S(1)} %copy.393), channel_id=1, source_target_pairs={{0,1},{1,2},{2,3},{3,4},{4,5},{5,6},{6,7},{7,8},{8,9},{9,10},{10,1... | collective-permute-start | bytes 30728 | tf_op jit(solution)/shard_map/ppermute | solution.py:22
  19.6 10.8 %collective-permute-start.3 = (f32[2,10,1,128]{3,0,2,1:T(2,128)S(1)}, f32[2,10,1,128]{3,0,2,1:T(2,128)S(1)}, u32[]{:S(2)}, u32[]{:S(2)}) collective-permute-start(f32[2,10,1,128]{3,0,2,1:T(2,128)S(1)} %copy.394), channel_id=1, source_target_pairs={{1,0},{2,1},{3,2},{4,3},{5,4},{6,5},{7,6},{8,7},{9,8},{10,9},{11,1... | collective-permute-start | bytes 30728 | tf_op jit(solution)/shard_map/ppermute | solution.py:24
  73.5 10.6 %collective-permute-start.4 = (f32[1,16,128]{2,1,0:T(8,128)S(1)}, f32[1,16,128]{2,1,0:T(8,128)S(1)}, u32[]{:S(2)}, u32[]{:S(2)}) collective-permute-start(f32[1,16,128]{2,1,0:T(8,128)S(1)} %get-tuple-element.72), channel_id=1, source_target_pairs={{0,64},{64,128},{128,192},{192,256},{256,320},{320,384},{384,448},... | collective-permute-start | bytes 24584 | tf_op jit(solution)/shard_map/ppermute | solution.py:22
  84.1 10.2 %collective-permute-start.6 = (f32[10,1,128]{2,1,0:T(1,128)S(1)}, f32[10,1,128]{2,1,0:T(1,128)S(1)}, u32[]{:S(2)}, u32[]{:S(2)}) collective-permute-start(f32[10,1,128]{2,1,0:T(1,128)S(1)} %get-tuple-element.56), channel_id=1, source_target_pairs={{0,1},{1,2},{2,3},{3,4},{4,5},{5,6},{6,7},{7,8},{8,9},{9,10},{10,1... | collective-permute-start | bytes 15368 | tf_op jit(solution)/shard_map/ppermute | solution.py:22
  91.9 8.3 %collective-permute-start.7 = (f32[10,1,128]{2,1,0:T(1,128)S(1)}, f32[10,1,128]{2,1,0:T(1,128)S(1)}, u32[]{:S(2)}, u32[]{:S(2)}) collective-permute-start(f32[10,1,128]{2,1,0:T(1,128)S(1)} %get-tuple-element.57), channel_id=1, source_target_pairs={{1,0},{2,1},{3,2},{4,3},{5,4},{6,5},{7,6},{8,7},{9,8},{10,9},{11,1... | collective-permute-start | bytes 15368 | tf_op jit(solution)/shard_map/ppermute | solution.py:24
  114.6 8.3 %collective-permute-start.11 = (f32[10,1,128]{2,1,0:T(1,128)S(1)}, f32[10,1,128]{2,1,0:T(1,128)S(1)}, u32[]{:S(2)}, u32[]{:S(2)}) collective-permute-start(f32[10,1,128]{2,1,0:T(1,128)S(1)} %get-tuple-element.55), channel_id=1, source_target_pairs={{1,0},{2,1},{3,2},{4,3},{5,4},{6,5},{7,6},{8,7},{9,8},{10,9},{11,1... | collective-permute-start | bytes 15368 | tf_op jit(solution)/shard_map/ppermute | solution.py:24
  143.2 8.2 %collective-permute-start.15 = (f32[6,1,64]{2,1,0:T(1,128)S(1)}, f32[6,1,64]{2,1,0:T(1,128)S(1)}, u32[]{:S(2)}, u32[]{:S(2)}) collective-permute-start(f32[6,1,64]{2,1,0:T(1,128)S(1)} %get-tuple-element.85), channel_id=1, source_target_pairs={{1,0},{2,1},{3,2},{4,3},{5,4},{6,5},{7,6},{8,7},{9,8},{10,9},{11,1... | collective-permute-start | bytes 4616 | tf_op jit(solution)/shard_map/ppermute | solution.py:24
  164.2 8.2 %collective-permute-start.19 = (f32[6,1,64]{2,1,0:T(1,128)S(1)}, f32[6,1,64]{2,1,0:T(1,128)S(1)}, u32[]{:S(2)}, u32[]{:S(2)}) collective-permute-start(f32[6,1,64]{2,1,0:T(1,128)S(1)} %get-tuple-element.83), channel_id=1, source_target_pairs={{1,0},{2,1},{3,2},{4,3},{5,4},{6,5},{7,6},{8,7},{9,8},{10,9},{11,1... | collective-permute-start | bytes 4616 | tf_op jit(solution)/shard_map/ppermute | solution.py:24
  173.2 52.1 %collective-permute-start.20 = (f32[1,4,32]{2,1,0:T(4,128)S(1)}, f32[1,4,32]{2,1,0:T(4,128)S(1)}, u32[]{:S(2)}, u32[]{:S(2)}) collective-permute-start(f32[1,4,32]{2,1,0:T(4,128)S(1)} %get-tuple-element.124), channel_id=1, source_target_pairs={{0,64},{64,128},{128,192},{192,256},{256,320},{320,384},{384,448},... | collective-permute-start | bytes 1544 | tf_op jit(solution)/shard_map/ppermute | solution.py:22
  176.8 48.4 %collective-permute-start.21 = (f32[1,4,32]{2,1,0:T(4,128)S(1)}, f32[1,4,32]{2,1,0:T(4,128)S(1)}, u32[]{:S(2)}, u32[]{:S(2)}) collective-permute-start(f32[1,4,32]{2,1,0:T(4,128)S(1)} %get-tuple-element.125), channel_id=1, source_target_pairs={{64,0},{128,64},{192,128},{256,192},{320,256},{384,320},{448,384},... | collective-permute-start | bytes 1544 | tf_op jit(solution)/shard_map/ppermute | solution.py:24
  229.7 8.2 %collective-permute-start.23 = (f32[4,1,32]{2,1,0:T(1,128)S(1)}, f32[4,1,32]{2,1,0:T(1,128)S(1)}, u32[]{:S(2)}, u32[]{:S(2)}) collective-permute-start(f32[4,1,32]{2,1,0:T(1,128)S(1)} %get-tuple-element.113), channel_id=1, source_target_pairs={{1,0},{2,1},{3,2},{4,3},{5,4},{6,5},{7,6},{8,7},{9,8},{10,9},{11,1... | collective-permute-start | bytes 1544 | tf_op jit(solution)/shard_map/ppermute | solution.py:24
  249.7 8.2 %collective-permute-start.27 = (f32[4,1,32]{2,1,0:T(1,128)S(1)}, f32[4,1,32]{2,1,0:T(1,128)S(1)}, u32[]{:S(2)}, u32[]{:S(2)}) collective-permute-start(f32[4,1,32]{2,1,0:T(1,128)S(1)} %get-tuple-element.111), channel_id=1, source_target_pairs={{1,0},{2,1},{3,2},{4,3},{5,4},{6,5},{7,6},{8,7},{9,8},{10,9},{11,1... | collective-permute-start | bytes 1544 | tf_op jit(solution)/shard_map/ppermute | solution.py:24
  335.6 11.6 %collective-permute-start.38 = (f32[4,1,32]{2,1,0:T(1,128)S(1)}, f32[4,1,32]{2,1,0:T(1,128)S(1)}, u32[]{:S(2)}, u32[]{:S(2)}) collective-permute-start(f32[4,1,32]{2,1,0:T(1,128)S(1)} %get-tuple-element.106), channel_id=1, source_target_pairs={{0,1},{1,2},{2,3},{3,4},{4,5},{5,6},{6,7},{7,8},{8,9},{9,10},{10,1... | collective-permute-start | bytes 1544 | tf_op jit(solution)/shard_map/ppermute | solution.py:22
  364.9 8.2 %collective-permute-start.43 = (f32[6,1,64]{2,1,0:T(1,128)S(1)}, f32[6,1,64]{2,1,0:T(1,128)S(1)}, u32[]{:S(2)}, u32[]{:S(2)}) collective-permute-start(f32[6,1,64]{2,1,0:T(1,128)S(1)} %get-tuple-element.81), channel_id=1, source_target_pairs={{1,0},{2,1},{3,2},{4,3},{5,4},{6,5},{7,6},{8,7},{9,8},{10,9},{11,1... | collective-permute-start | bytes 4616 | tf_op jit(solution)/shard_map/ppermute | solution.py:24
  384.9 8.3 %collective-permute-start.47 = (f32[10,1,128]{2,1,0:T(1,128)S(1)}, f32[10,1,128]{2,1,0:T(1,128)S(1)}, u32[]{:S(2)}, u32[]{:S(2)}) collective-permute-start(f32[10,1,128]{2,1,0:T(1,128)S(1)} %get-tuple-element.53), channel_id=1, source_target_pairs={{1,0},{2,1},{3,2},{4,3},{5,4},{6,5},{7,6},{8,7},{9,8},{10,9},{11,1... | collective-permute-start | bytes 15368 | tf_op jit(solution)/shard_map/ppermute | solution.py:24
  404.0 8.3 %collective-permute-start.51 = (f32[10,1,128]{2,1,0:T(1,128)S(1)}, f32[10,1,128]{2,1,0:T(1,128)S(1)}, u32[]{:S(2)}, u32[]{:S(2)}) collective-permute-start(f32[10,1,128]{2,1,0:T(1,128)S(1)} %get-tuple-element.51), channel_id=1, source_target_pairs={{1,0},{2,1},{3,2},{4,3},{5,4},{6,5},{7,6},{8,7},{9,8},{10,9},{11,1... | collective-permute-start | bytes 15368 | tf_op jit(solution)/shard_map/ppermute | solution.py:24
  423.0 8.3 %collective-permute-start.55 = (f32[10,1,128]{2,1,0:T(1,128)S(1)}, f32[10,1,128]{2,1,0:T(1,128)S(1)}, u32[]{:S(2)}, u32[]{:S(2)}) collective-permute-start(f32[10,1,128]{2,1,0:T(1,128)S(1)} %get-tuple-element.49), channel_id=1, source_target_pairs={{1,0},{2,1},{3,2},{4,3},{5,4},{6,5},{7,6},{8,7},{9,8},{10,9},{11,1... | collective-permute-start | bytes 15368 | tf_op jit(solution)/shard_map/ppermute | solution.py:24
  442.0 8.3 %collective-permute-start.59 = (f32[10,1,128]{2,1,0:T(1,128)S(1)}, f32[10,1,128]{2,1,0:T(1,128)S(1)}, u32[]{:S(2)}, u32[]{:S(2)}) collective-permute-start(f32[10,1,128]{2,1,0:T(1,128)S(1)} %get-tuple-element.47), channel_id=1, source_target_pairs={{1,0},{2,1},{3,2},{4,3},{5,4},{6,5},{7,6},{8,7},{9,8},{10,9},{11,1... | collective-permute-start | bytes 15368 | tf_op jit(solution)/shard_map/ppermute | solution.py:24
  469.1 8.2 %collective-permute-start.63 = (f32[6,1,64]{2,1,0:T(1,128)S(1)}, f32[6,1,64]{2,1,0:T(1,128)S(1)}, u32[]{:S(2)}, u32[]{:S(2)}) collective-permute-start(f32[6,1,64]{2,1,0:T(1,128)S(1)} %get-tuple-element.79), channel_id=1, source_target_pairs={{1,0},{2,1},{3,2},{4,3},{5,4},{6,5},{7,6},{8,7},{9,8},{10,9},{11,1... | collective-permute-start | bytes 4616 | tf_op jit(solution)/shard_map/ppermute | solution.py:24
  488.1 8.2 %collective-permute-start.67 = (f32[6,1,64]{2,1,0:T(1,128)S(1)}, f32[6,1,64]{2,1,0:T(1,128)S(1)}, u32[]{:S(2)}, u32[]{:S(2)}) collective-permute-start(f32[6,1,64]{2,1,0:T(1,128)S(1)} %get-tuple-element.77), channel_id=1, source_target_pairs={{1,0},{2,1},{3,2},{4,3},{5,4},{6,5},{7,6},{8,7},{9,8},{10,9},{11,1... | collective-permute-start | bytes 4616 | tf_op jit(solution)/shard_map/ppermute | solution.py:24
  608.6 11.6 %collective-permute-start.86 = (f32[4,1,32]{2,1,0:T(1,128)S(1)}, f32[4,1,32]{2,1,0:T(1,128)S(1)}, u32[]{:S(2)}, u32[]{:S(2)}) collective-permute-start(f32[4,1,32]{2,1,0:T(1,128)S(1)} %get-tuple-element.98), channel_id=1, source_target_pairs={{0,1},{1,2},{2,3},{3,4},{4,5},{5,6},{6,7},{7,8},{8,9},{9,10},{10,1... | collective-permute-start | bytes 1544 | tf_op jit(solution)/shard_map/ppermute | solution.py:22
  637.4 8.2 %collective-permute-start.91 = (f32[6,1,64]{2,1,0:T(1,128)S(1)}, f32[6,1,64]{2,1,0:T(1,128)S(1)}, u32[]{:S(2)}, u32[]{:S(2)}) collective-permute-start(f32[6,1,64]{2,1,0:T(1,128)S(1)} %get-tuple-element.75), channel_id=1, source_target_pairs={{1,0},{2,1},{3,2},{4,3},{5,4},{6,5},{7,6},{8,7},{9,8},{10,9},{11,1... | collective-permute-start | bytes 4616 | tf_op jit(solution)/shard_map/ppermute | solution.py:24
  656.9 8.3 %collective-permute-start.95 = (f32[10,1,128]{2,1,0:T(1,128)S(1)}, f32[10,1,128]{2,1,0:T(1,128)S(1)}, u32[]{:S(2)}, u32[]{:S(2)}) collective-permute-start(f32[10,1,128]{2,1,0:T(1,128)S(1)} %get-tuple-element.45), channel_id=1, source_target_pairs={{1,0},{2,1},{3,2},{4,3},{5,4},{6,5},{7,6},{8,7},{9,8},{10,9},{11,1... | collective-permute-start | bytes 15368 | tf_op jit(solution)/shard_map/ppermute | solution.py:24
  676.0 8.3 %collective-permute-start.99 = (f32[10,1,128]{2,1,0:T(1,128)S(1)}, f32[10,1,128]{2,1,0:T(1,128)S(1)}, u32[]{:S(2)}, u32[]{:S(2)}) collective-permute-start(f32[10,1,128]{2,1,0:T(1,128)S(1)} %get-tuple-element.43), channel_id=1, source_target_pairs={{1,0},{2,1},{3,2},{4,3},{5,4},{6,5},{7,6},{8,7},{9,8},{10,9},{11,1... | collective-permute-start | bytes 15368 | tf_op jit(solution)/shard_map/ppermute | solution.py:24
  (79 other events, 413.8 us)
where the time goes:
time: 688 us; the launch traced here: 685 us
  starting transfers between devices  266 us (39%)
  waiting for transfers between devices  209 us (30%)
  blocking collectives  118 us (17%)
  local copies, waits for them, and re-layouts  59.3 us (9%)
  other arithmetic  29.9 us (4%)
    ppermute x50, waiting for transfers between devices, with_halo(): lax.ppermute(head, axis, [((i + 1) % count, i) for i in range(ends)])  209 us
    ppermute x50, starting transfers between devices, with_halo(): lax.ppermute(tail, axis, [(i, (i + 1) % count) for i in range(ends)])  188 us
    ppermute x50, starting transfers between devices, with_halo(): lax.ppermute(head, axis, [((i + 1) % count, i) for i in range(ends)])  78 us
    all_gather x2, blocking collectives, collect(): return lax.all_gather(values, 'group', axis=1, tiled=True)  70.9 us
    all_gather x1, blocking collectives, shards(): lax.all_gather(coarsen_bands(band_sets[-1]), 'group', axis=2, tiled=True)  47.1 us
  transfers between devices with their start and end apart: 100, of which 47 were waited for; matrix products, arithmetic and copies ran while one was open for 3% of the time, Pallas kernels for 0%

commit v1 on v0

v1 whole, which is shorter than its diff:
```python
import functools

import jax
import jax.numpy as jnp
from jax import lax
from jax.experimental import pallas as pl
from jax.experimental.pallas import tpu as pltpu
from jax.sharding import PartitionSpec as P

OMEGA = 2.0 / 3.0
STORAGE = 0.01
COARSE_SWEEPS = 4
SOILS = 12

BX, BY, NZ = 8, 16, 128
WX, WY = 24, 32
PX = WX + 2
L1X = WX // 2
F32 = jnp.float32


def iota(shape, dim):
    return lax.broadcasted_iota(jnp.int32, shape, dim)


def turn(v, step, axis):
    size = v.shape[axis]
    return pltpu.roll(v, step % size, axis)


def bit_of(v, step, axis):
    return (iota(v.shape, axis) // step) % 2 == 0


def pair_sum(v, step, axis):
    return v + jnp.where(bit_of(v, step, axis), turn(v, -step, axis), turn(v, step, axis))


def pair_low(v, step, axis):
    return jnp.where(bit_of(v, step, axis), v, turn(v, step, axis))


def x_low(v):
    return jnp.concatenate([v[:1], v[:-1]], axis=0)


def x_high(v):
    return jnp.concatenate([v[1:], jnp.zeros_like(v[:1])], axis=0)


def x_pair(v):
    return jnp.sum(v.reshape((v.shape[0] // 2, 2) + v.shape[1:]), axis=1)


def x_even(v):
    return v.reshape((v.shape[0] // 2, 2) + v.shape[1:])[:, 0]


def x_repeat(v):
    size = v.shape[0]
    wide = jnp.broadcast_to(v[:, None], (size, 2) + v.shape[1:])
    return wide.reshape((2 * size,) + v.shape[1:])


def operate(v, storage, wx, wy, wz, sy, sz):
    fx = wx * (v - x_low(v))
    fy = wy * (v - turn(v, sy, 1))
    fz = wz * (v - turn(v, sz, 2))
    flux = (fx - x_high(fx)) + (fy - turn(fy, -sy, 1)) + (fz - turn(fz, -sz, 2))
    return storage * v + flux


def relax_factor(storage, wx, wy, wz, sy, sz):
    diagonal = storage + wx + x_high(wx) + wy + turn(wy, -sy, 1) + wz + turn(wz, -sz, 2)
    return jnp.where(diagonal > 0.0, OMEGA / diagonal, 0.0)


def restrict(v, sy, sz):
    return pair_sum(pair_sum(x_pair(v), sy, 1), sz, 2)


def coarsen(storage, wx, wy, wz, sy, sz):
    return (
        restrict(storage, sy, sz),
        pair_sum(pair_sum(x_even(wx), sy, 1), sz, 2),
        pair_low(pair_sum(x_pair(wy), sz, 2), sy, 1),
        pair_low(pair_sum(x_pair(wz), sy, 1), sz, 2),
    )


def operate_rows(v_ref, s_ref, wx_ref, wy_ref, wz_ref, at, size):
    v = v_ref[pl.ds(at, size)]
    wx = wx_ref[pl.ds(at, size)]
    fy = wy_ref[pl.ds(at, size)] * (v - turn(v, 1, 1))
    fz = wz_ref[pl.ds(at, size)] * (v - turn(v, 1, 2))
    flux = wx * (v - v_ref[pl.ds(at - 1, size)])
    flux = flux - wx_ref[pl.ds(at + 1, size)] * (v_ref[pl.ds(at + 1, size)] - v)
    flux = flux + (fy - turn(fy, -1, 1)) + (fz - turn(fz, -1, 2))
    return v, s_ref[pl.ds(at, size)] * v + flux


def inside_grid(at, size):
    shape = (size, WY, NZ)
    gx = BX * lax.axis_index("tile") - (WX - BX) // 2 + (at - 1) + iota(shape, 0)
    gy = BY * lax.axis_index("group") - (WY - BY) // 2 + iota(shape, 1)
    return (
        (gx >= 0)
        & (gx < BX * lax.axis_size("tile"))
        & (gy >= 0)
        & (gy < BY * lax.axis_size("group"))
    )


def blank_ends(ref):
    ref[0] = jnp.zeros((WY, NZ), F32)
    ref[PX - 1] = jnp.zeros((WY, NZ), F32)


def pack_level2(v):
    sub, lane = iota(v.shape, 1), iota(v.shape, 2)
    chosen = (sub >= 8) & (sub < 24) & (sub % 4 == 0) & ((sub - 8) // 4 == lane % 4)
    return jnp.sum(jnp.where(chosen, v, 0.0), axis=1)


def send_level2(msg_ref, fields):
    rows = [pack_level2(v[2:4]) for v in fields]
    spare = msg_ref.shape[1] - 2 * len(rows)
    rows.append(jnp.zeros((spare, NZ), F32))
    whole = jnp.concatenate(rows, axis=0)
    for peer in range(msg_ref.shape[0]):
        msg_ref[peer] = whole


def descend_top(r_ref, e1_ref, e2_ref, s_ref, wx_ref, wy_ref, wz_ref, di_ref, r1_ref, each_pair):
    def second(i, carry):
        at = 1 + 2 * i
        v, av = operate_rows(e1_ref, s_ref, wx_ref, wy_ref, wz_ref, at, 2)
        e2_ref[pl.ds(at, 2)] = v + di_ref[pl.ds(at, 2)] * (r_ref[pl.ds(at, 2)] - av)
        return carry

    lax.fori_loop(0, WX // 2, second, 0)

    def third(i, carry):
        at = 1 + 2 * i
        _, av = operate_rows(e2_ref, s_ref, wx_ref, wy_ref, wz_ref, at, 2)
        r1_ref[pl.ds(i, 1)] = restrict(r_ref[pl.ds(at, 2)] - av, 1, 1)
        each_pair(i, at)
        return carry

    lax.fori_loop(0, WX // 2, third, 0)


def descend_second(r1, s1, wx1, wy1, wz1, di1):
    first = r1 * di1
    second = first + di1 * (r1 - operate(first, s1, wx1, wy1, wz1, 2, 2))
    defect = r1 - operate(second, s1, wx1, wy1, wz1, 2, 2)
    return second, restrict(defect, 2, 2)


def assemble_kernel(
    core, ylow, yhigh, ks_ref, alpha_ref, shape_ref, span_ref,
    r_ref, s_ref, di_ref, wx_ref, wy_ref, wz_ref, e2_ref,
    r1_ref, s1_ref, di1_ref, wx1_ref, wy1_ref, wz1_ref, e21_ref, msg_ref,
    h_ref, k_ref, m_ref, e1_ref,
):
    def window(field, at):
        row = pl.ds(at - 1, 1)
        return jnp.concatenate([ylow[field, row], core[field, row], yhigh[field, row]], axis=1)

    for ref in (h_ref, k_ref, s_ref, wx_ref, wy_ref, wz_ref, di_ref, r_ref, e1_ref, e2_ref):
        blank_ends(ref)

    def soils(i, carry):
        at = 1 + i
        inside = inside_grid(at, 1)
        head = jnp.where(inside, window(0, at), -1.0)
        old = jnp.where(inside, window(1, at), -1.0)
        soil = window(2, at)
        ks = jnp.full(soil.shape, ks_ref[0])
        alpha = jnp.full(soil.shape, alpha_ref[0])
        shape_n = jnp.full(soil.shape, shape_ref[0])
        span = jnp.full(soil.shape, span_ref[0])
        for kind in range(1, SOILS):
            hit = soil == float(kind)
            ks = jnp.where(hit, ks_ref[kind], ks)
            alpha = jnp.where(hit, alpha_ref[kind], alpha)
            shape_n = jnp.where(hit, shape_ref[kind], shape_n)
            span = jnp.where(hit, span_ref[kind], span)
        shape_m = 1.0 - 1.0 / shape_n
        power = jnp.exp(shape_n * jnp.log(alpha * -head))
        old_power = jnp.exp(shape_n * jnp.log(alpha * -old))
        saturation = jnp.exp(-shape_m * jnp.log1p(power))
        old_saturation = jnp.exp(-shape_m * jnp.log1p(old_power))
        portion = 1.0 / (1.0 + power)
        factor = 1.0 - jnp.exp(shape_m * jnp.log(power / (1.0 + power)))
        conductivity = ks * jnp.sqrt(saturation) * factor * factor
        capacity = span * shape_m * shape_n * power / -head * saturation * portion
        row = pl.ds(at, 1)
        h_ref[row] = head
        k_ref[row] = jnp.where(inside, conductivity, 0.0)
        s_ref[row] = capacity + STORAGE
        m_ref[row] = span * (saturation - old_saturation) + STORAGE * (head - old)
        return carry

    lax.fori_loop(0, WX, soils, 0)

    def harmonic(a, b):
        total = a + b
        return jnp.where(total > 0.0, 2.0 * a * b / total, 0.0)

    def faces(i, carry):
        at = 1 + 2 * i
        k = k_ref[pl.ds(at, 2)]
        wx_ref[pl.ds(at, 2)] = harmonic(k, k_ref[pl.ds(at - 1, 2)])
        wy_ref[pl.ds(at, 2)] = harmonic(k, turn(k, 1, 1))
        wz = harmonic(k, turn(k, 1, 2))
        wz_ref[pl.ds(at, 2)] = jnp.where(iota(wz.shape, 2) == 0, 0.0, wz)
        return carry

    lax.fori_loop(0, WX // 2, faces, 0)

    def right_side(i, carry):
        at = 1 + 2 * i
        rows = pl.ds(at, 2)
        h, wx, wy, wz = h_ref[rows], wx_ref[rows], wy_ref[rows], wz_ref[rows]
        wx_up = wx_ref[pl.ds(at + 1, 2)]
        fy = wy * (h - turn(h, 1, 1))
        fz = wz * (h - turn(h, 1, 2) + 1.0)
        flux = wx * (h - h_ref[pl.ds(at - 1, 2)]) - wx_up * (h_ref[pl.ds(at + 1, 2)] - h)
        flux = flux + (fy - turn(fy, -1, 1)) + (fz - turn(fz, -1, 2))
        rhs = jnp.where(inside_grid(at, 2), -(m_ref[rows] + flux), 0.0)
        diagonal = s_ref[rows] + wx + wx_up + wy + turn(wy, -1, 1) + wz + turn(wz, -1, 2)
        di = OMEGA / diagonal
        r_ref[rows] = rhs
        di_ref[rows] = di
        e1_ref[rows] = rhs * di
        return carry

    lax.fori_loop(0, WX // 2, right_side, 0)

    def bands(i, at):
        rows = pl.ds(at, 2)
        s1, wx1, wy1, wz1 = coarsen(s_ref[rows], wx_ref[rows], wy_ref[rows], wz_ref[rows], 1, 1)
        row = pl.ds(i, 1)
        s1_ref[row], wx1_ref[row], wy1_ref[row], wz1_ref[row] = s1, wx1, wy1, wz1

    descend_top(r_ref, e1_ref, e2_ref, s_ref, wx_ref, wy_ref, wz_ref, di_ref, r1_ref, bands)

    s1, wx1, wy1, wz1 = s1_ref[...], wx1_ref[...], wy1_ref[...], wz1_ref[...]
    di1 = relax_factor(s1, wx1, wy1, wz1, 2, 2)
    di1_ref[...] = di1
    e21, r2 = descend_second(r1_ref[...], s1, wx1, wy1, wz1, di1)
    e21_ref[...] = e21
    send_level2(msg_ref, (r2,) + coarsen(s1, wx1, wy1, wz1, 2, 2))


def again_kernel(
    core, ylow, yhigh, rhs_ref, s_ref, di_ref, wx_ref, wy_ref, wz_ref,
    s1_ref, di1_ref, wx1_ref, wy1_ref, wz1_ref,
    u_ref, r_ref, e2_ref, r1_ref, e21_ref, msg_ref, pre_ref, e1_ref,
):
    for ref in (pre_ref, u_ref, r_ref, e1_ref, e2_ref):
        blank_ends(ref)
    pre_ref[1 : PX - 1, 0:8, :] = ylow[...]
    pre_ref[1 : PX - 1, 8:24, :] = core[...]
    pre_ref[1 : PX - 1, 24:32, :] = yhigh[...]

    def post(i, carry):
        at = 1 + 2 * i
        rows = pl.ds(at, 2)
        v, av = operate_rows(pre_ref, s_ref, wx_ref, wy_ref, wz_ref, at, 2)
        u_ref[rows] = v + di_ref[rows] * (rhs_ref[rows] - av)
        return carry

    lax.fori_loop(0, WX // 2, post, 0)

    def remain(i, carry):
        at = 1 + 2 * i
        rows = pl.ds(at, 2)
        _, av = operate_rows(u_ref, s_ref, wx_ref, wy_ref, wz_ref, at, 2)
        left = rhs_ref[rows] - av
        r_ref[rows] = left
        e1_ref[rows] = left * di_ref[rows]
        return carry

    lax.fori_loop(0, WX // 2, remain, 0)
    descend_top(
        r_ref, e1_ref, e2_ref, s_ref, wx_ref, wy_ref, wz_ref, di_ref, r1_ref, lambda i, at: None
    )
    e21, r2 = descend_second(
        r1_ref[...], s1_ref[...], wx1_ref[...], wy1_ref[...], wz1_ref[...], di1_ref[...]
    )
    e21_ref[...] = e21
    send_level2(msg_ref, (r2,))


def finish_kernel(
    core, ylow, yhigh, rhs_ref, s_ref, di_ref, wx_ref, wy_ref, wz_ref, u_ref, r_ref,
    out_ref, left_ref, pre_ref, v_ref,
):
    blank_ends(pre_ref)
    pre_ref[1 : PX - 1, 0:8, :] = ylow[...]
    pre_ref[1 : PX - 1, 8:24, :] = core[...]
    pre_ref[1 : PX - 1, 24:32, :] = yhigh[...]

    def post(i, carry):
        at = 7 + 2 * i
        rows = pl.ds(at, 2)
        v, av = operate_rows(pre_ref, s_ref, wx_ref, wy_ref, wz_ref, at, 2)
        v_ref[rows] = u_ref[rows] + v + di_ref[rows] * (r_ref[rows] - av)
        return carry

    lax.fori_loop(0, BX // 2 + 2, post, 0)

    def remain(i, carry):
        at = 9 + 2 * i
        rows = pl.ds(at, 2)
        v, av = operate_rows(v_ref, s_ref, wx_ref, wy_ref, wz_ref, at, 2)
        left = rhs_ref[rows] - av
        out_ref[pl.ds(2 * i, 2)] = v[:, 8:24]
        left_ref[pl.ds(2 * i, 2)] = left[:, 8:24]
        return carry

    lax.fori_loop(0, BX // 2, remain, 0)


def unpack_level2(field, own, low, high):
    tiles = own.shape[0]
    shape = (tiles, 16, NZ)
    sub, lane = iota(shape, 1), iota(shape, 2)
    halves = []
    for half in range(2):
        at = 2 * field + half

        def spread(ref, at=at):
            return jnp.broadcast_to(ref[:, at : at + 1, :], shape)

        v = jnp.where(sub < 4, spread(low), jnp.where(sub < 8, spread(own), spread(high)))
        v = jnp.where((lane % 4 == sub % 4) & (sub < 12), v, 0.0)
        halves.append(pair_sum(pair_sum(v, 1, 2), 2, 2))
    return jnp.stack(halves, axis=1).reshape((2 * tiles, 16, NZ))


def pack_level3(v):
    sub, lane = iota((16, NZ), 0), iota((16, NZ), 1)
    rows = []
    for j in range(v.shape[0] // 4):
        total = jnp.zeros((16, NZ), F32)
        for q in range(4):
            chosen = ((sub == 4) & (lane % 8 == 2 * q)) | ((sub == 6) & (lane % 8 == 2 * q + 1))
            total = total + jnp.where(chosen, v[4 * j + q], 0.0)
        rows.append(jnp.sum(total, axis=0, keepdims=True))
    return rows


def send_level3(msg_ref, fields):
    rows = [row for v in fields for row in pack_level3(v)]
    rows.append(jnp.zeros((msg_ref.shape[1] - len(rows), NZ), F32))
    whole = jnp.concatenate(rows, axis=0)
    for peer in range(msg_ref.shape[0]):
        msg_ref[peer] = whole


def descend_third(r2, s2, wx2, wy2, wz2, di2):
    first = r2 * di2
    second = first + di2 * (r2 - operate(first, s2, wx2, wy2, wz2, 1, 4))
    return second, restrict(r2 - operate(second, s2, wx2, wy2, wz2, 1, 4), 1, 4)


def third_kernel(
    own, low, high, r2_ref, s2_ref, di2_ref, wx2_ref, wy2_ref, wz2_ref, e22_ref, msg_ref
):
    r2, s2, wx2, wy2, wz2 = (unpack_level2(f, own, low, high) for f in range(5))
    di2 = relax_factor(s2, wx2, wy2, wz2, 1, 4)
    r2_ref[...], s2_ref[...], di2_ref[...] = r2, s2, di2
    wx2_ref[...], wy2_ref[...], wz2_ref[...] = wx2, wy2, wz2
    e22, r3 = descend_third(r2, s2, wx2, wy2, wz2, di2)
    e22_ref[...] = e22
    send_level3(msg_ref, (r3,) + coarsen(s2, wx2, wy2, wz2, 1, 4))


def third_again_kernel(
    own, low, high, s2_ref, di2_ref, wx2_ref, wy2_ref, wz2_ref, r2_ref, e22_ref, msg_ref
):
    r2 = unpack_level2(0, own, low, high)
    r2_ref[...] = r2
    e22, r3 = descend_third(
        r2, s2_ref[...], wx2_ref[...], wy2_ref[...], wz2_ref[...], di2_ref[...]
    )
    e22_ref[...] = e22
    send_level3(msg_ref, (r3,))


def third_x_low(v):
    inner = iota(v.shape, 2) % 8 >= 2
    return jnp.where(inner, turn(v, 2, 2), turn(x_low(v), -6, 2))


def third_x_high(v):
    inner = iota(v.shape, 2) % 8 < 6
    return jnp.where(inner, turn(v, -2, 2), turn(x_high(v), 6, 2))


def third_y_low(v):
    return jnp.where(iota(v.shape, 2) % 2 == 1, turn(v, 1, 2), turn(turn(v, 1, 1), -1, 2))


def third_y_high(v):
    return jnp.where(iota(v.shape, 2) % 2 == 0, turn(v, -1, 2), turn(turn(v, -1, 1), 1, 2))


def solve_third(r3, s3, wx3, wy3, wz3):
    inner = s3 + wx3 + third_x_high(wx3) + wz3 + turn(wz3, -8, 2)
    di = OMEGA / (inner + wy3 + third_y_high(wy3))
    above = jnp.sum(r3, axis=1, keepdims=True)
    below = jnp.sum(inner, axis=1, keepdims=True)
    line = pair_sum(jnp.broadcast_to(above, r3.shape), 1, 2)
    line = line / pair_sum(jnp.broadcast_to(below, r3.shape), 1, 2)
    v = line
    for _ in range(COARSE_SWEEPS):
        fx = wx3 * (v - third_x_low(v))
        fy = wy3 * (v - third_y_low(v))
        fz = wz3 * (v - turn(v, 8, 2))
        flux = (fx - third_x_high(fx)) + (fy - third_y_high(fy)) + (fz - turn(fz, -8, 2))
        v = v + di * (r3 - (s3 * v + flux))
    return v


def spread_third(v):
    group = lax.axis_index("group")
    dev = iota(v.shape, 1)
    near = [
        jnp.sum(jnp.where(dev == group + off, v, 0.0), axis=1, keepdims=True) for off in (-1, 0, 1)
    ]
    shape = (v.shape[0], 16, NZ)
    sub, lane = iota(shape, 1), iota(shape, 2)
    low, own, high = (jnp.broadcast_to(part, shape) for part in near)
    rows = jnp.where(sub < 4, low, jnp.where(sub < 8, own, high))
    parts = []
    for q in range(4):
        chosen = (lane % 8 == 2 * q + (sub % 4) // 2) & (sub < 12)
        parts.append(jnp.where(chosen, rows, 0.0))
    wide = jnp.stack(parts, axis=1).reshape((4 * v.shape[0], 16, NZ))
    return pair_sum(pair_sum(pair_sum(wide, 1, 2), 2, 2), 4, 2)


def near_tiles(v):
    tile = lax.axis_index("tile")
    parts = []
    for off in (-1, 0, 1):
        total = jnp.zeros((2,) + v.shape[1:], F32)
        for t in range(v.shape[0] // 2):
            total = total + jnp.where(tile + off == t, v[2 * t : 2 * t + 2], 0.0)
        parts.append(total)
    return jnp.concatenate(parts, axis=0)


def widen_y(v):
    shape = (v.shape[0], 8, NZ)
    sub = iota(shape, 1)
    parts = []
    for at in (2, 4, 6, 8):
        first = jnp.broadcast_to(v[:, at : at + 1], shape)
        second = jnp.broadcast_to(v[:, at + 1 : at + 2], shape)
        parts.append(jnp.where(sub < 4, first, second))
    return jnp.concatenate(parts, axis=1)


def climb_kernel(
    r3_ref, bands3_ref, r2_ref, s2_ref, di2_ref, wx2_ref, wy2_ref, wz2_ref, e22_ref,
    r1_ref, s1_ref, di1_ref, wx1_ref, wy1_ref, wz1_ref, e21_ref, e2_ref, pre_ref,
    *, groups, thirds, r3_rows, band_rows,
):
    def field(ref, f, rows):
        parts = [ref[pl.ds(thirds * f + j, groups, stride=rows), :] for j in range(thirds)]
        return jnp.stack(parts, axis=0)

    r3 = field(r3_ref, 0, r3_rows)
    s3, wx3, wy3, wz3 = (field(bands3_ref, f, band_rows) for f in range(1, 5))
    corr3 = solve_third(r3, s3, wx3, wy3, wz3)
    v = e22_ref[...] + x_repeat(spread_third(corr3))
    v = v + di2_ref[...] * (
        r2_ref[...]
        - operate(v, s2_ref[...], wx2_ref[...], wy2_ref[...], wz2_ref[...], 1, 4)
    )
    corr2 = widen_y(near_tiles(v))
    v = e21_ref[...] + x_repeat(corr2)
    v = v + di1_ref[...] * (
        r1_ref[...]
        - operate(v, s1_ref[...], wx1_ref[...], wy1_ref[...], wz1_ref[...], 2, 2)
    )
    own = x_repeat(v[4:8])
    pre_ref[...] = e2_ref[9:17, 8:24, :] + own[:, 8:24, :]


def call(body, outs, operands, scratch=(), smem=()):
    vmem = pl.BlockSpec(memory_space=pltpu.VMEM)
    return pl.pallas_call(
        body,
        out_shape=[jax.ShapeDtypeStruct(shape, F32) for shape in outs],
        in_specs=[
            pl.BlockSpec(memory_space=pltpu.SMEM) if i in smem else vmem
            for i in range(len(operands))
        ],
        out_specs=[vmem] * len(outs),
        scratch_shapes=[pltpu.VMEM(shape, F32) for shape in scratch],
        compiler_params=pltpu.CompilerParams(vmem_limit_bytes=48 * 1024 * 1024),
    )(*operands)


def beside(to_low, to_high, axis):
    ends = lax.axis_size(axis) - 1
    from_low = lax.ppermute(to_high, axis, [(i, i + 1) for i in range(ends)])
    from_high = lax.ppermute(to_low, axis, [(i + 1, i) for i in range(ends)])
    return from_low, from_high


def surround(cells, dim):
    low, high = beside(cells, cells, "tile")
    core = jnp.concatenate([low, cells, high], axis=dim)
    ydim = dim + 1
    first = lax.slice_in_dim(core, 0, 8, axis=ydim)
    last = lax.slice_in_dim(core, BY - 8, BY, axis=ydim)
    ylow, yhigh = beside(first, last, "group")
    return core, ylow, yhigh


def everyone(blocks, axis):
    return lax.all_to_all(blocks, axis, 0, 0, tiled=True)


def shards(pressure_head, old_head, soil_type, conduct_sat, alpha_param, shape_param, water_span):
    tiles, groups = lax.axis_size("tile"), lax.axis_size("group")
    thirds = tiles // 4
    top, one, two = (PX, WY, NZ), (L1X, WY, NZ), (2 * tiles, 16, NZ)
    band_rows, r3_rows = -(-5 * thirds // 8) * 8, -(-thirds // 8) * 8

    raw = jnp.stack([pressure_head, old_head, soil_type.astype(F32)])
    core, ylow, yhigh = surround(raw, 1)
    rhs, s0, di0, wx0, wy0, wz0, e2, r1, s1, di1, wx1, wy1, wz1, e21, msg = call(
        assemble_kernel,
        [top] * 7 + [one] * 7 + [(tiles, 16, NZ)],
        [core, ylow, yhigh, conduct_sat, alpha_param, shape_param, water_span],
        [top] * 4,
        smem=(3, 4, 5, 6),
    )
    bands0 = [s0, di0, wx0, wy0, wz0]
    bands1 = [s1, di1, wx1, wy1, wz1]

    own = everyone(msg, "tile")
    low, high = beside(own, own, "group")
    r2, s2, di2, wx2, wy2, wz2, e22, msg = call(
        third_kernel, [two] * 7 + [(groups, band_rows, NZ)], [own, low, high]
    )
    bands2 = [s2, di2, wx2, wy2, wz2]
    bands3 = everyone(msg, "group").reshape(groups * band_rows, NZ)
    climb = functools.partial(climb_kernel, groups=groups, thirds=thirds, band_rows=band_rows)
    (pre,) = call(
        functools.partial(climb, r3_rows=band_rows),
        [(BX, BY, NZ)],
        [bands3, bands3, r2, *bands2, e22, r1, *bands1, e21, e2],
    )

    core, ylow, yhigh = surround(pre, 0)
    u, rem, e2, r1, e21, msg = call(
        again_kernel,
        [top] * 3 + [one] * 2 + [(tiles, 8, NZ)],
        [core, ylow, yhigh, rhs, *bands0, *bands1],
        [top] * 2,
    )
    own = everyone(msg, "tile")
    low, high = beside(own, own, "group")
    r2, e22, msg = call(
        third_again_kernel, [two] * 2 + [(groups, r3_rows, NZ)], [own, low, high, *bands2]
    )
    r3 = everyone(msg, "group").reshape(groups * r3_rows, NZ)
    (pre,) = call(
        functools.partial(climb, r3_rows=r3_rows),
        [(BX, BY, NZ)],
        [r3, bands3, r2, *bands2, e22, r1, *bands1, e21, e2],
    )

    core, ylow, yhigh = surround(pre, 0)
    update, remainder = call(
        finish_kernel,
        [(BX, BY, NZ)] * 2,
        [core, ylow, yhigh, rhs, *bands0, u, rem],
        [top] * 2,
    )
    return update, remainder


def solution(mesh):
    spec = P("tile", "group", None)
    return jax.shard_map(
        shards,
        mesh=mesh,
        in_specs=(spec, spec, spec, P(), P(), P(), P()),
        out_specs=(spec, spec),
        check_vma=False,
    )
```

time: 688 us -> 203 us (0.30)
  the two profiles are of different devices: /device:TPU:31 before, /device:TPU:1 now
where the time goes in v1:
time: 203 us; the launch traced here: 201 us
  blocking collectives  95.5 us (47%)
  starting transfers between devices  58.9 us (29%)
  Pallas kernels  29.3 us (14%)
  waiting for transfers between devices  14.8 us (7%)
    all_to_all x4, blocking collectives, everyone(): return lax.all_to_all(blocks, axis, 0, 0, tiled=True)  95.5 us
    ppermute x8, starting transfers between devices, beside(): from_low = lax.ppermute(to_high, axis, [(i, i + 1) for i in range(ends)])  32.3 us
    pallas_call x7, Pallas kernels, call(): pl.pallas_call(body, out_shape=[jax.ShapeDtypeStruct(shape, F32) for shap...  29.3 us
    ppermute x8, starting transfers between devices, beside(): from_high = lax.ppermute(to_low, axis, [(i + 1, i) for i in range(ends)])  26.6 us
    ppermute x8, waiting for transfers between devices, beside(): from_low = lax.ppermute(to_high, axis, [(i, i + 1) for i in range(ends)])  12.6 us
  transfers between devices with their start and end apart: 16, of which 12 were waited for; matrix products, arithmetic and copies ran while one was open for 0% of the time, Pallas kernels for 0%

profile of v1, /device:TPU:1, one launch (start us, length us, event | category | flops | bytes accessed | tf_op | source)
XLA Modules:
  0.0 200.5 jit_solution(8616529577028297809)
XLA Ops:
  2.9 5.5 %collective-permute-start = (f32[3,8,16,128]{3,2,1,0:T(8,128)S(1)}, f32[3,8,16,128]{3,2,1,0:T(8,128)S(1)}, u32[]{:S(2)}, u32[]{:S(2)}) collective-permute-start(f32[3,8,16,128]{3,2,1,0:T(8,128)S(1)} %pad_maximum_fusion.1), channel_id=1, source_target_pairs={{0,64},{64,128},{128,192},{192,256},{256,320},{320,384},{384,448},... | collective-permute-start | bytes 589832 | tf_op jit(solution)/shard_map/ppermute | solution.py:513
  11.1 12.2 %collective-permute-start.3 = (f32[3,24,8,128]{3,2,1,0:T(8,128)S(1)}, f32[3,24,8,128]{3,2,1,0:T(8,128)S(1)}, u32[]{:S(2)}, u32[]{:S(2)}) collective-permute-start(f32[3,24,8,128]{3,2,1,0:T(8,128)S(1)} %get-tuple-element.66), channel_id=1, source_target_pairs={{1,0},{2,1},{3,2},{4,3},{5,4},{6,5},{7,6},{8,7},{9,8},{10,9},{11,1... | collective-permute-start | bytes 884744 | tf_op jit(solution)/shard_map/ppermute | solution.py:514
  23.3 1.9 collective-permute-start.2
  25.2 3.6 %collective-permute-done.2.ylow = f32[3,24,8,128]{3,2,1,0:T(8,128)S(1)} collective-permute-done((f32[3,24,8,128]{3,2,1,0:T(8,128)S(1)}, f32[3,24,8,128]{3,2,1,0:T(8,128)S(1)}, u32[]{:S(2)}, u32[]{:S(2)}) %collective-permute-start.2) | collective-permute-done | bytes 294944 | tf_op jit(solution)/shard_map/ppermute | solution.py:513
  28.9 11.4 %shard_map.86 = (f32[26,32,128]{2,1,0:T(8,128)S(1)}, f32[26,32,128]{2,1,0:T(8,128)S(1)}, f32[26,32,128]{2,1,0:T(8,128)S(1)}, f32[26,32,128]{2,1,0:T(8,128)S(1)},...) custom-call(f32[3,24,16,128]{3,2,1,0:T(8,128)S(1)} %pad_maximum_fusi, ...), custom_call_target="tpu_custom_call" | custom-call | tf_op jit(solution)/shard_map/pallas_call | solution.py:498
  40.3 19.9 %all_to_all.20.own = f32[12,16,128]{2,1,0:T(8,128)S(1)} all-to-all(f32[12,16,128]{2,1,0:T(8,128)S(1)} %get-tuple-element.34), channel_id=1, replica_groups=mesh['tile'=12,'group'=64] {'tile'}, dimensions={0} | all-to-all | bytes 196608 | tf_op jit(solution)/shard_map/all_to_all | solution.py:529
  60.2 1.9 collective-permute-start.5
  62.1 6.1 %collective-permute-start.4 = (f32[12,16,128]{2,1,0:T(8,128)S(1)}, f32[12,16,128]{2,1,0:T(8,128)S(1)}, u32[]{:S(2)}, u32[]{:S(2)}) collective-permute-start(f32[12,16,128]{2,1,0:T(8,128)S(1)} %all_to_all.20.own), channel_id=1, source_target_pairs={{0,1},{1,2},{2,3},{3,4},{4,5},{5,6},{6,7},{7,8},{8,9},{9,10},{10,1... | collective-permute-start | bytes 294920 | tf_op jit(solution)/shard_map/ppermute | solution.py:513
  69.8 2.1 %shard_map.87 = (f32[24,16,128]{2,1,0:T(8,128)S(1)}, f32[24,16,128]{2,1,0:T(8,128)S(1)}, f32[24,16,128]{2,1,0:T(8,128)S(1)}, f32[24,16,128]{2,1,0:T(8,128)S(1)},...) custom-call(f32[12,16,128]{2,1,0:T(8,128)S(1)} %all_to_all.20.own, ...), custom_call_target="tpu_custom_call" | custom-call | tf_op jit(solution)/shard_map/pallas_call | solution.py:498
  71.9 34.0 %all_to_all.21 = f32[64,16,128]{2,1,0:T(8,128)S(1)} all-to-all(f32[64,16,128]{2,1,0:T(8,128)S(1)} %get-tuple-element.35), channel_id=1, replica_groups=mesh['tile'=12,'group'=64] {'group'}, dimensions={0} | all-to-all | bytes 1048576 | tf_op jit(solution)/shard_map/all_to_all | solution.py:529
  105.9 2.0 shard_map.88
  109.2 4.0 %collective-permute-start.6 = (f32[8,16,128]{2,1,0:T(8,128)S(1)}, f32[8,16,128]{2,1,0:T(8,128)S(1)}, u32[]{:S(2)}, u32[]{:S(2)}) collective-permute-start(f32[8,16,128]{2,1,0:T(8,128)S(1)} %shard_map.88), channel_id=1, source_target_pairs={{0,64},{64,128},{128,192},{192,256},{256,320},{320,384},{384,448},... | collective-permute-start | bytes 196616 | tf_op jit(solution)/shard_map/ppermute | solution.py:513
  114.6 3.4 %collective-permute-start.9 = (f32[24,8,128]{2,1,0:T(8,128)S(1)}, f32[24,8,128]{2,1,0:T(8,128)S(1)}, u32[]{:S(2)}, u32[]{:S(2)}) collective-permute-start(f32[24,8,128]{2,1,0:T(8,128)S(1)} %get-tuple-element.70), channel_id=1, source_target_pairs={{1,0},{2,1},{3,2},{4,3},{5,4},{6,5},{7,6},{8,7},{9,8},{10,9},{11,1... | collective-permute-start | bytes 294920 | tf_op jit(solution)/shard_map/ppermute | solution.py:514
  118.0 3.0 %collective-permute-start.8 = (f32[24,8,128]{2,1,0:T(8,128)S(1)}, f32[24,8,128]{2,1,0:T(8,128)S(1)}, u32[]{:S(2)}, u32[]{:S(2)}) collective-permute-start(f32[24,8,128]{2,1,0:T(8,128)S(1)} %get-tuple-element.71), channel_id=1, source_target_pairs={{0,1},{1,2},{2,3},{3,4},{4,5},{5,6},{6,7},{7,8},{8,9},{9,10},{10,1... | collective-permute-start | bytes 294920 | tf_op jit(solution)/shard_map/ppermute | solution.py:513
  122.7 8.8 %shard_map.89 = (f32[26,32,128]{2,1,0:T(8,128)S(1)}, f32[26,32,128]{2,1,0:T(8,128)S(1)}, f32[26,32,128]{2,1,0:T(8,128)S(1)}, f32[12,32,128]{2,1,0:T(8,128)S(1)},...) custom-call(f32[24,16,128]{2,1,0:T(8,128)S(1)} %pad_maximum_fusion.2.core, ...), custom_call_target="tpu_custom_call" | custom-call | tf_op jit(solution)/shard_map/pallas_call | solution.py:498
  131.5 15.3 %all_to_all.22.own = f32[12,8,128]{2,1,0:T(8,128)S(1)} all-to-all(f32[12,8,128]{2,1,0:T(8,128)S(1)} %get-tuple-element.57), channel_id=1, replica_groups=mesh['tile'=12,'group'=64] {'tile'}, dimensions={0} | all-to-all | bytes 98304 | tf_op jit(solution)/shard_map/all_to_all | solution.py:529
  146.8 1.9 collective-permute-start.11
  148.7 5.5 %collective-permute-start.10 = (f32[12,8,128]{2,1,0:T(8,128)S(1)}, f32[12,8,128]{2,1,0:T(8,128)S(1)}, u32[]{:S(2)}, u32[]{:S(2)}) collective-permute-start(f32[12,8,128]{2,1,0:T(8,128)S(1)} %all_to_all.22.own), channel_id=1, source_target_pairs={{0,1},{1,2},{2,3},{3,4},{4,5},{5,6},{6,7},{7,8},{8,9},{9,10},{10,1... | collective-permute-start | bytes 147464 | tf_op jit(solution)/shard_map/ppermute | solution.py:513
  156.1 26.3 %all_to_all.23 = f32[64,8,128]{2,1,0:T(8,128)S(1)} all-to-all(f32[64,8,128]{2,1,0:T(8,128)S(1)} %get-tuple-element.58), channel_id=1, replica_groups=mesh['tile'=12,'group'=64] {'group'}, dimensions={0} | all-to-all | bytes 524288 | tf_op jit(solution)/shard_map/all_to_all | solution.py:529
  182.4 2.0 shard_map.91
  185.7 4.0 %collective-permute-start.12 = (f32[8,16,128]{2,1,0:T(8,128)S(1)}, f32[8,16,128]{2,1,0:T(8,128)S(1)}, u32[]{:S(2)}, u32[]{:S(2)}) collective-permute-start(f32[8,16,128]{2,1,0:T(8,128)S(1)} %shard_map.91), channel_id=1, source_target_pairs={{0,64},{64,128},{128,192},{192,256},{256,320},{320,384},{384,448},... | collective-permute-start | bytes 196616 | tf_op jit(solution)/shard_map/ppermute | solution.py:513
  191.0 3.3 %collective-permute-start.15 = (f32[24,8,128]{2,1,0:T(8,128)S(1)}, f32[24,8,128]{2,1,0:T(8,128)S(1)}, u32[]{:S(2)}, u32[]{:S(2)}) collective-permute-start(f32[24,8,128]{2,1,0:T(8,128)S(1)} %get-tuple-element.68), channel_id=1, source_target_pairs={{1,0},{2,1},{3,2},{4,3},{5,4},{6,5},{7,6},{8,7},{9,8},{10,9},{11,1... | collective-permute-start | bytes 294920 | tf_op jit(solution)/shard_map/ppermute | solution.py:514
  194.3 2.4 %collective-permute-start.14 = (f32[24,8,128]{2,1,0:T(8,128)S(1)}, f32[24,8,128]{2,1,0:T(8,128)S(1)}, u32[]{:S(2)}, u32[]{:S(2)}) collective-permute-start(f32[24,8,128]{2,1,0:T(8,128)S(1)} %get-tuple-element.69), channel_id=1, source_target_pairs={{0,1},{1,2},{2,3},{3,4},{4,5},{5,6},{6,7},{7,8},{8,9},{9,10},{10,1... | collective-permute-start | bytes 294920 | tf_op jit(solution)/shard_map/ppermute | solution.py:513
  198.3 2.2 %shard_map.92 = (f32[8,16,128]{2,1,0:T(8,128)}, f32[8,16,128]{2,1,0:T(8,128)}) custom-call(f32[24,16,128]{2,1,0:T(8,128)S(1)} %pad_maximum_fusion.3.core, f32[24,8,128]{2,1,0:T(8,128)S(1)} %collective-permute-done.14.ylow, f32[24,8,128]{2,1,0:T(8,128)S(1)} %collective-permute-done.15.yhigh, f32[26,32,128]{2,1,0:T(8,128)S(1)} %get-tuple-element.51.rhs_ref, ...), custom_call_target="tpu_custom_call" | custom-call | tf_op jit(solution)/shard_map/pallas_call | solution.py:498
  (39 shorter events, 16.9 us)
Async XLA Ops:
  0.6 0.9 copy-start.4
  0.6 0.9 copy-start.5
  1.6 7.9 %collective-permute-start.1 = (f32[3,8,16,128]{3,2,1,0:T(8,128)S(1)}, f32[3,8,16,128]{3,2,1,0:T(8,128)S(1)}, u32[]{:S(2)}, u32[]{:S(2)}) collective-permute-start(f32[3,8,16,128]{3,2,1,0:T(8,128)S(1)} %pad_maximum_fusion.1), channel_id=1, source_target_pairs={{64,0},{128,64},{192,128},{256,192},{320,256},{384,320},{448,384},... | collective-permute-start | bytes 589832 | tf_op jit(solution)/shard_map/ppermute | solution.py:514
  2.9 8.1 %collective-permute-start = (f32[3,8,16,128]{3,2,1,0:T(8,128)S(1)}, f32[3,8,16,128]{3,2,1,0:T(8,128)S(1)}, u32[]{:S(2)}, u32[]{:S(2)}) collective-permute-start(f32[3,8,16,128]{3,2,1,0:T(8,128)S(1)} %pad_maximum_fusion.1), channel_id=1, source_target_pairs={{0,64},{64,128},{128,192},{192,256},{256,320},{320,384},{384,448},... | collective-permute-start | bytes 589832 | tf_op jit(solution)/shard_map/ppermute | solution.py:513
  11.0 17.9 %copy-start.3 = (f32[12]{0:T(128)S(1)}, f32[12]{0:T(128)}, u32[]{:S(2)}) copy-start(f32[12]{0:T(128)} %span_ref.1) | copy-start | bytes 148
  11.0 17.8 %copy-start = (f32[12]{0:T(128)S(1)}, f32[12]{0:T(128)}, u32[]{:S(2)}) copy-start(f32[12]{0:T(128)} %ks_ref.1) | copy-start | bytes 148
  11.0 17.8 %copy-start.1 = (f32[12]{0:T(128)S(1)}, f32[12]{0:T(128)}, u32[]{:S(2)}) copy-start(f32[12]{0:T(128)} %alpha_ref.1) | copy-start | bytes 148
  11.0 17.8 %copy-start.2 = (f32[12]{0:T(128)S(1)}, f32[12]{0:T(128)}, u32[]{:S(2)}) copy-start(f32[12]{0:T(128)} %shape_ref.1) | copy-start | bytes 148
  11.1 14.2 %collective-permute-start.3 = (f32[3,24,8,128]{3,2,1,0:T(8,128)S(1)}, f32[3,24,8,128]{3,2,1,0:T(8,128)S(1)}, u32[]{:S(2)}, u32[]{:S(2)}) collective-permute-start(f32[3,24,8,128]{3,2,1,0:T(8,128)S(1)} %get-tuple-element.66), channel_id=1, source_target_pairs={{1,0},{2,1},{3,2},{4,3},{5,4},{6,5},{7,6},{8,7},{9,8},{10,9},{11,1... | collective-permute-start | bytes 884744 | tf_op jit(solution)/shard_map/ppermute | solution.py:514
  23.3 5.6 %collective-permute-start.2 = (f32[3,24,8,128]{3,2,1,0:T(8,128)S(1)}, f32[3,24,8,128]{3,2,1,0:T(8,128)S(1)}, u32[]{:S(2)}, u32[]{:S(2)}) collective-permute-start(f32[3,24,8,128]{3,2,1,0:T(8,128)S(1)} %get-tuple-element.67), channel_id=1, source_target_pairs={{0,1},{1,2},{2,3},{3,4},{4,5},{5,6},{6,7},{7,8},{8,9},{9,10},{10,1... | collective-permute-start | bytes 884744 | tf_op jit(solution)/shard_map/ppermute | solution.py:513
  60.2 8.4 %collective-permute-start.5 = (f32[12,16,128]{2,1,0:T(8,128)S(1)}, f32[12,16,128]{2,1,0:T(8,128)S(1)}, u32[]{:S(2)}, u32[]{:S(2)}) collective-permute-start(f32[12,16,128]{2,1,0:T(8,128)S(1)} %all_to_all.20.own), channel_id=1, source_target_pairs={{1,0},{2,1},{3,2},{4,3},{5,4},{6,5},{7,6},{8,7},{9,8},{10,9},{11,1... | collective-permute-start | bytes 294920 | tf_op jit(solution)/shard_map/ppermute | solution.py:514
  62.1 7.7 %collective-permute-start.4 = (f32[12,16,128]{2,1,0:T(8,128)S(1)}, f32[12,16,128]{2,1,0:T(8,128)S(1)}, u32[]{:S(2)}, u32[]{:S(2)}) collective-permute-start(f32[12,16,128]{2,1,0:T(8,128)S(1)} %all_to_all.20.own), channel_id=1, source_target_pairs={{0,1},{1,2},{2,3},{3,4},{4,5},{5,6},{6,7},{7,8},{8,9},{9,10},{10,1... | collective-permute-start | bytes 294920 | tf_op jit(solution)/shard_map/ppermute | solution.py:513
  107.9 5.3 %collective-permute-start.7 = (f32[8,16,128]{2,1,0:T(8,128)S(1)}, f32[8,16,128]{2,1,0:T(8,128)S(1)}, u32[]{:S(2)}, u32[]{:S(2)}) collective-permute-start(f32[8,16,128]{2,1,0:T(8,128)S(1)} %shard_map.88), channel_id=1, source_target_pairs={{64,0},{128,64},{192,128},{256,192},{320,256},{384,320},{448,384},... | collective-permute-start | bytes 196616 | tf_op jit(solution)/shard_map/ppermute | solution.py:514
  109.2 5.3 %collective-permute-start.6 = (f32[8,16,128]{2,1,0:T(8,128)S(1)}, f32[8,16,128]{2,1,0:T(8,128)S(1)}, u32[]{:S(2)}, u32[]{:S(2)}) collective-permute-start(f32[8,16,128]{2,1,0:T(8,128)S(1)} %shard_map.88), channel_id=1, source_target_pairs={{0,64},{64,128},{128,192},{192,256},{256,320},{320,384},{384,448},... | collective-permute-start | bytes 196616 | tf_op jit(solution)/shard_map/ppermute | solution.py:513
  114.6 6.8 %collective-permute-start.9 = (f32[24,8,128]{2,1,0:T(8,128)S(1)}, f32[24,8,128]{2,1,0:T(8,128)S(1)}, u32[]{:S(2)}, u32[]{:S(2)}) collective-permute-start(f32[24,8,128]{2,1,0:T(8,128)S(1)} %get-tuple-element.70), channel_id=1, source_target_pairs={{1,0},{2,1},{3,2},{4,3},{5,4},{6,5},{7,6},{8,7},{9,8},{10,9},{11,1... | collective-permute-start | bytes 294920 | tf_op jit(solution)/shard_map/ppermute | solution.py:514
  118.0 4.6 %collective-permute-start.8 = (f32[24,8,128]{2,1,0:T(8,128)S(1)}, f32[24,8,128]{2,1,0:T(8,128)S(1)}, u32[]{:S(2)}, u32[]{:S(2)}) collective-permute-start(f32[24,8,128]{2,1,0:T(8,128)S(1)} %get-tuple-element.71), channel_id=1, source_target_pairs={{0,1},{1,2},{2,3},{3,4},{4,5},{5,6},{6,7},{7,8},{8,9},{9,10},{10,1... | collective-permute-start | bytes 294920 | tf_op jit(solution)/shard_map/ppermute | solution.py:513
  146.8 7.4 %collective-permute-start.11 = (f32[12,8,128]{2,1,0:T(8,128)S(1)}, f32[12,8,128]{2,1,0:T(8,128)S(1)}, u32[]{:S(2)}, u32[]{:S(2)}) collective-permute-start(f32[12,8,128]{2,1,0:T(8,128)S(1)} %all_to_all.22.own), channel_id=1, source_target_pairs={{1,0},{2,1},{3,2},{4,3},{5,4},{6,5},{7,6},{8,7},{9,8},{10,9},{11,1... | collective-permute-start | bytes 147464 | tf_op jit(solution)/shard_map/ppermute | solution.py:514
  148.7 6.7 %collective-permute-start.10 = (f32[12,8,128]{2,1,0:T(8,128)S(1)}, f32[12,8,128]{2,1,0:T(8,128)S(1)}, u32[]{:S(2)}, u32[]{:S(2)}) collective-permute-start(f32[12,8,128]{2,1,0:T(8,128)S(1)} %all_to_all.22.own), channel_id=1, source_target_pairs={{0,1},{1,2},{2,3},{3,4},{4,5},{5,6},{6,7},{7,8},{8,9},{9,10},{10,1... | collective-permute-start | bytes 147464 | tf_op jit(solution)/shard_map/ppermute | solution.py:513
  184.4 5.3 %collective-permute-start.13 = (f32[8,16,128]{2,1,0:T(8,128)S(1)}, f32[8,16,128]{2,1,0:T(8,128)S(1)}, u32[]{:S(2)}, u32[]{:S(2)}) collective-permute-start(f32[8,16,128]{2,1,0:T(8,128)S(1)} %shard_map.91), channel_id=1, source_target_pairs={{64,0},{128,64},{192,128},{256,192},{320,256},{384,320},{448,384},... | collective-permute-start | bytes 196616 | tf_op jit(solution)/shard_map/ppermute | solution.py:514
  185.7 5.3 %collective-permute-start.12 = (f32[8,16,128]{2,1,0:T(8,128)S(1)}, f32[8,16,128]{2,1,0:T(8,128)S(1)}, u32[]{:S(2)}, u32[]{:S(2)}) collective-permute-start(f32[8,16,128]{2,1,0:T(8,128)S(1)} %shard_map.91), channel_id=1, source_target_pairs={{0,64},{64,128},{128,192},{192,256},{256,320},{320,384},{384,448},... | collective-permute-start | bytes 196616 | tf_op jit(solution)/shard_map/ppermute | solution.py:513
  191.0 6.0 %collective-permute-start.15 = (f32[24,8,128]{2,1,0:T(8,128)S(1)}, f32[24,8,128]{2,1,0:T(8,128)S(1)}, u32[]{:S(2)}, u32[]{:S(2)}) collective-permute-start(f32[24,8,128]{2,1,0:T(8,128)S(1)} %get-tuple-element.68), channel_id=1, source_target_pairs={{1,0},{2,1},{3,2},{4,3},{5,4},{6,5},{7,6},{8,7},{9,8},{10,9},{11,1... | collective-permute-start | bytes 294920 | tf_op jit(solution)/shard_map/ppermute | solution.py:514
  194.3 4.0 %collective-permute-start.14 = (f32[24,8,128]{2,1,0:T(8,128)S(1)}, f32[24,8,128]{2,1,0:T(8,128)S(1)}, u32[]{:S(2)}, u32[]{:S(2)}) collective-permute-start(f32[24,8,128]{2,1,0:T(8,128)S(1)} %get-tuple-element.69), channel_id=1, source_target_pairs={{0,1},{1,2},{2,3},{3,4},{4,5},{5,6},{6,7},{7,8},{8,9},{9,10},{10,1... | collective-permute-start | bytes 294920 | tf_op jit(solution)/shard_map/ppermute | solution.py:513

commit v2 on v1

--- a/solution.py
+++ b/solution.py
@@ -116,38 +116,71 @@
     ref[PX - 1] = jnp.zeros((WY, NZ), F32)
 
 
+def blank_level1(ref, size):
+    ref[0:size] = jnp.zeros((size, WY, NZ), F32)
+    ref[L1X - size :] = jnp.zeros((size, WY, NZ), F32)
+
+
 def pack_level2(v):
     sub, lane = iota(v.shape, 1), iota(v.shape, 2)
     chosen = (sub >= 8) & (sub < 24) & (sub % 4 == 0) & ((sub - 8) // 4 == lane % 4)
     return jnp.sum(jnp.where(chosen, v, 0.0), axis=1)
 
 
-def send_level2(msg_ref, fields):
-    rows = [pack_level2(v[2:4]) for v in fields]
-    spare = msg_ref.shape[1] - 2 * len(rows)
-    rows.append(jnp.zeros((spare, NZ), F32))
+def send(msg_ref, rows):
+    rows = list(rows)
+    parts, height = msg_ref.shape[1:3]
+    spare = parts * height - sum(row.shape[0] for row in rows)
+    if spare:
+        rows.append(jnp.zeros((spare, NZ), F32))
     whole = jnp.concatenate(rows, axis=0)
-    for peer in range(msg_ref.shape[0]):
-        msg_ref[peer] = whole
-
-
-def descend_top(r_ref, e1_ref, e2_ref, s_ref, wx_ref, wy_ref, wz_ref, di_ref, r1_ref, each_pair):
+    for part in range(parts):
+        piece = whole[part * height : (part + 1) * height]
+        for peer in range(msg_ref.shape[0]):
+            msg_ref[peer, part] = piece
+
+
+def pack_bands3(fields):
+    sub, lane = iota((1, WY, NZ), 1), iota((1, WY, NZ), 2)
+    total = jnp.zeros((1, WY, NZ), F32)
+    for f, v in enumerate(fields):
+        chosen = ((sub == 8) & (lane % 8 == 2 * f)) | ((sub == 16) & (lane % 8 == 2 * f + 1))
+        total = total + jnp.where(chosen, v, 0.0)
+    return jnp.sum(total, axis=1)
+
+
+def pack_ring1(v):
+    sub, lane = iota((2, WY, NZ), 1), iota((2, WY, NZ), 2)
+    rows = v[5:7]
+    parts = []
+    for k in range(4):
+        chosen = ((sub == 8 + 4 * k) & (lane % 2 == 0)) | ((sub == 10 + 4 * k) & (lane % 2 == 1))
+        parts.append(jnp.sum(jnp.where(chosen, rows, 0.0), axis=1, keepdims=True))
+    return jnp.concatenate([part[x] for x in range(2) for part in parts], axis=0)
+
+
+def pack_edge1(v):
+    sub, lane = iota((6, WY, NZ), 1), iota((6, WY, NZ), 2)
+    chosen = ((sub == 20) & (lane % 2 == 0)) | ((sub == 10) & (lane % 2 == 1))
+    return jnp.sum(jnp.where(chosen, v[3:9], 0.0), axis=1)
+
+
+def descend_top(r_ref, e1_ref, e2_ref, s_ref, wx_ref, wy_ref, wz_ref, di_ref, r1_ref):
     def second(i, carry):
         at = 1 + 2 * i
         v, av = operate_rows(e1_ref, s_ref, wx_ref, wy_ref, wz_ref, at, 2)
         e2_ref[pl.ds(at, 2)] = v + di_ref[pl.ds(at, 2)] * (r_ref[pl.ds(at, 2)] - av)
         return carry
 
-    lax.fori_loop(0, WX // 2, second, 0)
+    lax.fori_loop(1, WX // 2 - 1, second, 0)
 
     def third(i, carry):
         at = 1 + 2 * i
         _, av = operate_rows(e2_ref, s_ref, wx_ref, wy_ref, wz_ref, at, 2)
         r1_ref[pl.ds(i, 1)] = restrict(r_ref[pl.ds(at, 2)] - av, 1, 1)
-        each_pair(i, at)
-        return carry
-
-    lax.fori_loop(0, WX // 2, third, 0)
+        return carry
+
+    lax.fori_loop(2, WX // 2 - 2, third, 0)
 
 
 def descend_second(r1, s1, wx1, wy1, wz1, di1):
@@ -238,26 +271,34 @@
 
     lax.fori_loop(0, WX // 2, right_side, 0)
 
-    def bands(i, at):
-        rows = pl.ds(at, 2)
+    def bands(i, carry):
+        rows = pl.ds(1 + 2 * i, 2)
         s1, wx1, wy1, wz1 = coarsen(s_ref[rows], wx_ref[rows], wy_ref[rows], wz_ref[rows], 1, 1)
         row = pl.ds(i, 1)
         s1_ref[row], wx1_ref[row], wy1_ref[row], wz1_ref[row] = s1, wx1, wy1, wz1
-
-    descend_top(r_ref, e1_ref, e2_ref, s_ref, wx_ref, wy_ref, wz_ref, di_ref, r1_ref, bands)
+        return carry
+
+    lax.fori_loop(1, WX // 2 - 1, bands, 0)
+    for ref in (s1_ref, wx1_ref, wy1_ref, wz1_ref):
+        blank_level1(ref, 1)
+    blank_level1(r1_ref, 2)
+    descend_top(r_ref, e1_ref, e2_ref, s_ref, wx_ref, wy_ref, wz_ref, di_ref, r1_ref)
 
     s1, wx1, wy1, wz1 = s1_ref[...], wx1_ref[...], wy1_ref[...], wz1_ref[...]
     di1 = relax_factor(s1, wx1, wy1, wz1, 2, 2)
     di1_ref[...] = di1
     e21, r2 = descend_second(r1_ref[...], s1, wx1, wy1, wz1, di1)
     e21_ref[...] = e21
-    send_level2(msg_ref, (r2,) + coarsen(s1, wx1, wy1, wz1, 2, 2))
+    bands2 = coarsen(s1, wx1, wy1, wz1, 2, 2)
+    bands3 = coarsen(*(v[2:4] for v in bands2), 4, 4)
+    rows = [pack_level2(v[2:4]) for v in (r2,) + bands2]
+    send(msg_ref, rows + [pack_bands3(bands3)])
 
 
 def again_kernel(
     core, ylow, yhigh, rhs_ref, s_ref, di_ref, wx_ref, wy_ref, wz_ref,
     s1_ref, di1_ref, wx1_ref, wy1_ref, wz1_ref,
-    u_ref, r_ref, e2_ref, r1_ref, e21_ref, msg_ref, pre_ref, e1_ref,
+    u_ref, r_ref, e2_ref, r1_ref, e21_ref, msg_ref, edge_ref, pre_ref, e1_ref,
 ):
     for ref in (pre_ref, u_ref, r_ref, e1_ref, e2_ref):
         blank_ends(ref)
@@ -283,57 +324,26 @@
         e1_ref[rows] = left * di_ref[rows]
         return carry
 
-    lax.fori_loop(0, WX // 2, remain, 0)
-    descend_top(
-        r_ref, e1_ref, e2_ref, s_ref, wx_ref, wy_ref, wz_ref, di_ref, r1_ref, lambda i, at: None
-    )
+    lax.fori_loop(1, WX // 2 - 1, remain, 0)
+    descend_top(r_ref, e1_ref, e2_ref, s_ref, wx_ref, wy_ref, wz_ref, di_ref, r1_ref)
+    blank_level1(r1_ref, 2)
     e21, r2 = descend_second(
         r1_ref[...], s1_ref[...], wx1_ref[...], wy1_ref[...], wz1_ref[...], di1_ref[...]
     )
     e21_ref[...] = e21
-    send_level2(msg_ref, (r2,))
-
-
-def finish_kernel(
-    core, ylow, yhigh, rhs_ref, s_ref, di_ref, wx_ref, wy_ref, wz_ref, u_ref, r_ref,
-    out_ref, left_ref, pre_ref, v_ref,
-):
-    blank_ends(pre_ref)
-    pre_ref[1 : PX - 1, 0:8, :] = ylow[...]
-    pre_ref[1 : PX - 1, 8:24, :] = core[...]
-    pre_ref[1 : PX - 1, 24:32, :] = yhigh[...]
-
-    def post(i, carry):
-        at = 7 + 2 * i
-        rows = pl.ds(at, 2)
-        v, av = operate_rows(pre_ref, s_ref, wx_ref, wy_ref, wz_ref, at, 2)
-        v_ref[rows] = u_ref[rows] + v + di_ref[rows] * (r_ref[rows] - av)
-        return carry
-
-    lax.fori_loop(0, BX // 2 + 2, post, 0)
-
-    def remain(i, carry):
-        at = 9 + 2 * i
-        rows = pl.ds(at, 2)
-        v, av = operate_rows(v_ref, s_ref, wx_ref, wy_ref, wz_ref, at, 2)
-        left = rhs_ref[rows] - av
-        out_ref[pl.ds(2 * i, 2)] = v[:, 8:24]
-        left_ref[pl.ds(2 * i, 2)] = left[:, 8:24]
-        return carry
-
-    lax.fori_loop(0, BX // 2, remain, 0)
+    send(msg_ref, [pack_level2(r2[2:4]), pack_ring1(e21)])
+    send(edge_ref, [pack_edge1(e21)])
 
 
 def unpack_level2(field, own, low, high):
-    tiles = own.shape[0]
+    tiles = lax.axis_size("tile")
     shape = (tiles, 16, NZ)
     sub, lane = iota(shape, 1), iota(shape, 2)
     halves = []
     for half in range(2):
-        at = 2 * field + half
-
-        def spread(ref, at=at):
-            return jnp.broadcast_to(ref[:, at : at + 1, :], shape)
+
+        def spread(ref, half=half):
+            return jnp.broadcast_to(ref[0:tiles, field, half : half + 1, :], shape)
 
         v = jnp.where(sub < 4, spread(low), jnp.where(sub < 8, spread(own), spread(high)))
         v = jnp.where((lane % 4 == sub % 4) & (sub < 12), v, 0.0)
@@ -353,14 +363,6 @@
     return rows
 
 
-def send_level3(msg_ref, fields):
-    rows = [row for v in fields for row in pack_level3(v)]
-    rows.append(jnp.zeros((msg_ref.shape[1] - len(rows), NZ), F32))
-    whole = jnp.concatenate(rows, axis=0)
-    for peer in range(msg_ref.shape[0]):
-        msg_ref[peer] = whole
-
-
 def descend_third(r2, s2, wx2, wy2, wz2, di2):
     first = r2 * di2
     second = first + di2 * (r2 - operate(first, s2, wx2, wy2, wz2, 1, 4))
@@ -376,7 +378,9 @@
     wx2_ref[...], wy2_ref[...], wz2_ref[...] = wx2, wy2, wz2
     e22, r3 = descend_third(r2, s2, wx2, wy2, wz2, di2)
     e22_ref[...] = e22
-    send_level3(msg_ref, (r3,) + coarsen(s2, wx2, wy2, wz2, 1, 4))
+    s3, wx3, _, wz3 = coarsen(s2, wx2, wy2, wz2, 1, 4)
+    inner = s3 + wx3 + x_high(wx3) + wz3 + turn(wz3, -8, 2)
+    send(msg_ref, pack_level3(r3) + pack_level3(inner))
 
 
 def third_again_kernel(
@@ -388,60 +392,53 @@
         r2, s2_ref[...], wx2_ref[...], wy2_ref[...], wz2_ref[...], di2_ref[...]
     )
     e22_ref[...] = e22
-    send_level3(msg_ref, (r3,))
-
-
-def third_x_low(v):
-    inner = iota(v.shape, 2) % 8 >= 2
-    return jnp.where(inner, turn(v, 2, 2), turn(x_low(v), -6, 2))
-
-
-def third_x_high(v):
-    inner = iota(v.shape, 2) % 8 < 6
-    return jnp.where(inner, turn(v, -2, 2), turn(x_high(v), 6, 2))
-
-
-def third_y_low(v):
-    return jnp.where(iota(v.shape, 2) % 2 == 1, turn(v, 1, 2), turn(turn(v, 1, 1), -1, 2))
-
-
-def third_y_high(v):
-    return jnp.where(iota(v.shape, 2) % 2 == 0, turn(v, -1, 2), turn(turn(v, -1, 1), 1, 2))
-
-
-def solve_third(r3, s3, wx3, wy3, wz3):
-    inner = s3 + wx3 + third_x_high(wx3) + wz3 + turn(wz3, -8, 2)
-    di = OMEGA / (inner + wy3 + third_y_high(wy3))
-    above = jnp.sum(r3, axis=1, keepdims=True)
-    below = jnp.sum(inner, axis=1, keepdims=True)
-    line = pair_sum(jnp.broadcast_to(above, r3.shape), 1, 2)
-    line = line / pair_sum(jnp.broadcast_to(below, r3.shape), 1, 2)
-    v = line
+    send(msg_ref, pack_level3(r3))
+
+
+def third_masks(shape):
+    sub, lane = iota(shape, 1), iota(shape, 2)
+    return sub // 4, (sub % 4) // 2, lane % 8
+
+
+def octuple(v):
+    return pair_sum(pair_sum(pair_sum(v, 1, 2), 2, 2), 4, 2)
+
+
+def unpack_bands3(sources):
+    shape = (sources[0].shape[0], 24, NZ)
+    dev, half, slot = third_masks(shape)
+    rows = jnp.broadcast_to(sources[0], shape)
+    for d in range(1, 5):
+        rows = jnp.where(dev == d, jnp.broadcast_to(sources[d], shape), rows)
+    rows = jnp.where(dev < 5, rows, 0.0)
+    return [octuple(jnp.where(slot == 2 * f + half, rows, 0.0)) for f in range(4)]
+
+
+def unpack_r3(v):
+    group = lax.axis_index("group")
+    at = iota(v.shape, 1)
+    shape = (v.shape[0], 24, NZ)
+    dev, half, slot = third_masks(shape)
+    rows = jnp.zeros(shape, F32)
+    for d in range(5):
+        near = jnp.sum(jnp.where(at == group + (d - 2), v, 0.0), axis=1, keepdims=True)
+        rows = jnp.where(dev == d, jnp.broadcast_to(near, shape), rows)
+    parts = [jnp.where(slot == 2 * q + half, rows, 0.0) for q in range(4)]
+    return octuple(jnp.stack(parts, axis=1).reshape((4 * v.shape[0], 24, NZ)))
+
+
+def line_sums(v):
+    total = jnp.sum(v, axis=1, keepdims=True)
+    lane = iota(total.shape, 2) % 8
+    parts = [jnp.where(lane // 2 == q, total, 0.0) for q in range(4)]
+    return octuple(jnp.stack(parts, axis=1).reshape((4 * v.shape[0], 1, NZ)))
+
+
+def solve_third(r3, line, s3, di3, wx3, wy3, wz3):
+    v = jnp.broadcast_to(line, r3.shape)
     for _ in range(COARSE_SWEEPS):
-        fx = wx3 * (v - third_x_low(v))
-        fy = wy3 * (v - third_y_low(v))
-        fz = wz3 * (v - turn(v, 8, 2))
-        flux = (fx - third_x_high(fx)) + (fy - third_y_high(fy)) + (fz - turn(fz, -8, 2))
-        v = v + di * (r3 - (s3 * v + flux))
-    return v
-
-
-def spread_third(v):
-    group = lax.axis_index("group")
-    dev = iota(v.shape, 1)
-    near = [
-        jnp.sum(jnp.where(dev == group + off, v, 0.0), axis=1, keepdims=True) for off in (-1, 0, 1)
-    ]
-    shape = (v.shape[0], 16, NZ)
-    sub, lane = iota(shape, 1), iota(shape, 2)
-    low, own, high = (jnp.broadcast_to(part, shape) for part in near)
-    rows = jnp.where(sub < 4, low, jnp.where(sub < 8, own, high))
-    parts = []
-    for q in range(4):
-        chosen = (lane % 8 == 2 * q + (sub % 4) // 2) & (sub < 12)
-        parts.append(jnp.where(chosen, rows, 0.0))
-    wide = jnp.stack(parts, axis=1).reshape((4 * v.shape[0], 16, NZ))
-    return pair_sum(pair_sum(pair_sum(wide, 1, 2), 2, 2), 4, 2)
+        v = v + di3 * (r3 - operate(v, s3, wx3, wy3, wz3, 2, 8))
+    return turn(v, -4, 1)[:, 0:16]
 
 
 def near_tiles(v):
@@ -466,31 +463,125 @@
     return jnp.concatenate(parts, axis=1)
 
 
-def climb_kernel(
-    r3_ref, bands3_ref, r2_ref, s2_ref, di2_ref, wx2_ref, wy2_ref, wz2_ref, e22_ref,
-    r1_ref, s1_ref, di1_ref, wx1_ref, wy1_ref, wz1_ref, e21_ref, e2_ref, pre_ref,
-    *, groups, thirds, r3_rows, band_rows,
-):
-    def field(ref, f, rows):
-        parts = [ref[pl.ds(thirds * f + j, groups, stride=rows), :] for j in range(thirds)]
-        return jnp.stack(parts, axis=0)
-
-    r3 = field(r3_ref, 0, r3_rows)
-    s3, wx3, wy3, wz3 = (field(bands3_ref, f, band_rows) for f in range(1, 5))
-    corr3 = solve_third(r3, s3, wx3, wy3, wz3)
-    v = e22_ref[...] + x_repeat(spread_third(corr3))
+def climb_to_second(corr3, r2_ref, s2_ref, di2_ref, wx2_ref, wy2_ref, wz2_ref, e22_ref):
+    v = e22_ref[...] + x_repeat(corr3)
     v = v + di2_ref[...] * (
         r2_ref[...]
         - operate(v, s2_ref[...], wx2_ref[...], wy2_ref[...], wz2_ref[...], 1, 4)
     )
-    corr2 = widen_y(near_tiles(v))
-    v = e21_ref[...] + x_repeat(corr2)
-    v = v + di1_ref[...] * (
+    return x_repeat(widen_y(near_tiles(v)))
+
+
+def climb_to_first(v, r1_ref, s1_ref, di1_ref, wx1_ref, wy1_ref, wz1_ref):
+    return v + di1_ref[...] * (
         r1_ref[...]
         - operate(v, s1_ref[...], wx1_ref[...], wy1_ref[...], wz1_ref[...], 2, 2)
     )
-    own = x_repeat(v[4:8])
-    pre_ref[...] = e2_ref[9:17, 8:24, :] + own[:, 8:24, :]
+
+
+def strided(ref, first, thirds, groups, rows):
+    parts = [ref[pl.ds(first + j, groups, stride=rows), :] for j in range(thirds)]
+    return jnp.stack(parts, axis=0)
+
+
+def climb_kernel(
+    far_low, low, own, high, far_high, third_ref,
+    r2_ref, s2_ref, di2_ref, wx2_ref, wy2_ref, wz2_ref, e22_ref,
+    r1_ref, s1_ref, di1_ref, wx1_ref, wy1_ref, wz1_ref, e21_ref, e2_ref,
+    pre_ref, below_ref, s3_ref, di3_ref, wx3_ref, wy3_ref, wz3_ref,
+    *, groups, thirds, rows,
+):
+    sources = [far_low[:, 0:1, :]]
+    sources += [ref[:, 5, 0:1, :] for ref in (low, own, high)]
+    sources += [far_high[:, 0:1, :]]
+    s3, wx3, wy3, wz3 = unpack_bands3(sources)
+    di3 = relax_factor(s3, wx3, wy3, wz3, 2, 8)
+    s3_ref[...], di3_ref[...], wx3_ref[...], wy3_ref[...], wz3_ref[...] = s3, di3, wx3, wy3, wz3
+    r3 = strided(third_ref, 0, thirds, groups, rows)
+    below = line_sums(strided(third_ref, thirds, thirds, groups, rows))
+    below_ref[...] = below
+    corr3 = solve_third(unpack_r3(r3), line_sums(r3) / below, s3, di3, wx3, wy3, wz3)
+    corr2 = climb_to_second(corr3, r2_ref, s2_ref, di2_ref, wx2_ref, wy2_ref, wz2_ref, e22_ref)
+    v = climb_to_first(
+        e21_ref[...] + corr2, r1_ref, s1_ref, di1_ref, wx1_ref, wy1_ref, wz1_ref
+    )
+    own1 = x_repeat(v[4:8])
+    pre_ref[...] = e2_ref[9:17, 8:24, :] + own1[:, 8:24, :]
+
+
+def tile_rows(ref, off, at):
+    tile = lax.axis_index("tile")
+    total = jnp.zeros((2, NZ), F32)
+    for t in range(lax.axis_size("tile")):
+        total = total + jnp.where(tile + off == t, ref[t, at], 0.0)
+    return total
+
+
+def ring_row(own, low, high, off, first):
+    pairs = [tile_rows(own, off, first), tile_rows(own, off, first + 1)]
+    packed = [tile_rows(low, off, first + 1)[1:2]]
+    packed += [pair[k : k + 1] for pair in pairs for k in range(2)]
+    packed += [tile_rows(high, off, first)[0:1]]
+    return spread_pairs([row[None] for row in packed], 1)
+
+
+def spread_pairs(packed, height):
+    shape = (height, WY, NZ)
+    sub, lane = iota(shape, 1), iota(shape, 2)
+    rows = jnp.zeros(shape, F32)
+    for k, row in enumerate(packed):
+        rows = jnp.where(sub // 4 == k + 1, jnp.broadcast_to(row, shape), rows)
+    return pair_sum(jnp.where(lane % 2 == (sub // 2) % 2, rows, 0.0), 1, 2)
+
+
+def last_climb_kernel(
+    third_ref, below_ref, s3_ref, di3_ref, wx3_ref, wy3_ref, wz3_ref,
+    low, own, high,
+    r2_ref, s2_ref, di2_ref, wx2_ref, wy2_ref, wz2_ref, e22_ref,
+    r1_ref, s1_ref, di1_ref, wx1_ref, wy1_ref, wz1_ref, e21_ref,
+    e2_ref, rhs_ref, s_ref, di_ref, wx_ref, wy_ref, wz_ref, u_ref, r_ref,
+    out_ref, left_ref, pre_ref, v_ref,
+    *, groups, thirds, rows,
+):
+    r3 = strided(third_ref, 0, thirds, groups, rows)
+    corr3 = solve_third(
+        unpack_r3(r3), line_sums(r3) / below_ref[...],
+        s3_ref[...], di3_ref[...], wx3_ref[...], wy3_ref[...], wz3_ref[...],
+    )
+    corr2 = climb_to_second(corr3, r2_ref, s2_ref, di2_ref, wx2_ref, wy2_ref, wz2_ref, e22_ref)
+    tiles = lax.axis_size("tile")
+    middle = e21_ref[3:9]
+    sub = iota(middle.shape, 1)
+    edge_low = jnp.concatenate([low[tiles, k] for k in range(3)], axis=0)[:, None]
+    edge_high = jnp.concatenate([high[tiles, k] for k in range(3)], axis=0)[:, None]
+    nothing = jnp.zeros_like(edge_low)
+    edges = spread_pairs([edge_low] + [nothing] * 4 + [edge_high], 6)
+    kept = (sub >= 6) & (sub < 26)
+    middle = jnp.where(kept, middle, edges)
+    blank = jnp.zeros((2, WY, NZ), F32)
+    first, last = ring_row(own, low, high, -1, 3), ring_row(own, low, high, 1, 1)
+    e21 = jnp.concatenate([blank, first, middle, last, blank], axis=0)
+    v = climb_to_first(e21 + corr2, r1_ref, s1_ref, di1_ref, wx1_ref, wy1_ref, wz1_ref)
+    pre_ref[7:19] = e2_ref[7:19] + x_repeat(v[3:9])
+
+    def post(i, carry):
+        at = 8 + 2 * i
+        here = pl.ds(at, 2)
+        v, av = operate_rows(pre_ref, s_ref, wx_ref, wy_ref, wz_ref, at, 2)
+        v_ref[here] = u_ref[here] + v + di_ref[here] * (r_ref[here] - av)
+        return carry
+
+    lax.fori_loop(0, BX // 2 + 1, post, 0)
+
+    def remain(i, carry):
+        at = 9 + 2 * i
+        v, av = operate_rows(v_ref, s_ref, wx_ref, wy_ref, wz_ref, at, 2)
+        left = rhs_ref[pl.ds(at, 2)] - av
+        out_ref[pl.ds(2 * i, 2)] = v[:, 8:24]
+        left_ref[pl.ds(2 * i, 2)] = left[:, 8:24]
+        return carry
+
+    lax.fori_loop(0, BX // 2, remain, 0)
 
 
 def call(body, outs, operands, scratch=(), smem=()):
@@ -508,10 +599,10 @@
     )(*operands)
 
 
-def beside(to_low, to_high, axis):
-    ends = lax.axis_size(axis) - 1
-    from_low = lax.ppermute(to_high, axis, [(i, i + 1) for i in range(ends)])
-    from_high = lax.ppermute(to_low, axis, [(i + 1, i) for i in range(ends)])
+def beside(to_low, to_high, axis, step=1):
+    ends = lax.axis_size(axis) - step
+    from_low = lax.ppermute(to_high, axis, [(i, i + step) for i in range(ends)])
+    from_high = lax.ppermute(to_low, axis, [(i + step, i) for i in range(ends)])
     return from_low, from_high
 
 
@@ -533,13 +624,14 @@
     tiles, groups = lax.axis_size("tile"), lax.axis_size("group")
     thirds = tiles // 4
     top, one, two = (PX, WY, NZ), (L1X, WY, NZ), (2 * tiles, 16, NZ)
-    band_rows, r3_rows = -(-5 * thirds // 8) * 8, -(-thirds // 8) * 8
+    three, line = (tiles, 24, NZ), (tiles, 1, NZ)
+    rows_once, rows_again = 2 * thirds, -(-thirds // 2) * 2
 
     raw = jnp.stack([pressure_head, old_head, soil_type.astype(F32)])
     core, ylow, yhigh = surround(raw, 1)
     rhs, s0, di0, wx0, wy0, wz0, e2, r1, s1, di1, wx1, wy1, wz1, e21, msg = call(
         assemble_kernel,
-        [top] * 7 + [one] * 7 + [(tiles, 16, NZ)],
+        [top] * 7 + [one] * 7 + [(tiles, 6, 2, NZ)],
         [core, ylow, yhigh, conduct_sat, alpha_param, shape_param, water_span],
         [top] * 4,
         smem=(3, 4, 5, 6),
@@ -549,42 +641,38 @@
 
     own = everyone(msg, "tile")
     low, high = beside(own, own, "group")
+    far_low, far_high = beside(own[:, 5], own[:, 5], "group", 2)
     r2, s2, di2, wx2, wy2, wz2, e22, msg = call(
-        third_kernel, [two] * 7 + [(groups, band_rows, NZ)], [own, low, high]
+        third_kernel, [two] * 7 + [(groups, thirds, 2, NZ)], [own, low, high]
     )
     bands2 = [s2, di2, wx2, wy2, wz2]
-    bands3 = everyone(msg, "group").reshape(groups * band_rows, NZ)
-    climb = functools.partial(climb_kernel, groups=groups, thirds=thirds, band_rows=band_rows)
-    (pre,) = call(
-        functools.partial(climb, r3_rows=band_rows),
-        [(BX, BY, NZ)],
-        [bands3, bands3, r2, *bands2, e22, r1, *bands1, e21, e2],
+    third = everyone(msg, "group").reshape(groups * rows_once, NZ)
+    pre, below, *bands3 = call(
+        functools.partial(climb_kernel, groups=groups, thirds=thirds, rows=rows_once),
+        [(BX, BY, NZ), line] + [three] * 5,
+        [far_low, low, own, high, far_high, third, r2, *bands2, e22, r1, *bands1, e21, e2],
     )
 
     core, ylow, yhigh = surround(pre, 0)
-    u, rem, e2, r1, e21, msg = call(
+    u, rem, e2, r1, e21, msg, edge = call(
         again_kernel,
-        [top] * 3 + [one] * 2 + [(tiles, 8, NZ)],
+        [top] * 3 + [one] * 2 + [(tiles, 5, 2, NZ), (1, 5, 2, NZ)],
         [core, ylow, yhigh, rhs, *bands0, *bands1],
         [top] * 2,
     )
-    own = everyone(msg, "tile")
+    own = jnp.concatenate([everyone(msg, "tile"), edge], axis=0)
     low, high = beside(own, own, "group")
     r2, e22, msg = call(
-        third_again_kernel, [two] * 2 + [(groups, r3_rows, NZ)], [own, low, high, *bands2]
-    )
-    r3 = everyone(msg, "group").reshape(groups * r3_rows, NZ)
-    (pre,) = call(
-        functools.partial(climb, r3_rows=r3_rows),
-        [(BX, BY, NZ)],
-        [r3, bands3, r2, *bands2, e22, r1, *bands1, e21, e2],
-    )
-
-    core, ylow, yhigh = surround(pre, 0)
+        third_again_kernel,
+        [two] * 2 + [(groups, rows_again // 2, 2, NZ)],
+        [own, low, high, *bands2],
+    )
+    third = everyone(msg, "group").reshape(groups * rows_again, NZ)
     update, remainder = call(
-        finish_kernel,
+        functools.partial(last_climb_kernel, groups=groups, thirds=thirds, rows=rows_again),
         [(BX, BY, NZ)] * 2,
-        [core, ylow, yhigh, rhs, *bands0, u, rem],
+        [third, below, *bands3, low, own, high, r2, *bands2, e22, r1, *bands1, e21]
+        + [e2, rhs, *bands0, u, rem],
         [top] * 2,
     )
     return update, remainder

time: 203 us -> 196 us (0.966)
  blocking collectives: 95.5 us -> 62.5 us
  local copies, waits for them, and re-layouts: 0.1 us -> 13.1 us
  starting transfers between devices: 58.9 us -> 67.8 us
  waiting for transfers between devices: 14.8 us -> 20.9 us
    all_to_all x4 -> x3, blocking collectives: 95.5 us -> 62.5 us  [everyone(): return lax.all_to_all(blocks, axis, 0, 0, tiled=True)]
    all_to_all x0 -> x1, starting transfers between devices: none -> 16.5 us  [everyone(): return lax.all_to_all(blocks, axis, 0, 0, tiled=True)]
    unnamed x12 -> x61, local copies, waits for them, and re-layouts: 0.03 us -> 13 us
    ppermute x16 -> x14, starting transfers between devices: 58.9 us -> 51.3 us  [the longest x7 26.4 us: beside(): from_low = lax.ppermute(to_high, axis, [(i, i + step) for i in range(ends)])]
    all_to_all x0 -> x1, waiting for transfers between devices: none -> 5.9 us  [everyone(): return lax.all_to_all(blocks, axis, 0, 0, tiled=True)]
    ppermute x16 -> x14, waiting for transfers between devices: 14.8 us -> 15 us  [the longest x7 9.78 us: beside(): from_low = lax.ppermute(to_high, axis, [(i, i + step) for i in range(ends)])]
    pallas_call x7 -> x6, Pallas kernels: 29.3 us -> 29.1 us  [call(): pl.pallas_call(body, out_shape=[jax.ShapeDtypeStruct(shape, F32) for shap...]
  transfers between devices with their start and end apart: 16 -> 15, of which waited for: 12 -> 11; matrix products, arithmetic and copies ran while one was open for 0% -> 0% of each run, Pallas kernels for 0% -> 0%
where the time goes in v2:
time: 196 us; the launch traced here: 195 us
  starting transfers between devices  67.8 us (35%)
  blocking collectives  62.5 us (32%)
  Pallas kernels  29.1 us (15%)
  waiting for transfers between devices  20.9 us (11%)
  local copies, waits for them, and re-layouts  13.1 us (7%)
    all_to_all x3, blocking collectives, everyone(): return lax.all_to_all(blocks, axis, 0, 0, tiled=True)  62.5 us
    pallas_call x6, Pallas kernels, call(): pl.pallas_call(body, out_shape=[jax.ShapeDtypeStruct(shape, F32) for shap...  29.1 us
    ppermute x7, starting transfers between devices, beside(): from_low = lax.ppermute(to_high, axis, [(i, i + step) for i in range(ends)])  26.4 us
    ppermute x7, starting transfers between devices, beside(): from_high = lax.ppermute(to_low, axis, [(i + step, i) for i in range(ends)])  25 us
    all_to_all x1, starting transfers between devices, everyone(): return lax.all_to_all(blocks, axis, 0, 0, tiled=True)  16.5 us
    unnamed x61, local copies, waits for them, and re-layouts  13 us
    ppermute x7, waiting for transfers between devices, beside(): from_low = lax.ppermute(to_high, axis, [(i, i + step) for i in range(ends)])  9.78 us
    all_to_all x1, waiting for transfers between devices, everyone(): return lax.all_to_all(blocks, axis, 0, 0, tiled=True)  5.9 us
  transfers between devices with their start and end apart: 15, of which 11 were waited for; matrix products, arithmetic and copies ran while one was open for 0% of the time, Pallas kernels for 0%

profile of v2, /device:TPU:1, one launch (start us, length us, event | category | flops | bytes accessed | tf_op | source)
XLA Modules:
  0.0 195.3 jit_solution(287253627970391898)
XLA Ops:
  2.9 5.5 %collective-permute-start = (f32[3,8,16,128]{3,2,1,0:T(8,128)S(1)}, f32[3,8,16,128]{3,2,1,0:T(8,128)S(1)}, u32[]{:S(2)}, u32[]{:S(2)}) collective-permute-start(f32[3,8,16,128]{3,2,1,0:T(8,128)S(1)} %pad_maximum_fusion.1), channel_id=1, source_target_pairs={{0,64},{64,128},{128,192},{192,256},{256,320},{320,384},{384,448},... | collective-permute-start | bytes 589832 | tf_op jit(solution)/shard_map/ppermute | solution.py:604
  9.4 1.5 collective-permute-done
  11.1 12.2 %collective-permute-start.3 = (f32[3,24,8,128]{3,2,1,0:T(8,128)S(1)}, f32[3,24,8,128]{3,2,1,0:T(8,128)S(1)}, u32[]{:S(2)}, u32[]{:S(2)}) collective-permute-start(f32[3,24,8,128]{3,2,1,0:T(8,128)S(1)} %get-tuple-element.82), channel_id=1, source_target_pairs={{1,0},{2,1},{3,2},{4,3},{5,4},{6,5},{7,6},{8,7},{9,8},{10,9},{11,1... | collective-permute-start | bytes 884744 | tf_op jit(solution)/shard_map/ppermute | solution.py:605
  23.3 1.9 collective-permute-start.2
  25.2 3.6 %collective-permute-done.2.ylow = f32[3,24,8,128]{3,2,1,0:T(8,128)S(1)} collective-permute-done((f32[3,24,8,128]{3,2,1,0:T(8,128)S(1)}, f32[3,24,8,128]{3,2,1,0:T(8,128)S(1)}, u32[]{:S(2)}, u32[]{:S(2)}) %collective-permute-start.2) | collective-permute-done | bytes 294944 | tf_op jit(solution)/shard_map/ppermute | solution.py:604
  28.9 11.1 %shard_map.86 = (f32[26,32,128]{2,1,0:T(8,128)S(1)}, f32[26,32,128]{2,1,0:T(8,128)S(1)}, f32[26,32,128]{2,1,0:T(8,128)S(1)}, f32[26,32,128]{2,1,0:T(8,128)S(1)},...) custom-call(f32[3,24,16,128]{3,2,1,0:T(8,128)S(1)} %pad_maximum_fusi, ...), custom_call_target="tpu_custom_call" | custom-call | tf_op jit(solution)/shard_map/pallas_call | solution.py:589
  44.3 19.4 %all_to_all.20.own = f32[12,6,2,128]{3,2,1,0:T(2,128)S(1)} all-to-all(f32[12,6,2,128]{3,2,1,0:T(2,128)S(1)} %get-tuple-element.42), channel_id=1, replica_groups=mesh['tile'=12,'group'=64] {'tile'}, dimensions={0} | all-to-all | bytes 147456 | tf_op jit(solution)/shard_map/all_to_all | solution.py:620
  63.7 1.9 collective-permute-start.6
  65.6 6.2 %collective-permute-start.5 = (f32[12,6,2,128]{3,2,1,0:T(2,128)S(1)}, f32[12,6,2,128]{3,2,1,0:T(2,128)S(1)}, u32[]{:S(2)}, u32[]{:S(2)}) collective-permute-start(f32[12,6,2,128]{3,2,1,0:T(2,128)S(1)} %all_to_all.20.own), channel_id=1, source_target_pairs={{0,1},{1,2},{2,3},{3,4},{4,5},{5,6},{6,7},{7,8},{8,9},{9,10},{10,1... | collective-permute-start | bytes 221192 | tf_op jit(solution)/shard_map/ppermute | solution.py:604
  73.2 2.1 %shard_map.87 = (f32[24,16,128]{2,1,0:T(8,128)S(1)}, f32[24,16,128]{2,1,0:T(8,128)S(1)}, f32[24,16,128]{2,1,0:T(8,128)S(1)}, f32[24,16,128]{2,1,0:T(8,128)S(1)},...) custom-call(f32[12,6,2,128]{3,2,1,0:T(2,128)S(1)} %all_to_all.20.own, ...), custom_call_target="tpu_custom_call" | custom-call | tf_op jit(solution)/shard_map/pallas_call | solution.py:589
  77.4 16.5 %all-to-all-start.1 = ((f32[64,3,2,128]{3,2,1,0:T(2,128)}), f32[64,3,2,128]{3,2,1,0:T(2,128)S(1)}, u32[]{:S(2)}, u32[]{:S(2)}) async-start(f32[64,3,2,128]{3,2,1,0:T(2,128)} %copy-done.22), calls=%async_computation.1 | async-start | bytes 393216 | tf_op jit(solution)/shard_map/all_to_all | solution.py:620
  95.2 4.0 %collective-permute-start.4 = (f32[12,2,128]{2,1,0:T(2,128)S(1)}, f32[12,2,128]{2,1,0:T(2,128)S(1)}, u32[]{:S(2)}, u32[]{:S(2)}) collective-permute-start(f32[12,2,128]{2,1,0:T(2,128)S(1)} %slice_bitcast_fusion), channel_id=1, source_target_pairs={{0,2},{1,3},{2,4},{3,5},{4,6},{5,7},{6,8},{7,9},{8,10},{9,11},{10,... | collective-permute-start | bytes 36872 | tf_op jit(solution)/shard_map/ppermute | solution.py:604
  100.0 5.9 %all-to-all-done.1 = f32[64,3,2,128]{3,2,1,0:T(2,128)S(1)} async-done(((f32[64,3,2,128]{3,2,1,0:T(2,128)}), f32[64,3,2,128]{3,2,1,0:T(2,128)S(1)}, u32[]{:S(2)}, u32[]{:S(2)}) %all-to-all-start.1) | async-done | bytes 196640 | tf_op jit(solution)/shard_map/all_to_all | solution.py:620
  112.4 2.9 %shard_map.88 = (f32[8,16,128]{2,1,0:T(8,128)S(1)}, f32[12,1,128]{2,1,0:T(1,128)S(1)}, f32[12,24,128]{2,1,0:T(8,128)S(1)}, f32[12,24,128]{2,1,0:T(8,128)S(1)}, f...) custom-call(f32[12,2,128]{2,1,0:T(2,128)S(1)} %collective-permute-done.4.far_low, ...), custom_call_target="tpu_custom_call" | custom-call | tf_op jit(solution)/shard_map/pallas_call | solution.py:589
  115.3 2.3 %collective-permute-start.8 = (f32[8,16,128]{2,1,0:T(8,128)S(1)}, f32[8,16,128]{2,1,0:T(8,128)S(1)}, u32[]{:S(2)}, u32[]{:S(2)}) collective-permute-start(f32[8,16,128]{2,1,0:T(8,128)S(1)} %get-tuple-element.59), channel_id=1, source_target_pairs={{0,64},{64,128},{128,192},{192,256},{256,320},{320,384},{384,448},... | collective-permute-start | bytes 196616 | tf_op jit(solution)/shard_map/ppermute | solution.py:604
  118.9 3.7 %collective-permute-done.9 = f32[8,16,128]{2,1,0:T(8,128)S(1)} collective-permute-done((f32[8,16,128]{2,1,0:T(8,128)S(1)}, f32[8,16,128]{2,1,0:T(8,128)S(1)}, u32[]{:S(2)}, u32[]{:S(2)}) %collective-permute-start.9) | collective-permute-done | bytes 65568 | tf_op jit(solution)/shard_map/ppermute | solution.py:605
  122.6 3.7 %collective-permute-start.11 = (f32[24,8,128]{2,1,0:T(8,128)S(1)}, f32[24,8,128]{2,1,0:T(8,128)S(1)}, u32[]{:S(2)}, u32[]{:S(2)}) collective-permute-start(f32[24,8,128]{2,1,0:T(8,128)S(1)} %get-tuple-element.84), channel_id=1, source_target_pairs={{1,0},{2,1},{3,2},{4,3},{5,4},{6,5},{7,6},{8,7},{9,8},{10,9},{11,1... | collective-permute-start | bytes 294920 | tf_op jit(solution)/shard_map/ppermute | solution.py:605
  126.3 2.0 %collective-permute-start.10 = (f32[24,8,128]{2,1,0:T(8,128)S(1)}, f32[24,8,128]{2,1,0:T(8,128)S(1)}, u32[]{:S(2)}, u32[]{:S(2)}) collective-permute-start(f32[24,8,128]{2,1,0:T(8,128)S(1)} %get-tuple-element.85), channel_id=1, source_target_pairs={{0,1},{1,2},{2,3},{3,4},{4,5},{5,6},{6,7},{7,8},{8,9},{9,10},{10,1... | collective-permute-start | bytes 294920 | tf_op jit(solution)/shard_map/ppermute | solution.py:604
  130.0 7.2 %shard_map.89 = (f32[26,32,128]{2,1,0:T(8,128)S(1)}, f32[26,32,128]{2,1,0:T(8,128)S(1)}, f32[26,32,128]{2,1,0:T(8,128)S(1)}, f32[12,32,128]{2,1,0:T(8,128)S(1)},...) custom-call(f32[24,16,128]{2,1,0:T(8,128)S(1)} %constant_dynamic-update-slice_fusion.core, ...), custom_call_target="tpu_custom_call" | custom-call | tf_op jit(solution)/shard_map/pallas_call | solution.py:589
  137.3 14.3 %all_to_all.21 = f32[12,5,2,128]{3,2,1,0:T(2,128)S(1)} all-to-all(f32[12,5,2,128]{3,2,1,0:T(2,128)S(1)} %get-tuple-element.66), channel_id=1, replica_groups=mesh['tile'=12,'group'=64] {'tile'}, dimensions={0} | all-to-all | bytes 122880 | tf_op jit(solution)/shard_map/all_to_all | solution.py:620
  151.6 3.3 %collective-permute-start.13 = (f32[13,5,2,128]{3,2,1,0:T(2,128)S(1)}, f32[13,5,2,128]{3,2,1,0:T(2,128)S(1)}, u32[]{:S(2)}, u32[]{:S(2)}) collective-permute-start(f32[13,5,2,128]{3,2,1,0:T(2,128)S(1)} %constant_dynamic-update-slice_fusion.3.own), channel_id=1, source_target_pairs={{1,0},{2,1},{3,2},{4,3},{5,4},{6,5},{7,6},{8,7},{9,8},{10,9},{11,1... | collective-permute-start | bytes 199688 | tf_op jit(solution)/shard_map/ppermute | solution.py:605
  154.8 4.5 %collective-permute-start.12 = (f32[13,5,2,128]{3,2,1,0:T(2,128)S(1)}, f32[13,5,2,128]{3,2,1,0:T(2,128)S(1)}, u32[]{:S(2)}, u32[]{:S(2)}) collective-permute-start(f32[13,5,2,128]{3,2,1,0:T(2,128)S(1)} %constant_dynamic-update-slice_fusion.3.own), channel_id=1, source_target_pairs={{0,1},{1,2},{2,3},{3,4},{4,5},{5,6},{6,7},{7,8},{8,9},{9,10},{10,1... | collective-permute-start | bytes 199688 | tf_op jit(solution)/shard_map/ppermute | solution.py:604
  161.5 28.8 %all_to_all.22 = f32[64,2,2,128]{3,2,1,0:T(2,128)S(1)} all-to-all(f32[64,2,2,128]{3,2,1,0:T(2,128)S(1)} %get-tuple-element.68), channel_id=1, replica_groups=mesh['tile'=12,'group'=64] {'group'}, dimensions={0} | all-to-all | bytes 262144 | tf_op jit(solution)/shard_map/all_to_all | solution.py:620
  190.3 5.0 %shard_map.91 = (f32[8,16,128]{2,1,0:T(8,128)}, f32[8,16,128]{2,1,0:T(8,128)}) custom-call(f32[256,128]{1,0:T(8,128)S(1)} %bitcast.11, f32[12,1,128]{2,1,0:T(1,128)S(1)} %get-tuple-element.69.below_ref, f32[12,24,128]{2,1,0:T(8,128)S(1)} %get-tuple-element.70.s3_ref, f32[12,24,128]{2,1,0:T(8,128)S(1)} %get-tuple-element.71.di3_ref, ...), custom_call_target="tpu_custom_call" | custom-call | tf_op jit(solution)/shard_map/pallas_call | solution.py:589
  (84 shorter events, 24.9 us)
Async XLA Ops:
  1.6 7.9 %collective-permute-start.1 = (f32[3,8,16,128]{3,2,1,0:T(8,128)S(1)}, f32[3,8,16,128]{3,2,1,0:T(8,128)S(1)}, u32[]{:S(2)}, u32[]{:S(2)}) collective-permute-start(f32[3,8,16,128]{3,2,1,0:T(8,128)S(1)} %pad_maximum_fusion.1), channel_id=1, source_target_pairs={{64,0},{128,64},{192,128},{256,192},{320,256},{384,320},{448,384},... | collective-permute-start | bytes 589832 | tf_op jit(solution)/shard_map/ppermute | solution.py:605
  2.9 8.1 %collective-permute-start = (f32[3,8,16,128]{3,2,1,0:T(8,128)S(1)}, f32[3,8,16,128]{3,2,1,0:T(8,128)S(1)}, u32[]{:S(2)}, u32[]{:S(2)}) collective-permute-start(f32[3,8,16,128]{3,2,1,0:T(8,128)S(1)} %pad_maximum_fusion.1), channel_id=1, source_target_pairs={{0,64},{64,128},{128,192},{192,256},{256,320},{320,384},{384,448},... | collective-permute-start | bytes 589832 | tf_op jit(solution)/shard_map/ppermute | solution.py:604
  11.0 17.9 %copy-start.26 = (f32[12]{0:T(128)S(1)}, f32[12]{0:T(128)}, u32[]{:S(2)}) copy-start(f32[12]{0:T(128)} %span_ref.1) | copy-start | bytes 148
  11.0 17.8 %copy-start.23 = (f32[12]{0:T(128)S(1)}, f32[12]{0:T(128)}, u32[]{:S(2)}) copy-start(f32[12]{0:T(128)} %ks_ref.1) | copy-start | bytes 148
  11.0 17.8 %copy-start.24 = (f32[12]{0:T(128)S(1)}, f32[12]{0:T(128)}, u32[]{:S(2)}) copy-start(f32[12]{0:T(128)} %alpha_ref.1) | copy-start | bytes 148
  11.0 17.8 %copy-start.25 = (f32[12]{0:T(128)S(1)}, f32[12]{0:T(128)}, u32[]{:S(2)}) copy-start(f32[12]{0:T(128)} %shape_ref.1) | copy-start | bytes 148
  11.1 14.2 %collective-permute-start.3 = (f32[3,24,8,128]{3,2,1,0:T(8,128)S(1)}, f32[3,24,8,128]{3,2,1,0:T(8,128)S(1)}, u32[]{:S(2)}, u32[]{:S(2)}) collective-permute-start(f32[3,24,8,128]{3,2,1,0:T(8,128)S(1)} %get-tuple-element.82), channel_id=1, source_target_pairs={{1,0},{2,1},{3,2},{4,3},{5,4},{6,5},{7,6},{8,7},{9,8},{10,9},{11,1... | collective-permute-start | bytes 884744 | tf_op jit(solution)/shard_map/ppermute | solution.py:605
  23.3 5.6 %collective-permute-start.2 = (f32[3,24,8,128]{3,2,1,0:T(8,128)S(1)}, f32[3,24,8,128]{3,2,1,0:T(8,128)S(1)}, u32[]{:S(2)}, u32[]{:S(2)}) collective-permute-start(f32[3,24,8,128]{3,2,1,0:T(8,128)S(1)} %get-tuple-element.83), channel_id=1, source_target_pairs={{0,1},{1,2},{2,3},{3,4},{4,5},{5,6},{6,7},{7,8},{8,9},{9,10},{10,1... | collective-permute-start | bytes 884744 | tf_op jit(solution)/shard_map/ppermute | solution.py:604
  63.7 8.2 %collective-permute-start.6 = (f32[12,6,2,128]{3,2,1,0:T(2,128)S(1)}, f32[12,6,2,128]{3,2,1,0:T(2,128)S(1)}, u32[]{:S(2)}, u32[]{:S(2)}) collective-permute-start(f32[12,6,2,128]{3,2,1,0:T(2,128)S(1)} %all_to_all.20.own), channel_id=1, source_target_pairs={{1,0},{2,1},{3,2},{4,3},{5,4},{6,5},{7,6},{8,7},{9,8},{10,9},{11,1... | collective-permute-start | bytes 221192 | tf_op jit(solution)/shard_map/ppermute | solution.py:605
  65.6 7.6 %collective-permute-start.5 = (f32[12,6,2,128]{3,2,1,0:T(2,128)S(1)}, f32[12,6,2,128]{3,2,1,0:T(2,128)S(1)}, u32[]{:S(2)}, u32[]{:S(2)}) collective-permute-start(f32[12,6,2,128]{3,2,1,0:T(2,128)S(1)} %all_to_all.20.own), channel_id=1, source_target_pairs={{0,1},{1,2},{2,3},{3,4},{4,5},{5,6},{6,7},{7,8},{8,9},{9,10},{10,1... | collective-permute-start | bytes 221192 | tf_op jit(solution)/shard_map/ppermute | solution.py:604
  77.4 28.5 %all-to-all-start.1 = ((f32[64,3,2,128]{3,2,1,0:T(2,128)}), f32[64,3,2,128]{3,2,1,0:T(2,128)S(1)}, u32[]{:S(2)}, u32[]{:S(2)}) async-start(f32[64,3,2,128]{3,2,1,0:T(2,128)} %copy-done.22), calls=%async_computation.1 | async-start | bytes 393216 | tf_op jit(solution)/shard_map/all_to_all | solution.py:620
  93.9 5.3 %collective-permute-start.7 = (f32[12,2,128]{2,1,0:T(2,128)S(1)}, f32[12,2,128]{2,1,0:T(2,128)S(1)}, u32[]{:S(2)}, u32[]{:S(2)}) collective-permute-start(f32[12,2,128]{2,1,0:T(2,128)S(1)} %slice_bitcast_fusion), channel_id=1, source_target_pairs={{2,0},{3,1},{4,2},{5,3},{6,4},{7,5},{8,6},{9,7},{10,8},{11,9},{12,... | collective-permute-start | bytes 36872 | tf_op jit(solution)/shard_map/ppermute | solution.py:605
  95.2 4.8 %collective-permute-start.4 = (f32[12,2,128]{2,1,0:T(2,128)S(1)}, f32[12,2,128]{2,1,0:T(2,128)S(1)}, u32[]{:S(2)}, u32[]{:S(2)}) collective-permute-start(f32[12,2,128]{2,1,0:T(2,128)S(1)} %slice_bitcast_fusion), channel_id=1, source_target_pairs={{0,2},{1,3},{2,4},{3,5},{4,6},{5,7},{6,8},{7,9},{8,10},{9,11},{10,... | collective-permute-start | bytes 36872 | tf_op jit(solution)/shard_map/ppermute | solution.py:604
  112.4 17.6 %copy-start.3 = (f32[26,32,128]{2,1,0:T(8,128)S(1)}, f32[26,32,128]{2,1,0:T(8,128)}, u32[]{:S(2)}) copy-start(f32[26,32,128]{2,1,0:T(8,128)} %copy-done.2) | copy-start | bytes 1277956
  112.4 17.6 %copy-start.5 = (f32[26,32,128]{2,1,0:T(8,128)S(1)}, f32[26,32,128]{2,1,0:T(8,128)}, u32[]{:S(2)}) copy-start(f32[26,32,128]{2,1,0:T(8,128)} %copy-done.4) | copy-start | bytes 1277956
  115.2 14.7 %copy-start.1 = (f32[26,32,128]{2,1,0:T(8,128)S(1)}, f32[26,32,128]{2,1,0:T(8,128)}, u32[]{:S(2)}) copy-start(f32[26,32,128]{2,1,0:T(8,128)} %copy-done) | copy-start | bytes 1277956
  115.3 3.6 %collective-permute-start.8 = (f32[8,16,128]{2,1,0:T(8,128)S(1)}, f32[8,16,128]{2,1,0:T(8,128)S(1)}, u32[]{:S(2)}, u32[]{:S(2)}) collective-permute-start(f32[8,16,128]{2,1,0:T(8,128)S(1)} %get-tuple-element.59), channel_id=1, source_target_pairs={{0,64},{64,128},{128,192},{192,256},{256,320},{320,384},{384,448},... | collective-permute-start | bytes 196616 | tf_op jit(solution)/shard_map/ppermute | solution.py:604
  117.6 5.0 %collective-permute-start.9 = (f32[8,16,128]{2,1,0:T(8,128)S(1)}, f32[8,16,128]{2,1,0:T(8,128)S(1)}, u32[]{:S(2)}, u32[]{:S(2)}) collective-permute-start(f32[8,16,128]{2,1,0:T(8,128)S(1)} %get-tuple-element.59), channel_id=1, source_target_pairs={{64,0},{128,64},{192,128},{256,192},{320,256},{384,320},{448,384},... | collective-permute-start | bytes 196616 | tf_op jit(solution)/shard_map/ppermute | solution.py:605
  122.6 6.1 %collective-permute-start.11 = (f32[24,8,128]{2,1,0:T(8,128)S(1)}, f32[24,8,128]{2,1,0:T(8,128)S(1)}, u32[]{:S(2)}, u32[]{:S(2)}) collective-permute-start(f32[24,8,128]{2,1,0:T(8,128)S(1)} %get-tuple-element.84), channel_id=1, source_target_pairs={{1,0},{2,1},{3,2},{4,3},{5,4},{6,5},{7,6},{8,7},{9,8},{10,9},{11,1... | collective-permute-start | bytes 294920 | tf_op jit(solution)/shard_map/ppermute | solution.py:605
  126.3 3.6 %collective-permute-start.10 = (f32[24,8,128]{2,1,0:T(8,128)S(1)}, f32[24,8,128]{2,1,0:T(8,128)S(1)}, u32[]{:S(2)}, u32[]{:S(2)}) collective-permute-start(f32[24,8,128]{2,1,0:T(8,128)S(1)} %get-tuple-element.85), channel_id=1, source_target_pairs={{0,1},{1,2},{2,3},{3,4},{4,5},{5,6},{6,7},{7,8},{8,9},{9,10},{10,1... | collective-permute-start | bytes 294920 | tf_op jit(solution)/shard_map/ppermute | solution.py:604
  137.2 24.2 %copy-start.8 = (f32[26,32,128]{2,1,0:T(8,128)}, f32[26,32,128]{2,1,0:T(8,128)S(1)}, u32[]{:S(2)}) copy-start(f32[26,32,128]{2,1,0:T(8,128)S(1)} %get-tuple-element.80.u_ref) | copy-start | bytes 1277956
  137.2 24.2 %copy-start.9 = (f32[26,32,128]{2,1,0:T(8,128)}, f32[26,32,128]{2,1,0:T(8,128)S(1)}, u32[]{:S(2)}) copy-start(f32[26,32,128]{2,1,0:T(8,128)S(1)} %get-tuple-element.81.r_ref) | copy-start | bytes 1277956
  151.6 7.8 %collective-permute-start.13 = (f32[13,5,2,128]{3,2,1,0:T(2,128)S(1)}, f32[13,5,2,128]{3,2,1,0:T(2,128)S(1)}, u32[]{:S(2)}, u32[]{:S(2)}) collective-permute-start(f32[13,5,2,128]{3,2,1,0:T(2,128)S(1)} %constant_dynamic-update-slice_fusion.3.own), channel_id=1, source_target_pairs={{1,0},{2,1},{3,2},{4,3},{5,4},{6,5},{7,6},{8,7},{9,8},{10,9},{11,1... | collective-permute-start | bytes 199688 | tf_op jit(solution)/shard_map/ppermute | solution.py:605
  154.8 5.8 %collective-permute-start.12 = (f32[13,5,2,128]{3,2,1,0:T(2,128)S(1)}, f32[13,5,2,128]{3,2,1,0:T(2,128)S(1)}, u32[]{:S(2)}, u32[]{:S(2)}) collective-permute-start(f32[13,5,2,128]{3,2,1,0:T(2,128)S(1)} %constant_dynamic-update-slice_fusion.3.own), channel_id=1, source_target_pairs={{0,1},{1,2},{2,3},{3,4},{4,5},{5,6},{6,7},{7,8},{8,9},{9,10},{10,1... | collective-permute-start | bytes 199688 | tf_op jit(solution)/shard_map/ppermute | solution.py:604
  (20 other events, 20.2 us)

commit v3 on v2

--- a/solution.py
+++ b/solution.py
@@ -97,18 +97,6 @@
     flux = flux - wx_ref[pl.ds(at + 1, size)] * (v_ref[pl.ds(at + 1, size)] - v)
     flux = flux + (fy - turn(fy, -1, 1)) + (fz - turn(fz, -1, 2))
     return v, s_ref[pl.ds(at, size)] * v + flux
-
-
-def inside_grid(at, size):
-    shape = (size, WY, NZ)
-    gx = BX * lax.axis_index("tile") - (WX - BX) // 2 + (at - 1) + iota(shape, 0)
-    gy = BY * lax.axis_index("group") - (WY - BY) // 2 + iota(shape, 1)
-    return (
-        (gx >= 0)
-        & (gx < BX * lax.axis_size("tile"))
-        & (gy >= 0)
-        & (gy < BY * lax.axis_size("group"))
-    )
 
 
 def blank_ends(ref):
@@ -172,7 +160,7 @@
         e2_ref[pl.ds(at, 2)] = v + di_ref[pl.ds(at, 2)] * (r_ref[pl.ds(at, 2)] - av)
         return carry
 
-    lax.fori_loop(1, WX // 2 - 1, second, 0)
+    lax.fori_loop(1, WX // 2 - 1, second, 0, unroll=2)
 
     def third(i, carry):
         at = 1 + 2 * i
@@ -180,7 +168,7 @@
         r1_ref[pl.ds(i, 1)] = restrict(r_ref[pl.ds(at, 2)] - av, 1, 1)
         return carry
 
-    lax.fori_loop(2, WX // 2 - 2, third, 0)
+    lax.fori_loop(2, WX // 2 - 2, third, 0, unroll=2)
 
 
 def descend_second(r1, s1, wx1, wy1, wz1, di1):
@@ -190,31 +178,16 @@
     return second, restrict(defect, 2, 2)
 
 
-def assemble_kernel(
-    core, ylow, yhigh, ks_ref, alpha_ref, shape_ref, span_ref,
-    r_ref, s_ref, di_ref, wx_ref, wy_ref, wz_ref, e2_ref,
-    r1_ref, s1_ref, di1_ref, wx1_ref, wy1_ref, wz1_ref, e21_ref, msg_ref,
-    h_ref, k_ref, m_ref, e1_ref,
-):
-    def window(field, at):
-        row = pl.ds(at - 1, 1)
-        return jnp.concatenate([ylow[field, row], core[field, row], yhigh[field, row]], axis=1)
-
-    for ref in (h_ref, k_ref, s_ref, wx_ref, wy_ref, wz_ref, di_ref, r_ref, e1_ref, e2_ref):
-        blank_ends(ref)
-
-    def soils(i, carry):
-        at = 1 + i
-        inside = inside_grid(at, 1)
-        head = jnp.where(inside, window(0, at), -1.0)
-        old = jnp.where(inside, window(1, at), -1.0)
-        soil = window(2, at)
+def soil_kernel(head_ref, old_ref, soil_ref, ks_ref, alpha_ref, shape_ref, span_ref, out_ref):
+    def cells(i, carry):
+        row = pl.ds(i, 1)
+        head, old, soil = head_ref[row], old_ref[row], soil_ref[row]
         ks = jnp.full(soil.shape, ks_ref[0])
         alpha = jnp.full(soil.shape, alpha_ref[0])
         shape_n = jnp.full(soil.shape, shape_ref[0])
         span = jnp.full(soil.shape, span_ref[0])
         for kind in range(1, SOILS):
-            hit = soil == float(kind)
+            hit = soil == kind
             ks = jnp.where(hit, ks_ref[kind], ks)
             alpha = jnp.where(hit, alpha_ref[kind], alpha)
             shape_n = jnp.where(hit, shape_ref[kind], shape_n)
@@ -226,16 +199,32 @@
         old_saturation = jnp.exp(-shape_m * jnp.log1p(old_power))
         portion = 1.0 / (1.0 + power)
         factor = 1.0 - jnp.exp(shape_m * jnp.log(power / (1.0 + power)))
-        conductivity = ks * jnp.sqrt(saturation) * factor * factor
         capacity = span * shape_m * shape_n * power / -head * saturation * portion
-        row = pl.ds(at, 1)
-        h_ref[row] = head
-        k_ref[row] = jnp.where(inside, conductivity, 0.0)
-        s_ref[row] = capacity + STORAGE
-        m_ref[row] = span * (saturation - old_saturation) + STORAGE * (head - old)
-        return carry
-
-    lax.fori_loop(0, WX, soils, 0)
+        out_ref[0, row] = head
+        out_ref[1, row] = ks * jnp.sqrt(saturation) * factor * factor
+        out_ref[2, row] = capacity + STORAGE
+        out_ref[3, row] = span * (saturation - old_saturation) + STORAGE * (head - old)
+        return carry
+
+    lax.fori_loop(0, BX, cells, 0, unroll=2)
+
+
+def fill_window(ref, core, ylow, yhigh):
+    ref[1 : PX - 1, 0:8, :] = ylow
+    ref[1 : PX - 1, 8:24, :] = core
+    ref[1 : PX - 1, 24:32, :] = yhigh
+
+
+def assemble_kernel(
+    core, ylow, yhigh,
+    r_ref, s_ref, di_ref, wx_ref, wy_ref, wz_ref, e2_ref,
+    r1_ref, s1_ref, di1_ref, wx1_ref, wy1_ref, wz1_ref, e21_ref, msg_ref,
+    h_ref, k_ref, m_ref, e1_ref,
+):
+    for ref in (h_ref, k_ref, s_ref, wx_ref, wy_ref, wz_ref, di_ref, r_ref, e1_ref, e2_ref):
+        blank_ends(ref)
+    for f, ref in enumerate((h_ref, k_ref, s_ref, m_ref)):
+        fill_window(ref, core[f], ylow[f], yhigh[f])
 
     def harmonic(a, b):
         total = a + b
@@ -250,7 +239,7 @@
         wz_ref[pl.ds(at, 2)] = jnp.where(iota(wz.shape, 2) == 0, 0.0, wz)
         return carry
 
-    lax.fori_loop(0, WX // 2, faces, 0)
+    lax.fori_loop(0, WX // 2, faces, 0, unroll=2)
 
     def right_side(i, carry):
         at = 1 + 2 * i
@@ -261,15 +250,15 @@
         fz = wz * (h - turn(h, 1, 2) + 1.0)
         flux = wx * (h - h_ref[pl.ds(at - 1, 2)]) - wx_up * (h_ref[pl.ds(at + 1, 2)] - h)
         flux = flux + (fy - turn(fy, -1, 1)) + (fz - turn(fz, -1, 2))
-        rhs = jnp.where(inside_grid(at, 2), -(m_ref[rows] + flux), 0.0)
+        rhs = -(m_ref[rows] + flux)
         diagonal = s_ref[rows] + wx + wx_up + wy + turn(wy, -1, 1) + wz + turn(wz, -1, 2)
-        di = OMEGA / diagonal
+        di = jnp.where(diagonal > 0.0, OMEGA / diagonal, 0.0)
         r_ref[rows] = rhs
         di_ref[rows] = di
         e1_ref[rows] = rhs * di
         return carry
 
-    lax.fori_loop(0, WX // 2, right_side, 0)
+    lax.fori_loop(0, WX // 2, right_side, 0, unroll=2)
 
     def bands(i, carry):
         rows = pl.ds(1 + 2 * i, 2)
@@ -278,7 +267,7 @@
         s1_ref[row], wx1_ref[row], wy1_ref[row], wz1_ref[row] = s1, wx1, wy1, wz1
         return carry
 
-    lax.fori_loop(1, WX // 2 - 1, bands, 0)
+    lax.fori_loop(1, WX // 2 - 1, bands, 0, unroll=2)
     for ref in (s1_ref, wx1_ref, wy1_ref, wz1_ref):
         blank_level1(ref, 1)
     blank_level1(r1_ref, 2)
@@ -302,9 +291,7 @@
 ):
     for ref in (pre_ref, u_ref, r_ref, e1_ref, e2_ref):
         blank_ends(ref)
-    pre_ref[1 : PX - 1, 0:8, :] = ylow[...]
-    pre_ref[1 : PX - 1, 8:24, :] = core[...]
-    pre_ref[1 : PX - 1, 24:32, :] = yhigh[...]
+    fill_window(pre_ref, core[...], ylow[...], yhigh[...])
 
     def post(i, carry):
         at = 1 + 2 * i
@@ -313,7 +300,7 @@
         u_ref[rows] = v + di_ref[rows] * (rhs_ref[rows] - av)
         return carry
 
-    lax.fori_loop(0, WX // 2, post, 0)
+    lax.fori_loop(0, WX // 2, post, 0, unroll=2)
 
     def remain(i, carry):
         at = 1 + 2 * i
@@ -324,7 +311,7 @@
         e1_ref[rows] = left * di_ref[rows]
         return carry
 
-    lax.fori_loop(1, WX // 2 - 1, remain, 0)
+    lax.fori_loop(1, WX // 2 - 1, remain, 0, unroll=2)
     descend_top(r_ref, e1_ref, e2_ref, s_ref, wx_ref, wy_ref, wz_ref, di_ref, r1_ref)
     blank_level1(r1_ref, 2)
     e21, r2 = descend_second(
@@ -370,8 +357,16 @@
 
 
 def third_kernel(
-    own, low, high, r2_ref, s2_ref, di2_ref, wx2_ref, wy2_ref, wz2_ref, e22_ref, msg_ref
+    far_low, low, own, high, far_high,
+    r2_ref, s2_ref, di2_ref, wx2_ref, wy2_ref, wz2_ref, e22_ref,
+    s3_ref, di3_ref, wx3_ref, wy3_ref, wz3_ref, msg_ref,
 ):
+    sources = [far_low[:, 0:1, :]]
+    sources += [ref[:, 5, 0:1, :] for ref in (low, own, high)]
+    sources += [far_high[:, 0:1, :]]
+    s3, wx3, wy3, wz3 = unpack_bands3(sources)
+    s3_ref[...], wx3_ref[...], wy3_ref[...], wz3_ref[...] = s3, wx3, wy3, wz3
+    di3_ref[...] = relax_factor(s3, wx3, wy3, wz3, 2, 8)
     r2, s2, wx2, wy2, wz2 = (unpack_level2(f, own, low, high) for f in range(5))
     di2 = relax_factor(s2, wx2, wy2, wz2, 1, 4)
     r2_ref[...], s2_ref[...], di2_ref[...] = r2, s2, di2
@@ -485,22 +480,19 @@
 
 
 def climb_kernel(
-    far_low, low, own, high, far_high, third_ref,
+    third_ref, s3_ref, di3_ref, wx3_ref, wy3_ref, wz3_ref,
     r2_ref, s2_ref, di2_ref, wx2_ref, wy2_ref, wz2_ref, e22_ref,
     r1_ref, s1_ref, di1_ref, wx1_ref, wy1_ref, wz1_ref, e21_ref, e2_ref,
-    pre_ref, below_ref, s3_ref, di3_ref, wx3_ref, wy3_ref, wz3_ref,
+    pre_ref, below_ref,
     *, groups, thirds, rows,
 ):
-    sources = [far_low[:, 0:1, :]]
-    sources += [ref[:, 5, 0:1, :] for ref in (low, own, high)]
-    sources += [far_high[:, 0:1, :]]
-    s3, wx3, wy3, wz3 = unpack_bands3(sources)
-    di3 = relax_factor(s3, wx3, wy3, wz3, 2, 8)
-    s3_ref[...], di3_ref[...], wx3_ref[...], wy3_ref[...], wz3_ref[...] = s3, di3, wx3, wy3, wz3
     r3 = strided(third_ref, 0, thirds, groups, rows)
     below = line_sums(strided(third_ref, thirds, thirds, groups, rows))
     below_ref[...] = below
-    corr3 = solve_third(unpack_r3(r3), line_sums(r3) / below, s3, di3, wx3, wy3, wz3)
+    corr3 = solve_third(
+        unpack_r3(r3), line_sums(r3) / below,
+        s3_ref[...], di3_ref[...], wx3_ref[...], wy3_ref[...], wz3_ref[...],
+    )
     corr2 = climb_to_second(corr3, r2_ref, s2_ref, di2_ref, wx2_ref, wy2_ref, wz2_ref, e22_ref)
     v = climb_to_first(
         e21_ref[...] + corr2, r1_ref, s1_ref, di1_ref, wx1_ref, wy1_ref, wz1_ref
@@ -571,7 +563,7 @@
         v_ref[here] = u_ref[here] + v + di_ref[here] * (r_ref[here] - av)
         return carry
 
-    lax.fori_loop(0, BX // 2 + 1, post, 0)
+    lax.fori_loop(0, BX // 2 + 1, post, 0, unroll=True)
 
     def remain(i, carry):
         at = 9 + 2 * i
@@ -581,7 +573,7 @@
         left_ref[pl.ds(2 * i, 2)] = left[:, 8:24]
         return carry
 
-    lax.fori_loop(0, BX // 2, remain, 0)
+    lax.fori_loop(0, BX // 2, remain, 0, unroll=True)
 
 
 def call(body, outs, operands, scratch=(), smem=()):
@@ -595,7 +587,7 @@
         ],
         out_specs=[vmem] * len(outs),
         scratch_shapes=[pltpu.VMEM(shape, F32) for shape in scratch],
-        compiler_params=pltpu.CompilerParams(vmem_limit_bytes=48 * 1024 * 1024),
+        compiler_params=pltpu.CompilerParams(vmem_limit_bytes=16 * 1024 * 1024),
     )(*operands)
 
 
@@ -625,16 +617,20 @@
     thirds = tiles // 4
     top, one, two = (PX, WY, NZ), (L1X, WY, NZ), (2 * tiles, 16, NZ)
     three, line = (tiles, 24, NZ), (tiles, 1, NZ)
-    rows_once, rows_again = 2 * thirds, -(-thirds // 2) * 2
-
-    raw = jnp.stack([pressure_head, old_head, soil_type.astype(F32)])
-    core, ylow, yhigh = surround(raw, 1)
+    rows_once, rows_again = 2 * thirds, thirds
+
+    (fields,) = call(
+        soil_kernel,
+        [(4, BX, BY, NZ)],
+        [pressure_head, old_head, soil_type, conduct_sat, alpha_param, shape_param, water_span],
+        smem=(3, 4, 5, 6),
+    )
+    core, ylow, yhigh = surround(fields, 1)
     rhs, s0, di0, wx0, wy0, wz0, e2, r1, s1, di1, wx1, wy1, wz1, e21, msg = call(
         assemble_kernel,
         [top] * 7 + [one] * 7 + [(tiles, 6, 2, NZ)],
-        [core, ylow, yhigh, conduct_sat, alpha_param, shape_param, water_span],
+        [core, ylow, yhigh],
         [top] * 4,
-        smem=(3, 4, 5, 6),
     )
     bands0 = [s0, di0, wx0, wy0, wz0]
     bands1 = [s1, di1, wx1, wy1, wz1]
@@ -642,15 +638,18 @@
     own = everyone(msg, "tile")
     low, high = beside(own, own, "group")
     far_low, far_high = beside(own[:, 5], own[:, 5], "group", 2)
-    r2, s2, di2, wx2, wy2, wz2, e22, msg = call(
-        third_kernel, [two] * 7 + [(groups, thirds, 2, NZ)], [own, low, high]
-    )
+    r2, s2, di2, wx2, wy2, wz2, e22, s3, di3, wx3, wy3, wz3, msg = call(
+        third_kernel,
+        [two] * 7 + [three] * 5 + [(groups, thirds, 2, NZ)],
+        [far_low, low, own, high, far_high],
+    )
+    bands3 = [s3, di3, wx3, wy3, wz3]
     bands2 = [s2, di2, wx2, wy2, wz2]
     third = everyone(msg, "group").reshape(groups * rows_once, NZ)
-    pre, below, *bands3 = call(
+    pre, below = call(
         functools.partial(climb_kernel, groups=groups, thirds=thirds, rows=rows_once),
-        [(BX, BY, NZ), line] + [three] * 5,
-        [far_low, low, own, high, far_high, third, r2, *bands2, e22, r1, *bands1, e21, e2],
+        [(BX, BY, NZ), line],
+        [third, *bands3, r2, *bands2, e22, r1, *bands1, e21, e2],
     )
 
     core, ylow, yhigh = surround(pre, 0)
@@ -664,7 +663,7 @@
     low, high = beside(own, own, "group")
     r2, e22, msg = call(
         third_again_kernel,
-        [two] * 2 + [(groups, rows_again // 2, 2, NZ)],
+        [two] * 2 + [(groups, rows_again, 1, NZ)],
         [own, low, high, *bands2],
     )
     third = everyone(msg, "group").reshape(groups * rows_again, NZ)

time: 196 us -> 181 us (0.923)
  blocking collectives: 62.5 us -> 89 us
  starting transfers between devices: 67.8 us -> 51.1 us
  Pallas kernels: 29.1 us -> 18 us
  local copies, waits for them, and re-layouts: 13.1 us -> 5.24 us
  waiting for transfers between devices: 20.9 us -> 15.4 us
    all_to_all x3 -> x4, blocking collectives: 62.5 us -> 89 us  [everyone(): return lax.all_to_all(blocks, axis, 0, 0, tiled=True)]
    all_to_all x1 -> x0, starting transfers between devices: 16.5 us -> none  [everyone(): return lax.all_to_all(blocks, axis, 0, 0, tiled=True)]
    pallas_call x6 -> x7, Pallas kernels: 29.1 us -> 18 us  [call(): pl.pallas_call(body, out_shape=[jax.ShapeDtypeStruct(shape, F32) for shap...]
    unnamed x61 -> x17, local copies, waits for them, and re-layouts: 13 us -> 5.15 us
    all_to_all x1 -> x0, waiting for transfers between devices: 5.9 us -> none  [everyone(): return lax.all_to_all(blocks, axis, 0, 0, tiled=True)]
  transfers between devices with their start and end apart: 15 -> 14, of which waited for: 11 -> 8; matrix products, arithmetic and copies ran while one was open for 0% -> 0% of each run, Pallas kernels for 0% -> 0%
where the time goes in v3:
time: 181 us; the launch traced here: 180 us
  blocking collectives  89 us (49%)
  starting transfers between devices  51.1 us (28%)
  Pallas kernels  18 us (10%)
  waiting for transfers between devices  15.4 us (9%)
  local copies, waits for them, and re-layouts  5.24 us (3%)
    all_to_all x4, blocking collectives, everyone(): return lax.all_to_all(blocks, axis, 0, 0, tiled=True)  89 us
    ppermute x7, starting transfers between devices, beside(): from_low = lax.ppermute(to_high, axis, [(i, i + step) for i in range(ends)])  26.3 us
    ppermute x7, starting transfers between devices, beside(): from_high = lax.ppermute(to_low, axis, [(i + step, i) for i in range(ends)])  24.8 us
    pallas_call x7, Pallas kernels, call(): pl.pallas_call(body, out_shape=[jax.ShapeDtypeStruct(shape, F32) for shap...  18 us
    ppermute x7, waiting for transfers between devices, beside(): from_low = lax.ppermute(to_high, axis, [(i, i + step) for i in range(ends)])  9.54 us
    ppermute x7, waiting for transfers between devices, beside(): from_high = lax.ppermute(to_low, axis, [(i + step, i) for i in range(ends)])  5.86 us
    unnamed x17, local copies, waits for them, and re-layouts  5.15 us
  transfers between devices with their start and end apart: 14, of which 8 were waited for; matrix products, arithmetic and copies ran while one was open for 0% of the time, Pallas kernels for 0%

profile of v3, /device:TPU:1, one launch (start us, length us, event | category | flops | bytes accessed | tf_op | source)
XLA Modules:
  0.0 179.7 jit_solution(3546179994769042376)
XLA Ops:
  8.0 5.5 %collective-permute-start = (f32[4,8,16,128]{3,2,1,0:T(8,128)S(1)}, f32[4,8,16,128]{3,2,1,0:T(8,128)S(1)}, u32[]{:S(2)}, u32[]{:S(2)}) collective-permute-start(f32[4,8,16,128]{3,2,1,0:T(8,128)S(1)} %shard_map.86), channel_id=1, source_target_pairs={{0,64},{64,128},{128,192},{192,256},{256,320},{320,384},{384,448},... | collective-permute-start | bytes 786440 | tf_op jit(solution)/shard_map/ppermute | solution.py:596
  13.5 1.8 %collective-permute-done.1 = f32[4,8,16,128]{3,2,1,0:T(8,128)S(1)} collective-permute-done((f32[4,8,16,128]{3,2,1,0:T(8,128)S(1)}, f32[4,8,16,128]{3,2,1,0:T(8,128)S(1)}, u32[]{:S(2)}, u32[]{:S(2)}) %collective-permute-start.1) | collective-permute-done | bytes 262176 | tf_op jit(solution)/shard_map/ppermute | solution.py:597
  15.3 1.5 collective-permute-done
  16.9 12.1 %collective-permute-start.3 = (f32[4,24,8,128]{3,2,1,0:T(8,128)S(1)}, f32[4,24,8,128]{3,2,1,0:T(8,128)S(1)}, u32[]{:S(2)}, u32[]{:S(2)}) collective-permute-start(f32[4,24,8,128]{3,2,1,0:T(8,128)S(1)} %get-tuple-element.82), channel_id=1, source_target_pairs={{1,0},{2,1},{3,2},{4,3},{5,4},{6,5},{7,6},{8,7},{9,8},{10,9},{11,1... | collective-permute-start | bytes 1179656 | tf_op jit(solution)/shard_map/ppermute | solution.py:597
  29.0 1.9 %collective-permute-start.2 = (f32[4,24,8,128]{3,2,1,0:T(8,128)S(1)}, f32[4,24,8,128]{3,2,1,0:T(8,128)S(1)}, u32[]{:S(2)}, u32[]{:S(2)}) collective-permute-start(f32[4,24,8,128]{3,2,1,0:T(8,128)S(1)} %get-tuple-element.83), channel_id=1, source_target_pairs={{0,1},{1,2},{2,3},{3,4},{4,5},{5,6},{6,7},{7,8},{8,9},{9,10},{10,1... | collective-permute-start | bytes 1179656 | tf_op jit(solution)/shard_map/ppermute | solution.py:596
  31.0 4.7 %collective-permute-done.2.ylow = f32[4,24,8,128]{3,2,1,0:T(8,128)S(1)} collective-permute-done((f32[4,24,8,128]{3,2,1,0:T(8,128)S(1)}, f32[4,24,8,128]{3,2,1,0:T(8,128)S(1)}, u32[]{:S(2)}, u32[]{:S(2)}) %collective-permute-start.2) | collective-permute-done | bytes 393248 | tf_op jit(solution)/shard_map/ppermute | solution.py:596
  35.7 4.7 %shard_map.87 = (f32[26,32,128]{2,1,0:T(8,128)S(1)}, f32[26,32,128]{2,1,0:T(8,128)S(1)}, f32[26,32,128]{2,1,0:T(8,128)S(1)}, f32[26,32,128]{2,1,0:T(8,128)S(1)},...) custom-call(f32[4,24,16,128]{3,2,1,0:T(8,128)S(1)} %pad_maximum_fusi, ...), custom_call_target="tpu_custom_call" | custom-call | tf_op jit(solution)/shard_map/pallas_call | solution.py:581
  40.4 20.1 %all_to_all.20.own = f32[12,6,2,128]{3,2,1,0:T(2,128)S(1)} all-to-all(f32[12,6,2,128]{3,2,1,0:T(2,128)S(1)} %get-tuple-element.42), channel_id=1, replica_groups=mesh['tile'=12,'group'=64] {'tile'}, dimensions={0} | all-to-all | bytes 147456 | tf_op jit(solution)/shard_map/all_to_all | solution.py:612
  60.4 1.9 %collective-permute-start.6 = (f32[12,6,2,128]{3,2,1,0:T(2,128)S(1)}, f32[12,6,2,128]{3,2,1,0:T(2,128)S(1)}, u32[]{:S(2)}, u32[]{:S(2)}) collective-permute-start(f32[12,6,2,128]{3,2,1,0:T(2,128)S(1)} %all_to_all.20.own), channel_id=1, source_target_pairs={{1,0},{2,1},{3,2},{4,3},{5,4},{6,5},{7,6},{8,7},{9,8},{10,9},{11,1... | collective-permute-start | bytes 221192 | tf_op jit(solution)/shard_map/ppermute | solution.py:597
  62.3 6.2 %collective-permute-start.5 = (f32[12,6,2,128]{3,2,1,0:T(2,128)S(1)}, f32[12,6,2,128]{3,2,1,0:T(2,128)S(1)}, u32[]{:S(2)}, u32[]{:S(2)}) collective-permute-start(f32[12,6,2,128]{3,2,1,0:T(2,128)S(1)} %all_to_all.20.own), channel_id=1, source_target_pairs={{0,1},{1,2},{2,3},{3,4},{4,5},{5,6},{6,7},{7,8},{8,9},{9,10},{10,1... | collective-permute-start | bytes 221192 | tf_op jit(solution)/shard_map/ppermute | solution.py:596
  69.9 4.0 %collective-permute-start.4 = (f32[12,2,128]{2,1,0:T(2,128)S(1)}, f32[12,2,128]{2,1,0:T(2,128)S(1)}, u32[]{:S(2)}, u32[]{:S(2)}) collective-permute-start(f32[12,2,128]{2,1,0:T(2,128)S(1)} %slice_bitcast_fusion), channel_id=1, source_target_pairs={{0,2},{1,3},{2,4},{3,5},{4,6},{5,7},{6,8},{7,9},{8,10},{9,11},{10,... | collective-permute-start | bytes 36872 | tf_op jit(solution)/shard_map/ppermute | solution.py:596
  74.7 3.4 %shard_map.88 = (f32[24,16,128]{2,1,0:T(8,128)S(1)}, f32[24,16,128]{2,1,0:T(8,128)S(1)}, f32[24,16,128]{2,1,0:T(8,128)S(1)}, f32[24,16,128]{2,1,0:T(8,128)S(1)},...) custom-call(f32[12,2,128]{2,1,0:T(2,128)S(1)} %collective-permute-do, ...), custom_call_target="tpu_custom_call" | custom-call | tf_op jit(solution)/shard_map/pallas_call | solution.py:581
  78.1 30.9 %all_to_all.21 = f32[64,3,2,128]{3,2,1,0:T(2,128)S(1)} all-to-all(f32[64,3,2,128]{3,2,1,0:T(2,128)S(1)} %get-tuple-element.43), channel_id=1, replica_groups=mesh['tile'=12,'group'=64] {'group'}, dimensions={0} | all-to-all | bytes 393216 | tf_op jit(solution)/shard_map/all_to_all | solution.py:612
  109.0 1.5 shard_map.89
  110.5 2.2 %collective-permute-start.8 = (f32[8,16,128]{2,1,0:T(8,128)S(1)}, f32[8,16,128]{2,1,0:T(8,128)S(1)}, u32[]{:S(2)}, u32[]{:S(2)}) collective-permute-start(f32[8,16,128]{2,1,0:T(8,128)S(1)} %get-tuple-element.64), channel_id=1, source_target_pairs={{0,64},{64,128},{128,192},{192,256},{256,320},{320,384},{384,448},... | collective-permute-start | bytes 196616 | tf_op jit(solution)/shard_map/ppermute | solution.py:596
  114.1 3.7 %collective-permute-done.9 = f32[8,16,128]{2,1,0:T(8,128)S(1)} collective-permute-done((f32[8,16,128]{2,1,0:T(8,128)S(1)}, f32[8,16,128]{2,1,0:T(8,128)S(1)}, u32[]{:S(2)}, u32[]{:S(2)}) %collective-permute-start.9) | collective-permute-done | bytes 65568 | tf_op jit(solution)/shard_map/ppermute | solution.py:597
  117.8 3.7 %collective-permute-start.11 = (f32[24,8,128]{2,1,0:T(8,128)S(1)}, f32[24,8,128]{2,1,0:T(8,128)S(1)}, u32[]{:S(2)}, u32[]{:S(2)}) collective-permute-start(f32[24,8,128]{2,1,0:T(8,128)S(1)} %get-tuple-element.84), channel_id=1, source_target_pairs={{1,0},{2,1},{3,2},{4,3},{5,4},{6,5},{7,6},{8,7},{9,8},{10,9},{11,1... | collective-permute-start | bytes 294920 | tf_op jit(solution)/shard_map/ppermute | solution.py:597
  121.5 2.0 %collective-permute-start.10 = (f32[24,8,128]{2,1,0:T(8,128)S(1)}, f32[24,8,128]{2,1,0:T(8,128)S(1)}, u32[]{:S(2)}, u32[]{:S(2)}) collective-permute-start(f32[24,8,128]{2,1,0:T(8,128)S(1)} %get-tuple-element.85), channel_id=1, source_target_pairs={{0,1},{1,2},{2,3},{3,4},{4,5},{5,6},{6,7},{7,8},{8,9},{9,10},{10,1... | collective-permute-start | bytes 294920 | tf_op jit(solution)/shard_map/ppermute | solution.py:596
  125.1 4.1 %shard_map.90 = (f32[26,32,128]{2,1,0:T(8,128)S(1)}, f32[26,32,128]{2,1,0:T(8,128)S(1)}, f32[26,32,128]{2,1,0:T(8,128)S(1)}, f32[12,32,128]{2,1,0:T(8,128)S(1)},...) custom-call(f32[24,16,128]{2,1,0:T(8,128)S(1)} %constant_dynamic-update-slice_fusion.core, ...), custom_call_target="tpu_custom_call" | custom-call | tf_op jit(solution)/shard_map/pallas_call | solution.py:581
  129.2 14.3 %all_to_all.22 = f32[12,5,2,128]{3,2,1,0:T(2,128)S(1)} all-to-all(f32[12,5,2,128]{3,2,1,0:T(2,128)S(1)} %get-tuple-element.71), channel_id=1, replica_groups=mesh['tile'=12,'group'=64] {'tile'}, dimensions={0} | all-to-all | bytes 122880 | tf_op jit(solution)/shard_map/all_to_all | solution.py:612
  143.5 3.3 %collective-permute-start.13 = (f32[13,5,2,128]{3,2,1,0:T(2,128)S(1)}, f32[13,5,2,128]{3,2,1,0:T(2,128)S(1)}, u32[]{:S(2)}, u32[]{:S(2)}) collective-permute-start(f32[13,5,2,128]{3,2,1,0:T(2,128)S(1)} %constant_dynamic-update-slice_fusion.3.own), channel_id=1, source_target_pairs={{1,0},{2,1},{3,2},{4,3},{5,4},{6,5},{7,6},{8,7},{9,8},{10,9},{11,1... | collective-permute-start | bytes 199688 | tf_op jit(solution)/shard_map/ppermute | solution.py:597
  146.8 4.5 %collective-permute-start.12 = (f32[13,5,2,128]{3,2,1,0:T(2,128)S(1)}, f32[13,5,2,128]{3,2,1,0:T(2,128)S(1)}, u32[]{:S(2)}, u32[]{:S(2)}) collective-permute-start(f32[13,5,2,128]{3,2,1,0:T(2,128)S(1)} %constant_dynamic-update-slice_fusion.3.own), channel_id=1, source_target_pairs={{0,1},{1,2},{2,3},{3,4},{4,5},{5,6},{6,7},{7,8},{8,9},{9,10},{10,1... | collective-permute-start | bytes 199688 | tf_op jit(solution)/shard_map/ppermute | solution.py:596
  153.5 23.7 %all_to_all.23 = f32[64,3,1,128]{3,2,1,0:T(1,128)S(1)} all-to-all(f32[64,3,1,128]{3,2,1,0:T(1,128)S(1)} %get-tuple-element.73), channel_id=1, replica_groups=mesh['tile'=12,'group'=64] {'group'}, dimensions={0} | all-to-all | bytes 196608 | tf_op jit(solution)/shard_map/all_to_all | solution.py:612
  177.2 2.5 %shard_map.92 = (f32[8,16,128]{2,1,0:T(8,128)}, f32[8,16,128]{2,1,0:T(8,128)}) custom-call(f32[192,128]{1,0:T(8,128)S(1)} %bitcast.7, f32[12,1,128]{2,1,0:T(1,128)S(1)} %get-tuple-element.74.below_ref, f32[12,24,128]{2,1,0:T(8,128)S(1)} %get-tuple-element.44.s3_ref, f32[12,24,128]{2,1,0:T(8,128)S(1)} %get-tuple-element.45.di3_ref, ...), custom_call_target="tpu_custom_call" | custom-call | tf_op jit(solution)/shard_map/pallas_call | solution.py:581
  (38 shorter events, 14.8 us)
Async XLA Ops:
  0.6 0.8 copy-start
  1.5 0.8 copy-start.1
  2.3 0.8 copy-start.2
  3.2 0.7 copy-start.3
  3.8 0.7 copy-start.4
  4.5 0.7 copy-start.5
  5.1 0.7 copy-start.6
  6.7 8.6 %collective-permute-start.1 = (f32[4,8,16,128]{3,2,1,0:T(8,128)S(1)}, f32[4,8,16,128]{3,2,1,0:T(8,128)S(1)}, u32[]{:S(2)}, u32[]{:S(2)}) collective-permute-start(f32[4,8,16,128]{3,2,1,0:T(8,128)S(1)} %shard_map.86), channel_id=1, source_target_pairs={{64,0},{128,64},{192,128},{256,192},{320,256},{384,320},{448,384},... | collective-permute-start | bytes 786440 | tf_op jit(solution)/shard_map/ppermute | solution.py:597
  8.0 8.8 %collective-permute-start = (f32[4,8,16,128]{3,2,1,0:T(8,128)S(1)}, f32[4,8,16,128]{3,2,1,0:T(8,128)S(1)}, u32[]{:S(2)}, u32[]{:S(2)}) collective-permute-start(f32[4,8,16,128]{3,2,1,0:T(8,128)S(1)} %shard_map.86), channel_id=1, source_target_pairs={{0,64},{64,128},{128,192},{192,256},{256,320},{320,384},{384,448},... | collective-permute-start | bytes 786440 | tf_op jit(solution)/shard_map/ppermute | solution.py:596
  16.9 14.0 %collective-permute-start.3 = (f32[4,24,8,128]{3,2,1,0:T(8,128)S(1)}, f32[4,24,8,128]{3,2,1,0:T(8,128)S(1)}, u32[]{:S(2)}, u32[]{:S(2)}) collective-permute-start(f32[4,24,8,128]{3,2,1,0:T(8,128)S(1)} %get-tuple-element.82), channel_id=1, source_target_pairs={{1,0},{2,1},{3,2},{4,3},{5,4},{6,5},{7,6},{8,7},{9,8},{10,9},{11,1... | collective-permute-start | bytes 1179656 | tf_op jit(solution)/shard_map/ppermute | solution.py:597
  29.0 6.6 %collective-permute-start.2 = (f32[4,24,8,128]{3,2,1,0:T(8,128)S(1)}, f32[4,24,8,128]{3,2,1,0:T(8,128)S(1)}, u32[]{:S(2)}, u32[]{:S(2)}) collective-permute-start(f32[4,24,8,128]{3,2,1,0:T(8,128)S(1)} %get-tuple-element.83), channel_id=1, source_target_pairs={{0,1},{1,2},{2,3},{3,4},{4,5},{5,6},{6,7},{7,8},{8,9},{9,10},{10,1... | collective-permute-start | bytes 1179656 | tf_op jit(solution)/shard_map/ppermute | solution.py:596
  60.4 14.3 %collective-permute-start.6 = (f32[12,6,2,128]{3,2,1,0:T(2,128)S(1)}, f32[12,6,2,128]{3,2,1,0:T(2,128)S(1)}, u32[]{:S(2)}, u32[]{:S(2)}) collective-permute-start(f32[12,6,2,128]{3,2,1,0:T(2,128)S(1)} %all_to_all.20.own), channel_id=1, source_target_pairs={{1,0},{2,1},{3,2},{4,3},{5,4},{6,5},{7,6},{8,7},{9,8},{10,9},{11,1... | collective-permute-start | bytes 221192 | tf_op jit(solution)/shard_map/ppermute | solution.py:597
  62.3 12.3 %collective-permute-start.5 = (f32[12,6,2,128]{3,2,1,0:T(2,128)S(1)}, f32[12,6,2,128]{3,2,1,0:T(2,128)S(1)}, u32[]{:S(2)}, u32[]{:S(2)}) collective-permute-start(f32[12,6,2,128]{3,2,1,0:T(2,128)S(1)} %all_to_all.20.own), channel_id=1, source_target_pairs={{0,1},{1,2},{2,3},{3,4},{4,5},{5,6},{6,7},{7,8},{8,9},{9,10},{10,1... | collective-permute-start | bytes 221192 | tf_op jit(solution)/shard_map/ppermute | solution.py:596
  68.6 5.3 %collective-permute-start.7 = (f32[12,2,128]{2,1,0:T(2,128)S(1)}, f32[12,2,128]{2,1,0:T(2,128)S(1)}, u32[]{:S(2)}, u32[]{:S(2)}) collective-permute-start(f32[12,2,128]{2,1,0:T(2,128)S(1)} %slice_bitcast_fusion), channel_id=1, source_target_pairs={{2,0},{3,1},{4,2},{5,3},{6,4},{7,5},{8,6},{9,7},{10,8},{11,9},{12,... | collective-permute-start | bytes 36872 | tf_op jit(solution)/shard_map/ppermute | solution.py:597
  69.9 4.8 %collective-permute-start.4 = (f32[12,2,128]{2,1,0:T(2,128)S(1)}, f32[12,2,128]{2,1,0:T(2,128)S(1)}, u32[]{:S(2)}, u32[]{:S(2)}) collective-permute-start(f32[12,2,128]{2,1,0:T(2,128)S(1)} %slice_bitcast_fusion), channel_id=1, source_target_pairs={{0,2},{1,3},{2,4},{3,5},{4,6},{5,7},{6,8},{7,9},{8,10},{9,11},{10,... | collective-permute-start | bytes 36872 | tf_op jit(solution)/shard_map/ppermute | solution.py:596
  110.5 3.5 %collective-permute-start.8 = (f32[8,16,128]{2,1,0:T(8,128)S(1)}, f32[8,16,128]{2,1,0:T(8,128)S(1)}, u32[]{:S(2)}, u32[]{:S(2)}) collective-permute-start(f32[8,16,128]{2,1,0:T(8,128)S(1)} %get-tuple-element.64), channel_id=1, source_target_pairs={{0,64},{64,128},{128,192},{192,256},{256,320},{320,384},{384,448},... | collective-permute-start | bytes 196616 | tf_op jit(solution)/shard_map/ppermute | solution.py:596
  112.7 5.0 %collective-permute-start.9 = (f32[8,16,128]{2,1,0:T(8,128)S(1)}, f32[8,16,128]{2,1,0:T(8,128)S(1)}, u32[]{:S(2)}, u32[]{:S(2)}) collective-permute-start(f32[8,16,128]{2,1,0:T(8,128)S(1)} %get-tuple-element.64), channel_id=1, source_target_pairs={{64,0},{128,64},{192,128},{256,192},{320,256},{384,320},{448,384},... | collective-permute-start | bytes 196616 | tf_op jit(solution)/shard_map/ppermute | solution.py:597
  117.8 6.1 %collective-permute-start.11 = (f32[24,8,128]{2,1,0:T(8,128)S(1)}, f32[24,8,128]{2,1,0:T(8,128)S(1)}, u32[]{:S(2)}, u32[]{:S(2)}) collective-permute-start(f32[24,8,128]{2,1,0:T(8,128)S(1)} %get-tuple-element.84), channel_id=1, source_target_pairs={{1,0},{2,1},{3,2},{4,3},{5,4},{6,5},{7,6},{8,7},{9,8},{10,9},{11,1... | collective-permute-start | bytes 294920 | tf_op jit(solution)/shard_map/ppermute | solution.py:597
  121.5 3.6 %collective-permute-start.10 = (f32[24,8,128]{2,1,0:T(8,128)S(1)}, f32[24,8,128]{2,1,0:T(8,128)S(1)}, u32[]{:S(2)}, u32[]{:S(2)}) collective-permute-start(f32[24,8,128]{2,1,0:T(8,128)S(1)} %get-tuple-element.85), channel_id=1, source_target_pairs={{0,1},{1,2},{2,3},{3,4},{4,5},{5,6},{6,7},{7,8},{8,9},{9,10},{10,1... | collective-permute-start | bytes 294920 | tf_op jit(solution)/shard_map/ppermute | solution.py:596
  143.5 7.8 %collective-permute-start.13 = (f32[13,5,2,128]{3,2,1,0:T(2,128)S(1)}, f32[13,5,2,128]{3,2,1,0:T(2,128)S(1)}, u32[]{:S(2)}, u32[]{:S(2)}) collective-permute-start(f32[13,5,2,128]{3,2,1,0:T(2,128)S(1)} %constant_dynamic-update-slice_fusion.3.own), channel_id=1, source_target_pairs={{1,0},{2,1},{3,2},{4,3},{5,4},{6,5},{7,6},{8,7},{9,8},{10,9},{11,1... | collective-permute-start | bytes 199688 | tf_op jit(solution)/shard_map/ppermute | solution.py:597
  146.8 5.8 %collective-permute-start.12 = (f32[13,5,2,128]{3,2,1,0:T(2,128)S(1)}, f32[13,5,2,128]{3,2,1,0:T(2,128)S(1)}, u32[]{:S(2)}, u32[]{:S(2)}) collective-permute-start(f32[13,5,2,128]{3,2,1,0:T(2,128)S(1)} %constant_dynamic-update-slice_fusion.3.own), channel_id=1, source_target_pairs={{0,1},{1,2},{2,3},{3,4},{4,5},{5,6},{6,7},{7,8},{8,9},{9,10},{10,1... | collective-permute-start | bytes 199688 | tf_op jit(solution)/shard_map/ppermute | solution.py:596

commit v4 on v3

--- a/solution.py
+++ b/solution.py
@@ -160,7 +160,7 @@
         e2_ref[pl.ds(at, 2)] = v + di_ref[pl.ds(at, 2)] * (r_ref[pl.ds(at, 2)] - av)
         return carry
 
-    lax.fori_loop(1, WX // 2 - 1, second, 0, unroll=2)
+    lax.fori_loop(1, WX // 2 - 1, second, 0, unroll=5)
 
     def third(i, carry):
         at = 1 + 2 * i
@@ -168,7 +168,7 @@
         r1_ref[pl.ds(i, 1)] = restrict(r_ref[pl.ds(at, 2)] - av, 1, 1)
         return carry
 
-    lax.fori_loop(2, WX // 2 - 2, third, 0, unroll=2)
+    lax.fori_loop(2, WX // 2 - 2, third, 0, unroll=4)
 
 
 def descend_second(r1, s1, wx1, wy1, wz1, di1):
@@ -178,7 +178,21 @@
     return second, restrict(defect, 2, 2)
 
 
-def soil_kernel(head_ref, old_ref, soil_ref, ks_ref, alpha_ref, shape_ref, span_ref, out_ref):
+def soil_kernel(
+    head_in, old_in, soil_in, ks_in, alpha_in, shape_in, span_in, out_ref,
+    head_ref, old_ref, soil_ref, ks_ref, alpha_ref, shape_ref, span_ref, sems,
+):
+    given = (ks_in, alpha_in, shape_in, span_in, head_in, old_in, soil_in)
+    held = (ks_ref, alpha_ref, shape_ref, span_ref, head_ref, old_ref, soil_ref)
+    copies = [
+        pltpu.make_async_copy(src, dst, sems.at[i])
+        for i, (src, dst) in enumerate(zip(given, held, strict=True))
+    ]
+    for copy in copies:
+        copy.start()
+    for copy in copies:
+        copy.wait()
+
     def cells(i, carry):
         row = pl.ds(i, 1)
         head, old, soil = head_ref[row], old_ref[row], soil_ref[row]
@@ -239,7 +253,7 @@
         wz_ref[pl.ds(at, 2)] = jnp.where(iota(wz.shape, 2) == 0, 0.0, wz)
         return carry
 
-    lax.fori_loop(0, WX // 2, faces, 0, unroll=2)
+    lax.fori_loop(0, WX // 2, faces, 0, unroll=4)
 
     def right_side(i, carry):
         at = 1 + 2 * i
@@ -258,7 +272,7 @@
         e1_ref[rows] = rhs * di
         return carry
 
-    lax.fori_loop(0, WX // 2, right_side, 0, unroll=2)
+    lax.fori_loop(0, WX // 2, right_side, 0, unroll=4)
 
     def bands(i, carry):
         rows = pl.ds(1 + 2 * i, 2)
@@ -267,7 +281,7 @@
         s1_ref[row], wx1_ref[row], wy1_ref[row], wz1_ref[row] = s1, wx1, wy1, wz1
         return carry
 
-    lax.fori_loop(1, WX // 2 - 1, bands, 0, unroll=2)
+    lax.fori_loop(1, WX // 2 - 1, bands, 0, unroll=5)
     for ref in (s1_ref, wx1_ref, wy1_ref, wz1_ref):
         blank_level1(ref, 1)
     blank_level1(r1_ref, 2)
@@ -300,7 +314,7 @@
         u_ref[rows] = v + di_ref[rows] * (rhs_ref[rows] - av)
         return carry
 
-    lax.fori_loop(0, WX // 2, post, 0, unroll=2)
+    lax.fori_loop(0, WX // 2, post, 0, unroll=4)
 
     def remain(i, carry):
         at = 1 + 2 * i
@@ -311,7 +325,7 @@
         e1_ref[rows] = left * di_ref[rows]
         return carry
 
-    lax.fori_loop(1, WX // 2 - 1, remain, 0, unroll=2)
+    lax.fori_loop(1, WX // 2 - 1, remain, 0, unroll=5)
     descend_top(r_ref, e1_ref, e2_ref, s_ref, wx_ref, wy_ref, wz_ref, di_ref, r1_ref)
     blank_level1(r1_ref, 2)
     e21, r2 = descend_second(
@@ -320,6 +334,25 @@
     e21_ref[...] = e21
     send(msg_ref, [pack_level2(r2[2:4]), pack_ring1(e21)])
     send(edge_ref, [pack_edge1(e21)])
+
+
+def message_rows(ref):
+    tiles = lax.axis_size("tile")
+    return lambda field, half: ref[0:tiles, field, half : half + 1, :]
+
+
+def pair_rows(refs):
+    even = lax.axis_index("group") % 2 == 0
+
+    def pick(ref, core):
+        return lambda field, half: ref[:, core, field, half : half + 1, :]
+
+    six = [pick(ref, core) for ref in refs for core in range(2)]
+
+    def choose(first, second):
+        return lambda field, half: jnp.where(even, first(field, half), second(field, half))
+
+    return [choose(six[i], six[i + 1]) for i in range(5)]
 
 
 def unpack_level2(field, own, low, high):
@@ -329,8 +362,8 @@
     halves = []
     for half in range(2):
 
-        def spread(ref, half=half):
-            return jnp.broadcast_to(ref[0:tiles, field, half : half + 1, :], shape)
+        def spread(pick, half=half):
+            return jnp.broadcast_to(pick(field, half), shape)
 
         v = jnp.where(sub < 4, spread(low), jnp.where(sub < 8, spread(own), spread(high)))
         v = jnp.where((lane % 4 == sub % 4) & (sub < 12), v, 0.0)
@@ -350,6 +383,18 @@
     return rows
 
 
+def pack_sums3(v):
+    v = v + turn(v, -2, 1)
+    sub, lane = iota((16, NZ), 0), iota((16, NZ), 1)
+    rows = []
+    for first in range(0, v.shape[0], 8):
+        total = jnp.zeros((16, NZ), F32)
+        for q in range(min(8, v.shape[0] - first)):
+            total = total + jnp.where((sub == 4) & (lane % 8 == q), v[first + q], 0.0)
+        rows.append(jnp.sum(total, axis=0, keepdims=True))
+    return rows
+
+
 def descend_third(r2, s2, wx2, wy2, wz2, di2):
     first = r2 * di2
     second = first + di2 * (r2 - operate(first, s2, wx2, wy2, wz2, 1, 4))
@@ -357,13 +402,13 @@
 
 
 def third_kernel(
-    far_low, low, own, high, far_high,
+    before, here, after,
     r2_ref, s2_ref, di2_ref, wx2_ref, wy2_ref, wz2_ref, e22_ref,
     s3_ref, di3_ref, wx3_ref, wy3_ref, wz3_ref, msg_ref,
 ):
-    sources = [far_low[:, 0:1, :]]
-    sources += [ref[:, 5, 0:1, :] for ref in (low, own, high)]
-    sources += [far_high[:, 0:1, :]]
+    near = pair_rows((before, here, after))
+    _, low, own, high, _ = near
+    sources = [rows(5, 0) for rows in near]
     s3, wx3, wy3, wz3 = unpack_bands3(sources)
     s3_ref[...], wx3_ref[...], wy3_ref[...], wz3_ref[...] = s3, wx3, wy3, wz3
     di3_ref[...] = relax_factor(s3, wx3, wy3, wz3, 2, 8)
@@ -375,13 +420,13 @@
     e22_ref[...] = e22
     s3, wx3, _, wz3 = coarsen(s2, wx2, wy2, wz2, 1, 4)
     inner = s3 + wx3 + x_high(wx3) + wz3 + turn(wz3, -8, 2)
-    send(msg_ref, pack_level3(r3) + pack_level3(inner))
+    send(msg_ref, pack_level3(r3) + pack_sums3(inner))
 
 
 def third_again_kernel(
     own, low, high, s2_ref, di2_ref, wx2_ref, wy2_ref, wz2_ref, r2_ref, e22_ref, msg_ref
 ):
-    r2 = unpack_level2(0, own, low, high)
+    r2 = unpack_level2(0, message_rows(own), message_rows(low), message_rows(high))
     r2_ref[...] = r2
     e22, r3 = descend_third(
         r2, s2_ref[...], wx2_ref[...], wy2_ref[...], wz2_ref[...], di2_ref[...]
@@ -422,11 +467,12 @@
     return octuple(jnp.stack(parts, axis=1).reshape((4 * v.shape[0], 24, NZ)))
 
 
-def line_sums(v):
+def line_sums(v, held):
     total = jnp.sum(v, axis=1, keepdims=True)
     lane = iota(total.shape, 2) % 8
-    parts = [jnp.where(lane // 2 == q, total, 0.0) for q in range(4)]
-    return octuple(jnp.stack(parts, axis=1).reshape((4 * v.shape[0], 1, NZ)))
+    parts = [jnp.where(lane * held // 8 == q, total, 0.0) for q in range(held)]
+    wide = jnp.stack(parts, axis=1).reshape((held * v.shape[0], 1, NZ))
+    return octuple(wide[: lax.axis_size("tile")])
 
 
 def solve_third(r3, line, s3, di3, wx3, wy3, wz3):
@@ -487,10 +533,10 @@
     *, groups, thirds, rows,
 ):
     r3 = strided(third_ref, 0, thirds, groups, rows)
-    below = line_sums(strided(third_ref, thirds, thirds, groups, rows))
+    below = line_sums(strided(third_ref, thirds, rows - thirds, groups, rows), 8)
     below_ref[...] = below
     corr3 = solve_third(
-        unpack_r3(r3), line_sums(r3) / below,
+        unpack_r3(r3), line_sums(r3, 4) / below,
         s3_ref[...], di3_ref[...], wx3_ref[...], wy3_ref[...], wz3_ref[...],
     )
     corr2 = climb_to_second(corr3, r2_ref, s2_ref, di2_ref, wx2_ref, wy2_ref, wz2_ref, e22_ref)
@@ -537,7 +583,7 @@
 ):
     r3 = strided(third_ref, 0, thirds, groups, rows)
     corr3 = solve_third(
-        unpack_r3(r3), line_sums(r3) / below_ref[...],
+        unpack_r3(r3), line_sums(r3, 4) / below_ref[...],
         s3_ref[...], di3_ref[...], wx3_ref[...], wy3_ref[...], wz3_ref[...],
     )
     corr2 = climb_to_second(corr3, r2_ref, s2_ref, di2_ref, wx2_ref, wy2_ref, wz2_ref, e22_ref)
@@ -576,15 +622,12 @@
     lax.fori_loop(0, BX // 2, remain, 0, unroll=True)
 
 
-def call(body, outs, operands, scratch=(), smem=()):
+def call(body, outs, operands, scratch=()):
     vmem = pl.BlockSpec(memory_space=pltpu.VMEM)
     return pl.pallas_call(
         body,
         out_shape=[jax.ShapeDtypeStruct(shape, F32) for shape in outs],
-        in_specs=[
-            pl.BlockSpec(memory_space=pltpu.SMEM) if i in smem else vmem
-            for i in range(len(operands))
-        ],
+        in_specs=[vmem] * len(operands),
         out_specs=[vmem] * len(outs),
         scratch_shapes=[pltpu.VMEM(shape, F32) for shape in scratch],
         compiler_params=pltpu.CompilerParams(vmem_limit_bytes=16 * 1024 * 1024),
@@ -612,36 +655,54 @@
     return lax.all_to_all(blocks, axis, 0, 0, tiled=True)
 
 
+def pairs_of_tiles(block):
+    tiles, groups = lax.axis_size("tile"), lax.axis_size("group")
+    members = [
+        [t * groups + 2 * pair + core for t in range(tiles) for core in range(2)]
+        for pair in range(groups // 2)
+    ]
+    given = lax.all_to_all(
+        block, ("tile", "group"), 0, 0, axis_index_groups=members, tiled=True
+    )
+    return given.reshape((tiles, 2) + block.shape[1:])
+
+
 def shards(pressure_head, old_head, soil_type, conduct_sat, alpha_param, shape_param, water_span):
     tiles, groups = lax.axis_size("tile"), lax.axis_size("group")
     thirds = tiles // 4
     top, one, two = (PX, WY, NZ), (L1X, WY, NZ), (2 * tiles, 16, NZ)
     three, line = (tiles, 24, NZ), (tiles, 1, NZ)
-    rows_once, rows_again = 2 * thirds, thirds
-
-    (fields,) = call(
+    rows_once, rows_again = thirds + -(-tiles // 8), thirds
+
+    fields = pl.pallas_call(
         soil_kernel,
-        [(4, BX, BY, NZ)],
-        [pressure_head, old_head, soil_type, conduct_sat, alpha_param, shape_param, water_span],
-        smem=(3, 4, 5, 6),
-    )
+        out_shape=jax.ShapeDtypeStruct((4, BX, BY, NZ), F32),
+        in_specs=[pl.BlockSpec(memory_space=pltpu.HBM)] * 7,
+        out_specs=pl.BlockSpec(memory_space=pltpu.VMEM),
+        scratch_shapes=[
+            pltpu.VMEM((BX, BY, NZ), F32),
+            pltpu.VMEM((BX, BY, NZ), F32),
+            pltpu.VMEM((BX, BY, NZ), jnp.int32),
+            *[pltpu.SMEM((SOILS,), F32) for _ in range(4)],
+            pltpu.SemaphoreType.DMA((7,)),
+        ],
+    )(pressure_head, old_head, soil_type, conduct_sat, alpha_param, shape_param, water_span)
     core, ylow, yhigh = surround(fields, 1)
     rhs, s0, di0, wx0, wy0, wz0, e2, r1, s1, di1, wx1, wy1, wz1, e21, msg = call(
         assemble_kernel,
-        [top] * 7 + [one] * 7 + [(tiles, 6, 2, NZ)],
+        [top] * 7 + [one] * 7 + [(2 * tiles, 6, 2, NZ)],
         [core, ylow, yhigh],
         [top] * 4,
     )
     bands0 = [s0, di0, wx0, wy0, wz0]
     bands1 = [s1, di1, wx1, wy1, wz1]
 
-    own = everyone(msg, "tile")
-    low, high = beside(own, own, "group")
-    far_low, far_high = beside(own[:, 5], own[:, 5], "group", 2)
+    here = pairs_of_tiles(msg)
+    before, after = beside(here, here, "group", 2)
     r2, s2, di2, wx2, wy2, wz2, e22, s3, di3, wx3, wy3, wz3, msg = call(
         third_kernel,
-        [two] * 7 + [three] * 5 + [(groups, thirds, 2, NZ)],
-        [far_low, low, own, high, far_high],
+        [two] * 7 + [three] * 5 + [(groups, rows_once, 1, NZ)],
+        [before, here, after],
     )
     bands3 = [s3, di3, wx3, wy3, wz3]
     bands2 = [s2, di2, wx2, wy2, wz2]

time: 181 us -> 171 us (0.945)
  starting transfers between devices: 51.1 us -> 43.1 us
  local copies, waits for them, and re-layouts: 5.24 us -> 0.1 us
  blocking collectives: 89 us -> 92 us
  waiting for transfers between devices: 15.4 us -> 17.8 us
  Pallas kernels: 18 us -> 15.8 us
    all_to_all x0 -> x1, blocking collectives: none -> 23.1 us  [pairs_of_tiles(): lax.all_to_all(block, ('tile', 'group'), 0, 0, axis_index_groups=members,...]
    all_to_all x4 -> x3, blocking collectives: 89 us -> 68.8 us  [everyone(): return lax.all_to_all(blocks, axis, 0, 0, tiled=True)]
    ppermute x7 -> x6, starting transfers between devices: 26.3 us -> 20.2 us  [beside(): from_low = lax.ppermute(to_high, axis, [(i, i + step) for i in range(ends)])]
    unnamed x17 -> x3, local copies, waits for them, and re-layouts: 5.15 us -> 0.02 us
    pallas_call x7 -> x6, Pallas kernels: 18 us -> 13.7 us  [call(): pl.pallas_call(body, out_shape=[jax.ShapeDtypeStruct(shape, F32) for shap...]
    ppermute x7 -> x6, waiting for transfers between devices: 5.86 us -> 8.11 us  [beside(): from_high = lax.ppermute(to_low, axis, [(i + step, i) for i in range(ends)])]
    pallas_call x0 -> x1, Pallas kernels: none -> 2.08 us  [shards(): pl.pallas_call(soil_kernel, out_shape=jax.ShapeDtypeStruct((4, BX, BY, NZ...]
    ppermute x7 -> x6, starting transfers between devices: 24.8 us -> 22.9 us  [beside(): from_high = lax.ppermute(to_low, axis, [(i + step, i) for i in range(ends)])]
  transfers between devices with their start and end apart: 14 -> 12, of which waited for: 8 -> 9; matrix products, arithmetic and copies ran while one was open for 0% -> 0% of each run, Pallas kernels for 0% -> 0%
where the time goes in v4:
time: 171 us
  blocking collectives  92 us (54%)
  starting transfers between devices  43.1 us (25%)
  waiting for transfers between devices  17.8 us (10%)
  Pallas kernels  15.8 us (9%)
    all_to_all x3, blocking collectives, everyone(): return lax.all_to_all(blocks, axis, 0, 0, tiled=True)  68.8 us
    all_to_all x1, blocking collectives, pairs_of_tiles(): lax.all_to_all(block, ('tile', 'group'), 0, 0, axis_index_groups=members,...  23.1 us
    ppermute x6, starting transfers between devices, beside(): from_high = lax.ppermute(to_low, axis, [(i + step, i) for i in range(ends)])  22.9 us
    ppermute x6, starting transfers between devices, beside(): from_low = lax.ppermute(to_high, axis, [(i, i + step) for i in range(ends)])  20.2 us
    pallas_call x6, Pallas kernels, call(): pl.pallas_call(body, out_shape=[jax.ShapeDtypeStruct(shape, F32) for shap...  13.7 us
    ppermute x6, waiting for transfers between devices, beside(): from_low = lax.ppermute(to_high, axis, [(i, i + step) for i in range(ends)])  9.71 us
    ppermute x6, waiting for transfers between devices, beside(): from_high = lax.ppermute(to_low, axis, [(i + step, i) for i in range(ends)])  8.11 us
  transfers between devices with their start and end apart: 12, of which 9 were waited for; matrix products, arithmetic and copies ran while one was open for 0% of the time, Pallas kernels for 0%

profile of v4, /device:TPU:1, one launch (start us, length us, event | category | flops | bytes accessed | tf_op | source)
XLA Modules:
  0.0 170.5 jit_solution(3347457957899723830)
XLA Ops:
  0.6 2.1 %shard_map.86 = f32[4,8,16,128]{3,2,1,0:T(8,128)} custom-call(f32[8,16,128]{2,1,0:T(8,128)} %head_in.1, f32[8,16,128]{2,1,0:T(8,128)} %old_in.1, s32[8,16,128]{2,1,0:T(8,128)} %soil_in.1, f32[12]{0:T(128)} %ks_in.1, f32[12]{0:T(128)} %alpha_in.1, f32[12]{0:T(128)} %shape_in.1, f32[12]{0:T(128)} %span_in.1), custom_call_target="tpu_custom_call" | custom-call | tf_op jit(solution)/shard_map/pallas_call | solution.py:677
  4.0 5.5 %collective-permute-start = (f32[4,8,16,128]{3,2,1,0:T(8,128)}, f32[4,8,16,128]{3,2,1,0:T(8,128)S(1)}, u32[]{:S(2)}, u32[]{:S(2)}) collective-permute-start(f32[4,8,16,128]{3,2,1,0:T(8,128)} %shard_map.86), channel_id=1, source_target_pairs={{0,64},{64,128},{128,192},{192,256},{256,320},{320,384},{384,448},... | collective-permute-start | bytes 786440 | tf_op jit(solution)/shard_map/ppermute | solution.py:639
  9.5 2.0 %collective-permute-done.1 = f32[4,8,16,128]{3,2,1,0:T(8,128)S(1)} collective-permute-done((f32[4,8,16,128]{3,2,1,0:T(8,128)}, f32[4,8,16,128]{3,2,1,0:T(8,128)S(1)}, u32[]{:S(2)}, u32[]{:S(2)}) %collective-permute-start.1) | collective-permute-done | bytes 262176 | tf_op jit(solution)/shard_map/ppermute | solution.py:640
  11.5 1.6 collective-permute-done
  14.2 12.1 %collective-permute-start.3 = (f32[4,24,8,128]{3,2,1,0:T(8,128)S(1)}, f32[4,24,8,128]{3,2,1,0:T(8,128)S(1)}, u32[]{:S(2)}, u32[]{:S(2)}) collective-permute-start(f32[4,24,8,128]{3,2,1,0:T(8,128)S(1)} %get-tuple-element.82), channel_id=1, source_target_pairs={{1,0},{2,1},{3,2},{4,3},{5,4},{6,5},{7,6},{8,7},{9,8},{10,9},{11,1... | collective-permute-start | bytes 1179656 | tf_op jit(solution)/shard_map/ppermute | solution.py:640
  26.3 1.9 %collective-permute-start.2 = (f32[4,24,8,128]{3,2,1,0:T(8,128)S(1)}, f32[4,24,8,128]{3,2,1,0:T(8,128)S(1)}, u32[]{:S(2)}, u32[]{:S(2)}) collective-permute-start(f32[4,24,8,128]{3,2,1,0:T(8,128)S(1)} %get-tuple-element.83), channel_id=1, source_target_pairs={{0,1},{1,2},{2,3},{3,4},{4,5},{5,6},{6,7},{7,8},{8,9},{9,10},{10,1... | collective-permute-start | bytes 1179656 | tf_op jit(solution)/shard_map/ppermute | solution.py:639
  28.2 4.7 %collective-permute-done.2.ylow = f32[4,24,8,128]{3,2,1,0:T(8,128)S(1)} collective-permute-done((f32[4,24,8,128]{3,2,1,0:T(8,128)S(1)}, f32[4,24,8,128]{3,2,1,0:T(8,128)S(1)}, u32[]{:S(2)}, u32[]{:S(2)}) %collective-permute-start.2) | collective-permute-done | bytes 393248 | tf_op jit(solution)/shard_map/ppermute | solution.py:639
  32.9 3.0 %shard_map.87 = (f32[26,32,128]{2,1,0:T(8,128)S(1)}, f32[26,32,128]{2,1,0:T(8,128)S(1)}, f32[26,32,128]{2,1,0:T(8,128)S(1)}, f32[26,32,128]{2,1,0:T(8,128)S(1)},...) custom-call(f32[4,24,16,128]{3,2,1,0:T(8,128)S(1)} %pad_maximum_fusi, ...), custom_call_target="tpu_custom_call" | custom-call | tf_op jit(solution)/shard_map/pallas_call | solution.py:627
  35.9 23.1 %all_to_all.20 = f32[24,6,2,128]{3,2,1,0:T(2,128)S(1)} all-to-all(f32[24,6,2,128]{3,2,1,0:T(2,128)S(1)} %get-tuple-element.42), channel_id=1, replica_groups={{0,1,64,65,128,129,192,193,256,257,320,321,384,385,448,449,512,513,576,..., dimensions={0} | all-to-all | bytes 294912 | tf_op jit(solution)/shard_map/all_to_all | solution.py:664
  60.3 5.0 %collective-permute-start.4 = (f32[12,2,6,2,128]{4,3,2,1,0:T(2,128)S(1)}, f32[12,2,6,2,128]{4,3,2,1,0:T(2,128)S(1)}, u32[]{:S(2)}, u32[]{:S(2)}) collective-permute-start(f32[12,2,6,2,128]{4,3,2,1,0:T(2,128)S(1)} %bitcast.5), channel_id=1, source_target_pairs={{0,2},{1,3},{2,4},{3,5},{4,6},{5,7},{6,8},{7,9},{8,10},{9,11},{10,... | collective-permute-start | bytes 442376 | tf_op jit(solution)/shard_map/ppermute | solution.py:639
  65.3 1.4 collective-permute-done.5.after
  67.6 3.5 %shard_map.88 = (f32[24,16,128]{2,1,0:T(8,128)S(1)}, f32[24,16,128]{2,1,0:T(8,128)S(1)}, f32[24,16,128]{2,1,0:T(8,128)S(1)}, f32[24,16,128]{2,1,0:T(8,128)S(1)},...) custom-call(f32[12,2,6,2,128]{4,3,2,1,0:T(2,128)S(1)} %collective-pe, ...), custom_call_target="tpu_custom_call" | custom-call | tf_op jit(solution)/shard_map/pallas_call | solution.py:627
  71.1 29.4 %all_to_all.21 = f32[64,5,1,128]{3,2,1,0:T(1,128)S(1)} all-to-all(f32[64,5,1,128]{3,2,1,0:T(1,128)S(1)} %get-tuple-element.43), channel_id=1, replica_groups=mesh['tile'=12,'group'=64] {'group'}, dimensions={0} | all-to-all | bytes 327680 | tf_op jit(solution)/shard_map/all_to_all | solution.py:655
  100.5 1.5 shard_map.89
  104.7 4.3 %collective-permute-done.7 = f32[8,16,128]{2,1,0:T(8,128)S(1)} collective-permute-done((f32[8,16,128]{2,1,0:T(8,128)S(1)}, f32[8,16,128]{2,1,0:T(8,128)S(1)}, u32[]{:S(2)}, u32[]{:S(2)}) %collective-permute-start.7) | collective-permute-done | bytes 65568 | tf_op jit(solution)/shard_map/ppermute | solution.py:640
  109.0 3.5 %collective-permute-start.9 = (f32[24,8,128]{2,1,0:T(8,128)S(1)}, f32[24,8,128]{2,1,0:T(8,128)S(1)}, u32[]{:S(2)}, u32[]{:S(2)}) collective-permute-start(f32[24,8,128]{2,1,0:T(8,128)S(1)} %get-tuple-element.84), channel_id=1, source_target_pairs={{1,0},{2,1},{3,2},{4,3},{5,4},{6,5},{7,6},{8,7},{9,8},{10,9},{11,1... | collective-permute-start | bytes 294920 | tf_op jit(solution)/shard_map/ppermute | solution.py:640
  112.5 2.1 %collective-permute-start.8 = (f32[24,8,128]{2,1,0:T(8,128)S(1)}, f32[24,8,128]{2,1,0:T(8,128)S(1)}, u32[]{:S(2)}, u32[]{:S(2)}) collective-permute-start(f32[24,8,128]{2,1,0:T(8,128)S(1)} %get-tuple-element.85), channel_id=1, source_target_pairs={{0,1},{1,2},{2,3},{3,4},{4,5},{5,6},{6,7},{7,8},{8,9},{9,10},{10,1... | collective-permute-start | bytes 294920 | tf_op jit(solution)/shard_map/ppermute | solution.py:639
  116.2 2.4 %shard_map.90 = (f32[26,32,128]{2,1,0:T(8,128)S(1)}, f32[26,32,128]{2,1,0:T(8,128)S(1)}, f32[26,32,128]{2,1,0:T(8,128)S(1)}, f32[12,32,128]{2,1,0:T(8,128)S(1)},...) custom-call(f32[24,16,128]{2,1,0:T(8,128)S(1)} %constant_dynamic-update-slice_fusion.core, ...), custom_call_target="tpu_custom_call" | custom-call | tf_op jit(solution)/shard_map/pallas_call | solution.py:627
  118.6 15.9 %all_to_all.22 = f32[12,5,2,128]{3,2,1,0:T(2,128)S(1)} all-to-all(f32[12,5,2,128]{3,2,1,0:T(2,128)S(1)} %get-tuple-element.71), channel_id=1, replica_groups=mesh['tile'=12,'group'=64] {'tile'}, dimensions={0} | all-to-all | bytes 122880 | tf_op jit(solution)/shard_map/all_to_all | solution.py:655
  134.5 3.5 %collective-permute-start.11 = (f32[13,5,2,128]{3,2,1,0:T(2,128)S(1)}, f32[13,5,2,128]{3,2,1,0:T(2,128)S(1)}, u32[]{:S(2)}, u32[]{:S(2)}) collective-permute-start(f32[13,5,2,128]{3,2,1,0:T(2,128)S(1)} %constant_dynamic-update-slice_fusion.3.own), channel_id=1, source_target_pairs={{1,0},{2,1},{3,2},{4,3},{5,4},{6,5},{7,6},{8,7},{9,8},{10,9},{11,1... | collective-permute-start | bytes 199688 | tf_op jit(solution)/shard_map/ppermute | solution.py:640
  138.0 4.4 %collective-permute-start.10 = (f32[13,5,2,128]{3,2,1,0:T(2,128)S(1)}, f32[13,5,2,128]{3,2,1,0:T(2,128)S(1)}, u32[]{:S(2)}, u32[]{:S(2)}) collective-permute-start(f32[13,5,2,128]{3,2,1,0:T(2,128)S(1)} %constant_dynamic-update-slice_fusion.3.own), channel_id=1, source_target_pairs={{0,1},{1,2},{2,3},{3,4},{4,5},{5,6},{6,7},{7,8},{8,9},{9,10},{10,1... | collective-permute-start | bytes 199688 | tf_op jit(solution)/shard_map/ppermute | solution.py:639
  142.4 1.3 collective-permute-done.10.low
  144.5 23.5 %all_to_all.23 = f32[64,3,1,128]{3,2,1,0:T(1,128)S(1)} all-to-all(f32[64,3,1,128]{3,2,1,0:T(1,128)S(1)} %get-tuple-element.73), channel_id=1, replica_groups=mesh['tile'=12,'group'=64] {'group'}, dimensions={0} | all-to-all | bytes 196608 | tf_op jit(solution)/shard_map/all_to_all | solution.py:655
  168.0 2.5 %shard_map.92 = (f32[8,16,128]{2,1,0:T(8,128)}, f32[8,16,128]{2,1,0:T(8,128)}) custom-call(f32[192,128]{1,0:T(8,128)S(1)} %bitcast.7, f32[12,1,128]{2,1,0:T(1,128)S(1)} %get-tuple-element.74.below_ref, f32[12,24,128]{2,1,0:T(8,128)S(1)} %get-tuple-element.44.s3_ref, f32[12,24,128]{2,1,0:T(8,128)S(1)} %get-tuple-element.45.di3_ref, ...), custom_call_target="tpu_custom_call" | custom-call | tf_op jit(solution)/shard_map/pallas_call | solution.py:627
  (19 shorter events, 9.6 us)
Async XLA Ops:
  2.7 8.8 %collective-permute-start.1 = (f32[4,8,16,128]{3,2,1,0:T(8,128)}, f32[4,8,16,128]{3,2,1,0:T(8,128)S(1)}, u32[]{:S(2)}, u32[]{:S(2)}) collective-permute-start(f32[4,8,16,128]{3,2,1,0:T(8,128)} %shard_map.86), channel_id=1, source_target_pairs={{64,0},{128,64},{192,128},{256,192},{320,256},{384,320},{448,384},... | collective-permute-start | bytes 786440 | tf_op jit(solution)/shard_map/ppermute | solution.py:640
  4.0 9.1 %collective-permute-start = (f32[4,8,16,128]{3,2,1,0:T(8,128)}, f32[4,8,16,128]{3,2,1,0:T(8,128)S(1)}, u32[]{:S(2)}, u32[]{:S(2)}) collective-permute-start(f32[4,8,16,128]{3,2,1,0:T(8,128)} %shard_map.86), channel_id=1, source_target_pairs={{0,64},{64,128},{128,192},{192,256},{256,320},{320,384},{384,448},... | collective-permute-start | bytes 786440 | tf_op jit(solution)/shard_map/ppermute | solution.py:639
  14.2 14.0 %collective-permute-start.3 = (f32[4,24,8,128]{3,2,1,0:T(8,128)S(1)}, f32[4,24,8,128]{3,2,1,0:T(8,128)S(1)}, u32[]{:S(2)}, u32[]{:S(2)}) collective-permute-start(f32[4,24,8,128]{3,2,1,0:T(8,128)S(1)} %get-tuple-element.82), channel_id=1, source_target_pairs={{1,0},{2,1},{3,2},{4,3},{5,4},{6,5},{7,6},{8,7},{9,8},{10,9},{11,1... | collective-permute-start | bytes 1179656 | tf_op jit(solution)/shard_map/ppermute | solution.py:640
  26.3 6.6 %collective-permute-start.2 = (f32[4,24,8,128]{3,2,1,0:T(8,128)S(1)}, f32[4,24,8,128]{3,2,1,0:T(8,128)S(1)}, u32[]{:S(2)}, u32[]{:S(2)}) collective-permute-start(f32[4,24,8,128]{3,2,1,0:T(8,128)S(1)} %get-tuple-element.83), channel_id=1, source_target_pairs={{0,1},{1,2},{2,3},{3,4},{4,5},{5,6},{6,7},{7,8},{8,9},{9,10},{10,1... | collective-permute-start | bytes 1179656 | tf_op jit(solution)/shard_map/ppermute | solution.py:639
  59.0 7.8 %collective-permute-start.5 = (f32[12,2,6,2,128]{4,3,2,1,0:T(2,128)S(1)}, f32[12,2,6,2,128]{4,3,2,1,0:T(2,128)S(1)}, u32[]{:S(2)}, u32[]{:S(2)}) collective-permute-start(f32[12,2,6,2,128]{4,3,2,1,0:T(2,128)S(1)} %bitcast.4), channel_id=1, source_target_pairs={{2,0},{3,1},{4,2},{5,3},{6,4},{7,5},{8,6},{9,7},{10,8},{11,9},{12,... | collective-permute-start | bytes 442376 | tf_op jit(solution)/shard_map/ppermute | solution.py:640
  60.3 7.3 %collective-permute-start.4 = (f32[12,2,6,2,128]{4,3,2,1,0:T(2,128)S(1)}, f32[12,2,6,2,128]{4,3,2,1,0:T(2,128)S(1)}, u32[]{:S(2)}, u32[]{:S(2)}) collective-permute-start(f32[12,2,6,2,128]{4,3,2,1,0:T(2,128)S(1)} %bitcast.5), channel_id=1, source_target_pairs={{0,2},{1,3},{2,4},{3,5},{4,6},{5,7},{6,8},{7,9},{8,10},{9,11},{10,... | collective-permute-start | bytes 442376 | tf_op jit(solution)/shard_map/ppermute | solution.py:639
  102.0 2.6 %collective-permute-start.6 = (f32[8,16,128]{2,1,0:T(8,128)S(1)}, f32[8,16,128]{2,1,0:T(8,128)S(1)}, u32[]{:S(2)}, u32[]{:S(2)}) collective-permute-start(f32[8,16,128]{2,1,0:T(8,128)S(1)} %get-tuple-element.64), channel_id=1, source_target_pairs={{0,64},{64,128},{128,192},{192,256},{256,320},{320,384},{384,448},... | collective-permute-start | bytes 196616 | tf_op jit(solution)/shard_map/ppermute | solution.py:639
  103.3 5.6 %collective-permute-start.7 = (f32[8,16,128]{2,1,0:T(8,128)S(1)}, f32[8,16,128]{2,1,0:T(8,128)S(1)}, u32[]{:S(2)}, u32[]{:S(2)}) collective-permute-start(f32[8,16,128]{2,1,0:T(8,128)S(1)} %get-tuple-element.64), channel_id=1, source_target_pairs={{64,0},{128,64},{192,128},{256,192},{320,256},{384,320},{448,384},... | collective-permute-start | bytes 196616 | tf_op jit(solution)/shard_map/ppermute | solution.py:640
  109.0 5.9 %collective-permute-start.9 = (f32[24,8,128]{2,1,0:T(8,128)S(1)}, f32[24,8,128]{2,1,0:T(8,128)S(1)}, u32[]{:S(2)}, u32[]{:S(2)}) collective-permute-start(f32[24,8,128]{2,1,0:T(8,128)S(1)} %get-tuple-element.84), channel_id=1, source_target_pairs={{1,0},{2,1},{3,2},{4,3},{5,4},{6,5},{7,6},{8,7},{9,8},{10,9},{11,1... | collective-permute-start | bytes 294920 | tf_op jit(solution)/shard_map/ppermute | solution.py:640
  112.5 3.7 %collective-permute-start.8 = (f32[24,8,128]{2,1,0:T(8,128)S(1)}, f32[24,8,128]{2,1,0:T(8,128)S(1)}, u32[]{:S(2)}, u32[]{:S(2)}) collective-permute-start(f32[24,8,128]{2,1,0:T(8,128)S(1)} %get-tuple-element.85), channel_id=1, source_target_pairs={{0,1},{1,2},{2,3},{3,4},{4,5},{5,6},{6,7},{7,8},{8,9},{9,10},{10,1... | collective-permute-start | bytes 294920 | tf_op jit(solution)/shard_map/ppermute | solution.py:639
  134.5 7.9 %collective-permute-start.11 = (f32[13,5,2,128]{3,2,1,0:T(2,128)S(1)}, f32[13,5,2,128]{3,2,1,0:T(2,128)S(1)}, u32[]{:S(2)}, u32[]{:S(2)}) collective-permute-start(f32[13,5,2,128]{3,2,1,0:T(2,128)S(1)} %constant_dynamic-update-slice_fusion.3.own), channel_id=1, source_target_pairs={{1,0},{2,1},{3,2},{4,3},{5,4},{6,5},{7,6},{8,7},{9,8},{10,9},{11,1... | collective-permute-start | bytes 199688 | tf_op jit(solution)/shard_map/ppermute | solution.py:640
  138.0 5.7 %collective-permute-start.10 = (f32[13,5,2,128]{3,2,1,0:T(2,128)S(1)}, f32[13,5,2,128]{3,2,1,0:T(2,128)S(1)}, u32[]{:S(2)}, u32[]{:S(2)}) collective-permute-start(f32[13,5,2,128]{3,2,1,0:T(2,128)S(1)} %constant_dynamic-update-slice_fusion.3.own), channel_id=1, source_target_pairs={{0,1},{1,2},{2,3},{3,4},{4,5},{5,6},{6,7},{7,8},{8,9},{9,10},{10,1... | collective-permute-start | bytes 199688 | tf_op jit(solution)/shard_map/ppermute | solution.py:639

commit v5 on v4

--- a/solution.py
+++ b/solution.py
@@ -1,4 +1,5 @@
 import functools
+import math
 
 import jax
 import jax.numpy as jnp
@@ -223,14 +224,16 @@
     lax.fori_loop(0, BX, cells, 0, unroll=2)
 
 
-def fill_window(ref, core, ylow, yhigh):
+def fill_window(ref, xlow, own, xhigh, ylow, yhigh):
+    ref[1 : 1 + BX, 8:24, :] = xlow
+    ref[1 + BX : 1 + 2 * BX, 8:24, :] = own
+    ref[1 + 2 * BX : 1 + 3 * BX, 8:24, :] = xhigh
     ref[1 : PX - 1, 0:8, :] = ylow
-    ref[1 : PX - 1, 8:24, :] = core
     ref[1 : PX - 1, 24:32, :] = yhigh
 
 
 def assemble_kernel(
-    core, ylow, yhigh,
+    xlow, own, xhigh, ylow, yhigh,
     r_ref, s_ref, di_ref, wx_ref, wy_ref, wz_ref, e2_ref,
     r1_ref, s1_ref, di1_ref, wx1_ref, wy1_ref, wz1_ref, e21_ref, msg_ref,
     h_ref, k_ref, m_ref, e1_ref,
@@ -238,7 +241,7 @@
     for ref in (h_ref, k_ref, s_ref, wx_ref, wy_ref, wz_ref, di_ref, r_ref, e1_ref, e2_ref):
         blank_ends(ref)
     for f, ref in enumerate((h_ref, k_ref, s_ref, m_ref)):
-        fill_window(ref, core[f], ylow[f], yhigh[f])
+        fill_window(ref, xlow[f], own[f], xhigh[f], ylow[f], yhigh[f])
 
     def harmonic(a, b):
         total = a + b
@@ -299,13 +302,13 @@
 
 
 def again_kernel(
-    core, ylow, yhigh, rhs_ref, s_ref, di_ref, wx_ref, wy_ref, wz_ref,
+    xlow, own, xhigh, ylow, yhigh, rhs_ref, s_ref, di_ref, wx_ref, wy_ref, wz_ref,
     s1_ref, di1_ref, wx1_ref, wy1_ref, wz1_ref,
     u_ref, r_ref, e2_ref, r1_ref, e21_ref, msg_ref, edge_ref, pre_ref, e1_ref,
 ):
     for ref in (pre_ref, u_ref, r_ref, e1_ref, e2_ref):
         blank_ends(ref)
-    fill_window(pre_ref, core[...], ylow[...], yhigh[...])
+    fill_window(pre_ref, xlow[...], own[...], xhigh[...], ylow[...], yhigh[...])
 
     def post(i, carry):
         at = 1 + 2 * i
@@ -341,18 +344,22 @@
     return lambda field, half: ref[0:tiles, field, half : half + 1, :]
 
 
-def pair_rows(refs):
+def pair_rows(here, before, after):
     even = lax.axis_index("group") % 2 == 0
-
-    def pick(ref, core):
-        return lambda field, half: ref[:, core, field, half : half + 1, :]
-
-    six = [pick(ref, core) for ref in refs for core in range(2)]
 
     def choose(first, second):
         return lambda field, half: jnp.where(even, first(field, half), second(field, half))
 
-    return [choose(six[i], six[i + 1]) for i in range(5)]
+    one, two = message_rows(here.at[:, 0]), message_rows(here.at[:, 1])
+    return choose(message_rows(before), one), choose(one, two), choose(two, message_rows(after))
+
+
+def band_rows3(here, before, after):
+    even = lax.axis_index("group") % 2 == 0
+    six = [ref[:, 5, half : half + 1, :] for ref in (before,) for half in range(2)]
+    six += [here[:, core, 5, 0:1, :] for core in range(2)]
+    six += [after[:, 5, half : half + 1, :] for half in range(2)]
+    return [jnp.where(even, six[i], six[i + 1]) for i in range(5)]
 
 
 def unpack_level2(field, own, low, high):
@@ -401,17 +408,25 @@
     return second, restrict(r2 - operate(second, s2, wx2, wy2, wz2, 1, 4), 1, 4)
 
 
+def sides_kernel(here, low_ref, high_ref):
+    low_ref[:, 0:5], high_ref[:, 0:5] = here[:, 0, 0:5], here[:, 1, 0:5]
+    for core in range(2):
+        rows = here[:, core, 5, 0:1, :]
+        low_ref[:, 5, core : core + 1, :] = rows
+        high_ref[:, 5, core : core + 1, :] = rows
+
+
+def bands3_kernel(before, here, after, s3_ref, di3_ref, wx3_ref, wy3_ref, wz3_ref):
+    s3, wx3, wy3, wz3 = unpack_bands3(band_rows3(here, before, after))
+    s3_ref[...], wx3_ref[...], wy3_ref[...], wz3_ref[...] = s3, wx3, wy3, wz3
+    di3_ref[...] = relax_factor(s3, wx3, wy3, wz3, 2, 8)
+
+
 def third_kernel(
     before, here, after,
-    r2_ref, s2_ref, di2_ref, wx2_ref, wy2_ref, wz2_ref, e22_ref,
-    s3_ref, di3_ref, wx3_ref, wy3_ref, wz3_ref, msg_ref,
+    r2_ref, s2_ref, di2_ref, wx2_ref, wy2_ref, wz2_ref, e22_ref, msg_ref,
 ):
-    near = pair_rows((before, here, after))
-    _, low, own, high, _ = near
-    sources = [rows(5, 0) for rows in near]
-    s3, wx3, wy3, wz3 = unpack_bands3(sources)
-    s3_ref[...], wx3_ref[...], wy3_ref[...], wz3_ref[...] = s3, wx3, wy3, wz3
-    di3_ref[...] = relax_factor(s3, wx3, wy3, wz3, 2, 8)
+    low, own, high = pair_rows(here, before, after)
     r2, s2, wx2, wy2, wz2 = (unpack_level2(f, own, low, high) for f in range(5))
     di2 = relax_factor(s2, wx2, wy2, wz2, 1, 4)
     r2_ref[...], s2_ref[...], di2_ref[...] = r2, s2, di2
@@ -623,6 +638,7 @@
 
 
 def call(body, outs, operands, scratch=()):
+    cells = sum(math.prod(shape) for shape in outs)
     vmem = pl.BlockSpec(memory_space=pltpu.VMEM)
     return pl.pallas_call(
         body,
@@ -631,6 +647,9 @@
         out_specs=[vmem] * len(outs),
         scratch_shapes=[pltpu.VMEM(shape, F32) for shape in scratch],
         compiler_params=pltpu.CompilerParams(vmem_limit_bytes=16 * 1024 * 1024),
+        cost_estimate=pl.CostEstimate(
+            flops=20 * cells, bytes_accessed=8 * cells, transcendentals=0
+        ),
     )(*operands)
 
 
@@ -643,12 +662,14 @@
 
 def surround(cells, dim):
     low, high = beside(cells, cells, "tile")
-    core = jnp.concatenate([low, cells, high], axis=dim)
     ydim = dim + 1
-    first = lax.slice_in_dim(core, 0, 8, axis=ydim)
-    last = lax.slice_in_dim(core, BY - 8, BY, axis=ydim)
-    ylow, yhigh = beside(first, last, "group")
-    return core, ylow, yhigh
+
+    def part(first):
+        pieces = [lax.slice_in_dim(v, first, first + 8, axis=ydim) for v in (low, cells, high)]
+        return jnp.concatenate(pieces, axis=dim)
+
+    ylow, yhigh = beside(part(0), part(BY - 8), "group")
+    return low, cells, high, ylow, yhigh
 
 
 def everyone(blocks, axis):
@@ -687,24 +708,25 @@
             pltpu.SemaphoreType.DMA((7,)),
         ],
     )(pressure_head, old_head, soil_type, conduct_sat, alpha_param, shape_param, water_span)
-    core, ylow, yhigh = surround(fields, 1)
+    around = surround(fields, 1)
     rhs, s0, di0, wx0, wy0, wz0, e2, r1, s1, di1, wx1, wy1, wz1, e21, msg = call(
         assemble_kernel,
         [top] * 7 + [one] * 7 + [(2 * tiles, 6, 2, NZ)],
-        [core, ylow, yhigh],
+        list(around),
         [top] * 4,
     )
     bands0 = [s0, di0, wx0, wy0, wz0]
     bands1 = [s1, di1, wx1, wy1, wz1]
 
     here = pairs_of_tiles(msg)
-    before, after = beside(here, here, "group", 2)
-    r2, s2, di2, wx2, wy2, wz2, e22, s3, di3, wx3, wy3, wz3, msg = call(
+    to_low, to_high = call(sides_kernel, [(tiles, 6, 2, NZ)] * 2, [here])
+    before, after = beside(to_low, to_high, "group", 2)
+    r2, s2, di2, wx2, wy2, wz2, e22, msg = call(
         third_kernel,
-        [two] * 7 + [three] * 5 + [(groups, rows_once, 1, NZ)],
+        [two] * 7 + [(groups, rows_once, 1, NZ)],
         [before, here, after],
     )
-    bands3 = [s3, di3, wx3, wy3, wz3]
+    bands3 = call(bands3_kernel, [three] * 5, [before, here, after])
     bands2 = [s2, di2, wx2, wy2, wz2]
     third = everyone(msg, "group").reshape(groups * rows_once, NZ)
     pre, below = call(
@@ -713,11 +735,11 @@
         [third, *bands3, r2, *bands2, e22, r1, *bands1, e21, e2],
     )
 
-    core, ylow, yhigh = surround(pre, 0)
+    around = surround(pre, 0)
     u, rem, e2, r1, e21, msg, edge = call(
         again_kernel,
         [top] * 3 + [one] * 2 + [(tiles, 5, 2, NZ), (1, 5, 2, NZ)],
-        [core, ylow, yhigh, rhs, *bands0, *bands1],
+        [*around, rhs, *bands0, *bands1],
         [top] * 2,
     )
     own = jnp.concatenate([everyone(msg, "tile"), edge], axis=0)

time: 171 us -> 187 us (1.094)
  blocking collectives: 92 us -> 70 us
  local copies, waits for them, and re-layouts: 0.1 us -> 21 us
  starting transfers between devices: 43.1 us -> 58.2 us
  waiting for transfers between devices: 17.8 us -> 20.2 us
    all_to_all x3 -> x2, blocking collectives: 68.8 us -> 41 us  [everyone(): return lax.all_to_all(blocks, axis, 0, 0, tiled=True)]
    unnamed x3 -> x75, local copies, waits for them, and re-layouts: 0.02 us -> 20 us
    all_to_all x0 -> x1, starting transfers between devices: none -> 16.4 us  [everyone(): return lax.all_to_all(blocks, axis, 0, 0, tiled=True)]
    ppermute x6, starting transfers between devices: 22.9 us -> 15.2 us  [beside(): from_high = lax.ppermute(to_low, axis, [(i + step, i) for i in range(ends)])]
    ppermute x6, starting transfers between devices: 20.2 us -> 26.7 us  [beside(): from_low = lax.ppermute(to_high, axis, [(i, i + step) for i in range(ends)])]
    all_to_all x1, blocking collectives: 23.1 us -> 29 us  [pairs_of_tiles(): lax.all_to_all(block, ('tile', 'group'), 0, 0, axis_index_groups=members,...]
    ppermute x6, waiting for transfers between devices: 9.71 us -> 4.24 us  [beside(): from_low = lax.ppermute(to_high, axis, [(i, i + step) for i in range(ends)])]
    all_to_all x0 -> x1, waiting for transfers between devices: none -> 5.3 us  [everyone(): return lax.all_to_all(blocks, axis, 0, 0, tiled=True)]
  transfers between devices with their start and end apart: 12 -> 13, of which waited for: 9 -> 9; matrix products, arithmetic and copies ran while one was open for 0% -> 1% of each run, Pallas kernels for 0% -> 1%
where the time goes in v5:
time: 187 us; the launch traced here: 186 us
  blocking collectives  70 us (37%)
  starting transfers between devices  58.2 us (31%)
  local copies, waits for them, and re-layouts  21 us (11%)
  waiting for transfers between devices  20.2 us (11%)
  Pallas kernels  15.8 us (8%)
    all_to_all x2, blocking collectives, everyone(): return lax.all_to_all(blocks, axis, 0, 0, tiled=True)  41 us
    all_to_all x1, blocking collectives, pairs_of_tiles(): lax.all_to_all(block, ('tile', 'group'), 0, 0, axis_index_groups=members,...  29 us
    ppermute x6, starting transfers between devices, beside(): from_low = lax.ppermute(to_high, axis, [(i, i + step) for i in range(ends)])  26.7 us
    unnamed x75, local copies, waits for them, and re-layouts  20 us
    all_to_all x1, starting transfers between devices, everyone(): return lax.all_to_all(blocks, axis, 0, 0, tiled=True)  16.4 us
    ppermute x6, starting transfers between devices, beside(): from_high = lax.ppermute(to_low, axis, [(i + step, i) for i in range(ends)])  15.2 us
    pallas_call x8, Pallas kernels, call(): pl.pallas_call(body, out_shape=[jax.ShapeDtypeStruct(shape, F32) for shap...  13.7 us
    ppermute x6, waiting for transfers between devices, beside(): from_high = lax.ppermute(to_low, axis, [(i + step, i) for i in range(ends)])  10.6 us
  transfers between devices with their start and end apart: 13, of which 9 were waited for; matrix products, arithmetic and copies ran while one was open for 1% of the time, Pallas kernels for 1%

profile of v5, /device:TPU:1, one launch (start us, length us, event | category | flops | bytes accessed | tf_op | source)
XLA Modules:
  0.0 186.3 jit_solution(1761530140013332498)
XLA Ops:
  0.6 2.1 %shard_map.86.own = f32[4,8,16,128]{3,2,1,0:T(8,128)} custom-call(f32[8,16,128]{2,1,0:T(8,128)} %head_in.1, f32[8,16,128]{2,1,0:T(8,128)} %old_in.1, s32[8,16,128]{2,1,0:T(8,128)} %soil_in.1, f32[12]{0:T(128)} %ks_in.1, f32[12]{0:T(128)} %alpha_in.1, f32[12]{0:T(128)} %shape_in.1, f32[12]{0:T(128)} %span_in.1), custom_call_target="tpu_custom_call" | custom-call | tf_op jit(solution)/shard_map/pallas_call | solution.py:698
  4.0 5.5 %collective-permute-start = (f32[4,8,16,128]{3,2,1,0:T(8,128)}, f32[4,8,16,128]{3,2,1,0:T(8,128)S(1)}, u32[]{:S(2)}, u32[]{:S(2)}) collective-permute-start(f32[4,8,16,128]{3,2,1,0:T(8,128)} %shard_map.86.own), channel_id=1, source_target_pairs={{0,64},{64,128},{128,192},{192,256},{256,320},{320,384},{384,448},... | collective-permute-start | bytes 786440 | tf_op jit(solution)/shard_map/ppermute | solution.py:658
  11.6 1.6 collective-permute-done.xlow
  13.2 6.2 %collective-permute-start.2 = (f32[4,24,8,128]{3,2,1,0:T(8,128)S(1)}, f32[4,24,8,128]{3,2,1,0:T(8,128)S(1)}, u32[]{:S(2)}, u32[]{:S(2)}) collective-permute-start(f32[4,24,8,128]{3,2,1,0:T(8,128)S(1)} %pad_maximum_fusion), channel_id=1, source_target_pairs={{0,1},{1,2},{2,3},{3,4},{4,5},{5,6},{6,7},{7,8},{8,9},{9,10},{10,1... | collective-permute-start | bytes 1179656 | tf_op jit(solution)/shard_map/ppermute | solution.py:658
  19.4 7.3 %collective-permute-start.3 = (f32[4,24,8,128]{3,2,1,0:T(8,128)S(1)}, f32[4,24,8,128]{3,2,1,0:T(8,128)S(1)}, u32[]{:S(2)}, u32[]{:S(2)}) collective-permute-start(f32[4,24,8,128]{3,2,1,0:T(8,128)S(1)} %pad_maximum_fusion.1), channel_id=1, source_target_pairs={{1,0},{2,1},{3,2},{4,3},{5,4},{6,5},{7,6},{8,7},{9,8},{10,9},{11,1... | collective-permute-start | bytes 1179656 | tf_op jit(solution)/shard_map/ppermute | solution.py:659
  26.8 1.9 %collective-permute-done.3.yhigh = f32[4,24,8,128]{3,2,1,0:T(8,128)S(1)} collective-permute-done((f32[4,24,8,128]{3,2,1,0:T(8,128)S(1)}, f32[4,24,8,128]{3,2,1,0:T(8,128)S(1)}, u32[]{:S(2)}, u32[]{:S(2)}) %collective-permute-start.3) | collective-permute-done | bytes 393248 | tf_op jit(solution)/shard_map/ppermute | solution.py:659
  28.7 2.9 %shard_map.87 = (f32[26,32,128]{2,1,0:T(8,128)S(1)}, f32[26,32,128]{2,1,0:T(8,128)S(1)}, f32[26,32,128]{2,1,0:T(8,128)S(1)}, f32[26,32,128]{2,1,0:T(8,128)S(1)},...) custom-call(f32[4,8,16,128]{3,2,1,0:T(8,128)S(1)} %collective-permut, ...), custom_call_target="tpu_custom_call" | custom-call | flops 22528000 | bytes 9011200 | tf_op jit(solution)/shard_map/pallas_call | solution.py:643
  35.3 29.0 %all_to_all.20 = f32[24,6,2,128]{3,2,1,0:T(2,128)S(1)} all-to-all(f32[24,6,2,128]{3,2,1,0:T(2,128)S(1)} %get-tuple-element.44), channel_id=1, replica_groups={{0,1,64,65,128,129,192,193,256,257,320,321,384,385,448,449,512,513,576,..., dimensions={0} | all-to-all | bytes 294912 | tf_op jit(solution)/shard_map/all_to_all | solution.py:685
  64.3 3.1 %collective-permute-start.4 = (f32[12,6,2,128]{3,2,1,0:T(2,128)S(1)}, f32[12,6,2,128]{3,2,1,0:T(2,128)S(1)}, u32[]{:S(2)}, u32[]{:S(2)}) collective-permute-start(f32[12,6,2,128]{3,2,1,0:T(2,128)S(1)} %get-tuple-element.45), channel_id=1, source_target_pairs={{0,2},{1,3},{2,4},{3,5},{4,6},{5,7},{6,8},{7,9},{8,10},{9,11},{10,... | collective-permute-start | bytes 221192 | tf_op jit(solution)/shard_map/ppermute | solution.py:658
  68.8 3.7 %collective-permute-done.5.after = f32[12,6,2,128]{3,2,1,0:T(2,128)S(1)} collective-permute-done((f32[12,6,2,128]{3,2,1,0:T(2,128)S(1)}, f32[12,6,2,128]{3,2,1,0:T(2,128)S(1)}, u32[]{:S(2)}, u32[]{:S(2)}) %collective-permute-start.5) | collective-permute-done | bytes 73760 | tf_op jit(solution)/shard_map/ppermute | solution.py:659
  72.5 2.2 %shard_map.89 = (f32[24,16,128]{2,1,0:T(8,128)S(1)}, f32[24,16,128]{2,1,0:T(8,128)S(1)}, f32[24,16,128]{2,1,0:T(8,128)S(1)}, f32[24,16,128]{2,1,0:T(8,128)S(1)},...) custom-call(f32[12,6,2,128]{3,2,1,0:T(2,128)S(1)} %collective-permut, ...), custom_call_target="tpu_custom_call" | custom-call | flops 7700480 | bytes 3080192 | tf_op jit(solution)/shard_map/pallas_call | solution.py:643
  76.8 16.4 %all-to-all-start.1 = ((f32[64,5,1,128]{3,2,1,0:T(1,128)}), f32[64,5,1,128]{3,2,1,0:T(1,128)S(1)}, u32[]{:S(2)}, u32[]{:S(2)}) async-start(f32[64,5,1,128]{3,2,1,0:T(1,128)} %copy-done.36), calls=%async_computation.1 | async-start | bytes 327680 | tf_op jit(solution)/shard_map/all_to_all | solution.py:676
  99.6 5.3 %all-to-all-done.1 = f32[64,5,1,128]{3,2,1,0:T(1,128)S(1)} async-done(((f32[64,5,1,128]{3,2,1,0:T(1,128)}), f32[64,5,1,128]{3,2,1,0:T(1,128)S(1)}, u32[]{:S(2)}, u32[]{:S(2)}) %all-to-all-start.1) | async-done | bytes 163872 | tf_op jit(solution)/shard_map/all_to_all | solution.py:676
  114.1 1.5 shard_map.91
  117.1 4.0 %collective-permute-start.6 = (f32[8,16,128]{2,1,0:T(8,128)S(1)}, f32[8,16,128]{2,1,0:T(8,128)S(1)}, u32[]{:S(2)}, u32[]{:S(2)}) collective-permute-start(f32[8,16,128]{2,1,0:T(8,128)S(1)} %get-tuple-element.68.own), channel_id=1, source_target_pairs={{0,64},{64,128},{128,192},{192,256},{256,320},{320,384},{384,448},... | collective-permute-start | bytes 196616 | tf_op jit(solution)/shard_map/ppermute | solution.py:658
  122.4 3.4 %collective-permute-start.8 = (f32[24,8,128]{2,1,0:T(8,128)S(1)}, f32[24,8,128]{2,1,0:T(8,128)S(1)}, u32[]{:S(2)}, u32[]{:S(2)}) collective-permute-start(f32[24,8,128]{2,1,0:T(8,128)S(1)} %pad_maximum_fusion.2), channel_id=1, source_target_pairs={{0,1},{1,2},{2,3},{3,4},{4,5},{5,6},{6,7},{7,8},{8,9},{9,10},{10,1... | collective-permute-start | bytes 294920 | tf_op jit(solution)/shard_map/ppermute | solution.py:658
  125.8 1.9 %collective-permute-start.9 = (f32[24,8,128]{2,1,0:T(8,128)S(1)}, f32[24,8,128]{2,1,0:T(8,128)S(1)}, u32[]{:S(2)}, u32[]{:S(2)}) collective-permute-start(f32[24,8,128]{2,1,0:T(8,128)S(1)} %pad_maximum_fusion.3), channel_id=1, source_target_pairs={{1,0},{2,1},{3,2},{4,3},{5,4},{6,5},{7,6},{8,7},{9,8},{10,9},{11,1... | collective-permute-start | bytes 294920 | tf_op jit(solution)/shard_map/ppermute | solution.py:659
  127.8 4.0 %collective-permute-done.9.yhigh = f32[24,8,128]{2,1,0:T(8,128)S(1)} collective-permute-done((f32[24,8,128]{2,1,0:T(8,128)S(1)}, f32[24,8,128]{2,1,0:T(8,128)S(1)}, u32[]{:S(2)}, u32[]{:S(2)}) %collective-permute-start.9) | collective-permute-done | bytes 98336 | tf_op jit(solution)/shard_map/ppermute | solution.py:659
  131.8 2.3 %shard_map.92 = (f32[26,32,128]{2,1,0:T(8,128)S(1)}, f32[26,32,128]{2,1,0:T(8,128)S(1)}, f32[26,32,128]{2,1,0:T(8,128)S(1)}, f32[12,32,128]{2,1,0:T(8,128)S(1)},...) custom-call(f32[8,16,128]{2,1,0:T(8,128)S(1)} %collective-permute-done.6.xlow, ...), custom_call_target="tpu_custom_call" | custom-call | flops 8688640 | bytes 3475456 | tf_op jit(solution)/shard_map/pallas_call | solution.py:643
  134.1 15.8 %all_to_all.21 = f32[12,5,2,128]{3,2,1,0:T(2,128)S(1)} all-to-all(f32[12,5,2,128]{3,2,1,0:T(2,128)S(1)} %get-tuple-element.75), channel_id=1, replica_groups=mesh['tile'=12,'group'=64] {'tile'}, dimensions={0} | all-to-all | bytes 122880 | tf_op jit(solution)/shard_map/all_to_all | solution.py:676
  149.9 1.9 %collective-permute-start.11 = (f32[13,5,2,128]{3,2,1,0:T(2,128)S(1)}, f32[13,5,2,128]{3,2,1,0:T(2,128)S(1)}, u32[]{:S(2)}, u32[]{:S(2)}) collective-permute-start(f32[13,5,2,128]{3,2,1,0:T(2,128)S(1)} %constant_dynamic-update-slice_fusion.own), channel_id=1, source_target_pairs={{1,0},{2,1},{3,2},{4,3},{5,4},{6,5},{7,6},{8,7},{9,8},{10,9},{11,1... | collective-permute-start | bytes 199688 | tf_op jit(solution)/shard_map/ppermute | solution.py:659
  151.8 4.5 %collective-permute-start.10 = (f32[13,5,2,128]{3,2,1,0:T(2,128)S(1)}, f32[13,5,2,128]{3,2,1,0:T(2,128)S(1)}, u32[]{:S(2)}, u32[]{:S(2)}) collective-permute-start(f32[13,5,2,128]{3,2,1,0:T(2,128)S(1)} %constant_dynamic-update-slice_fusion.own), channel_id=1, source_target_pairs={{0,1},{1,2},{2,3},{3,4},{4,5},{5,6},{6,7},{7,8},{8,9},{9,10},{10,1... | collective-permute-start | bytes 199688 | tf_op jit(solution)/shard_map/ppermute | solution.py:658
  158.5 25.2 %all_to_all.22 = f32[64,3,1,128]{3,2,1,0:T(1,128)S(1)} all-to-all(f32[64,3,1,128]{3,2,1,0:T(1,128)S(1)} %get-tuple-element.77), channel_id=1, replica_groups=mesh['tile'=12,'group'=64] {'group'}, dimensions={0} | all-to-all | bytes 196608 | tf_op jit(solution)/shard_map/all_to_all | solution.py:676
  183.7 2.6 %shard_map.94 = (f32[8,16,128]{2,1,0:T(8,128)}, f32[8,16,128]{2,1,0:T(8,128)}) custom-call(f32[192,128]{1,0:T(8,128)S(1)} %bitcast.7, f32[12,1,128]{2,1,0:T(1,128)S(1)} %get-tuple-element.78.below_ref, f32[12,24,128]{2,1,0:T(8,128)S(1)} %copy-done.9, f32[12,24,128]{2,1,0:T(8,128)S(1)} %copy-done.12, f32[12,24,128]{2,1,0:T(8,128)S(1)} %copy-done.15, ...), custom_call_target="tpu_custom_call" | custom-call | flops 655360 | bytes 262144 | tf_op jit(solution)/shard_map/pallas_call | solution.py:643
  (100 shorter events, 31.0 us)
Async XLA Ops:
  2.7 8.8 %collective-permute-start.1 = (f32[4,8,16,128]{3,2,1,0:T(8,128)}, f32[4,8,16,128]{3,2,1,0:T(8,128)S(1)}, u32[]{:S(2)}, u32[]{:S(2)}) collective-permute-start(f32[4,8,16,128]{3,2,1,0:T(8,128)} %shard_map.86.own), channel_id=1, source_target_pairs={{64,0},{128,64},{192,128},{256,192},{320,256},{384,320},{448,384},... | collective-permute-start | bytes 786440 | tf_op jit(solution)/shard_map/ppermute | solution.py:659
  4.0 9.1 %collective-permute-start = (f32[4,8,16,128]{3,2,1,0:T(8,128)}, f32[4,8,16,128]{3,2,1,0:T(8,128)S(1)}, u32[]{:S(2)}, u32[]{:S(2)}) collective-permute-start(f32[4,8,16,128]{3,2,1,0:T(8,128)} %shard_map.86.own), channel_id=1, source_target_pairs={{0,64},{64,128},{128,192},{192,256},{256,320},{320,384},{384,448},... | collective-permute-start | bytes 786440 | tf_op jit(solution)/shard_map/ppermute | solution.py:658
  13.2 13.6 %collective-permute-start.2 = (f32[4,24,8,128]{3,2,1,0:T(8,128)S(1)}, f32[4,24,8,128]{3,2,1,0:T(8,128)S(1)}, u32[]{:S(2)}, u32[]{:S(2)}) collective-permute-start(f32[4,24,8,128]{3,2,1,0:T(8,128)S(1)} %pad_maximum_fusion), channel_id=1, source_target_pairs={{0,1},{1,2},{2,3},{3,4},{4,5},{5,6},{6,7},{7,8},{8,9},{9,10},{10,1... | collective-permute-start | bytes 1179656 | tf_op jit(solution)/shard_map/ppermute | solution.py:658
  19.4 9.3 %copy-start = (f32[4,8,16,128]{3,2,1,0:T(8,128)S(1)}, f32[4,8,16,128]{3,2,1,0:T(8,128)}, u32[]{:S(2)}) copy-start(f32[4,8,16,128]{3,2,1,0:T(8,128)} %shard_map.86.own) | copy-start | bytes 786436
  19.4 9.2 %collective-permute-start.3 = (f32[4,24,8,128]{3,2,1,0:T(8,128)S(1)}, f32[4,24,8,128]{3,2,1,0:T(8,128)S(1)}, u32[]{:S(2)}, u32[]{:S(2)}) collective-permute-start(f32[4,24,8,128]{3,2,1,0:T(8,128)S(1)} %pad_maximum_fusion.1), channel_id=1, source_target_pairs={{1,0},{2,1},{3,2},{4,3},{5,4},{6,5},{7,6},{8,7},{9,8},{10,9},{11,1... | collective-permute-start | bytes 1179656 | tf_op jit(solution)/shard_map/ppermute | solution.py:659
  35.3 33.6 %copy-start.1 = (f32[26,32,128]{2,1,0:T(8,128)}, f32[26,32,128]{2,1,0:T(8,128)S(1)}, u32[]{:S(2)}) copy-start(f32[26,32,128]{2,1,0:T(8,128)S(1)} %get-tuple-element.72.wx_ref) | copy-start | bytes 1277956
  64.3 4.5 %collective-permute-start.4 = (f32[12,6,2,128]{3,2,1,0:T(2,128)S(1)}, f32[12,6,2,128]{3,2,1,0:T(2,128)S(1)}, u32[]{:S(2)}, u32[]{:S(2)}) collective-permute-start(f32[12,6,2,128]{3,2,1,0:T(2,128)S(1)} %get-tuple-element.45), channel_id=1, source_target_pairs={{0,2},{1,3},{2,4},{3,5},{4,6},{5,7},{6,8},{7,9},{8,10},{9,11},{10,... | collective-permute-start | bytes 221192 | tf_op jit(solution)/shard_map/ppermute | solution.py:658
  67.4 5.1 %collective-permute-start.5 = (f32[12,6,2,128]{3,2,1,0:T(2,128)S(1)}, f32[12,6,2,128]{3,2,1,0:T(2,128)S(1)}, u32[]{:S(2)}, u32[]{:S(2)}) collective-permute-start(f32[12,6,2,128]{3,2,1,0:T(2,128)S(1)} %get-tuple-element.46), channel_id=1, source_target_pairs={{2,0},{3,1},{4,2},{5,3},{6,4},{7,5},{8,6},{9,7},{10,8},{11,9},{12,... | collective-permute-start | bytes 221192 | tf_op jit(solution)/shard_map/ppermute | solution.py:659
  68.8 5.9 %copy-start.24 = (f32[12,6,2,128]{3,2,1,0:T(2,128)}, f32[12,6,2,128]{3,2,1,0:T(2,128)S(1)}, u32[]{:S(2)}) copy-start(f32[12,6,2,128]{3,2,1,0:T(2,128)S(1)} %collective-permute-done.4.before) | copy-start | bytes 221188
  76.8 28.1 %all-to-all-start.1 = ((f32[64,5,1,128]{3,2,1,0:T(1,128)}), f32[64,5,1,128]{3,2,1,0:T(1,128)S(1)}, u32[]{:S(2)}, u32[]{:S(2)}) async-start(f32[64,5,1,128]{3,2,1,0:T(1,128)} %copy-done.36), calls=%async_computation.1 | async-start | bytes 327680 | tf_op jit(solution)/shard_map/all_to_all | solution.py:676
  114.1 17.6 %copy-start.4 = (f32[26,32,128]{2,1,0:T(8,128)S(1)}, f32[26,32,128]{2,1,0:T(8,128)}, u32[]{:S(2)}) copy-start(f32[26,32,128]{2,1,0:T(8,128)} %copy-done.3) | copy-start | bytes 1277956
  114.1 17.6 %copy-start.6 = (f32[26,32,128]{2,1,0:T(8,128)S(1)}, f32[26,32,128]{2,1,0:T(8,128)}, u32[]{:S(2)}) copy-start(f32[26,32,128]{2,1,0:T(8,128)} %copy-done.5) | copy-start | bytes 1277956
  115.7 16.1 %copy-start.2 = (f32[26,32,128]{2,1,0:T(8,128)S(1)}, f32[26,32,128]{2,1,0:T(8,128)}, u32[]{:S(2)}) copy-start(f32[26,32,128]{2,1,0:T(8,128)} %copy-done.1) | copy-start | bytes 1277956
  115.7 5.4 %collective-permute-start.7 = (f32[8,16,128]{2,1,0:T(8,128)S(1)}, f32[8,16,128]{2,1,0:T(8,128)S(1)}, u32[]{:S(2)}, u32[]{:S(2)}) collective-permute-start(f32[8,16,128]{2,1,0:T(8,128)S(1)} %get-tuple-element.68.own), channel_id=1, source_target_pairs={{64,0},{128,64},{192,128},{256,192},{320,256},{384,320},{448,384},... | collective-permute-start | bytes 196616 | tf_op jit(solution)/shard_map/ppermute | solution.py:659
  117.1 5.3 %collective-permute-start.6 = (f32[8,16,128]{2,1,0:T(8,128)S(1)}, f32[8,16,128]{2,1,0:T(8,128)S(1)}, u32[]{:S(2)}, u32[]{:S(2)}) collective-permute-start(f32[8,16,128]{2,1,0:T(8,128)S(1)} %get-tuple-element.68.own), channel_id=1, source_target_pairs={{0,64},{64,128},{128,192},{192,256},{256,320},{320,384},{384,448},... | collective-permute-start | bytes 196616 | tf_op jit(solution)/shard_map/ppermute | solution.py:658
  122.4 5.3 %collective-permute-start.8 = (f32[24,8,128]{2,1,0:T(8,128)S(1)}, f32[24,8,128]{2,1,0:T(8,128)S(1)}, u32[]{:S(2)}, u32[]{:S(2)}) collective-permute-start(f32[24,8,128]{2,1,0:T(8,128)S(1)} %pad_maximum_fusion.2), channel_id=1, source_target_pairs={{0,1},{1,2},{2,3},{3,4},{4,5},{5,6},{6,7},{7,8},{8,9},{9,10},{10,1... | collective-permute-start | bytes 294920 | tf_op jit(solution)/shard_map/ppermute | solution.py:658
  125.8 5.9 %collective-permute-start.9 = (f32[24,8,128]{2,1,0:T(8,128)S(1)}, f32[24,8,128]{2,1,0:T(8,128)S(1)}, u32[]{:S(2)}, u32[]{:S(2)}) collective-permute-start(f32[24,8,128]{2,1,0:T(8,128)S(1)} %pad_maximum_fusion.3), channel_id=1, source_target_pairs={{1,0},{2,1},{3,2},{4,3},{5,4},{6,5},{7,6},{8,7},{9,8},{10,9},{11,1... | collective-permute-start | bytes 294920 | tf_op jit(solution)/shard_map/ppermute | solution.py:659
  149.9 6.5 %collective-permute-start.11 = (f32[13,5,2,128]{3,2,1,0:T(2,128)S(1)}, f32[13,5,2,128]{3,2,1,0:T(2,128)S(1)}, u32[]{:S(2)}, u32[]{:S(2)}) collective-permute-start(f32[13,5,2,128]{3,2,1,0:T(2,128)S(1)} %constant_dynamic-update-slice_fusion.own), channel_id=1, source_target_pairs={{1,0},{2,1},{3,2},{4,3},{5,4},{6,5},{7,6},{8,7},{9,8},{10,9},{11,1... | collective-permute-start | bytes 199688 | tf_op jit(solution)/shard_map/ppermute | solution.py:659
  151.8 5.8 %collective-permute-start.10 = (f32[13,5,2,128]{3,2,1,0:T(2,128)S(1)}, f32[13,5,2,128]{3,2,1,0:T(2,128)S(1)}, u32[]{:S(2)}, u32[]{:S(2)}) collective-permute-start(f32[13,5,2,128]{3,2,1,0:T(2,128)S(1)} %constant_dynamic-update-slice_fusion.own), channel_id=1, source_target_pairs={{0,1},{1,2},{2,3},{3,4},{4,5},{5,6},{6,7},{7,8},{8,9},{9,10},{10,1... | collective-permute-start | bytes 199688 | tf_op jit(solution)/shard_map/ppermute | solution.py:658
  157.6 26.0 %copy-start.12 = (f32[12,24,128]{2,1,0:T(8,128)S(1)}, f32[12,24,128]{2,1,0:T(8,128)}, u32[]{:S(2)}) copy-start(f32[12,24,128]{2,1,0:T(8,128)} %copy-done.10) | copy-start | bytes 442372
  157.6 26.0 %copy-start.15 = (f32[12,24,128]{2,1,0:T(8,128)S(1)}, f32[12,24,128]{2,1,0:T(8,128)}, u32[]{:S(2)}) copy-start(f32[12,24,128]{2,1,0:T(8,128)} %copy-done.13) | copy-start | bytes 442372
  157.6 26.0 %copy-start.18 = (f32[12,24,128]{2,1,0:T(8,128)S(1)}, f32[12,24,128]{2,1,0:T(8,128)}, u32[]{:S(2)}) copy-start(f32[12,24,128]{2,1,0:T(8,128)} %copy-done.16) | copy-start | bytes 442372
  157.7 26.0 %copy-start.21 = (f32[12,24,128]{2,1,0:T(8,128)S(1)}, f32[12,24,128]{2,1,0:T(8,128)}, u32[]{:S(2)}) copy-start(f32[12,24,128]{2,1,0:T(8,128)} %copy-done.19) | copy-start | bytes 442372
  158.5 25.2 %copy-start.9 = (f32[12,24,128]{2,1,0:T(8,128)S(1)}, f32[12,24,128]{2,1,0:T(8,128)}, u32[]{:S(2)}) copy-start(f32[12,24,128]{2,1,0:T(8,128)} %copy-done.7) | copy-start | bytes 442372
  (26 other events, 22.2 us)

commit v6 on v5

--- a/solution.py
+++ b/solution.py
@@ -416,16 +416,14 @@
         high_ref[:, 5, core : core + 1, :] = rows
 
 
-def bands3_kernel(before, here, after, s3_ref, di3_ref, wx3_ref, wy3_ref, wz3_ref):
+def third_kernel(
+    before, here, after,
+    r2_ref, s2_ref, di2_ref, wx2_ref, wy2_ref, wz2_ref, e22_ref,
+    s3_ref, di3_ref, wx3_ref, wy3_ref, wz3_ref, msg_ref,
+):
     s3, wx3, wy3, wz3 = unpack_bands3(band_rows3(here, before, after))
     s3_ref[...], wx3_ref[...], wy3_ref[...], wz3_ref[...] = s3, wx3, wy3, wz3
     di3_ref[...] = relax_factor(s3, wx3, wy3, wz3, 2, 8)
-
-
-def third_kernel(
-    before, here, after,
-    r2_ref, s2_ref, di2_ref, wx2_ref, wy2_ref, wz2_ref, e22_ref, msg_ref,
-):
     low, own, high = pair_rows(here, before, after)
     r2, s2, wx2, wy2, wz2 = (unpack_level2(f, own, low, high) for f in range(5))
     di2 = relax_factor(s2, wx2, wy2, wz2, 1, 4)
@@ -721,12 +719,11 @@
     here = pairs_of_tiles(msg)
     to_low, to_high = call(sides_kernel, [(tiles, 6, 2, NZ)] * 2, [here])
     before, after = beside(to_low, to_high, "group", 2)
-    r2, s2, di2, wx2, wy2, wz2, e22, msg = call(
+    r2, s2, di2, wx2, wy2, wz2, e22, *bands3, msg = call(
         third_kernel,
-        [two] * 7 + [(groups, rows_once, 1, NZ)],
+        [two] * 7 + [three] * 5 + [(groups, rows_once, 1, NZ)],
         [before, here, after],
     )
-    bands3 = call(bands3_kernel, [three] * 5, [before, here, after])
     bands2 = [s2, di2, wx2, wy2, wz2]
     third = everyone(msg, "group").reshape(groups * rows_once, NZ)
     pre, below = call(

time: 187 us -> 173 us (0.925)
  blocking collectives: 70 us -> 97.7 us
  local copies, waits for them, and re-layouts: 21 us -> 1.06 us
  starting transfers between devices: 58.2 us -> 41.7 us
  waiting for transfers between devices: 20.2 us -> 14.9 us
    all_to_all x2 -> x3, blocking collectives: 41 us -> 68.7 us  [everyone(): return lax.all_to_all(blocks, axis, 0, 0, tiled=True)]
    unnamed x75 -> x3, local copies, waits for them, and re-layouts: 20 us -> 0.01 us
    all_to_all x1 -> x0, starting transfers between devices: 16.4 us -> none  [everyone(): return lax.all_to_all(blocks, axis, 0, 0, tiled=True)]
    all_to_all x1 -> x0, waiting for transfers between devices: 5.3 us -> none  [everyone(): return lax.all_to_all(blocks, axis, 0, 0, tiled=True)]
    pallas_call x8 -> x7, Pallas kernels: 13.7 us -> 13.9 us  [call(): pl.pallas_call(body, out_shape=[jax.ShapeDtypeStruct(shape, F32) for shap...]
  transfers between devices with their start and end apart: 13 -> 12, of which waited for: 9 -> 8; matrix products, arithmetic and copies ran while one was open for 1% -> 1% of each run, Pallas kernels for 1% -> 0%
where the time goes in v6:
time: 173 us; the launch traced here: 172 us
  blocking collectives  97.7 us (56%)
  starting transfers between devices  41.7 us (24%)
  Pallas kernels  16 us (9%)
  waiting for transfers between devices  14.9 us (9%)
    all_to_all x3, blocking collectives, everyone(): return lax.all_to_all(blocks, axis, 0, 0, tiled=True)  68.7 us
    all_to_all x1, blocking collectives, pairs_of_tiles(): lax.all_to_all(block, ('tile', 'group'), 0, 0, axis_index_groups=members,...  29 us
    ppermute x6, starting transfers between devices, beside(): from_low = lax.ppermute(to_high, axis, [(i, i + step) for i in range(ends)])  26.7 us
    ppermute x6, starting transfers between devices, beside(): from_high = lax.ppermute(to_low, axis, [(i + step, i) for i in range(ends)])  15 us
    pallas_call x7, Pallas kernels, call(): pl.pallas_call(body, out_shape=[jax.ShapeDtypeStruct(shape, F32) for shap...  13.9 us
    ppermute x6, waiting for transfers between devices, beside(): from_high = lax.ppermute(to_low, axis, [(i + step, i) for i in range(ends)])  10.6 us
    ppermute x6, waiting for transfers between devices, beside(): from_low = lax.ppermute(to_high, axis, [(i, i + step) for i in range(ends)])  4.24 us
  transfers between devices with their start and end apart: 12, of which 8 were waited for; matrix products, arithmetic and copies ran while one was open for 1% of the time, Pallas kernels for 0%

profile of v6, /device:TPU:1, one launch (start us, length us, event | category | flops | bytes accessed | tf_op | source)
XLA Modules:
  0.0 172.4 jit_solution(4361201171601452289)
XLA Ops:
  0.6 2.1 %shard_map.86.own = f32[4,8,16,128]{3,2,1,0:T(8,128)} custom-call(f32[8,16,128]{2,1,0:T(8,128)} %head_in.1, f32[8,16,128]{2,1,0:T(8,128)} %old_in.1, s32[8,16,128]{2,1,0:T(8,128)} %soil_in.1, f32[12]{0:T(128)} %ks_in.1, f32[12]{0:T(128)} %alpha_in.1, f32[12]{0:T(128)} %shape_in.1, f32[12]{0:T(128)} %span_in.1), custom_call_target="tpu_custom_call" | custom-call | tf_op jit(solution)/shard_map/pallas_call | solution.py:696
  4.0 5.5 %collective-permute-start = (f32[4,8,16,128]{3,2,1,0:T(8,128)}, f32[4,8,16,128]{3,2,1,0:T(8,128)S(1)}, u32[]{:S(2)}, u32[]{:S(2)}) collective-permute-start(f32[4,8,16,128]{3,2,1,0:T(8,128)} %shard_map.86.own), channel_id=1, source_target_pairs={{0,64},{64,128},{128,192},{192,256},{256,320},{320,384},{384,448},... | collective-permute-start | bytes 786440 | tf_op jit(solution)/shard_map/ppermute | solution.py:656
  11.5 1.6 collective-permute-done.xlow
  13.2 6.2 %collective-permute-start.2 = (f32[4,24,8,128]{3,2,1,0:T(8,128)S(1)}, f32[4,24,8,128]{3,2,1,0:T(8,128)S(1)}, u32[]{:S(2)}, u32[]{:S(2)}) collective-permute-start(f32[4,24,8,128]{3,2,1,0:T(8,128)S(1)} %pad_maximum_fusion), channel_id=1, source_target_pairs={{0,1},{1,2},{2,3},{3,4},{4,5},{5,6},{6,7},{7,8},{8,9},{9,10},{10,1... | collective-permute-start | bytes 1179656 | tf_op jit(solution)/shard_map/ppermute | solution.py:656
  19.4 7.3 %collective-permute-start.3 = (f32[4,24,8,128]{3,2,1,0:T(8,128)S(1)}, f32[4,24,8,128]{3,2,1,0:T(8,128)S(1)}, u32[]{:S(2)}, u32[]{:S(2)}) collective-permute-start(f32[4,24,8,128]{3,2,1,0:T(8,128)S(1)} %pad_maximum_fusion.1), channel_id=1, source_target_pairs={{1,0},{2,1},{3,2},{4,3},{5,4},{6,5},{7,6},{8,7},{9,8},{10,9},{11,1... | collective-permute-start | bytes 1179656 | tf_op jit(solution)/shard_map/ppermute | solution.py:657
  26.8 1.9 %collective-permute-done.3.yhigh = f32[4,24,8,128]{3,2,1,0:T(8,128)S(1)} collective-permute-done((f32[4,24,8,128]{3,2,1,0:T(8,128)S(1)}, f32[4,24,8,128]{3,2,1,0:T(8,128)S(1)}, u32[]{:S(2)}, u32[]{:S(2)}) %collective-permute-start.3) | collective-permute-done | bytes 393248 | tf_op jit(solution)/shard_map/ppermute | solution.py:657
  28.7 3.1 %shard_map.87 = (f32[26,32,128]{2,1,0:T(8,128)S(1)}, f32[26,32,128]{2,1,0:T(8,128)S(1)}, f32[26,32,128]{2,1,0:T(8,128)S(1)}, f32[26,32,128]{2,1,0:T(8,128)S(1)},...) custom-call(f32[4,8,16,128]{3,2,1,0:T(8,128)S(1)} %collective-permut, ...), custom_call_target="tpu_custom_call" | custom-call | flops 22528000 | bytes 9011200 | tf_op jit(solution)/shard_map/pallas_call | solution.py:641
  31.8 29.0 %all_to_all.20 = f32[24,6,2,128]{3,2,1,0:T(2,128)S(1)} all-to-all(f32[24,6,2,128]{3,2,1,0:T(2,128)S(1)} %get-tuple-element.44), channel_id=1, replica_groups={{0,1,64,65,128,129,192,193,256,257,320,321,384,385,448,449,512,513,576,..., dimensions={0} | all-to-all | bytes 294912 | tf_op jit(solution)/shard_map/all_to_all | solution.py:683
  60.8 3.1 %collective-permute-start.4 = (f32[12,6,2,128]{3,2,1,0:T(2,128)S(1)}, f32[12,6,2,128]{3,2,1,0:T(2,128)S(1)}, u32[]{:S(2)}, u32[]{:S(2)}) collective-permute-start(f32[12,6,2,128]{3,2,1,0:T(2,128)S(1)} %get-tuple-element.45), channel_id=1, source_target_pairs={{0,2},{1,3},{2,4},{3,5},{4,6},{5,7},{6,8},{7,9},{8,10},{9,11},{10,... | collective-permute-start | bytes 221192 | tf_op jit(solution)/shard_map/ppermute | solution.py:656
  65.3 3.7 %collective-permute-done.5.after = f32[12,6,2,128]{3,2,1,0:T(2,128)S(1)} collective-permute-done((f32[12,6,2,128]{3,2,1,0:T(2,128)S(1)}, f32[12,6,2,128]{3,2,1,0:T(2,128)S(1)}, u32[]{:S(2)}, u32[]{:S(2)}) %collective-permute-start.5) | collective-permute-done | bytes 73760 | tf_op jit(solution)/shard_map/ppermute | solution.py:657
  69.0 3.5 %shard_map.89 = (f32[24,16,128]{2,1,0:T(8,128)S(1)}, f32[24,16,128]{2,1,0:T(8,128)S(1)}, f32[24,16,128]{2,1,0:T(8,128)S(1)}, f32[24,16,128]{2,1,0:T(8,128)S(1)},...) custom-call(f32[12,6,2,128]{3,2,1,0:T(2,128)S(1)} %collective-permut, ...), custom_call_target="tpu_custom_call" | custom-call | flops 11386880 | bytes 4554752 | tf_op jit(solution)/shard_map/pallas_call | solution.py:641
  72.5 27.9 %all_to_all.21 = f32[64,5,1,128]{3,2,1,0:T(1,128)S(1)} all-to-all(f32[64,5,1,128]{3,2,1,0:T(1,128)S(1)} %get-tuple-element.47), channel_id=1, replica_groups=mesh['tile'=12,'group'=64] {'group'}, dimensions={0} | all-to-all | bytes 327680 | tf_op jit(solution)/shard_map/all_to_all | solution.py:674
  100.4 1.5 shard_map.90
  103.2 4.0 %collective-permute-start.6 = (f32[8,16,128]{2,1,0:T(8,128)S(1)}, f32[8,16,128]{2,1,0:T(8,128)S(1)}, u32[]{:S(2)}, u32[]{:S(2)}) collective-permute-start(f32[8,16,128]{2,1,0:T(8,128)S(1)} %get-tuple-element.68.own), channel_id=1, source_target_pairs={{0,64},{64,128},{128,192},{192,256},{256,320},{320,384},{384,448},... | collective-permute-start | bytes 196616 | tf_op jit(solution)/shard_map/ppermute | solution.py:656
  108.6 3.4 %collective-permute-start.8 = (f32[24,8,128]{2,1,0:T(8,128)S(1)}, f32[24,8,128]{2,1,0:T(8,128)S(1)}, u32[]{:S(2)}, u32[]{:S(2)}) collective-permute-start(f32[24,8,128]{2,1,0:T(8,128)S(1)} %pad_maximum_fusion.2), channel_id=1, source_target_pairs={{0,1},{1,2},{2,3},{3,4},{4,5},{5,6},{6,7},{7,8},{8,9},{9,10},{10,1... | collective-permute-start | bytes 294920 | tf_op jit(solution)/shard_map/ppermute | solution.py:656
  112.0 1.9 %collective-permute-start.9 = (f32[24,8,128]{2,1,0:T(8,128)S(1)}, f32[24,8,128]{2,1,0:T(8,128)S(1)}, u32[]{:S(2)}, u32[]{:S(2)}) collective-permute-start(f32[24,8,128]{2,1,0:T(8,128)S(1)} %pad_maximum_fusion.3), channel_id=1, source_target_pairs={{1,0},{2,1},{3,2},{4,3},{5,4},{6,5},{7,6},{8,7},{9,8},{10,9},{11,1... | collective-permute-start | bytes 294920 | tf_op jit(solution)/shard_map/ppermute | solution.py:657
  113.9 4.0 %collective-permute-done.9.yhigh = f32[24,8,128]{2,1,0:T(8,128)S(1)} collective-permute-done((f32[24,8,128]{2,1,0:T(8,128)S(1)}, f32[24,8,128]{2,1,0:T(8,128)S(1)}, u32[]{:S(2)}, u32[]{:S(2)}) %collective-permute-start.9) | collective-permute-done | bytes 98336 | tf_op jit(solution)/shard_map/ppermute | solution.py:657
  117.9 2.4 %shard_map.91 = (f32[26,32,128]{2,1,0:T(8,128)S(1)}, f32[26,32,128]{2,1,0:T(8,128)S(1)}, f32[26,32,128]{2,1,0:T(8,128)S(1)}, f32[12,32,128]{2,1,0:T(8,128)S(1)},...) custom-call(f32[8,16,128]{2,1,0:T(8,128)S(1)} %collective-permute-done.6.xlow, ...), custom_call_target="tpu_custom_call" | custom-call | flops 8688640 | bytes 3475456 | tf_op jit(solution)/shard_map/pallas_call | solution.py:641
  120.4 15.8 %all_to_all.22 = f32[12,5,2,128]{3,2,1,0:T(2,128)S(1)} all-to-all(f32[12,5,2,128]{3,2,1,0:T(2,128)S(1)} %get-tuple-element.75), channel_id=1, replica_groups=mesh['tile'=12,'group'=64] {'tile'}, dimensions={0} | all-to-all | bytes 122880 | tf_op jit(solution)/shard_map/all_to_all | solution.py:674
  136.2 1.9 %collective-permute-start.11 = (f32[13,5,2,128]{3,2,1,0:T(2,128)S(1)}, f32[13,5,2,128]{3,2,1,0:T(2,128)S(1)}, u32[]{:S(2)}, u32[]{:S(2)}) collective-permute-start(f32[13,5,2,128]{3,2,1,0:T(2,128)S(1)} %constant_dynamic-update-slice_fusion.own), channel_id=1, source_target_pairs={{1,0},{2,1},{3,2},{4,3},{5,4},{6,5},{7,6},{8,7},{9,8},{10,9},{11,1... | collective-permute-start | bytes 199688 | tf_op jit(solution)/shard_map/ppermute | solution.py:657
  138.1 4.5 %collective-permute-start.10 = (f32[13,5,2,128]{3,2,1,0:T(2,128)S(1)}, f32[13,5,2,128]{3,2,1,0:T(2,128)S(1)}, u32[]{:S(2)}, u32[]{:S(2)}) collective-permute-start(f32[13,5,2,128]{3,2,1,0:T(2,128)S(1)} %constant_dynamic-update-slice_fusion.own), channel_id=1, source_target_pairs={{0,1},{1,2},{2,3},{3,4},{4,5},{5,6},{6,7},{7,8},{8,9},{9,10},{10,1... | collective-permute-start | bytes 199688 | tf_op jit(solution)/shard_map/ppermute | solution.py:656
  142.6 1.3 collective-permute-done.10.low
  144.8 25.0 %all_to_all.23 = f32[64,3,1,128]{3,2,1,0:T(1,128)S(1)} all-to-all(f32[64,3,1,128]{3,2,1,0:T(1,128)S(1)} %get-tuple-element.77), channel_id=1, replica_groups=mesh['tile'=12,'group'=64] {'group'}, dimensions={0} | all-to-all | bytes 196608 | tf_op jit(solution)/shard_map/all_to_all | solution.py:674
  169.8 2.5 %shard_map.93 = (f32[8,16,128]{2,1,0:T(8,128)}, f32[8,16,128]{2,1,0:T(8,128)}) custom-call(f32[192,128]{1,0:T(8,128)S(1)} %bitcast.6, f32[12,1,128]{2,1,0:T(1,128)S(1)} %get-tuple-element.78.below_ref, f32[12,24,128]{2,1,0:T(8,128)S(1)} %get-tuple-element.48.s3_ref, f32[12,24,128]{2,1,0:T(8,128)S(1)} %get-tuple-element.49.di3_ref, ...), custom_call_target="tpu_custom_call" | custom-call | flops 655360 | bytes 262144 | tf_op jit(solution)/shard_map/pallas_call | solution.py:641
  (26 shorter events, 8.3 us)
Async XLA Ops:
  2.7 8.8 %collective-permute-start.1 = (f32[4,8,16,128]{3,2,1,0:T(8,128)}, f32[4,8,16,128]{3,2,1,0:T(8,128)S(1)}, u32[]{:S(2)}, u32[]{:S(2)}) collective-permute-start(f32[4,8,16,128]{3,2,1,0:T(8,128)} %shard_map.86.own), channel_id=1, source_target_pairs={{64,0},{128,64},{192,128},{256,192},{320,256},{384,320},{448,384},... | collective-permute-start | bytes 786440 | tf_op jit(solution)/shard_map/ppermute | solution.py:657
  4.0 9.1 %collective-permute-start = (f32[4,8,16,128]{3,2,1,0:T(8,128)}, f32[4,8,16,128]{3,2,1,0:T(8,128)S(1)}, u32[]{:S(2)}, u32[]{:S(2)}) collective-permute-start(f32[4,8,16,128]{3,2,1,0:T(8,128)} %shard_map.86.own), channel_id=1, source_target_pairs={{0,64},{64,128},{128,192},{192,256},{256,320},{320,384},{384,448},... | collective-permute-start | bytes 786440 | tf_op jit(solution)/shard_map/ppermute | solution.py:656
  13.2 13.6 %collective-permute-start.2 = (f32[4,24,8,128]{3,2,1,0:T(8,128)S(1)}, f32[4,24,8,128]{3,2,1,0:T(8,128)S(1)}, u32[]{:S(2)}, u32[]{:S(2)}) collective-permute-start(f32[4,24,8,128]{3,2,1,0:T(8,128)S(1)} %pad_maximum_fusion), channel_id=1, source_target_pairs={{0,1},{1,2},{2,3},{3,4},{4,5},{5,6},{6,7},{7,8},{8,9},{9,10},{10,1... | collective-permute-start | bytes 1179656 | tf_op jit(solution)/shard_map/ppermute | solution.py:656
  19.4 9.3 %copy-start = (f32[4,8,16,128]{3,2,1,0:T(8,128)S(1)}, f32[4,8,16,128]{3,2,1,0:T(8,128)}, u32[]{:S(2)}) copy-start(f32[4,8,16,128]{3,2,1,0:T(8,128)} %shard_map.86.own) | copy-start | bytes 786436
  19.4 9.2 %collective-permute-start.3 = (f32[4,24,8,128]{3,2,1,0:T(8,128)S(1)}, f32[4,24,8,128]{3,2,1,0:T(8,128)S(1)}, u32[]{:S(2)}, u32[]{:S(2)}) collective-permute-start(f32[4,24,8,128]{3,2,1,0:T(8,128)S(1)} %pad_maximum_fusion.1), channel_id=1, source_target_pairs={{1,0},{2,1},{3,2},{4,3},{5,4},{6,5},{7,6},{8,7},{9,8},{10,9},{11,1... | collective-permute-start | bytes 1179656 | tf_op jit(solution)/shard_map/ppermute | solution.py:657
  60.8 4.5 %collective-permute-start.4 = (f32[12,6,2,128]{3,2,1,0:T(2,128)S(1)}, f32[12,6,2,128]{3,2,1,0:T(2,128)S(1)}, u32[]{:S(2)}, u32[]{:S(2)}) collective-permute-start(f32[12,6,2,128]{3,2,1,0:T(2,128)S(1)} %get-tuple-element.45), channel_id=1, source_target_pairs={{0,2},{1,3},{2,4},{3,5},{4,6},{5,7},{6,8},{7,9},{8,10},{9,11},{10,... | collective-permute-start | bytes 221192 | tf_op jit(solution)/shard_map/ppermute | solution.py:656
  63.9 5.1 %collective-permute-start.5 = (f32[12,6,2,128]{3,2,1,0:T(2,128)S(1)}, f32[12,6,2,128]{3,2,1,0:T(2,128)S(1)}, u32[]{:S(2)}, u32[]{:S(2)}) collective-permute-start(f32[12,6,2,128]{3,2,1,0:T(2,128)S(1)} %get-tuple-element.46), channel_id=1, source_target_pairs={{2,0},{3,1},{4,2},{5,3},{6,4},{7,5},{8,6},{9,7},{10,8},{11,9},{12,... | collective-permute-start | bytes 221192 | tf_op jit(solution)/shard_map/ppermute | solution.py:657
  101.9 5.3 %collective-permute-start.7 = (f32[8,16,128]{2,1,0:T(8,128)S(1)}, f32[8,16,128]{2,1,0:T(8,128)S(1)}, u32[]{:S(2)}, u32[]{:S(2)}) collective-permute-start(f32[8,16,128]{2,1,0:T(8,128)S(1)} %get-tuple-element.68.own), channel_id=1, source_target_pairs={{64,0},{128,64},{192,128},{256,192},{320,256},{384,320},{448,384},... | collective-permute-start | bytes 196616 | tf_op jit(solution)/shard_map/ppermute | solution.py:657
  103.2 5.3 %collective-permute-start.6 = (f32[8,16,128]{2,1,0:T(8,128)S(1)}, f32[8,16,128]{2,1,0:T(8,128)S(1)}, u32[]{:S(2)}, u32[]{:S(2)}) collective-permute-start(f32[8,16,128]{2,1,0:T(8,128)S(1)} %get-tuple-element.68.own), channel_id=1, source_target_pairs={{0,64},{64,128},{128,192},{192,256},{256,320},{320,384},{384,448},... | collective-permute-start | bytes 196616 | tf_op jit(solution)/shard_map/ppermute | solution.py:656
  108.6 5.3 %collective-permute-start.8 = (f32[24,8,128]{2,1,0:T(8,128)S(1)}, f32[24,8,128]{2,1,0:T(8,128)S(1)}, u32[]{:S(2)}, u32[]{:S(2)}) collective-permute-start(f32[24,8,128]{2,1,0:T(8,128)S(1)} %pad_maximum_fusion.2), channel_id=1, source_target_pairs={{0,1},{1,2},{2,3},{3,4},{4,5},{5,6},{6,7},{7,8},{8,9},{9,10},{10,1... | collective-permute-start | bytes 294920 | tf_op jit(solution)/shard_map/ppermute | solution.py:656
  112.0 5.9 %collective-permute-start.9 = (f32[24,8,128]{2,1,0:T(8,128)S(1)}, f32[24,8,128]{2,1,0:T(8,128)S(1)}, u32[]{:S(2)}, u32[]{:S(2)}) collective-permute-start(f32[24,8,128]{2,1,0:T(8,128)S(1)} %pad_maximum_fusion.3), channel_id=1, source_target_pairs={{1,0},{2,1},{3,2},{4,3},{5,4},{6,5},{7,6},{8,7},{9,8},{10,9},{11,1... | collective-permute-start | bytes 294920 | tf_op jit(solution)/shard_map/ppermute | solution.py:657
  136.2 6.5 %collective-permute-start.11 = (f32[13,5,2,128]{3,2,1,0:T(2,128)S(1)}, f32[13,5,2,128]{3,2,1,0:T(2,128)S(1)}, u32[]{:S(2)}, u32[]{:S(2)}) collective-permute-start(f32[13,5,2,128]{3,2,1,0:T(2,128)S(1)} %constant_dynamic-update-slice_fusion.own), channel_id=1, source_target_pairs={{1,0},{2,1},{3,2},{4,3},{5,4},{6,5},{7,6},{8,7},{9,8},{10,9},{11,1... | collective-permute-start | bytes 199688 | tf_op jit(solution)/shard_map/ppermute | solution.py:657
  138.1 5.8 %collective-permute-start.10 = (f32[13,5,2,128]{3,2,1,0:T(2,128)S(1)}, f32[13,5,2,128]{3,2,1,0:T(2,128)S(1)}, u32[]{:S(2)}, u32[]{:S(2)}) collective-permute-start(f32[13,5,2,128]{3,2,1,0:T(2,128)S(1)} %constant_dynamic-update-slice_fusion.own), channel_id=1, source_target_pairs={{0,1},{1,2},{2,3},{3,4},{4,5},{5,6},{6,7},{7,8},{8,9},{9,10},{10,1... | collective-permute-start | bytes 199688 | tf_op jit(solution)/shard_map/ppermute | solution.py:656

commit v7 on v6

--- a/solution.py
+++ b/solution.py
@@ -145,7 +145,7 @@
     for k in range(4):
         chosen = ((sub == 8 + 4 * k) & (lane % 2 == 0)) | ((sub == 10 + 4 * k) & (lane % 2 == 1))
         parts.append(jnp.sum(jnp.where(chosen, rows, 0.0), axis=1, keepdims=True))
-    return jnp.concatenate([part[x] for x in range(2) for part in parts], axis=0)
+    return [jnp.concatenate([part[x] for part in parts], axis=0) for x in range(2)]
 
 
 def pack_edge1(v):
@@ -224,16 +224,28 @@
     lax.fori_loop(0, BX, cells, 0, unroll=2)
 
 
-def fill_window(ref, xlow, own, xhigh, ylow, yhigh):
-    ref[1 : 1 + BX, 8:24, :] = xlow
+def is_even(axis, step=1):
+    return (lax.axis_index(axis) // step) % 2 == 0
+
+
+def sides(first, second, axis, step=1):
+    even = is_even(axis, step)
+    return jnp.where(even, second, first), jnp.where(even, first, second)
+
+
+def fill_window(ref, xfirst, own, xsecond, yfirst, ysecond):
+    ref[1 : 1 + BX, 8:24, :], ref[1 + 2 * BX : 1 + 3 * BX, 8:24, :] = sides(xfirst, xsecond, "tile")
     ref[1 + BX : 1 + 2 * BX, 8:24, :] = own
-    ref[1 + 2 * BX : 1 + 3 * BX, 8:24, :] = xhigh
-    ref[1 : PX - 1, 0:8, :] = ylow
-    ref[1 : PX - 1, 24:32, :] = yhigh
+    ylow, yhigh = sides(yfirst, ysecond, "group")
+    for y, part in ((0, ylow), (24, yhigh)):
+        low, high = sides(part[:BX], part[2 * BX :], "tile")
+        ref[1 : 1 + BX, y : y + 8, :] = low
+        ref[1 + BX : 1 + 2 * BX, y : y + 8, :] = part[BX : 2 * BX]
+        ref[1 + 2 * BX : 1 + 3 * BX, y : y + 8, :] = high
 
 
 def assemble_kernel(
-    xlow, own, xhigh, ylow, yhigh,
+    xfirst, own, xsecond, yfirst, ysecond,
     r_ref, s_ref, di_ref, wx_ref, wy_ref, wz_ref, e2_ref,
     r1_ref, s1_ref, di1_ref, wx1_ref, wy1_ref, wz1_ref, e21_ref, msg_ref,
     h_ref, k_ref, m_ref, e1_ref,
@@ -241,7 +253,7 @@
     for ref in (h_ref, k_ref, s_ref, wx_ref, wy_ref, wz_ref, di_ref, r_ref, e1_ref, e2_ref):
         blank_ends(ref)
     for f, ref in enumerate((h_ref, k_ref, s_ref, m_ref)):
-        fill_window(ref, xlow[f], own[f], xhigh[f], ylow[f], yhigh[f])
+        fill_window(ref, xfirst[f], own[f], xsecond[f], yfirst[f], ysecond[f])
 
     def harmonic(a, b):
         total = a + b
@@ -302,13 +314,13 @@
 
 
 def again_kernel(
-    xlow, own, xhigh, ylow, yhigh, rhs_ref, s_ref, di_ref, wx_ref, wy_ref, wz_ref,
+    xfirst, own, xsecond, yfirst, ysecond, rhs_ref, s_ref, di_ref, wx_ref, wy_ref, wz_ref,
     s1_ref, di1_ref, wx1_ref, wy1_ref, wz1_ref,
     u_ref, r_ref, e2_ref, r1_ref, e21_ref, msg_ref, edge_ref, pre_ref, e1_ref,
 ):
     for ref in (pre_ref, u_ref, r_ref, e1_ref, e2_ref):
         blank_ends(ref)
-    fill_window(pre_ref, xlow[...], own[...], xhigh[...], ylow[...], yhigh[...])
+    fill_window(pre_ref, xfirst[...], own[...], xsecond[...], yfirst[...], ysecond[...])
 
     def post(i, carry):
         at = 1 + 2 * i
@@ -335,7 +347,12 @@
         r1_ref[...], s1_ref[...], wx1_ref[...], wy1_ref[...], wz1_ref[...], di1_ref[...]
     )
     e21_ref[...] = e21
-    send(msg_ref, [pack_level2(r2[2:4]), pack_ring1(e21)])
+    tile = lax.axis_index("tile")
+    to_low, to_high = pack_ring1(e21)
+    for peer in range(msg_ref.shape[0]):
+        ring = jnp.where(tile > peer, to_low, to_high)
+        msg_ref[peer, 0] = pack_level2(r2[2:4])
+        msg_ref[peer, 1], msg_ref[peer, 2] = ring[0:2], ring[2:4]
     send(edge_ref, [pack_edge1(e21)])
 
 
@@ -344,21 +361,29 @@
     return lambda field, half: ref[0:tiles, field, half : half + 1, :]
 
 
-def pair_rows(here, before, after):
-    even = lax.axis_index("group") % 2 == 0
-
-    def choose(first, second):
-        return lambda field, half: jnp.where(even, first(field, half), second(field, half))
-
+def choose(which, one, two):
+    return lambda field, half: jnp.where(which, one(field, half), two(field, half))
+
+
+def both_sides(first, second, step):
+    even = is_even("group", step)
+    one, two = message_rows(first), message_rows(second)
+    return choose(even, two, one), choose(even, one, two)
+
+
+def pair_rows(here, first, second):
+    before, after = both_sides(first, second, 2)
+    even = is_even("group")
     one, two = message_rows(here.at[:, 0]), message_rows(here.at[:, 1])
-    return choose(message_rows(before), one), choose(one, two), choose(two, message_rows(after))
-
-
-def band_rows3(here, before, after):
-    even = lax.axis_index("group") % 2 == 0
-    six = [ref[:, 5, half : half + 1, :] for ref in (before,) for half in range(2)]
+    return choose(even, before, one), choose(even, one, two), choose(even, two, after)
+
+
+def band_rows3(here, first, second):
+    before, after = both_sides(first, second, 2)
+    even = is_even("group")
+    six = [before(5, half) for half in range(2)]
     six += [here[:, core, 5, 0:1, :] for core in range(2)]
-    six += [after[:, 5, half : half + 1, :] for half in range(2)]
+    six += [after(5, half) for half in range(2)]
     return [jnp.where(even, six[i], six[i + 1]) for i in range(5)]
 
 
@@ -408,23 +433,26 @@
     return second, restrict(r2 - operate(second, s2, wx2, wy2, wz2, 1, 4), 1, 4)
 
 
-def sides_kernel(here, low_ref, high_ref):
-    low_ref[:, 0:5], high_ref[:, 0:5] = here[:, 0, 0:5], here[:, 1, 0:5]
+def sides_kernel(here, first_ref, second_ref):
+    even = is_even("group", 2)
+    low, high = here[:, 0, 0:5], here[:, 1, 0:5]
+    first_ref[:, 0:5] = jnp.where(even, high, low)
+    second_ref[:, 0:5] = jnp.where(even, low, high)
     for core in range(2):
         rows = here[:, core, 5, 0:1, :]
-        low_ref[:, 5, core : core + 1, :] = rows
-        high_ref[:, 5, core : core + 1, :] = rows
+        first_ref[:, 5, core : core + 1, :] = rows
+        second_ref[:, 5, core : core + 1, :] = rows
 
 
 def third_kernel(
-    before, here, after,
+    first, here, second,
     r2_ref, s2_ref, di2_ref, wx2_ref, wy2_ref, wz2_ref, e22_ref,
     s3_ref, di3_ref, wx3_ref, wy3_ref, wz3_ref, msg_ref,
 ):
-    s3, wx3, wy3, wz3 = unpack_bands3(band_rows3(here, before, after))
+    s3, wx3, wy3, wz3 = unpack_bands3(band_rows3(here, first, second))
     s3_ref[...], wx3_ref[...], wy3_ref[...], wz3_ref[...] = s3, wx3, wy3, wz3
     di3_ref[...] = relax_factor(s3, wx3, wy3, wz3, 2, 8)
-    low, own, high = pair_rows(here, before, after)
+    low, own, high = pair_rows(here, first, second)
     r2, s2, wx2, wy2, wz2 = (unpack_level2(f, own, low, high) for f in range(5))
     di2 = relax_factor(s2, wx2, wy2, wz2, 1, 4)
     r2_ref[...], s2_ref[...], di2_ref[...] = r2, s2, di2
@@ -437,9 +465,9 @@
 
 
 def third_again_kernel(
-    own, low, high, s2_ref, di2_ref, wx2_ref, wy2_ref, wz2_ref, r2_ref, e22_ref, msg_ref
+    own, first, second, s2_ref, di2_ref, wx2_ref, wy2_ref, wz2_ref, r2_ref, e22_ref, msg_ref
 ):
-    r2 = unpack_level2(0, message_rows(own), message_rows(low), message_rows(high))
+    r2 = unpack_level2(0, message_rows(own), *both_sides(first, second, 1))
     r2_ref[...] = r2
     e22, r3 = descend_third(
         r2, s2_ref[...], wx2_ref[...], wy2_ref[...], wz2_ref[...], di2_ref[...]
@@ -560,19 +588,21 @@
     pre_ref[...] = e2_ref[9:17, 8:24, :] + own1[:, 8:24, :]
 
 
-def tile_rows(ref, off, at):
+def tile_rows(refs, even, off, at):
     tile = lax.axis_index("tile")
     total = jnp.zeros((2, NZ), F32)
     for t in range(lax.axis_size("tile")):
-        total = total + jnp.where(tile + off == t, ref[t, at], 0.0)
+        rows = refs[0][t, at] if len(refs) == 1 else jnp.where(even, refs[0][t, at], refs[1][t, at])
+        total = total + jnp.where(tile + off == t, rows, 0.0)
     return total
 
 
-def ring_row(own, low, high, off, first):
-    pairs = [tile_rows(own, off, first), tile_rows(own, off, first + 1)]
-    packed = [tile_rows(low, off, first + 1)[1:2]]
+def ring_row(own, first, second, off):
+    even = is_even("group")
+    pairs = [tile_rows((own,), even, off, 1), tile_rows((own,), even, off, 2)]
+    packed = [tile_rows((second, first), even, off, 2)[1:2]]
     packed += [pair[k : k + 1] for pair in pairs for k in range(2)]
-    packed += [tile_rows(high, off, first)[0:1]]
+    packed += [tile_rows((first, second), even, off, 1)[0:1]]
     return spread_pairs([row[None] for row in packed], 1)
 
 
@@ -587,7 +617,7 @@
 
 def last_climb_kernel(
     third_ref, below_ref, s3_ref, di3_ref, wx3_ref, wy3_ref, wz3_ref,
-    low, own, high,
+    first, own, second,
     r2_ref, s2_ref, di2_ref, wx2_ref, wy2_ref, wz2_ref, e22_ref,
     r1_ref, s1_ref, di1_ref, wx1_ref, wy1_ref, wz1_ref, e21_ref,
     e2_ref, rhs_ref, s_ref, di_ref, wx_ref, wy_ref, wz_ref, u_ref, r_ref,
@@ -603,15 +633,16 @@
     tiles = lax.axis_size("tile")
     middle = e21_ref[3:9]
     sub = iota(middle.shape, 1)
-    edge_low = jnp.concatenate([low[tiles, k] for k in range(3)], axis=0)[:, None]
-    edge_high = jnp.concatenate([high[tiles, k] for k in range(3)], axis=0)[:, None]
+    edge_first = jnp.concatenate([first[tiles, k] for k in range(3)], axis=0)[:, None]
+    edge_second = jnp.concatenate([second[tiles, k] for k in range(3)], axis=0)[:, None]
+    edge_low, edge_high = sides(edge_first, edge_second, "group")
     nothing = jnp.zeros_like(edge_low)
     edges = spread_pairs([edge_low] + [nothing] * 4 + [edge_high], 6)
     kept = (sub >= 6) & (sub < 26)
     middle = jnp.where(kept, middle, edges)
     blank = jnp.zeros((2, WY, NZ), F32)
-    first, last = ring_row(own, low, high, -1, 3), ring_row(own, low, high, 1, 1)
-    e21 = jnp.concatenate([blank, first, middle, last, blank], axis=0)
+    ends = [ring_row(own, first, second, off) for off in (-1, 1)]
+    e21 = jnp.concatenate([blank, ends[0], middle, ends[1], blank], axis=0)
     v = climb_to_first(e21 + corr2, r1_ref, s1_ref, di1_ref, wx1_ref, wy1_ref, wz1_ref)
     pre_ref[7:19] = e2_ref[7:19] + x_repeat(v[3:9])
 
@@ -651,23 +682,31 @@
     )(*operands)
 
 
-def beside(to_low, to_high, axis, step=1):
-    ends = lax.axis_size(axis) - step
-    from_low = lax.ppermute(to_high, axis, [(i, i + step) for i in range(ends)])
-    from_high = lax.ppermute(to_low, axis, [(i + step, i) for i in range(ends)])
-    return from_low, from_high
+def swaps(to_first, to_second, axis, step=1):
+    count = lax.axis_size(axis)
+
+    def swap(cells, odd):
+        ups = [
+            (i, i + step) for i in range(count - step) if (i // step) % 2 == odd
+        ]
+        return lax.ppermute(cells, axis, ups + [(j, i) for i, j in ups])
+
+    return swap(to_first, 0), swap(to_second, 1)
 
 
 def surround(cells, dim):
-    low, high = beside(cells, cells, "tile")
+    first, second = swaps(cells, cells, "tile")
     ydim = dim + 1
-
-    def part(first):
-        pieces = [lax.slice_in_dim(v, first, first + 8, axis=ydim) for v in (low, cells, high)]
-        return jnp.concatenate(pieces, axis=dim)
-
-    ylow, yhigh = beside(part(0), part(BY - 8), "group")
-    return low, cells, high, ylow, yhigh
+    even = is_even("group")
+
+    def halves(v):
+        low = lax.slice_in_dim(v, 0, 8, axis=ydim)
+        high = lax.slice_in_dim(v, BY - 8, BY, axis=ydim)
+        return jnp.where(even, high, low), jnp.where(even, low, high)
+
+    parts = [halves(v) for v in (first, cells, second)]
+    to_first, to_second = (jnp.concatenate(list(v), axis=dim) for v in zip(*parts, strict=True))
+    return first, cells, second, *swaps(to_first, to_second, "group")
 
 
 def everyone(blocks, axis):
@@ -717,12 +756,12 @@
     bands1 = [s1, di1, wx1, wy1, wz1]
 
     here = pairs_of_tiles(msg)
-    to_low, to_high = call(sides_kernel, [(tiles, 6, 2, NZ)] * 2, [here])
-    before, after = beside(to_low, to_high, "group", 2)
+    to_first, to_second = call(sides_kernel, [(tiles, 6, 2, NZ)] * 2, [here])
+    first, second = swaps(to_first, to_second, "group", 2)
     r2, s2, di2, wx2, wy2, wz2, e22, *bands3, msg = call(
         third_kernel,
         [two] * 7 + [three] * 5 + [(groups, rows_once, 1, NZ)],
-        [before, here, after],
+        [first, here, second],
     )
     bands2 = [s2, di2, wx2, wy2, wz2]
     third = everyone(msg, "group").reshape(groups * rows_once, NZ)
@@ -735,22 +774,22 @@
     around = surround(pre, 0)
     u, rem, e2, r1, e21, msg, edge = call(
         again_kernel,
-        [top] * 3 + [one] * 2 + [(tiles, 5, 2, NZ), (1, 5, 2, NZ)],
+        [top] * 3 + [one] * 2 + [(tiles, 3, 2, NZ), (1, 3, 2, NZ)],
         [*around, rhs, *bands0, *bands1],
         [top] * 2,
     )
     own = jnp.concatenate([everyone(msg, "tile"), edge], axis=0)
-    low, high = beside(own, own, "group")
+    first, second = swaps(own, own, "group")
     r2, e22, msg = call(
         third_again_kernel,
         [two] * 2 + [(groups, rows_again, 1, NZ)],
-        [own, low, high, *bands2],
+        [own, first, second, *bands2],
     )
     third = everyone(msg, "group").reshape(groups * rows_again, NZ)
     update, remainder = call(
         functools.partial(last_climb_kernel, groups=groups, thirds=thirds, rows=rows_again),
         [(BX, BY, NZ)] * 2,
-        [third, below, *bands3, low, own, high, r2, *bands2, e22, r1, *bands1, e21]
+        [third, below, *bands3, first, own, second, r2, *bands2, e22, r1, *bands1, e21]
         + [e2, rhs, *bands0, u, rem],
         [top] * 2,
     )

time: 173 us -> 163 us (0.942)
  blocking collectives: 97.7 us -> 87.4 us
  waiting for transfers between devices: 14.9 us -> 18.2 us
  starting transfers between devices: 41.7 us -> 38.8 us
    all_to_all x1, blocking collectives: 29 us -> 22.6 us  [pairs_of_tiles(): lax.all_to_all(block, ('tile', 'group'), 0, 0, axis_index_groups=members,...]
    all_to_all x3, blocking collectives: 68.7 us -> 64.8 us  [everyone(): return lax.all_to_all(blocks, axis, 0, 0, tiled=True)]
    ppermute x12, waiting for transfers between devices: 14.9 us -> 18.2 us  [swap(): return lax.ppermute(cells, axis, ups + [(j, i) for i, j in ups])]
    ppermute x12, starting transfers between devices: 41.7 us -> 38.8 us  [swap(): return lax.ppermute(cells, axis, ups + [(j, i) for i, j in ups])]
  transfers between devices with their start and end apart: 12 -> 12, of which waited for: 8 -> 6; matrix products, arithmetic and copies ran while one was open for 1% -> 1% of each run, Pallas kernels for 0% -> 0%
where the time goes in v7:
time: 163 us; the launch traced here: 162 us
  blocking collectives  87.4 us (54%)
  starting transfers between devices  38.8 us (24%)
  waiting for transfers between devices  18.2 us (11%)
  Pallas kernels  15.8 us (10%)
    all_to_all x3, blocking collectives, everyone(): return lax.all_to_all(blocks, axis, 0, 0, tiled=True)  64.8 us
    ppermute x12, starting transfers between devices, swap(): return lax.ppermute(cells, axis, ups + [(j, i) for i, j in ups])  38.8 us
    all_to_all x1, blocking collectives, pairs_of_tiles(): lax.all_to_all(block, ('tile', 'group'), 0, 0, axis_index_groups=members,...  22.6 us
    ppermute x12, waiting for transfers between devices, swap(): return lax.ppermute(cells, axis, ups + [(j, i) for i, j in ups])  18.2 us
    pallas_call x7, Pallas kernels, call(): pl.pallas_call(body, out_shape=[jax.ShapeDtypeStruct(shape, F32) for shap...  13.7 us
  transfers between devices with their start and end apart: 12, of which 6 were waited for; matrix products, arithmetic and copies ran while one was open for 1% of the time, Pallas kernels for 0%

profile of v7, /device:TPU:1, one launch (start us, length us, event | category | flops | bytes accessed | tf_op | source)
XLA Modules:
  0.0 162.2 jit_solution(2145227749384430890)
XLA Ops:
  0.6 2.1 %shard_map.86.own = f32[4,8,16,128]{3,2,1,0:T(8,128)} custom-call(f32[8,16,128]{2,1,0:T(8,128)} %head_in.1, f32[8,16,128]{2,1,0:T(8,128)} %old_in.1, s32[8,16,128]{2,1,0:T(8,128)} %soil_in.1, f32[12]{0:T(128)} %ks_in.1, f32[12]{0:T(128)} %alpha_in.1, f32[12]{0:T(128)} %shape_in.1, f32[12]{0:T(128)} %span_in.1), custom_call_target="tpu_custom_call" | custom-call | tf_op jit(solution)/shard_map/pallas_call | solution.py:735
  3.4 8.2 %collective-permute-start = (f32[4,8,16,128]{3,2,1,0:T(8,128)}, f32[4,8,16,128]{3,2,1,0:T(8,128)S(1)}, u32[]{:S(2)}, u32[]{:S(2)}) collective-permute-start(f32[4,8,16,128]{3,2,1,0:T(8,128)} %shard_map.86.own), channel_id=1, source_target_pairs={{0,64},{128,192},{256,320},{384,448},{512,576},{640,704},{64,0},{1... | collective-permute-start | bytes 786440 | tf_op jit(solution)/shard_map/ppermute | solution.py:692
  12.6 2.9 %collective-permute-done.xfirst = f32[4,8,16,128]{3,2,1,0:T(8,128)S(1)} collective-permute-done((f32[4,8,16,128]{3,2,1,0:T(8,128)}, f32[4,8,16,128]{3,2,1,0:T(8,128)S(1)}, u32[]{:S(2)}, u32[]{:S(2)}) %collective-permute-start) | collective-permute-done | bytes 262176 | tf_op jit(solution)/shard_map/ppermute | solution.py:692
  15.6 8.8 %collective-permute-start.2 = (f32[4,24,8,128]{3,2,1,0:T(8,128)S(1)}, f32[4,24,8,128]{3,2,1,0:T(8,128)S(1)}, u32[]{:S(2)}, u32[]{:S(2)}) collective-permute-start(f32[4,24,8,128]{3,2,1,0:T(8,128)S(1)} %pad_maximum_fusion), channel_id=1, source_target_pairs={{0,1},{2,3},{4,5},{6,7},{8,9},{10,11},{12,13},{14,15},{16,17},{18,... | collective-permute-start | bytes 1179656 | tf_op jit(solution)/shard_map/ppermute | solution.py:692
  24.4 2.1 %collective-permute-start.3 = (f32[4,24,8,128]{3,2,1,0:T(8,128)S(1)}, f32[4,24,8,128]{3,2,1,0:T(8,128)S(1)}, u32[]{:S(2)}, u32[]{:S(2)}) collective-permute-start(f32[4,24,8,128]{3,2,1,0:T(8,128)S(1)} %pad_maximum_fusion.1), channel_id=1, source_target_pairs={{1,2},{3,4},{5,6},{7,8},{9,10},{11,12},{13,14},{15,16},{17,18},{19... | collective-permute-start | bytes 1179656 | tf_op jit(solution)/shard_map/ppermute | solution.py:692
  26.5 7.2 %collective-permute-done.3.ysecond = f32[4,24,8,128]{3,2,1,0:T(8,128)S(1)} collective-permute-done((f32[4,24,8,128]{3,2,1,0:T(8,128)S(1)}, f32[4,24,8,128]{3,2,1,0:T(8,128)S(1)}, u32[]{:S(2)}, u32[]{:S(2)}) %collective-permute-start.3) | collective-permute-done | bytes 393248 | tf_op jit(solution)/shard_map/ppermute | solution.py:692
  33.7 3.0 %shard_map.87 = (f32[26,32,128]{2,1,0:T(8,128)S(1)}, f32[26,32,128]{2,1,0:T(8,128)S(1)}, f32[26,32,128]{2,1,0:T(8,128)S(1)}, f32[26,32,128]{2,1,0:T(8,128)S(1)},...) custom-call(f32[4,8,16,128]{3,2,1,0:T(8,128)S(1)} %collective-permut, ...), custom_call_target="tpu_custom_call" | custom-call | flops 22528000 | bytes 9011200 | tf_op jit(solution)/shard_map/pallas_call | solution.py:672
  36.6 22.6 %all_to_all.20 = f32[24,6,2,128]{3,2,1,0:T(2,128)S(1)} all-to-all(f32[24,6,2,128]{3,2,1,0:T(2,128)S(1)} %get-tuple-element.44), channel_id=1, replica_groups={{0,1,64,65,128,129,192,193,256,257,320,321,384,385,448,449,512,513,576,..., dimensions={0} | all-to-all | bytes 294912 | tf_op jit(solution)/shard_map/all_to_all | solution.py:722
  59.3 3.1 %collective-permute-start.4 = (f32[12,6,2,128]{3,2,1,0:T(2,128)S(1)}, f32[12,6,2,128]{3,2,1,0:T(2,128)S(1)}, u32[]{:S(2)}, u32[]{:S(2)}) collective-permute-start(f32[12,6,2,128]{3,2,1,0:T(2,128)S(1)} %get-tuple-element.45), channel_id=1, source_target_pairs={{0,2},{1,3},{4,6},{5,7},{8,10},{9,11},{12,14},{13,15},{16,18},{17,... | collective-permute-start | bytes 221192 | tf_op jit(solution)/shard_map/ppermute | solution.py:692
  63.1 1.3 collective-permute-done.4.first
  64.4 3.5 %shard_map.89 = (f32[24,16,128]{2,1,0:T(8,128)S(1)}, f32[24,16,128]{2,1,0:T(8,128)S(1)}, f32[24,16,128]{2,1,0:T(8,128)S(1)}, f32[24,16,128]{2,1,0:T(8,128)S(1)},...) custom-call(f32[12,6,2,128]{3,2,1,0:T(2,128)S(1)} %collective-permut, ...), custom_call_target="tpu_custom_call" | custom-call | flops 11386880 | bytes 4554752 | tf_op jit(solution)/shard_map/pallas_call | solution.py:672
  67.9 29.7 %all_to_all.21 = f32[64,5,1,128]{3,2,1,0:T(1,128)S(1)} all-to-all(f32[64,5,1,128]{3,2,1,0:T(1,128)S(1)} %get-tuple-element.47), channel_id=1, replica_groups=mesh['tile'=12,'group'=64] {'group'}, dimensions={0} | all-to-all | bytes 327680 | tf_op jit(solution)/shard_map/all_to_all | solution.py:713
  97.6 1.5 shard_map.90
  99.8 4.1 %collective-permute-start.6 = (f32[8,16,128]{2,1,0:T(8,128)S(1)}, f32[8,16,128]{2,1,0:T(8,128)S(1)}, u32[]{:S(2)}, u32[]{:S(2)}) collective-permute-start(f32[8,16,128]{2,1,0:T(8,128)S(1)} %get-tuple-element.68.own), channel_id=1, source_target_pairs={{0,64},{128,192},{256,320},{384,448},{512,576},{640,704},{64,0},{1... | collective-permute-start | bytes 196616 | tf_op jit(solution)/shard_map/ppermute | solution.py:692
  103.9 1.6 collective-permute-done.6.xfirst
  105.6 3.5 %collective-permute-start.8 = (f32[24,8,128]{2,1,0:T(8,128)S(1)}, f32[24,8,128]{2,1,0:T(8,128)S(1)}, u32[]{:S(2)}, u32[]{:S(2)}) collective-permute-start(f32[24,8,128]{2,1,0:T(8,128)S(1)} %pad_maximum_fusion.2), channel_id=1, source_target_pairs={{0,1},{2,3},{4,5},{6,7},{8,9},{10,11},{12,13},{14,15},{16,17},{18,... | collective-permute-start | bytes 294920 | tf_op jit(solution)/shard_map/ppermute | solution.py:692
  109.1 1.9 %collective-permute-start.9 = (f32[24,8,128]{2,1,0:T(8,128)S(1)}, f32[24,8,128]{2,1,0:T(8,128)S(1)}, u32[]{:S(2)}, u32[]{:S(2)}) collective-permute-start(f32[24,8,128]{2,1,0:T(8,128)S(1)} %pad_maximum_fusion.3), channel_id=1, source_target_pairs={{1,2},{3,4},{5,6},{7,8},{9,10},{11,12},{13,14},{15,16},{17,18},{19... | collective-permute-start | bytes 294920 | tf_op jit(solution)/shard_map/ppermute | solution.py:692
  111.0 4.0 %collective-permute-done.9.ysecond = f32[24,8,128]{2,1,0:T(8,128)S(1)} collective-permute-done((f32[24,8,128]{2,1,0:T(8,128)S(1)}, f32[24,8,128]{2,1,0:T(8,128)S(1)}, u32[]{:S(2)}, u32[]{:S(2)}) %collective-permute-start.9) | collective-permute-done | bytes 98336 | tf_op jit(solution)/shard_map/ppermute | solution.py:692
  115.0 2.3 %shard_map.91 = (f32[26,32,128]{2,1,0:T(8,128)S(1)}, f32[26,32,128]{2,1,0:T(8,128)S(1)}, f32[26,32,128]{2,1,0:T(8,128)S(1)}, f32[12,32,128]{2,1,0:T(8,128)S(1)},...) custom-call(f32[8,16,128]{2,1,0:T(8,128)S(1)} %collective-permute-done.6.xfirst, ...), custom_call_target="tpu_custom_call" | custom-call | flops 8555520 | bytes 3422208 | tf_op jit(solution)/shard_map/pallas_call | solution.py:672
  117.3 14.8 %all_to_all.22 = f32[12,3,2,128]{3,2,1,0:T(2,128)S(1)} all-to-all(f32[12,3,2,128]{3,2,1,0:T(2,128)S(1)} %get-tuple-element.75), channel_id=1, replica_groups=mesh['tile'=12,'group'=64] {'tile'}, dimensions={0} | all-to-all | bytes 73728 | tf_op jit(solution)/shard_map/all_to_all | solution.py:713
  132.1 3.4 %collective-permute-start.11 = (f32[13,3,2,128]{3,2,1,0:T(2,128)S(1)}, f32[13,3,2,128]{3,2,1,0:T(2,128)S(1)}, u32[]{:S(2)}, u32[]{:S(2)}) collective-permute-start(f32[13,3,2,128]{3,2,1,0:T(2,128)S(1)} %constant_dynamic-update-slice_fusion.own), channel_id=1, source_target_pairs={{1,2},{3,4},{5,6},{7,8},{9,10},{11,12},{13,14},{15,16},{17,18},{19... | collective-permute-start | bytes 119816 | tf_op jit(solution)/shard_map/ppermute | solution.py:692
  135.4 1.9 %collective-permute-start.10 = (f32[13,3,2,128]{3,2,1,0:T(2,128)S(1)}, f32[13,3,2,128]{3,2,1,0:T(2,128)S(1)}, u32[]{:S(2)}, u32[]{:S(2)}) collective-permute-start(f32[13,3,2,128]{3,2,1,0:T(2,128)S(1)} %constant_dynamic-update-slice_fusion.own), channel_id=1, source_target_pairs={{0,1},{2,3},{4,5},{6,7},{8,9},{10,11},{12,13},{14,15},{16,17},{18,... | collective-permute-start | bytes 119816 | tf_op jit(solution)/shard_map/ppermute | solution.py:692
  139.4 20.3 %all_to_all.23 = f32[64,3,1,128]{3,2,1,0:T(1,128)S(1)} all-to-all(f32[64,3,1,128]{3,2,1,0:T(1,128)S(1)} %get-tuple-element.77), channel_id=1, replica_groups=mesh['tile'=12,'group'=64] {'group'}, dimensions={0} | all-to-all | bytes 196608 | tf_op jit(solution)/shard_map/all_to_all | solution.py:713
  159.7 2.5 %shard_map.93 = (f32[8,16,128]{2,1,0:T(8,128)}, f32[8,16,128]{2,1,0:T(8,128)}) custom-call(f32[192,128]{1,0:T(8,128)S(1)} %bitcast.6, f32[12,1,128]{2,1,0:T(1,128)S(1)} %get-tuple-element.78.below_ref, f32[12,24,128]{2,1,0:T(8,128)S(1)} %get-tuple-element.48.s3_ref, f32[12,24,128]{2,1,0:T(8,128)S(1)} %get-tuple-element.49.di3_ref, ...), custom_call_target="tpu_custom_call" | custom-call | flops 655360 | bytes 262144 | tf_op jit(solution)/shard_map/pallas_call | solution.py:672
  (26 shorter events, 5.3 us)
Async XLA Ops:
  2.7 9.9 %collective-permute-start.1 = (f32[4,8,16,128]{3,2,1,0:T(8,128)}, f32[4,8,16,128]{3,2,1,0:T(8,128)S(1)}, u32[]{:S(2)}, u32[]{:S(2)}) collective-permute-start(f32[4,8,16,128]{3,2,1,0:T(8,128)} %shard_map.86.own), channel_id=1, source_target_pairs={{64,128},{192,256},{320,384},{448,512},{576,640},{128,64},{256,192... | collective-permute-start | bytes 786440 | tf_op jit(solution)/shard_map/ppermute | solution.py:692
  3.4 12.1 %collective-permute-start = (f32[4,8,16,128]{3,2,1,0:T(8,128)}, f32[4,8,16,128]{3,2,1,0:T(8,128)S(1)}, u32[]{:S(2)}, u32[]{:S(2)}) collective-permute-start(f32[4,8,16,128]{3,2,1,0:T(8,128)} %shard_map.86.own), channel_id=1, source_target_pairs={{0,64},{128,192},{256,320},{384,448},{512,576},{640,704},{64,0},{1... | collective-permute-start | bytes 786440 | tf_op jit(solution)/shard_map/ppermute | solution.py:692
  15.6 10.9 %collective-permute-start.2 = (f32[4,24,8,128]{3,2,1,0:T(8,128)S(1)}, f32[4,24,8,128]{3,2,1,0:T(8,128)S(1)}, u32[]{:S(2)}, u32[]{:S(2)}) collective-permute-start(f32[4,24,8,128]{3,2,1,0:T(8,128)S(1)} %pad_maximum_fusion), channel_id=1, source_target_pairs={{0,1},{2,3},{4,5},{6,7},{8,9},{10,11},{12,13},{14,15},{16,17},{18,... | collective-permute-start | bytes 1179656 | tf_op jit(solution)/shard_map/ppermute | solution.py:692
  24.4 9.3 %copy-start = (f32[4,8,16,128]{3,2,1,0:T(8,128)S(1)}, f32[4,8,16,128]{3,2,1,0:T(8,128)}, u32[]{:S(2)}) copy-start(f32[4,8,16,128]{3,2,1,0:T(8,128)} %shard_map.86.own) | copy-start | bytes 786436
  24.4 9.2 %collective-permute-start.3 = (f32[4,24,8,128]{3,2,1,0:T(8,128)S(1)}, f32[4,24,8,128]{3,2,1,0:T(8,128)S(1)}, u32[]{:S(2)}, u32[]{:S(2)}) collective-permute-start(f32[4,24,8,128]{3,2,1,0:T(8,128)S(1)} %pad_maximum_fusion.1), channel_id=1, source_target_pairs={{1,2},{3,4},{5,6},{7,8},{9,10},{11,12},{13,14},{15,16},{17,18},{19... | collective-permute-start | bytes 1179656 | tf_op jit(solution)/shard_map/ppermute | solution.py:692
  59.3 5.1 %collective-permute-start.4 = (f32[12,6,2,128]{3,2,1,0:T(2,128)S(1)}, f32[12,6,2,128]{3,2,1,0:T(2,128)S(1)}, u32[]{:S(2)}, u32[]{:S(2)}) collective-permute-start(f32[12,6,2,128]{3,2,1,0:T(2,128)S(1)} %get-tuple-element.45), channel_id=1, source_target_pairs={{0,2},{1,3},{4,6},{5,7},{8,10},{9,11},{12,14},{13,15},{16,18},{17,... | collective-permute-start | bytes 221192 | tf_op jit(solution)/shard_map/ppermute | solution.py:692
  62.5 2.0 %collective-permute-start.5 = (f32[12,6,2,128]{3,2,1,0:T(2,128)S(1)}, f32[12,6,2,128]{3,2,1,0:T(2,128)S(1)}, u32[]{:S(2)}, u32[]{:S(2)}) collective-permute-start(f32[12,6,2,128]{3,2,1,0:T(2,128)S(1)} %get-tuple-element.46), channel_id=1, source_target_pairs={{2,4},{3,5},{6,8},{7,9},{10,12},{11,13},{14,16},{15,17},{18,20},{1... | collective-permute-start | bytes 221192 | tf_op jit(solution)/shard_map/ppermute | solution.py:692
  99.1 4.8 %collective-permute-start.7 = (f32[8,16,128]{2,1,0:T(8,128)S(1)}, f32[8,16,128]{2,1,0:T(8,128)S(1)}, u32[]{:S(2)}, u32[]{:S(2)}) collective-permute-start(f32[8,16,128]{2,1,0:T(8,128)S(1)} %get-tuple-element.68.own), channel_id=1, source_target_pairs={{64,128},{192,256},{320,384},{448,512},{576,640},{128,64},{256,192... | collective-permute-start | bytes 196616 | tf_op jit(solution)/shard_map/ppermute | solution.py:692
  99.8 5.7 %collective-permute-start.6 = (f32[8,16,128]{2,1,0:T(8,128)S(1)}, f32[8,16,128]{2,1,0:T(8,128)S(1)}, u32[]{:S(2)}, u32[]{:S(2)}) collective-permute-start(f32[8,16,128]{2,1,0:T(8,128)S(1)} %get-tuple-element.68.own), channel_id=1, source_target_pairs={{0,64},{128,192},{256,320},{384,448},{512,576},{640,704},{64,0},{1... | collective-permute-start | bytes 196616 | tf_op jit(solution)/shard_map/ppermute | solution.py:692
  105.6 5.4 %collective-permute-start.8 = (f32[24,8,128]{2,1,0:T(8,128)S(1)}, f32[24,8,128]{2,1,0:T(8,128)S(1)}, u32[]{:S(2)}, u32[]{:S(2)}) collective-permute-start(f32[24,8,128]{2,1,0:T(8,128)S(1)} %pad_maximum_fusion.2), channel_id=1, source_target_pairs={{0,1},{2,3},{4,5},{6,7},{8,9},{10,11},{12,13},{14,15},{16,17},{18,... | collective-permute-start | bytes 294920 | tf_op jit(solution)/shard_map/ppermute | solution.py:692
  109.1 5.9 %collective-permute-start.9 = (f32[24,8,128]{2,1,0:T(8,128)S(1)}, f32[24,8,128]{2,1,0:T(8,128)S(1)}, u32[]{:S(2)}, u32[]{:S(2)}) collective-permute-start(f32[24,8,128]{2,1,0:T(8,128)S(1)} %pad_maximum_fusion.3), channel_id=1, source_target_pairs={{1,2},{3,4},{5,6},{7,8},{9,10},{11,12},{13,14},{15,16},{17,18},{19... | collective-permute-start | bytes 294920 | tf_op jit(solution)/shard_map/ppermute | solution.py:692
  132.1 5.3 %collective-permute-start.11 = (f32[13,3,2,128]{3,2,1,0:T(2,128)S(1)}, f32[13,3,2,128]{3,2,1,0:T(2,128)S(1)}, u32[]{:S(2)}, u32[]{:S(2)}) collective-permute-start(f32[13,3,2,128]{3,2,1,0:T(2,128)S(1)} %constant_dynamic-update-slice_fusion.own), channel_id=1, source_target_pairs={{1,2},{3,4},{5,6},{7,8},{9,10},{11,12},{13,14},{15,16},{17,18},{19... | collective-permute-start | bytes 119816 | tf_op jit(solution)/shard_map/ppermute | solution.py:692
  135.4 3.1 %collective-permute-start.10 = (f32[13,3,2,128]{3,2,1,0:T(2,128)S(1)}, f32[13,3,2,128]{3,2,1,0:T(2,128)S(1)}, u32[]{:S(2)}, u32[]{:S(2)}) collective-permute-start(f32[13,3,2,128]{3,2,1,0:T(2,128)S(1)} %constant_dynamic-update-slice_fusion.own), channel_id=1, source_target_pairs={{0,1},{2,3},{4,5},{6,7},{8,9},{10,11},{12,13},{14,15},{16,17},{18,... | collective-permute-start | bytes 119816 | tf_op jit(solution)/shard_map/ppermute | solution.py:692

commit v8 on v7

--- a/solution.py
+++ b/solution.py
@@ -224,19 +224,19 @@
     lax.fori_loop(0, BX, cells, 0, unroll=2)
 
 
-def is_even(axis, step=1):
-    return (lax.axis_index(axis) // step) % 2 == 0
-
-
-def sides(first, second, axis, step=1):
-    even = is_even(axis, step)
+def is_even(axis, step=1, lead=0):
+    return (lax.axis_index(axis) // step) % 2 == lead
+
+
+def sides(first, second, axis, lead=0):
+    even = is_even(axis, 1, lead)
     return jnp.where(even, second, first), jnp.where(even, first, second)
 
 
 def fill_window(ref, xfirst, own, xsecond, yfirst, ysecond):
     ref[1 : 1 + BX, 8:24, :], ref[1 + 2 * BX : 1 + 3 * BX, 8:24, :] = sides(xfirst, xsecond, "tile")
     ref[1 + BX : 1 + 2 * BX, 8:24, :] = own
-    ylow, yhigh = sides(yfirst, ysecond, "group")
+    ylow, yhigh = sides(yfirst, ysecond, "group", 1)
     for y, part in ((0, ylow), (24, yhigh)):
         low, high = sides(part[:BX], part[2 * BX :], "tile")
         ref[1 : 1 + BX, y : y + 8, :] = low
@@ -365,21 +365,21 @@
     return lambda field, half: jnp.where(which, one(field, half), two(field, half))
 
 
-def both_sides(first, second, step):
-    even = is_even("group", step)
+def both_sides(first, second, step, lead):
+    even = is_even("group", step, lead)
     one, two = message_rows(first), message_rows(second)
     return choose(even, two, one), choose(even, one, two)
 
 
 def pair_rows(here, first, second):
-    before, after = both_sides(first, second, 2)
+    before, after = both_sides(first, second, 2, 1)
     even = is_even("group")
     one, two = message_rows(here.at[:, 0]), message_rows(here.at[:, 1])
     return choose(even, before, one), choose(even, one, two), choose(even, two, after)
 
 
 def band_rows3(here, first, second):
-    before, after = both_sides(first, second, 2)
+    before, after = both_sides(first, second, 2, 1)
     even = is_even("group")
     six = [before(5, half) for half in range(2)]
     six += [here[:, core, 5, 0:1, :] for core in range(2)]
@@ -416,15 +416,16 @@
 
 
 def pack_sums3(v):
-    v = v + turn(v, -2, 1)
-    sub, lane = iota((16, NZ), 0), iota((16, NZ), 1)
-    rows = []
-    for first in range(0, v.shape[0], 8):
-        total = jnp.zeros((16, NZ), F32)
-        for q in range(min(8, v.shape[0] - first)):
-            total = total + jnp.where((sub == 4) & (lane % 8 == q), v[first + q], 0.0)
-        rows.append(jnp.sum(total, axis=0, keepdims=True))
-    return rows
+    even = is_even("group")
+    tiles = v.shape[0]
+    start = jnp.where(even, 8, 4)
+    sub, lane = iota((24, NZ), 0), iota((24, NZ), 1)
+    once = (sub >= start) & (sub < start + 8) & (sub % 2 == 0)
+    total = jnp.zeros((24, NZ), F32)
+    for q in range(tiles // 2):
+        part = jnp.where(even, v[q], v[tiles // 2 + q])
+        total = total + jnp.where(once & (lane % 8 == q), part, 0.0)
+    return [jnp.sum(total, axis=0, keepdims=True)]
 
 
 def descend_third(r2, s2, wx2, wy2, wz2, di2):
@@ -434,7 +435,7 @@
 
 
 def sides_kernel(here, first_ref, second_ref):
-    even = is_even("group", 2)
+    even = is_even("group", 2, 1)
     low, high = here[:, 0, 0:5], here[:, 1, 0:5]
     first_ref[:, 0:5] = jnp.where(even, high, low)
     second_ref[:, 0:5] = jnp.where(even, low, high)
@@ -452,6 +453,7 @@
     s3, wx3, wy3, wz3 = unpack_bands3(band_rows3(here, first, second))
     s3_ref[...], wx3_ref[...], wy3_ref[...], wz3_ref[...] = s3, wx3, wy3, wz3
     di3_ref[...] = relax_factor(s3, wx3, wy3, wz3, 2, 8)
+    inner = s3 + wx3 + x_high(wx3) + wz3 + turn(wz3, -8, 2)
     low, own, high = pair_rows(here, first, second)
     r2, s2, wx2, wy2, wz2 = (unpack_level2(f, own, low, high) for f in range(5))
     di2 = relax_factor(s2, wx2, wy2, wz2, 1, 4)
@@ -459,15 +461,13 @@
     wx2_ref[...], wy2_ref[...], wz2_ref[...] = wx2, wy2, wz2
     e22, r3 = descend_third(r2, s2, wx2, wy2, wz2, di2)
     e22_ref[...] = e22
-    s3, wx3, _, wz3 = coarsen(s2, wx2, wy2, wz2, 1, 4)
-    inner = s3 + wx3 + x_high(wx3) + wz3 + turn(wz3, -8, 2)
     send(msg_ref, pack_level3(r3) + pack_sums3(inner))
 
 
 def third_again_kernel(
     own, first, second, s2_ref, di2_ref, wx2_ref, wy2_ref, wz2_ref, r2_ref, e22_ref, msg_ref
 ):
-    r2 = unpack_level2(0, message_rows(own), *both_sides(first, second, 1))
+    r2 = unpack_level2(0, message_rows(own), *both_sides(first, second, 1, 0))
     r2_ref[...] = r2
     e22, r3 = descend_third(
         r2, s2_ref[...], wx2_ref[...], wy2_ref[...], wz2_ref[...], di2_ref[...]
@@ -513,7 +513,7 @@
     lane = iota(total.shape, 2) % 8
     parts = [jnp.where(lane * held // 8 == q, total, 0.0) for q in range(held)]
     wide = jnp.stack(parts, axis=1).reshape((held * v.shape[0], 1, NZ))
-    return octuple(wide[: lax.axis_size("tile")])
+    return octuple(wide)
 
 
 def solve_third(r3, line, s3, di3, wx3, wy3, wz3):
@@ -574,7 +574,12 @@
     *, groups, thirds, rows,
 ):
     r3 = strided(third_ref, 0, thirds, groups, rows)
-    below = line_sums(strided(third_ref, thirds, rows - thirds, groups, rows), 8)
+    tiles = lax.axis_size("tile")
+    sums = strided(third_ref, thirds, 1, groups, rows)
+    odd = iota(sums.shape, 1) % 2
+    below = jnp.concatenate(
+        [line_sums(jnp.where(odd == half, sums, 0.0), 8)[: tiles // 2] for half in range(2)], axis=0
+    )
     below_ref[...] = below
     corr3 = solve_third(
         unpack_r3(r3), line_sums(r3, 4) / below,
@@ -682,7 +687,7 @@
     )(*operands)
 
 
-def swaps(to_first, to_second, axis, step=1):
+def swaps(to_first, to_second, axis, step=1, lead=0):
     count = lax.axis_size(axis)
 
     def swap(cells, odd):
@@ -691,13 +696,13 @@
         ]
         return lax.ppermute(cells, axis, ups + [(j, i) for i, j in ups])
 
-    return swap(to_first, 0), swap(to_second, 1)
+    return swap(to_first, lead), swap(to_second, 1 - lead)
 
 
 def surround(cells, dim):
     first, second = swaps(cells, cells, "tile")
     ydim = dim + 1
-    even = is_even("group")
+    even = is_even("group", 1, 1)
 
     def halves(v):
         low = lax.slice_in_dim(v, 0, 8, axis=ydim)
@@ -706,7 +711,7 @@
 
     parts = [halves(v) for v in (first, cells, second)]
     to_first, to_second = (jnp.concatenate(list(v), axis=dim) for v in zip(*parts, strict=True))
-    return first, cells, second, *swaps(to_first, to_second, "group")
+    return first, cells, second, *swaps(to_first, to_second, "group", 1, 1)
 
 
 def everyone(blocks, axis):
@@ -730,7 +735,7 @@
     thirds = tiles // 4
     top, one, two = (PX, WY, NZ), (L1X, WY, NZ), (2 * tiles, 16, NZ)
     three, line = (tiles, 24, NZ), (tiles, 1, NZ)
-    rows_once, rows_again = thirds + -(-tiles // 8), thirds
+    rows_once, rows_again = thirds + 1, thirds
 
     fields = pl.pallas_call(
         soil_kernel,
@@ -757,7 +762,7 @@
 
     here = pairs_of_tiles(msg)
     to_first, to_second = call(sides_kernel, [(tiles, 6, 2, NZ)] * 2, [here])
-    first, second = swaps(to_first, to_second, "group", 2)
+    first, second = swaps(to_first, to_second, "group", 2, 1)
     r2, s2, di2, wx2, wy2, wz2, e22, *bands3, msg = call(
         third_kernel,
         [two] * 7 + [three] * 5 + [(groups, rows_once, 1, NZ)],

time: 163 us -> 157 us (0.963)
  waiting for transfers between devices: 18.2 us -> 11 us
  starting transfers between devices: 38.8 us -> 41.2 us
    ppermute x12, waiting for transfers between devices: 18.2 us -> 11 us  [swap(): return lax.ppermute(cells, axis, ups + [(j, i) for i, j in ups])]
    all_to_all x3, blocking collectives: 64.8 us -> 60.7 us  [everyone(): return lax.all_to_all(blocks, axis, 0, 0, tiled=True)]
    all_to_all x1, blocking collectives: 22.6 us -> 26 us  [pairs_of_tiles(): lax.all_to_all(block, ('tile', 'group'), 0, 0, axis_index_groups=members,...]
    ppermute x12, starting transfers between devices: 38.8 us -> 41.2 us  [swap(): return lax.ppermute(cells, axis, ups + [(j, i) for i, j in ups])]
  transfers between devices with their start and end apart: 12 -> 12, of which waited for: 6 -> 7; matrix products, arithmetic and copies ran while one was open for 1% -> 1% of each run, Pallas kernels for 0% -> 0%
where the time goes in v8:
time: 157 us
  blocking collectives  86.7 us (55%)
  starting transfers between devices  41.2 us (26%)
  Pallas kernels  15.6 us (10%)
  waiting for transfers between devices  11 us (7%)
    all_to_all x3, blocking collectives, everyone(): return lax.all_to_all(blocks, axis, 0, 0, tiled=True)  60.7 us
    ppermute x12, starting transfers between devices, swap(): return lax.ppermute(cells, axis, ups + [(j, i) for i, j in ups])  41.2 us
    all_to_all x1, blocking collectives, pairs_of_tiles(): lax.all_to_all(block, ('tile', 'group'), 0, 0, axis_index_groups=members,...  26 us
    pallas_call x7, Pallas kernels, call(): pl.pallas_call(body, out_shape=[jax.ShapeDtypeStruct(shape, F32) for shap...  13.5 us
    ppermute x12, waiting for transfers between devices, swap(): return lax.ppermute(cells, axis, ups + [(j, i) for i, j in ups])  11 us
  transfers between devices with their start and end apart: 12, of which 7 were waited for; matrix products, arithmetic and copies ran while one was open for 1% of the time, Pallas kernels for 0%

profile of v8, /device:TPU:1, one launch (start us, length us, event | category | flops | bytes accessed | tf_op | source)
XLA Modules:
  0.0 156.6 jit_solution(6309739573980599745)
XLA Ops:
  0.6 2.1 %shard_map.86.own = f32[4,8,16,128]{3,2,1,0:T(8,128)} custom-call(f32[8,16,128]{2,1,0:T(8,128)} %head_in.1, f32[8,16,128]{2,1,0:T(8,128)} %old_in.1, s32[8,16,128]{2,1,0:T(8,128)} %soil_in.1, f32[12]{0:T(128)} %ks_in.1, f32[12]{0:T(128)} %alpha_in.1, f32[12]{0:T(128)} %shape_in.1, f32[12]{0:T(128)} %span_in.1), custom_call_target="tpu_custom_call" | custom-call | tf_op jit(solution)/shard_map/pallas_call | solution.py:740
  3.4 8.2 %collective-permute-start = (f32[4,8,16,128]{3,2,1,0:T(8,128)}, f32[4,8,16,128]{3,2,1,0:T(8,128)S(1)}, u32[]{:S(2)}, u32[]{:S(2)}) collective-permute-start(f32[4,8,16,128]{3,2,1,0:T(8,128)} %shard_map.86.own), channel_id=1, source_target_pairs={{0,64},{128,192},{256,320},{384,448},{512,576},{640,704},{64,0},{1... | collective-permute-start | bytes 786440 | tf_op jit(solution)/shard_map/ppermute | solution.py:697
  12.6 2.9 %collective-permute-done.xfirst = f32[4,8,16,128]{3,2,1,0:T(8,128)S(1)} collective-permute-done((f32[4,8,16,128]{3,2,1,0:T(8,128)}, f32[4,8,16,128]{3,2,1,0:T(8,128)S(1)}, u32[]{:S(2)}, u32[]{:S(2)}) %collective-permute-start) | collective-permute-done | bytes 262176 | tf_op jit(solution)/shard_map/ppermute | solution.py:697
  15.6 6.5 %collective-permute-start.2 = (f32[4,24,8,128]{3,2,1,0:T(8,128)S(1)}, f32[4,24,8,128]{3,2,1,0:T(8,128)S(1)}, u32[]{:S(2)}, u32[]{:S(2)}) collective-permute-start(f32[4,24,8,128]{3,2,1,0:T(8,128)S(1)} %pad_maximum_fusion), channel_id=1, source_target_pairs={{1,2},{3,4},{5,6},{7,8},{9,10},{11,12},{13,14},{15,16},{17,18},{19... | collective-permute-start | bytes 1179656 | tf_op jit(solution)/shard_map/ppermute | solution.py:697
  22.1 3.1 %collective-permute-start.3 = (f32[4,24,8,128]{3,2,1,0:T(8,128)S(1)}, f32[4,24,8,128]{3,2,1,0:T(8,128)S(1)}, u32[]{:S(2)}, u32[]{:S(2)}) collective-permute-start(f32[4,24,8,128]{3,2,1,0:T(8,128)S(1)} %pad_maximum_fusion.1), channel_id=1, source_target_pairs={{0,1},{2,3},{4,5},{6,7},{8,9},{10,11},{12,13},{14,15},{16,17},{18,... | collective-permute-start | bytes 1179656 | tf_op jit(solution)/shard_map/ppermute | solution.py:697
  25.3 2.3 %collective-permute-done.2.yfirst = f32[4,24,8,128]{3,2,1,0:T(8,128)S(1)} collective-permute-done((f32[4,24,8,128]{3,2,1,0:T(8,128)S(1)}, f32[4,24,8,128]{3,2,1,0:T(8,128)S(1)}, u32[]{:S(2)}, u32[]{:S(2)}) %collective-permute-start.2) | collective-permute-done | bytes 393248 | tf_op jit(solution)/shard_map/ppermute | solution.py:697
  27.6 3.0 %shard_map.87 = (f32[26,32,128]{2,1,0:T(8,128)S(1)}, f32[26,32,128]{2,1,0:T(8,128)S(1)}, f32[26,32,128]{2,1,0:T(8,128)S(1)}, f32[26,32,128]{2,1,0:T(8,128)S(1)},...) custom-call(f32[4,8,16,128]{3,2,1,0:T(8,128)S(1)} %collective-permut, ...), custom_call_target="tpu_custom_call" | custom-call | flops 22528000 | bytes 9011200 | tf_op jit(solution)/shard_map/pallas_call | solution.py:677
  30.5 26.0 %all_to_all.20 = f32[24,6,2,128]{3,2,1,0:T(2,128)S(1)} all-to-all(f32[24,6,2,128]{3,2,1,0:T(2,128)S(1)} %get-tuple-element.44), channel_id=1, replica_groups={{0,1,64,65,128,129,192,193,256,257,320,321,384,385,448,449,512,513,576,..., dimensions={0} | all-to-all | bytes 294912 | tf_op jit(solution)/shard_map/all_to_all | solution.py:727
  57.3 6.1 %collective-permute-start.5 = (f32[12,6,2,128]{3,2,1,0:T(2,128)S(1)}, f32[12,6,2,128]{3,2,1,0:T(2,128)S(1)}, u32[]{:S(2)}, u32[]{:S(2)}) collective-permute-start(f32[12,6,2,128]{3,2,1,0:T(2,128)S(1)} %get-tuple-element.46), channel_id=1, source_target_pairs={{0,2},{1,3},{4,6},{5,7},{8,10},{9,11},{12,14},{13,15},{16,18},{17,... | collective-permute-start | bytes 221192 | tf_op jit(solution)/shard_map/ppermute | solution.py:697
  63.4 1.7 %collective-permute-done.5.second = f32[12,6,2,128]{3,2,1,0:T(2,128)S(1)} collective-permute-done((f32[12,6,2,128]{3,2,1,0:T(2,128)S(1)}, f32[12,6,2,128]{3,2,1,0:T(2,128)S(1)}, u32[]{:S(2)}, u32[]{:S(2)}) %collective-permute-start.5) | collective-permute-done | bytes 73760 | tf_op jit(solution)/shard_map/ppermute | solution.py:697
  65.1 3.3 %shard_map.89 = (f32[24,16,128]{2,1,0:T(8,128)S(1)}, f32[24,16,128]{2,1,0:T(8,128)S(1)}, f32[24,16,128]{2,1,0:T(8,128)S(1)}, f32[24,16,128]{2,1,0:T(8,128)S(1)},...) custom-call(f32[12,6,2,128]{3,2,1,0:T(2,128)S(1)} %collective-permut, ...), custom_call_target="tpu_custom_call" | custom-call | flops 11223040 | bytes 4489216 | tf_op jit(solution)/shard_map/pallas_call | solution.py:677
  68.4 25.6 %all_to_all.21 = f32[64,4,1,128]{3,2,1,0:T(1,128)S(1)} all-to-all(f32[64,4,1,128]{3,2,1,0:T(1,128)S(1)} %get-tuple-element.47), channel_id=1, replica_groups=mesh['tile'=12,'group'=64] {'group'}, dimensions={0} | all-to-all | bytes 262144 | tf_op jit(solution)/shard_map/all_to_all | solution.py:718
  94.0 1.5 shard_map.90
  96.2 3.8 %collective-permute-start.6 = (f32[8,16,128]{2,1,0:T(8,128)S(1)}, f32[8,16,128]{2,1,0:T(8,128)S(1)}, u32[]{:S(2)}, u32[]{:S(2)}) collective-permute-start(f32[8,16,128]{2,1,0:T(8,128)S(1)} %get-tuple-element.68.own), channel_id=1, source_target_pairs={{0,64},{128,192},{256,320},{384,448},{512,576},{640,704},{64,0},{1... | collective-permute-start | bytes 196616 | tf_op jit(solution)/shard_map/ppermute | solution.py:697
  100.1 1.6 %collective-permute-done.6.xfirst = f32[8,16,128]{2,1,0:T(8,128)S(1)} collective-permute-done((f32[8,16,128]{2,1,0:T(8,128)S(1)}, f32[8,16,128]{2,1,0:T(8,128)S(1)}, u32[]{:S(2)}, u32[]{:S(2)}) %collective-permute-start.6) | collective-permute-done | bytes 65568 | tf_op jit(solution)/shard_map/ppermute | solution.py:697
  101.7 3.5 %collective-permute-start.8 = (f32[24,8,128]{2,1,0:T(8,128)S(1)}, f32[24,8,128]{2,1,0:T(8,128)S(1)}, u32[]{:S(2)}, u32[]{:S(2)}) collective-permute-start(f32[24,8,128]{2,1,0:T(8,128)S(1)} %pad_maximum_fusion.2), channel_id=1, source_target_pairs={{1,2},{3,4},{5,6},{7,8},{9,10},{11,12},{13,14},{15,16},{17,18},{19... | collective-permute-start | bytes 294920 | tf_op jit(solution)/shard_map/ppermute | solution.py:697
  105.3 1.9 %collective-permute-start.9 = (f32[24,8,128]{2,1,0:T(8,128)S(1)}, f32[24,8,128]{2,1,0:T(8,128)S(1)}, u32[]{:S(2)}, u32[]{:S(2)}) collective-permute-start(f32[24,8,128]{2,1,0:T(8,128)S(1)} %pad_maximum_fusion.3), channel_id=1, source_target_pairs={{0,1},{2,3},{4,5},{6,7},{8,9},{10,11},{12,13},{14,15},{16,17},{18,... | collective-permute-start | bytes 294920 | tf_op jit(solution)/shard_map/ppermute | solution.py:697
  108.5 2.3 %shard_map.91 = (f32[26,32,128]{2,1,0:T(8,128)S(1)}, f32[26,32,128]{2,1,0:T(8,128)S(1)}, f32[26,32,128]{2,1,0:T(8,128)S(1)}, f32[12,32,128]{2,1,0:T(8,128)S(1)},...) custom-call(f32[8,16,128]{2,1,0:T(8,128)S(1)} %collective-permute-done.6.xfirst, ...), custom_call_target="tpu_custom_call" | custom-call | flops 8555520 | bytes 3422208 | tf_op jit(solution)/shard_map/pallas_call | solution.py:677
  110.8 15.0 %all_to_all.22 = f32[12,3,2,128]{3,2,1,0:T(2,128)S(1)} all-to-all(f32[12,3,2,128]{3,2,1,0:T(2,128)S(1)} %get-tuple-element.75), channel_id=1, replica_groups=mesh['tile'=12,'group'=64] {'tile'}, dimensions={0} | all-to-all | bytes 73728 | tf_op jit(solution)/shard_map/all_to_all | solution.py:718
  125.8 4.2 %collective-permute-start.11 = (f32[13,3,2,128]{3,2,1,0:T(2,128)S(1)}, f32[13,3,2,128]{3,2,1,0:T(2,128)S(1)}, u32[]{:S(2)}, u32[]{:S(2)}) collective-permute-start(f32[13,3,2,128]{3,2,1,0:T(2,128)S(1)} %constant_dynamic-update-slice_fusion.own), channel_id=1, source_target_pairs={{1,2},{3,4},{5,6},{7,8},{9,10},{11,12},{13,14},{15,16},{17,18},{19... | collective-permute-start | bytes 119816 | tf_op jit(solution)/shard_map/ppermute | solution.py:697
  130.0 1.9 %collective-permute-start.10 = (f32[13,3,2,128]{3,2,1,0:T(2,128)S(1)}, f32[13,3,2,128]{3,2,1,0:T(2,128)S(1)}, u32[]{:S(2)}, u32[]{:S(2)}) collective-permute-start(f32[13,3,2,128]{3,2,1,0:T(2,128)S(1)} %constant_dynamic-update-slice_fusion.own), channel_id=1, source_target_pairs={{0,1},{2,3},{4,5},{6,7},{8,9},{10,11},{12,13},{14,15},{16,17},{18,... | collective-permute-start | bytes 119816 | tf_op jit(solution)/shard_map/ppermute | solution.py:697
  131.9 1.2 collective-permute-done.10.first
  133.9 20.2 %all_to_all.23 = f32[64,3,1,128]{3,2,1,0:T(1,128)S(1)} all-to-all(f32[64,3,1,128]{3,2,1,0:T(1,128)S(1)} %get-tuple-element.77), channel_id=1, replica_groups=mesh['tile'=12,'group'=64] {'group'}, dimensions={0} | all-to-all | bytes 196608 | tf_op jit(solution)/shard_map/all_to_all | solution.py:718
  154.1 2.5 %shard_map.93 = (f32[8,16,128]{2,1,0:T(8,128)}, f32[8,16,128]{2,1,0:T(8,128)}) custom-call(f32[192,128]{1,0:T(8,128)S(1)} %bitcast.6, f32[12,1,128]{2,1,0:T(1,128)S(1)} %get-tuple-element.78.below_ref, f32[12,24,128]{2,1,0:T(8,128)S(1)} %get-tuple-element.48.s3_ref, f32[12,24,128]{2,1,0:T(8,128)S(1)} %get-tuple-element.49.di3_ref, ...), custom_call_target="tpu_custom_call" | custom-call | flops 655360 | bytes 262144 | tf_op jit(solution)/shard_map/pallas_call | solution.py:677
  (26 shorter events, 5.3 us)
Async XLA Ops:
  2.7 9.9 %collective-permute-start.1 = (f32[4,8,16,128]{3,2,1,0:T(8,128)}, f32[4,8,16,128]{3,2,1,0:T(8,128)S(1)}, u32[]{:S(2)}, u32[]{:S(2)}) collective-permute-start(f32[4,8,16,128]{3,2,1,0:T(8,128)} %shard_map.86.own), channel_id=1, source_target_pairs={{64,128},{192,256},{320,384},{448,512},{576,640},{128,64},{256,192... | collective-permute-start | bytes 786440 | tf_op jit(solution)/shard_map/ppermute | solution.py:697
  3.4 12.1 %collective-permute-start = (f32[4,8,16,128]{3,2,1,0:T(8,128)}, f32[4,8,16,128]{3,2,1,0:T(8,128)S(1)}, u32[]{:S(2)}, u32[]{:S(2)}) collective-permute-start(f32[4,8,16,128]{3,2,1,0:T(8,128)} %shard_map.86.own), channel_id=1, source_target_pairs={{0,64},{128,192},{256,320},{384,448},{512,576},{640,704},{64,0},{1... | collective-permute-start | bytes 786440 | tf_op jit(solution)/shard_map/ppermute | solution.py:697
  15.6 12.0 %collective-permute-start.2 = (f32[4,24,8,128]{3,2,1,0:T(8,128)S(1)}, f32[4,24,8,128]{3,2,1,0:T(8,128)S(1)}, u32[]{:S(2)}, u32[]{:S(2)}) collective-permute-start(f32[4,24,8,128]{3,2,1,0:T(8,128)S(1)} %pad_maximum_fusion), channel_id=1, source_target_pairs={{1,2},{3,4},{5,6},{7,8},{9,10},{11,12},{13,14},{15,16},{17,18},{19... | collective-permute-start | bytes 1179656 | tf_op jit(solution)/shard_map/ppermute | solution.py:697
  22.1 5.5 %copy-start = (f32[4,8,16,128]{3,2,1,0:T(8,128)S(1)}, f32[4,8,16,128]{3,2,1,0:T(8,128)}, u32[]{:S(2)}) copy-start(f32[4,8,16,128]{3,2,1,0:T(8,128)} %shard_map.86.own) | copy-start | bytes 786436
  22.1 5.4 %collective-permute-start.3 = (f32[4,24,8,128]{3,2,1,0:T(8,128)S(1)}, f32[4,24,8,128]{3,2,1,0:T(8,128)S(1)}, u32[]{:S(2)}, u32[]{:S(2)}) collective-permute-start(f32[4,24,8,128]{3,2,1,0:T(8,128)S(1)} %pad_maximum_fusion.1), channel_id=1, source_target_pairs={{0,1},{2,3},{4,5},{6,7},{8,9},{10,11},{12,13},{14,15},{16,17},{18,... | collective-permute-start | bytes 1179656 | tf_op jit(solution)/shard_map/ppermute | solution.py:697
  56.6 6.8 %collective-permute-start.4 = (f32[12,6,2,128]{3,2,1,0:T(2,128)S(1)}, f32[12,6,2,128]{3,2,1,0:T(2,128)S(1)}, u32[]{:S(2)}, u32[]{:S(2)}) collective-permute-start(f32[12,6,2,128]{3,2,1,0:T(2,128)S(1)} %get-tuple-element.45), channel_id=1, source_target_pairs={{2,4},{3,5},{6,8},{7,9},{10,12},{11,13},{14,16},{15,17},{18,20},{1... | collective-permute-start | bytes 221192 | tf_op jit(solution)/shard_map/ppermute | solution.py:697
  57.3 7.8 %collective-permute-start.5 = (f32[12,6,2,128]{3,2,1,0:T(2,128)S(1)}, f32[12,6,2,128]{3,2,1,0:T(2,128)S(1)}, u32[]{:S(2)}, u32[]{:S(2)}) collective-permute-start(f32[12,6,2,128]{3,2,1,0:T(2,128)S(1)} %get-tuple-element.46), channel_id=1, source_target_pairs={{0,2},{1,3},{4,6},{5,7},{8,10},{9,11},{12,14},{13,15},{16,18},{17,... | collective-permute-start | bytes 221192 | tf_op jit(solution)/shard_map/ppermute | solution.py:697
  95.5 4.5 %collective-permute-start.7 = (f32[8,16,128]{2,1,0:T(8,128)S(1)}, f32[8,16,128]{2,1,0:T(8,128)S(1)}, u32[]{:S(2)}, u32[]{:S(2)}) collective-permute-start(f32[8,16,128]{2,1,0:T(8,128)S(1)} %get-tuple-element.68.own), channel_id=1, source_target_pairs={{64,128},{192,256},{320,384},{448,512},{576,640},{128,64},{256,192... | collective-permute-start | bytes 196616 | tf_op jit(solution)/shard_map/ppermute | solution.py:697
  96.2 5.5 %collective-permute-start.6 = (f32[8,16,128]{2,1,0:T(8,128)S(1)}, f32[8,16,128]{2,1,0:T(8,128)S(1)}, u32[]{:S(2)}, u32[]{:S(2)}) collective-permute-start(f32[8,16,128]{2,1,0:T(8,128)S(1)} %get-tuple-element.68.own), channel_id=1, source_target_pairs={{0,64},{128,192},{256,320},{384,448},{512,576},{640,704},{64,0},{1... | collective-permute-start | bytes 196616 | tf_op jit(solution)/shard_map/ppermute | solution.py:697
  101.7 5.9 %collective-permute-start.8 = (f32[24,8,128]{2,1,0:T(8,128)S(1)}, f32[24,8,128]{2,1,0:T(8,128)S(1)}, u32[]{:S(2)}, u32[]{:S(2)}) collective-permute-start(f32[24,8,128]{2,1,0:T(8,128)S(1)} %pad_maximum_fusion.2), channel_id=1, source_target_pairs={{1,2},{3,4},{5,6},{7,8},{9,10},{11,12},{13,14},{15,16},{17,18},{19... | collective-permute-start | bytes 294920 | tf_op jit(solution)/shard_map/ppermute | solution.py:697
  105.3 3.2 %collective-permute-start.9 = (f32[24,8,128]{2,1,0:T(8,128)S(1)}, f32[24,8,128]{2,1,0:T(8,128)S(1)}, u32[]{:S(2)}, u32[]{:S(2)}) collective-permute-start(f32[24,8,128]{2,1,0:T(8,128)S(1)} %pad_maximum_fusion.3), channel_id=1, source_target_pairs={{0,1},{2,3},{4,5},{6,7},{8,9},{10,11},{12,13},{14,15},{16,17},{18,... | collective-permute-start | bytes 294920 | tf_op jit(solution)/shard_map/ppermute | solution.py:697
  125.8 6.1 %collective-permute-start.11 = (f32[13,3,2,128]{3,2,1,0:T(2,128)S(1)}, f32[13,3,2,128]{3,2,1,0:T(2,128)S(1)}, u32[]{:S(2)}, u32[]{:S(2)}) collective-permute-start(f32[13,3,2,128]{3,2,1,0:T(2,128)S(1)} %constant_dynamic-update-slice_fusion.own), channel_id=1, source_target_pairs={{1,2},{3,4},{5,6},{7,8},{9,10},{11,12},{13,14},{15,16},{17,18},{19... | collective-permute-start | bytes 119816 | tf_op jit(solution)/shard_map/ppermute | solution.py:697
  130.0 3.1 %collective-permute-start.10 = (f32[13,3,2,128]{3,2,1,0:T(2,128)S(1)}, f32[13,3,2,128]{3,2,1,0:T(2,128)S(1)}, u32[]{:S(2)}, u32[]{:S(2)}) collective-permute-start(f32[13,3,2,128]{3,2,1,0:T(2,128)S(1)} %constant_dynamic-update-slice_fusion.own), channel_id=1, source_target_pairs={{0,1},{2,3},{4,5},{6,7},{8,9},{10,11},{12,13},{14,15},{16,17},{18,... | collective-permute-start | bytes 119816 | tf_op jit(solution)/shard_map/ppermute | solution.py:697

commit v9 on v8

--- a/solution.py
+++ b/solution.py
@@ -523,17 +523,6 @@
     return turn(v, -4, 1)[:, 0:16]
 
 
-def near_tiles(v):
-    tile = lax.axis_index("tile")
-    parts = []
-    for off in (-1, 0, 1):
-        total = jnp.zeros((2,) + v.shape[1:], F32)
-        for t in range(v.shape[0] // 2):
-            total = total + jnp.where(tile + off == t, v[2 * t : 2 * t + 2], 0.0)
-        parts.append(total)
-    return jnp.concatenate(parts, axis=0)
-
-
 def widen_y(v):
     shape = (v.shape[0], 8, NZ)
     sub = iota(shape, 1)
@@ -545,19 +534,31 @@
     return jnp.concatenate(parts, axis=1)
 
 
-def climb_to_second(corr3, r2_ref, s2_ref, di2_ref, wx2_ref, wy2_ref, wz2_ref, e22_ref):
-    v = e22_ref[...] + x_repeat(corr3)
-    v = v + di2_ref[...] * (
-        r2_ref[...]
-        - operate(v, s2_ref[...], wx2_ref[...], wy2_ref[...], wz2_ref[...], 1, 4)
-    )
-    return x_repeat(widen_y(near_tiles(v)))
+def climb_to_second(
+    corr3, r2_ref, s2_ref, di2_ref, wx2_ref, wy2_ref, wz2_ref, e22_ref, corr3_ref, corr2_ref
+):
+    tile, tiles = lax.axis_index("tile"), lax.axis_size("tile")
+    start = jnp.clip(tile - 2, 0, tiles - 4)
+    corr3_ref[...] = corr3
+    rows = pl.ds(2 * start, 8)
+    v = e22_ref[rows] + x_repeat(corr3_ref[pl.ds(start, 4)])
+    v = v + di2_ref[rows] * (
+        r2_ref[rows]
+        - operate(v, s2_ref[rows], wx2_ref[rows], wy2_ref[rows], wz2_ref[rows], 1, 4)
+    )
+    corr2_ref[0:4] = jnp.zeros((4, 16, NZ), F32)
+    corr2_ref[4:12] = v
+    corr2_ref[12:16] = jnp.zeros((4, 16, NZ), F32)
+    near = corr2_ref[pl.ds(2 * (tile - start) + 2, 6)]
+    return x_repeat(widen_y(near))
 
 
 def climb_to_first(v, r1_ref, s1_ref, di1_ref, wx1_ref, wy1_ref, wz1_ref):
-    return v + di1_ref[...] * (
-        r1_ref[...]
-        - operate(v, s1_ref[...], wx1_ref[...], wy1_ref[...], wz1_ref[...], 2, 2)
+    rows = slice(2, 10)
+    v = v[rows]
+    return v + di1_ref[rows] * (
+        r1_ref[rows]
+        - operate(v, s1_ref[rows], wx1_ref[rows], wy1_ref[rows], wz1_ref[rows], 2, 2)
     )
 
 
@@ -570,7 +571,7 @@
     third_ref, s3_ref, di3_ref, wx3_ref, wy3_ref, wz3_ref,
     r2_ref, s2_ref, di2_ref, wx2_ref, wy2_ref, wz2_ref, e22_ref,
     r1_ref, s1_ref, di1_ref, wx1_ref, wy1_ref, wz1_ref, e21_ref, e2_ref,
-    pre_ref, below_ref,
+    pre_ref, below_ref, corr3_ref, corr2_ref,
     *, groups, thirds, rows,
 ):
     r3 = strided(third_ref, 0, thirds, groups, rows)
@@ -585,11 +586,13 @@
         unpack_r3(r3), line_sums(r3, 4) / below,
         s3_ref[...], di3_ref[...], wx3_ref[...], wy3_ref[...], wz3_ref[...],
     )
-    corr2 = climb_to_second(corr3, r2_ref, s2_ref, di2_ref, wx2_ref, wy2_ref, wz2_ref, e22_ref)
+    corr2 = climb_to_second(
+        corr3, r2_ref, s2_ref, di2_ref, wx2_ref, wy2_ref, wz2_ref, e22_ref, corr3_ref, corr2_ref
+    )
     v = climb_to_first(
         e21_ref[...] + corr2, r1_ref, s1_ref, di1_ref, wx1_ref, wy1_ref, wz1_ref
     )
-    own1 = x_repeat(v[4:8])
+    own1 = x_repeat(v[2:6])
     pre_ref[...] = e2_ref[9:17, 8:24, :] + own1[:, 8:24, :]
 
 
@@ -626,7 +629,7 @@
     r2_ref, s2_ref, di2_ref, wx2_ref, wy2_ref, wz2_ref, e22_ref,
     r1_ref, s1_ref, di1_ref, wx1_ref, wy1_ref, wz1_ref, e21_ref,
     e2_ref, rhs_ref, s_ref, di_ref, wx_ref, wy_ref, wz_ref, u_ref, r_ref,
-    out_ref, left_ref, pre_ref, v_ref,
+    out_ref, left_ref, pre_ref, v_ref, corr3_ref, corr2_ref,
     *, groups, thirds, rows,
 ):
     r3 = strided(third_ref, 0, thirds, groups, rows)
@@ -634,7 +637,9 @@
         unpack_r3(r3), line_sums(r3, 4) / below_ref[...],
         s3_ref[...], di3_ref[...], wx3_ref[...], wy3_ref[...], wz3_ref[...],
     )
-    corr2 = climb_to_second(corr3, r2_ref, s2_ref, di2_ref, wx2_ref, wy2_ref, wz2_ref, e22_ref)
+    corr2 = climb_to_second(
+        corr3, r2_ref, s2_ref, di2_ref, wx2_ref, wy2_ref, wz2_ref, e22_ref, corr3_ref, corr2_ref
+    )
     tiles = lax.axis_size("tile")
     middle = e21_ref[3:9]
     sub = iota(middle.shape, 1)
@@ -649,7 +654,7 @@
     ends = [ring_row(own, first, second, off) for off in (-1, 1)]
     e21 = jnp.concatenate([blank, ends[0], middle, ends[1], blank], axis=0)
     v = climb_to_first(e21 + corr2, r1_ref, s1_ref, di1_ref, wx1_ref, wy1_ref, wz1_ref)
-    pre_ref[7:19] = e2_ref[7:19] + x_repeat(v[3:9])
+    pre_ref[7:19] = e2_ref[7:19] + x_repeat(v[1:7])
 
     def post(i, carry):
         at = 8 + 2 * i
@@ -774,6 +779,7 @@
         functools.partial(climb_kernel, groups=groups, thirds=thirds, rows=rows_once),
         [(BX, BY, NZ), line],
         [third, *bands3, r2, *bands2, e22, r1, *bands1, e21, e2],
+        [(tiles, 16, NZ), (16, 16, NZ)],
     )
 
     around = surround(pre, 0)
@@ -796,7 +802,7 @@
         [(BX, BY, NZ)] * 2,
         [third, below, *bands3, first, own, second, r2, *bands2, e22, r1, *bands1, e21]
         + [e2, rhs, *bands0, u, rem],
-        [top] * 2,
+        [top] * 2 + [(tiles, 16, NZ), (16, 16, NZ)],
     )
     return update, remainder
 

time: 157 us -> 157 us (level)
  no operation moved by 1% of the time
where the time goes in v9:
time: 157 us; the launch traced here: 156 us
  blocking collectives  86.7 us (55%)
  starting transfers between devices  41.2 us (26%)
  Pallas kernels  15.4 us (10%)
  waiting for transfers between devices  11 us (7%)
    all_to_all x3, blocking collectives, everyone(): return lax.all_to_all(blocks, axis, 0, 0, tiled=True)  60.7 us
    ppermute x12, starting transfers between devices, swap(): return lax.ppermute(cells, axis, ups + [(j, i) for i, j in ups])  41.2 us
    all_to_all x1, blocking collectives, pairs_of_tiles(): lax.all_to_all(block, ('tile', 'group'), 0, 0, axis_index_groups=members,...  26 us
    pallas_call x7, Pallas kernels, call(): pl.pallas_call(body, out_shape=[jax.ShapeDtypeStruct(shape, F32) for shap...  13.3 us
    ppermute x12, waiting for transfers between devices, swap(): return lax.ppermute(cells, axis, ups + [(j, i) for i, j in ups])  11 us
  transfers between devices with their start and end apart: 12, of which 7 were waited for; matrix products, arithmetic and copies ran while one was open for 1% of the time, Pallas kernels for 0%

profile of v9, /device:TPU:1, one launch (start us, length us, event | category | flops | bytes accessed | tf_op | source)
XLA Modules:
  0.0 156.4 jit_solution(2225118032268068818)
XLA Ops:
  0.6 2.1 %shard_map.86.own = f32[4,8,16,128]{3,2,1,0:T(8,128)} custom-call(f32[8,16,128]{2,1,0:T(8,128)} %head_in.1, f32[8,16,128]{2,1,0:T(8,128)} %old_in.1, s32[8,16,128]{2,1,0:T(8,128)} %soil_in.1, f32[12]{0:T(128)} %ks_in.1, f32[12]{0:T(128)} %alpha_in.1, f32[12]{0:T(128)} %shape_in.1, f32[12]{0:T(128)} %span_in.1), custom_call_target="tpu_custom_call" | custom-call | tf_op jit(solution)/shard_map/pallas_call | solution.py:745
  3.4 8.2 %collective-permute-start = (f32[4,8,16,128]{3,2,1,0:T(8,128)}, f32[4,8,16,128]{3,2,1,0:T(8,128)S(1)}, u32[]{:S(2)}, u32[]{:S(2)}) collective-permute-start(f32[4,8,16,128]{3,2,1,0:T(8,128)} %shard_map.86.own), channel_id=1, source_target_pairs={{0,64},{128,192},{256,320},{384,448},{512,576},{640,704},{64,0},{1... | collective-permute-start | bytes 786440 | tf_op jit(solution)/shard_map/ppermute | solution.py:702
  12.6 2.9 %collective-permute-done.xfirst = f32[4,8,16,128]{3,2,1,0:T(8,128)S(1)} collective-permute-done((f32[4,8,16,128]{3,2,1,0:T(8,128)}, f32[4,8,16,128]{3,2,1,0:T(8,128)S(1)}, u32[]{:S(2)}, u32[]{:S(2)}) %collective-permute-start) | collective-permute-done | bytes 262176 | tf_op jit(solution)/shard_map/ppermute | solution.py:702
  15.6 6.5 %collective-permute-start.2 = (f32[4,24,8,128]{3,2,1,0:T(8,128)S(1)}, f32[4,24,8,128]{3,2,1,0:T(8,128)S(1)}, u32[]{:S(2)}, u32[]{:S(2)}) collective-permute-start(f32[4,24,8,128]{3,2,1,0:T(8,128)S(1)} %pad_maximum_fusion), channel_id=1, source_target_pairs={{1,2},{3,4},{5,6},{7,8},{9,10},{11,12},{13,14},{15,16},{17,18},{19... | collective-permute-start | bytes 1179656 | tf_op jit(solution)/shard_map/ppermute | solution.py:702
  22.1 3.1 %collective-permute-start.3 = (f32[4,24,8,128]{3,2,1,0:T(8,128)S(1)}, f32[4,24,8,128]{3,2,1,0:T(8,128)S(1)}, u32[]{:S(2)}, u32[]{:S(2)}) collective-permute-start(f32[4,24,8,128]{3,2,1,0:T(8,128)S(1)} %pad_maximum_fusion.1), channel_id=1, source_target_pairs={{0,1},{2,3},{4,5},{6,7},{8,9},{10,11},{12,13},{14,15},{16,17},{18,... | collective-permute-start | bytes 1179656 | tf_op jit(solution)/shard_map/ppermute | solution.py:702
  25.3 2.3 %collective-permute-done.2.yfirst = f32[4,24,8,128]{3,2,1,0:T(8,128)S(1)} collective-permute-done((f32[4,24,8,128]{3,2,1,0:T(8,128)S(1)}, f32[4,24,8,128]{3,2,1,0:T(8,128)S(1)}, u32[]{:S(2)}, u32[]{:S(2)}) %collective-permute-start.2) | collective-permute-done | bytes 393248 | tf_op jit(solution)/shard_map/ppermute | solution.py:702
  27.6 3.0 %shard_map.87 = (f32[26,32,128]{2,1,0:T(8,128)S(1)}, f32[26,32,128]{2,1,0:T(8,128)S(1)}, f32[26,32,128]{2,1,0:T(8,128)S(1)}, f32[26,32,128]{2,1,0:T(8,128)S(1)},...) custom-call(f32[4,8,16,128]{3,2,1,0:T(8,128)S(1)} %collective-permut, ...), custom_call_target="tpu_custom_call" | custom-call | flops 22528000 | bytes 9011200 | tf_op jit(solution)/shard_map/pallas_call | solution.py:682
  30.5 26.0 %all_to_all.20 = f32[24,6,2,128]{3,2,1,0:T(2,128)S(1)} all-to-all(f32[24,6,2,128]{3,2,1,0:T(2,128)S(1)} %get-tuple-element.44), channel_id=1, replica_groups={{0,1,64,65,128,129,192,193,256,257,320,321,384,385,448,449,512,513,576,..., dimensions={0} | all-to-all | bytes 294912 | tf_op jit(solution)/shard_map/all_to_all | solution.py:732
  57.3 6.1 %collective-permute-start.5 = (f32[12,6,2,128]{3,2,1,0:T(2,128)S(1)}, f32[12,6,2,128]{3,2,1,0:T(2,128)S(1)}, u32[]{:S(2)}, u32[]{:S(2)}) collective-permute-start(f32[12,6,2,128]{3,2,1,0:T(2,128)S(1)} %get-tuple-element.46), channel_id=1, source_target_pairs={{0,2},{1,3},{4,6},{5,7},{8,10},{9,11},{12,14},{13,15},{16,18},{17,... | collective-permute-start | bytes 221192 | tf_op jit(solution)/shard_map/ppermute | solution.py:702
  63.4 1.7 %collective-permute-done.5.second = f32[12,6,2,128]{3,2,1,0:T(2,128)S(1)} collective-permute-done((f32[12,6,2,128]{3,2,1,0:T(2,128)S(1)}, f32[12,6,2,128]{3,2,1,0:T(2,128)S(1)}, u32[]{:S(2)}, u32[]{:S(2)}) %collective-permute-start.5) | collective-permute-done | bytes 73760 | tf_op jit(solution)/shard_map/ppermute | solution.py:702
  65.1 3.3 %shard_map.89 = (f32[24,16,128]{2,1,0:T(8,128)S(1)}, f32[24,16,128]{2,1,0:T(8,128)S(1)}, f32[24,16,128]{2,1,0:T(8,128)S(1)}, f32[24,16,128]{2,1,0:T(8,128)S(1)},...) custom-call(f32[12,6,2,128]{3,2,1,0:T(2,128)S(1)} %collective-permut, ...), custom_call_target="tpu_custom_call" | custom-call | flops 11223040 | bytes 4489216 | tf_op jit(solution)/shard_map/pallas_call | solution.py:682
  68.4 25.6 %all_to_all.21 = f32[64,4,1,128]{3,2,1,0:T(1,128)S(1)} all-to-all(f32[64,4,1,128]{3,2,1,0:T(1,128)S(1)} %get-tuple-element.47), channel_id=1, replica_groups=mesh['tile'=12,'group'=64] {'group'}, dimensions={0} | all-to-all | bytes 262144 | tf_op jit(solution)/shard_map/all_to_all | solution.py:723
  94.0 1.4 shard_map.90
  96.2 3.8 %collective-permute-start.6 = (f32[8,16,128]{2,1,0:T(8,128)S(1)}, f32[8,16,128]{2,1,0:T(8,128)S(1)}, u32[]{:S(2)}, u32[]{:S(2)}) collective-permute-start(f32[8,16,128]{2,1,0:T(8,128)S(1)} %get-tuple-element.68.own), channel_id=1, source_target_pairs={{0,64},{128,192},{256,320},{384,448},{512,576},{640,704},{64,0},{1... | collective-permute-start | bytes 196616 | tf_op jit(solution)/shard_map/ppermute | solution.py:702
  100.0 1.6 %collective-permute-done.6.xfirst = f32[8,16,128]{2,1,0:T(8,128)S(1)} collective-permute-done((f32[8,16,128]{2,1,0:T(8,128)S(1)}, f32[8,16,128]{2,1,0:T(8,128)S(1)}, u32[]{:S(2)}, u32[]{:S(2)}) %collective-permute-start.6) | collective-permute-done | bytes 65568 | tf_op jit(solution)/shard_map/ppermute | solution.py:702
  101.7 3.5 %collective-permute-start.8 = (f32[24,8,128]{2,1,0:T(8,128)S(1)}, f32[24,8,128]{2,1,0:T(8,128)S(1)}, u32[]{:S(2)}, u32[]{:S(2)}) collective-permute-start(f32[24,8,128]{2,1,0:T(8,128)S(1)} %pad_maximum_fusion.2), channel_id=1, source_target_pairs={{1,2},{3,4},{5,6},{7,8},{9,10},{11,12},{13,14},{15,16},{17,18},{19... | collective-permute-start | bytes 294920 | tf_op jit(solution)/shard_map/ppermute | solution.py:702
  105.2 1.9 %collective-permute-start.9 = (f32[24,8,128]{2,1,0:T(8,128)S(1)}, f32[24,8,128]{2,1,0:T(8,128)S(1)}, u32[]{:S(2)}, u32[]{:S(2)}) collective-permute-start(f32[24,8,128]{2,1,0:T(8,128)S(1)} %pad_maximum_fusion.3), channel_id=1, source_target_pairs={{0,1},{2,3},{4,5},{6,7},{8,9},{10,11},{12,13},{14,15},{16,17},{18,... | collective-permute-start | bytes 294920 | tf_op jit(solution)/shard_map/ppermute | solution.py:702
  108.4 2.3 %shard_map.91 = (f32[26,32,128]{2,1,0:T(8,128)S(1)}, f32[26,32,128]{2,1,0:T(8,128)S(1)}, f32[26,32,128]{2,1,0:T(8,128)S(1)}, f32[12,32,128]{2,1,0:T(8,128)S(1)},...) custom-call(f32[8,16,128]{2,1,0:T(8,128)S(1)} %collective-permute-done.6.xfirst, ...), custom_call_target="tpu_custom_call" | custom-call | flops 8555520 | bytes 3422208 | tf_op jit(solution)/shard_map/pallas_call | solution.py:682
  110.7 15.0 %all_to_all.22 = f32[12,3,2,128]{3,2,1,0:T(2,128)S(1)} all-to-all(f32[12,3,2,128]{3,2,1,0:T(2,128)S(1)} %get-tuple-element.75), channel_id=1, replica_groups=mesh['tile'=12,'group'=64] {'tile'}, dimensions={0} | all-to-all | bytes 73728 | tf_op jit(solution)/shard_map/all_to_all | solution.py:723
  125.7 4.2 %collective-permute-start.11 = (f32[13,3,2,128]{3,2,1,0:T(2,128)S(1)}, f32[13,3,2,128]{3,2,1,0:T(2,128)S(1)}, u32[]{:S(2)}, u32[]{:S(2)}) collective-permute-start(f32[13,3,2,128]{3,2,1,0:T(2,128)S(1)} %constant_dynamic-update-slice_fusion.own), channel_id=1, source_target_pairs={{1,2},{3,4},{5,6},{7,8},{9,10},{11,12},{13,14},{15,16},{17,18},{19... | collective-permute-start | bytes 119816 | tf_op jit(solution)/shard_map/ppermute | solution.py:702
  129.9 1.9 %collective-permute-start.10 = (f32[13,3,2,128]{3,2,1,0:T(2,128)S(1)}, f32[13,3,2,128]{3,2,1,0:T(2,128)S(1)}, u32[]{:S(2)}, u32[]{:S(2)}) collective-permute-start(f32[13,3,2,128]{3,2,1,0:T(2,128)S(1)} %constant_dynamic-update-slice_fusion.own), channel_id=1, source_target_pairs={{0,1},{2,3},{4,5},{6,7},{8,9},{10,11},{12,13},{14,15},{16,17},{18,... | collective-permute-start | bytes 119816 | tf_op jit(solution)/shard_map/ppermute | solution.py:702
  131.9 1.2 collective-permute-done.10.first
  133.9 20.2 %all_to_all.23 = f32[64,3,1,128]{3,2,1,0:T(1,128)S(1)} all-to-all(f32[64,3,1,128]{3,2,1,0:T(1,128)S(1)} %get-tuple-element.77), channel_id=1, replica_groups=mesh['tile'=12,'group'=64] {'group'}, dimensions={0} | all-to-all | bytes 196608 | tf_op jit(solution)/shard_map/all_to_all | solution.py:723
  154.1 2.4 %shard_map.93 = (f32[8,16,128]{2,1,0:T(8,128)}, f32[8,16,128]{2,1,0:T(8,128)}) custom-call(f32[192,128]{1,0:T(8,128)S(1)} %bitcast.6, f32[12,1,128]{2,1,0:T(1,128)S(1)} %get-tuple-element.78.below_ref, f32[12,24,128]{2,1,0:T(8,128)S(1)} %get-tuple-element.48.s3_ref, f32[12,24,128]{2,1,0:T(8,128)S(1)} %get-tuple-element.49.di3_ref, ...), custom_call_target="tpu_custom_call" | custom-call | flops 655360 | bytes 262144 | tf_op jit(solution)/shard_map/pallas_call | solution.py:682
  (26 shorter events, 5.3 us)
Async XLA Ops:
  2.7 9.9 %collective-permute-start.1 = (f32[4,8,16,128]{3,2,1,0:T(8,128)}, f32[4,8,16,128]{3,2,1,0:T(8,128)S(1)}, u32[]{:S(2)}, u32[]{:S(2)}) collective-permute-start(f32[4,8,16,128]{3,2,1,0:T(8,128)} %shard_map.86.own), channel_id=1, source_target_pairs={{64,128},{192,256},{320,384},{448,512},{576,640},{128,64},{256,192... | collective-permute-start | bytes 786440 | tf_op jit(solution)/shard_map/ppermute | solution.py:702
  3.4 12.1 %collective-permute-start = (f32[4,8,16,128]{3,2,1,0:T(8,128)}, f32[4,8,16,128]{3,2,1,0:T(8,128)S(1)}, u32[]{:S(2)}, u32[]{:S(2)}) collective-permute-start(f32[4,8,16,128]{3,2,1,0:T(8,128)} %shard_map.86.own), channel_id=1, source_target_pairs={{0,64},{128,192},{256,320},{384,448},{512,576},{640,704},{64,0},{1... | collective-permute-start | bytes 786440 | tf_op jit(solution)/shard_map/ppermute | solution.py:702
  15.6 12.0 %collective-permute-start.2 = (f32[4,24,8,128]{3,2,1,0:T(8,128)S(1)}, f32[4,24,8,128]{3,2,1,0:T(8,128)S(1)}, u32[]{:S(2)}, u32[]{:S(2)}) collective-permute-start(f32[4,24,8,128]{3,2,1,0:T(8,128)S(1)} %pad_maximum_fusion), channel_id=1, source_target_pairs={{1,2},{3,4},{5,6},{7,8},{9,10},{11,12},{13,14},{15,16},{17,18},{19... | collective-permute-start | bytes 1179656 | tf_op jit(solution)/shard_map/ppermute | solution.py:702
  22.1 5.5 %copy-start = (f32[4,8,16,128]{3,2,1,0:T(8,128)S(1)}, f32[4,8,16,128]{3,2,1,0:T(8,128)}, u32[]{:S(2)}) copy-start(f32[4,8,16,128]{3,2,1,0:T(8,128)} %shard_map.86.own) | copy-start | bytes 786436
  22.1 5.4 %collective-permute-start.3 = (f32[4,24,8,128]{3,2,1,0:T(8,128)S(1)}, f32[4,24,8,128]{3,2,1,0:T(8,128)S(1)}, u32[]{:S(2)}, u32[]{:S(2)}) collective-permute-start(f32[4,24,8,128]{3,2,1,0:T(8,128)S(1)} %pad_maximum_fusion.1), channel_id=1, source_target_pairs={{0,1},{2,3},{4,5},{6,7},{8,9},{10,11},{12,13},{14,15},{16,17},{18,... | collective-permute-start | bytes 1179656 | tf_op jit(solution)/shard_map/ppermute | solution.py:702
  56.6 6.8 %collective-permute-start.4 = (f32[12,6,2,128]{3,2,1,0:T(2,128)S(1)}, f32[12,6,2,128]{3,2,1,0:T(2,128)S(1)}, u32[]{:S(2)}, u32[]{:S(2)}) collective-permute-start(f32[12,6,2,128]{3,2,1,0:T(2,128)S(1)} %get-tuple-element.45), channel_id=1, source_target_pairs={{2,4},{3,5},{6,8},{7,9},{10,12},{11,13},{14,16},{15,17},{18,20},{1... | collective-permute-start | bytes 221192 | tf_op jit(solution)/shard_map/ppermute | solution.py:702
  57.3 7.8 %collective-permute-start.5 = (f32[12,6,2,128]{3,2,1,0:T(2,128)S(1)}, f32[12,6,2,128]{3,2,1,0:T(2,128)S(1)}, u32[]{:S(2)}, u32[]{:S(2)}) collective-permute-start(f32[12,6,2,128]{3,2,1,0:T(2,128)S(1)} %get-tuple-element.46), channel_id=1, source_target_pairs={{0,2},{1,3},{4,6},{5,7},{8,10},{9,11},{12,14},{13,15},{16,18},{17,... | collective-permute-start | bytes 221192 | tf_op jit(solution)/shard_map/ppermute | solution.py:702
  95.5 4.5 %collective-permute-start.7 = (f32[8,16,128]{2,1,0:T(8,128)S(1)}, f32[8,16,128]{2,1,0:T(8,128)S(1)}, u32[]{:S(2)}, u32[]{:S(2)}) collective-permute-start(f32[8,16,128]{2,1,0:T(8,128)S(1)} %get-tuple-element.68.own), channel_id=1, source_target_pairs={{64,128},{192,256},{320,384},{448,512},{576,640},{128,64},{256,192... | collective-permute-start | bytes 196616 | tf_op jit(solution)/shard_map/ppermute | solution.py:702
  96.2 5.5 %collective-permute-start.6 = (f32[8,16,128]{2,1,0:T(8,128)S(1)}, f32[8,16,128]{2,1,0:T(8,128)S(1)}, u32[]{:S(2)}, u32[]{:S(2)}) collective-permute-start(f32[8,16,128]{2,1,0:T(8,128)S(1)} %get-tuple-element.68.own), channel_id=1, source_target_pairs={{0,64},{128,192},{256,320},{384,448},{512,576},{640,704},{64,0},{1... | collective-permute-start | bytes 196616 | tf_op jit(solution)/shard_map/ppermute | solution.py:702
  101.7 5.9 %collective-permute-start.8 = (f32[24,8,128]{2,1,0:T(8,128)S(1)}, f32[24,8,128]{2,1,0:T(8,128)S(1)}, u32[]{:S(2)}, u32[]{:S(2)}) collective-permute-start(f32[24,8,128]{2,1,0:T(8,128)S(1)} %pad_maximum_fusion.2), channel_id=1, source_target_pairs={{1,2},{3,4},{5,6},{7,8},{9,10},{11,12},{13,14},{15,16},{17,18},{19... | collective-permute-start | bytes 294920 | tf_op jit(solution)/shard_map/ppermute | solution.py:702
  105.2 3.2 %collective-permute-start.9 = (f32[24,8,128]{2,1,0:T(8,128)S(1)}, f32[24,8,128]{2,1,0:T(8,128)S(1)}, u32[]{:S(2)}, u32[]{:S(2)}) collective-permute-start(f32[24,8,128]{2,1,0:T(8,128)S(1)} %pad_maximum_fusion.3), channel_id=1, source_target_pairs={{0,1},{2,3},{4,5},{6,7},{8,9},{10,11},{12,13},{14,15},{16,17},{18,... | collective-permute-start | bytes 294920 | tf_op jit(solution)/shard_map/ppermute | solution.py:702
  125.7 6.1 %collective-permute-start.11 = (f32[13,3,2,128]{3,2,1,0:T(2,128)S(1)}, f32[13,3,2,128]{3,2,1,0:T(2,128)S(1)}, u32[]{:S(2)}, u32[]{:S(2)}) collective-permute-start(f32[13,3,2,128]{3,2,1,0:T(2,128)S(1)} %constant_dynamic-update-slice_fusion.own), channel_id=1, source_target_pairs={{1,2},{3,4},{5,6},{7,8},{9,10},{11,12},{13,14},{15,16},{17,18},{19... | collective-permute-start | bytes 119816 | tf_op jit(solution)/shard_map/ppermute | solution.py:702
  129.9 3.1 %collective-permute-start.10 = (f32[13,3,2,128]{3,2,1,0:T(2,128)S(1)}, f32[13,3,2,128]{3,2,1,0:T(2,128)S(1)}, u32[]{:S(2)}, u32[]{:S(2)}) collective-permute-start(f32[13,3,2,128]{3,2,1,0:T(2,128)S(1)} %constant_dynamic-update-slice_fusion.own), channel_id=1, source_target_pairs={{0,1},{2,3},{4,5},{6,7},{8,9},{10,11},{12,13},{14,15},{16,17},{18,... | collective-permute-start | bytes 119816 | tf_op jit(solution)/shard_map/ppermute | solution.py:702

commit v10 on v9

--- a/solution.py
+++ b/solution.py
@@ -183,8 +183,8 @@
     head_in, old_in, soil_in, ks_in, alpha_in, shape_in, span_in, out_ref,
     head_ref, old_ref, soil_ref, ks_ref, alpha_ref, shape_ref, span_ref, sems,
 ):
-    given = (ks_in, alpha_in, shape_in, span_in, head_in, old_in, soil_in)
-    held = (ks_ref, alpha_ref, shape_ref, span_ref, head_ref, old_ref, soil_ref)
+    given = (head_in, old_in, soil_in, ks_in, alpha_in, shape_in, span_in)
+    held = (head_ref, old_ref, soil_ref, ks_ref, alpha_ref, shape_ref, span_ref)
     copies = [
         pltpu.make_async_copy(src, dst, sems.at[i])
         for i, (src, dst) in enumerate(zip(given, held, strict=True))
@@ -221,7 +221,7 @@
         out_ref[3, row] = span * (saturation - old_saturation) + STORAGE * (head - old)
         return carry
 
-    lax.fori_loop(0, BX, cells, 0, unroll=2)
+    lax.fori_loop(0, BX, cells, 0, unroll=4)
 
 
 def is_even(axis, step=1, lead=0):
@@ -571,12 +571,13 @@
     third_ref, s3_ref, di3_ref, wx3_ref, wy3_ref, wz3_ref,
     r2_ref, s2_ref, di2_ref, wx2_ref, wy2_ref, wz2_ref, e22_ref,
     r1_ref, s1_ref, di1_ref, wx1_ref, wy1_ref, wz1_ref, e21_ref, e2_ref,
-    pre_ref, below_ref, corr3_ref, corr2_ref,
+    pre_ref, below_ref, corr3_ref, corr2_ref, rows_ref,
     *, groups, thirds, rows,
 ):
-    r3 = strided(third_ref, 0, thirds, groups, rows)
+    rows_ref[0 : groups * rows] = third_ref[...]
+    r3 = strided(rows_ref, 0, thirds, groups, rows)
     tiles = lax.axis_size("tile")
-    sums = strided(third_ref, thirds, 1, groups, rows)
+    sums = strided(rows_ref, thirds, 1, groups, rows)
     odd = iota(sums.shape, 1) % 2
     below = jnp.concatenate(
         [line_sums(jnp.where(odd == half, sums, 0.0), 8)[: tiles // 2] for half in range(2)], axis=0
@@ -629,10 +630,11 @@
     r2_ref, s2_ref, di2_ref, wx2_ref, wy2_ref, wz2_ref, e22_ref,
     r1_ref, s1_ref, di1_ref, wx1_ref, wy1_ref, wz1_ref, e21_ref,
     e2_ref, rhs_ref, s_ref, di_ref, wx_ref, wy_ref, wz_ref, u_ref, r_ref,
-    out_ref, left_ref, pre_ref, v_ref, corr3_ref, corr2_ref,
+    out_ref, left_ref, pre_ref, v_ref, corr3_ref, corr2_ref, rows_ref,
     *, groups, thirds, rows,
 ):
-    r3 = strided(third_ref, 0, thirds, groups, rows)
+    rows_ref[0 : groups * rows] = third_ref[...]
+    r3 = strided(rows_ref, 0, thirds, groups, rows)
     corr3 = solve_third(
         unpack_r3(r3), line_sums(r3, 4) / below_ref[...],
         s3_ref[...], di3_ref[...], wx3_ref[...], wy3_ref[...], wz3_ref[...],
@@ -779,7 +781,7 @@
         functools.partial(climb_kernel, groups=groups, thirds=thirds, rows=rows_once),
         [(BX, BY, NZ), line],
         [third, *bands3, r2, *bands2, e22, r1, *bands1, e21, e2],
-        [(tiles, 16, NZ), (16, 16, NZ)],
+        [(tiles, 16, NZ), (16, 16, NZ), (groups * rows_once + 8, NZ)],
     )
 
     around = surround(pre, 0)
@@ -802,7 +804,7 @@
         [(BX, BY, NZ)] * 2,
         [third, below, *bands3, first, own, second, r2, *bands2, e22, r1, *bands1, e21]
         + [e2, rhs, *bands0, u, rem],
-        [top] * 2 + [(tiles, 16, NZ), (16, 16, NZ)],
+        [top] * 2 + [(tiles, 16, NZ), (16, 16, NZ), (groups * rows_again + 8, NZ)],
     )
     return update, remainder
 

time: 157 us -> 157 us (level)
  no operation moved by 1% of the time
where the time goes in v10:
time: 157 us; the launch traced here: 156 us
  blocking collectives  86.7 us (55%)
  starting transfers between devices  41.2 us (26%)
  Pallas kernels  15.4 us (10%)
  waiting for transfers between devices  11 us (7%)
    all_to_all x3, blocking collectives, everyone(): return lax.all_to_all(blocks, axis, 0, 0, tiled=True)  60.7 us
    ppermute x12, starting transfers between devices, swap(): return lax.ppermute(cells, axis, ups + [(j, i) for i, j in ups])  41.2 us
    all_to_all x1, blocking collectives, pairs_of_tiles(): lax.all_to_all(block, ('tile', 'group'), 0, 0, axis_index_groups=members,...  26 us
    pallas_call x7, Pallas kernels, call(): pl.pallas_call(body, out_shape=[jax.ShapeDtypeStruct(shape, F32) for shap...  13.3 us
    ppermute x12, waiting for transfers between devices, swap(): return lax.ppermute(cells, axis, ups + [(j, i) for i, j in ups])  11 us
  transfers between devices with their start and end apart: 12, of which 7 were waited for; matrix products, arithmetic and copies ran while one was open for 1% of the time, Pallas kernels for 0%

profile of v10, /device:TPU:1, one launch (start us, length us, event | category | flops | bytes accessed | tf_op | source)
XLA Modules:
  0.0 156.4 jit_solution(1976957718296306858)
XLA Ops:
  0.6 2.1 %shard_map.86.own = f32[4,8,16,128]{3,2,1,0:T(8,128)} custom-call(f32[8,16,128]{2,1,0:T(8,128)} %head_in.1, f32[8,16,128]{2,1,0:T(8,128)} %old_in.1, s32[8,16,128]{2,1,0:T(8,128)} %soil_in.1, f32[12]{0:T(128)} %ks_in.1, f32[12]{0:T(128)} %alpha_in.1, f32[12]{0:T(128)} %shape_in.1, f32[12]{0:T(128)} %span_in.1), custom_call_target="tpu_custom_call" | custom-call | tf_op jit(solution)/shard_map/pallas_call | solution.py:747
  3.4 8.2 %collective-permute-start = (f32[4,8,16,128]{3,2,1,0:T(8,128)}, f32[4,8,16,128]{3,2,1,0:T(8,128)S(1)}, u32[]{:S(2)}, u32[]{:S(2)}) collective-permute-start(f32[4,8,16,128]{3,2,1,0:T(8,128)} %shard_map.86.own), channel_id=1, source_target_pairs={{0,64},{128,192},{256,320},{384,448},{512,576},{640,704},{64,0},{1... | collective-permute-start | bytes 786440 | tf_op jit(solution)/shard_map/ppermute | solution.py:704
  12.6 2.9 %collective-permute-done.xfirst = f32[4,8,16,128]{3,2,1,0:T(8,128)S(1)} collective-permute-done((f32[4,8,16,128]{3,2,1,0:T(8,128)}, f32[4,8,16,128]{3,2,1,0:T(8,128)S(1)}, u32[]{:S(2)}, u32[]{:S(2)}) %collective-permute-start) | collective-permute-done | bytes 262176 | tf_op jit(solution)/shard_map/ppermute | solution.py:704
  15.6 6.5 %collective-permute-start.2 = (f32[4,24,8,128]{3,2,1,0:T(8,128)S(1)}, f32[4,24,8,128]{3,2,1,0:T(8,128)S(1)}, u32[]{:S(2)}, u32[]{:S(2)}) collective-permute-start(f32[4,24,8,128]{3,2,1,0:T(8,128)S(1)} %pad_maximum_fusion), channel_id=1, source_target_pairs={{1,2},{3,4},{5,6},{7,8},{9,10},{11,12},{13,14},{15,16},{17,18},{19... | collective-permute-start | bytes 1179656 | tf_op jit(solution)/shard_map/ppermute | solution.py:704
  22.1 3.1 %collective-permute-start.3 = (f32[4,24,8,128]{3,2,1,0:T(8,128)S(1)}, f32[4,24,8,128]{3,2,1,0:T(8,128)S(1)}, u32[]{:S(2)}, u32[]{:S(2)}) collective-permute-start(f32[4,24,8,128]{3,2,1,0:T(8,128)S(1)} %pad_maximum_fusion.1), channel_id=1, source_target_pairs={{0,1},{2,3},{4,5},{6,7},{8,9},{10,11},{12,13},{14,15},{16,17},{18,... | collective-permute-start | bytes 1179656 | tf_op jit(solution)/shard_map/ppermute | solution.py:704
  25.2 2.3 %collective-permute-done.2.yfirst = f32[4,24,8,128]{3,2,1,0:T(8,128)S(1)} collective-permute-done((f32[4,24,8,128]{3,2,1,0:T(8,128)S(1)}, f32[4,24,8,128]{3,2,1,0:T(8,128)S(1)}, u32[]{:S(2)}, u32[]{:S(2)}) %collective-permute-start.2) | collective-permute-done | bytes 393248 | tf_op jit(solution)/shard_map/ppermute | solution.py:704
  27.5 3.0 %shard_map.87 = (f32[26,32,128]{2,1,0:T(8,128)S(1)}, f32[26,32,128]{2,1,0:T(8,128)S(1)}, f32[26,32,128]{2,1,0:T(8,128)S(1)}, f32[26,32,128]{2,1,0:T(8,128)S(1)},...) custom-call(f32[4,8,16,128]{3,2,1,0:T(8,128)S(1)} %collective-permut, ...), custom_call_target="tpu_custom_call" | custom-call | flops 22528000 | bytes 9011200 | tf_op jit(solution)/shard_map/pallas_call | solution.py:684
  30.5 26.0 %all_to_all.20 = f32[24,6,2,128]{3,2,1,0:T(2,128)S(1)} all-to-all(f32[24,6,2,128]{3,2,1,0:T(2,128)S(1)} %get-tuple-element.44), channel_id=1, replica_groups={{0,1,64,65,128,129,192,193,256,257,320,321,384,385,448,449,512,513,576,..., dimensions={0} | all-to-all | bytes 294912 | tf_op jit(solution)/shard_map/all_to_all | solution.py:734
  57.3 6.1 %collective-permute-start.5 = (f32[12,6,2,128]{3,2,1,0:T(2,128)S(1)}, f32[12,6,2,128]{3,2,1,0:T(2,128)S(1)}, u32[]{:S(2)}, u32[]{:S(2)}) collective-permute-start(f32[12,6,2,128]{3,2,1,0:T(2,128)S(1)} %get-tuple-element.46), channel_id=1, source_target_pairs={{0,2},{1,3},{4,6},{5,7},{8,10},{9,11},{12,14},{13,15},{16,18},{17,... | collective-permute-start | bytes 221192 | tf_op jit(solution)/shard_map/ppermute | solution.py:704
  63.4 1.7 %collective-permute-done.5.second = f32[12,6,2,128]{3,2,1,0:T(2,128)S(1)} collective-permute-done((f32[12,6,2,128]{3,2,1,0:T(2,128)S(1)}, f32[12,6,2,128]{3,2,1,0:T(2,128)S(1)}, u32[]{:S(2)}, u32[]{:S(2)}) %collective-permute-start.5) | collective-permute-done | bytes 73760 | tf_op jit(solution)/shard_map/ppermute | solution.py:704
  65.1 3.3 %shard_map.89 = (f32[24,16,128]{2,1,0:T(8,128)S(1)}, f32[24,16,128]{2,1,0:T(8,128)S(1)}, f32[24,16,128]{2,1,0:T(8,128)S(1)}, f32[24,16,128]{2,1,0:T(8,128)S(1)},...) custom-call(f32[12,6,2,128]{3,2,1,0:T(2,128)S(1)} %collective-permut, ...), custom_call_target="tpu_custom_call" | custom-call | flops 11223040 | bytes 4489216 | tf_op jit(solution)/shard_map/pallas_call | solution.py:684
  68.4 25.6 %all_to_all.21 = f32[64,4,1,128]{3,2,1,0:T(1,128)S(1)} all-to-all(f32[64,4,1,128]{3,2,1,0:T(1,128)S(1)} %get-tuple-element.47), channel_id=1, replica_groups=mesh['tile'=12,'group'=64] {'group'}, dimensions={0} | all-to-all | bytes 262144 | tf_op jit(solution)/shard_map/all_to_all | solution.py:725
  94.0 1.5 shard_map.90
  96.2 3.8 %collective-permute-start.6 = (f32[8,16,128]{2,1,0:T(8,128)S(1)}, f32[8,16,128]{2,1,0:T(8,128)S(1)}, u32[]{:S(2)}, u32[]{:S(2)}) collective-permute-start(f32[8,16,128]{2,1,0:T(8,128)S(1)} %get-tuple-element.68.own), channel_id=1, source_target_pairs={{0,64},{128,192},{256,320},{384,448},{512,576},{640,704},{64,0},{1... | collective-permute-start | bytes 196616 | tf_op jit(solution)/shard_map/ppermute | solution.py:704
  100.0 1.6 %collective-permute-done.6.xfirst = f32[8,16,128]{2,1,0:T(8,128)S(1)} collective-permute-done((f32[8,16,128]{2,1,0:T(8,128)S(1)}, f32[8,16,128]{2,1,0:T(8,128)S(1)}, u32[]{:S(2)}, u32[]{:S(2)}) %collective-permute-start.6) | collective-permute-done | bytes 65568 | tf_op jit(solution)/shard_map/ppermute | solution.py:704
  101.7 3.5 %collective-permute-start.8 = (f32[24,8,128]{2,1,0:T(8,128)S(1)}, f32[24,8,128]{2,1,0:T(8,128)S(1)}, u32[]{:S(2)}, u32[]{:S(2)}) collective-permute-start(f32[24,8,128]{2,1,0:T(8,128)S(1)} %pad_maximum_fusion.2), channel_id=1, source_target_pairs={{1,2},{3,4},{5,6},{7,8},{9,10},{11,12},{13,14},{15,16},{17,18},{19... | collective-permute-start | bytes 294920 | tf_op jit(solution)/shard_map/ppermute | solution.py:704
  105.2 1.9 %collective-permute-start.9 = (f32[24,8,128]{2,1,0:T(8,128)S(1)}, f32[24,8,128]{2,1,0:T(8,128)S(1)}, u32[]{:S(2)}, u32[]{:S(2)}) collective-permute-start(f32[24,8,128]{2,1,0:T(8,128)S(1)} %pad_maximum_fusion.3), channel_id=1, source_target_pairs={{0,1},{2,3},{4,5},{6,7},{8,9},{10,11},{12,13},{14,15},{16,17},{18,... | collective-permute-start | bytes 294920 | tf_op jit(solution)/shard_map/ppermute | solution.py:704
  108.4 2.3 %shard_map.91 = (f32[26,32,128]{2,1,0:T(8,128)S(1)}, f32[26,32,128]{2,1,0:T(8,128)S(1)}, f32[26,32,128]{2,1,0:T(8,128)S(1)}, f32[12,32,128]{2,1,0:T(8,128)S(1)},...) custom-call(f32[8,16,128]{2,1,0:T(8,128)S(1)} %collective-permute-done.6.xfirst, ...), custom_call_target="tpu_custom_call" | custom-call | flops 8555520 | bytes 3422208 | tf_op jit(solution)/shard_map/pallas_call | solution.py:684
  110.7 15.0 %all_to_all.22 = f32[12,3,2,128]{3,2,1,0:T(2,128)S(1)} all-to-all(f32[12,3,2,128]{3,2,1,0:T(2,128)S(1)} %get-tuple-element.75), channel_id=1, replica_groups=mesh['tile'=12,'group'=64] {'tile'}, dimensions={0} | all-to-all | bytes 73728 | tf_op jit(solution)/shard_map/all_to_all | solution.py:725
  125.7 4.2 %collective-permute-start.11 = (f32[13,3,2,128]{3,2,1,0:T(2,128)S(1)}, f32[13,3,2,128]{3,2,1,0:T(2,128)S(1)}, u32[]{:S(2)}, u32[]{:S(2)}) collective-permute-start(f32[13,3,2,128]{3,2,1,0:T(2,128)S(1)} %constant_dynamic-update-slice_fusion.own), channel_id=1, source_target_pairs={{1,2},{3,4},{5,6},{7,8},{9,10},{11,12},{13,14},{15,16},{17,18},{19... | collective-permute-start | bytes 119816 | tf_op jit(solution)/shard_map/ppermute | solution.py:704
  129.9 1.9 %collective-permute-start.10 = (f32[13,3,2,128]{3,2,1,0:T(2,128)S(1)}, f32[13,3,2,128]{3,2,1,0:T(2,128)S(1)}, u32[]{:S(2)}, u32[]{:S(2)}) collective-permute-start(f32[13,3,2,128]{3,2,1,0:T(2,128)S(1)} %constant_dynamic-update-slice_fusion.own), channel_id=1, source_target_pairs={{0,1},{2,3},{4,5},{6,7},{8,9},{10,11},{12,13},{14,15},{16,17},{18,... | collective-permute-start | bytes 119816 | tf_op jit(solution)/shard_map/ppermute | solution.py:704
  131.9 1.2 collective-permute-done.10.first
  133.9 20.2 %all_to_all.23 = f32[64,3,1,128]{3,2,1,0:T(1,128)S(1)} all-to-all(f32[64,3,1,128]{3,2,1,0:T(1,128)S(1)} %get-tuple-element.77), channel_id=1, replica_groups=mesh['tile'=12,'group'=64] {'group'}, dimensions={0} | all-to-all | bytes 196608 | tf_op jit(solution)/shard_map/all_to_all | solution.py:725
  154.1 2.4 %shard_map.93 = (f32[8,16,128]{2,1,0:T(8,128)}, f32[8,16,128]{2,1,0:T(8,128)}) custom-call(f32[192,128]{1,0:T(8,128)S(1)} %bitcast.6, f32[12,1,128]{2,1,0:T(1,128)S(1)} %get-tuple-element.78.below_ref, f32[12,24,128]{2,1,0:T(8,128)S(1)} %get-tuple-element.48.s3_ref, f32[12,24,128]{2,1,0:T(8,128)S(1)} %get-tuple-element.49.di3_ref, ...), custom_call_target="tpu_custom_call" | custom-call | flops 655360 | bytes 262144 | tf_op jit(solution)/shard_map/pallas_call | solution.py:684
  (26 shorter events, 5.3 us)
Async XLA Ops:
  2.7 9.9 %collective-permute-start.1 = (f32[4,8,16,128]{3,2,1,0:T(8,128)}, f32[4,8,16,128]{3,2,1,0:T(8,128)S(1)}, u32[]{:S(2)}, u32[]{:S(2)}) collective-permute-start(f32[4,8,16,128]{3,2,1,0:T(8,128)} %shard_map.86.own), channel_id=1, source_target_pairs={{64,128},{192,256},{320,384},{448,512},{576,640},{128,64},{256,192... | collective-permute-start | bytes 786440 | tf_op jit(solution)/shard_map/ppermute | solution.py:704
  3.4 12.1 %collective-permute-start = (f32[4,8,16,128]{3,2,1,0:T(8,128)}, f32[4,8,16,128]{3,2,1,0:T(8,128)S(1)}, u32[]{:S(2)}, u32[]{:S(2)}) collective-permute-start(f32[4,8,16,128]{3,2,1,0:T(8,128)} %shard_map.86.own), channel_id=1, source_target_pairs={{0,64},{128,192},{256,320},{384,448},{512,576},{640,704},{64,0},{1... | collective-permute-start | bytes 786440 | tf_op jit(solution)/shard_map/ppermute | solution.py:704
  15.6 12.0 %collective-permute-start.2 = (f32[4,24,8,128]{3,2,1,0:T(8,128)S(1)}, f32[4,24,8,128]{3,2,1,0:T(8,128)S(1)}, u32[]{:S(2)}, u32[]{:S(2)}) collective-permute-start(f32[4,24,8,128]{3,2,1,0:T(8,128)S(1)} %pad_maximum_fusion), channel_id=1, source_target_pairs={{1,2},{3,4},{5,6},{7,8},{9,10},{11,12},{13,14},{15,16},{17,18},{19... | collective-permute-start | bytes 1179656 | tf_op jit(solution)/shard_map/ppermute | solution.py:704
  22.1 5.5 %copy-start = (f32[4,8,16,128]{3,2,1,0:T(8,128)S(1)}, f32[4,8,16,128]{3,2,1,0:T(8,128)}, u32[]{:S(2)}) copy-start(f32[4,8,16,128]{3,2,1,0:T(8,128)} %shard_map.86.own) | copy-start | bytes 786436
  22.1 5.4 %collective-permute-start.3 = (f32[4,24,8,128]{3,2,1,0:T(8,128)S(1)}, f32[4,24,8,128]{3,2,1,0:T(8,128)S(1)}, u32[]{:S(2)}, u32[]{:S(2)}) collective-permute-start(f32[4,24,8,128]{3,2,1,0:T(8,128)S(1)} %pad_maximum_fusion.1), channel_id=1, source_target_pairs={{0,1},{2,3},{4,5},{6,7},{8,9},{10,11},{12,13},{14,15},{16,17},{18,... | collective-permute-start | bytes 1179656 | tf_op jit(solution)/shard_map/ppermute | solution.py:704
  56.6 6.8 %collective-permute-start.4 = (f32[12,6,2,128]{3,2,1,0:T(2,128)S(1)}, f32[12,6,2,128]{3,2,1,0:T(2,128)S(1)}, u32[]{:S(2)}, u32[]{:S(2)}) collective-permute-start(f32[12,6,2,128]{3,2,1,0:T(2,128)S(1)} %get-tuple-element.45), channel_id=1, source_target_pairs={{2,4},{3,5},{6,8},{7,9},{10,12},{11,13},{14,16},{15,17},{18,20},{1... | collective-permute-start | bytes 221192 | tf_op jit(solution)/shard_map/ppermute | solution.py:704
  57.3 7.8 %collective-permute-start.5 = (f32[12,6,2,128]{3,2,1,0:T(2,128)S(1)}, f32[12,6,2,128]{3,2,1,0:T(2,128)S(1)}, u32[]{:S(2)}, u32[]{:S(2)}) collective-permute-start(f32[12,6,2,128]{3,2,1,0:T(2,128)S(1)} %get-tuple-element.46), channel_id=1, source_target_pairs={{0,2},{1,3},{4,6},{5,7},{8,10},{9,11},{12,14},{13,15},{16,18},{17,... | collective-permute-start | bytes 221192 | tf_op jit(solution)/shard_map/ppermute | solution.py:704
  95.5 4.5 %collective-permute-start.7 = (f32[8,16,128]{2,1,0:T(8,128)S(1)}, f32[8,16,128]{2,1,0:T(8,128)S(1)}, u32[]{:S(2)}, u32[]{:S(2)}) collective-permute-start(f32[8,16,128]{2,1,0:T(8,128)S(1)} %get-tuple-element.68.own), channel_id=1, source_target_pairs={{64,128},{192,256},{320,384},{448,512},{576,640},{128,64},{256,192... | collective-permute-start | bytes 196616 | tf_op jit(solution)/shard_map/ppermute | solution.py:704
  96.2 5.5 %collective-permute-start.6 = (f32[8,16,128]{2,1,0:T(8,128)S(1)}, f32[8,16,128]{2,1,0:T(8,128)S(1)}, u32[]{:S(2)}, u32[]{:S(2)}) collective-permute-start(f32[8,16,128]{2,1,0:T(8,128)S(1)} %get-tuple-element.68.own), channel_id=1, source_target_pairs={{0,64},{128,192},{256,320},{384,448},{512,576},{640,704},{64,0},{1... | collective-permute-start | bytes 196616 | tf_op jit(solution)/shard_map/ppermute | solution.py:704
  101.7 5.9 %collective-permute-start.8 = (f32[24,8,128]{2,1,0:T(8,128)S(1)}, f32[24,8,128]{2,1,0:T(8,128)S(1)}, u32[]{:S(2)}, u32[]{:S(2)}) collective-permute-start(f32[24,8,128]{2,1,0:T(8,128)S(1)} %pad_maximum_fusion.2), channel_id=1, source_target_pairs={{1,2},{3,4},{5,6},{7,8},{9,10},{11,12},{13,14},{15,16},{17,18},{19... | collective-permute-start | bytes 294920 | tf_op jit(solution)/shard_map/ppermute | solution.py:704
  105.2 3.2 %collective-permute-start.9 = (f32[24,8,128]{2,1,0:T(8,128)S(1)}, f32[24,8,128]{2,1,0:T(8,128)S(1)}, u32[]{:S(2)}, u32[]{:S(2)}) collective-permute-start(f32[24,8,128]{2,1,0:T(8,128)S(1)} %pad_maximum_fusion.3), channel_id=1, source_target_pairs={{0,1},{2,3},{4,5},{6,7},{8,9},{10,11},{12,13},{14,15},{16,17},{18,... | collective-permute-start | bytes 294920 | tf_op jit(solution)/shard_map/ppermute | solution.py:704
  125.7 6.1 %collective-permute-start.11 = (f32[13,3,2,128]{3,2,1,0:T(2,128)S(1)}, f32[13,3,2,128]{3,2,1,0:T(2,128)S(1)}, u32[]{:S(2)}, u32[]{:S(2)}) collective-permute-start(f32[13,3,2,128]{3,2,1,0:T(2,128)S(1)} %constant_dynamic-update-slice_fusion.own), channel_id=1, source_target_pairs={{1,2},{3,4},{5,6},{7,8},{9,10},{11,12},{13,14},{15,16},{17,18},{19... | collective-permute-start | bytes 119816 | tf_op jit(solution)/shard_map/ppermute | solution.py:704
  129.9 3.1 %collective-permute-start.10 = (f32[13,3,2,128]{3,2,1,0:T(2,128)S(1)}, f32[13,3,2,128]{3,2,1,0:T(2,128)S(1)}, u32[]{:S(2)}, u32[]{:S(2)}) collective-permute-start(f32[13,3,2,128]{3,2,1,0:T(2,128)S(1)} %constant_dynamic-update-slice_fusion.own), channel_id=1, source_target_pairs={{0,1},{2,3},{4,5},{6,7},{8,9},{10,11},{12,13},{14,15},{16,17},{18,... | collective-permute-start | bytes 119816 | tf_op jit(solution)/shard_map/ppermute | solution.py:704

commit v11 on v10

--- a/solution.py
+++ b/solution.py
@@ -482,7 +482,13 @@
 
 
 def octuple(v):
-    return pair_sum(pair_sum(pair_sum(v, 1, 2), 2, 2), 4, 2)
+    v = pair_sum(v, 1, 2)
+    v = v + turn(v, 2, 2)
+    return v + turn(v, 4, 2)
+
+
+def shifted(v, lanes):
+    return turn(v, -lanes, 2) if lanes else v
 
 
 def unpack_bands3(sources):
@@ -492,7 +498,7 @@
     for d in range(1, 5):
         rows = jnp.where(dev == d, jnp.broadcast_to(sources[d], shape), rows)
     rows = jnp.where(dev < 5, rows, 0.0)
-    return [octuple(jnp.where(slot == 2 * f + half, rows, 0.0)) for f in range(4)]
+    return [octuple(jnp.where(slot == half, shifted(rows, 2 * f), 0.0)) for f in range(4)]
 
 
 def unpack_r3(v):
@@ -504,14 +510,15 @@
     for d in range(5):
         near = jnp.sum(jnp.where(at == group + (d - 2), v, 0.0), axis=1, keepdims=True)
         rows = jnp.where(dev == d, jnp.broadcast_to(near, shape), rows)
-    parts = [jnp.where(slot == 2 * q + half, rows, 0.0) for q in range(4)]
+    parts = [jnp.where(slot == half, shifted(rows, 2 * q), 0.0) for q in range(4)]
     return octuple(jnp.stack(parts, axis=1).reshape((4 * v.shape[0], 24, NZ)))
 
 
 def line_sums(v, held):
     total = jnp.sum(v, axis=1, keepdims=True)
     lane = iota(total.shape, 2) % 8
-    parts = [jnp.where(lane * held // 8 == q, total, 0.0) for q in range(held)]
+    width = 8 // held
+    parts = [jnp.where(lane < width, shifted(total, width * q), 0.0) for q in range(held)]
     wide = jnp.stack(parts, axis=1).reshape((held * v.shape[0], 1, NZ))
     return octuple(wide)
 

time: 157 us -> 157 us (level)
  no operation moved by 1% of the time
where the time goes in v11:
time: 157 us; the launch traced here: 156 us
  blocking collectives  86.7 us (55%)
  starting transfers between devices  41.2 us (26%)
  Pallas kernels  15.2 us (10%)
  waiting for transfers between devices  11 us (7%)
    all_to_all x3, blocking collectives, everyone(): return lax.all_to_all(blocks, axis, 0, 0, tiled=True)  60.7 us
    ppermute x12, starting transfers between devices, swap(): return lax.ppermute(cells, axis, ups + [(j, i) for i, j in ups])  41.2 us
    all_to_all x1, blocking collectives, pairs_of_tiles(): lax.all_to_all(block, ('tile', 'group'), 0, 0, axis_index_groups=members,...  26 us
    pallas_call x7, Pallas kernels, call(): pl.pallas_call(body, out_shape=[jax.ShapeDtypeStruct(shape, F32) for shap...  13.1 us
    ppermute x12, waiting for transfers between devices, swap(): return lax.ppermute(cells, axis, ups + [(j, i) for i, j in ups])  11 us
  transfers between devices with their start and end apart: 12, of which 7 were waited for; matrix products, arithmetic and copies ran while one was open for 1% of the time, Pallas kernels for 0%

profile of v11, /device:TPU:1, one launch (start us, length us, event | category | flops | bytes accessed | tf_op | source)
XLA Modules:
  0.0 156.2 jit_solution(18189575146308773920)
XLA Ops:
  0.6 2.1 %shard_map.86.own = f32[4,8,16,128]{3,2,1,0:T(8,128)} custom-call(f32[8,16,128]{2,1,0:T(8,128)} %head_in.1, f32[8,16,128]{2,1,0:T(8,128)} %old_in.1, s32[8,16,128]{2,1,0:T(8,128)} %soil_in.1, f32[12]{0:T(128)} %ks_in.1, f32[12]{0:T(128)} %alpha_in.1, f32[12]{0:T(128)} %shape_in.1, f32[12]{0:T(128)} %span_in.1), custom_call_target="tpu_custom_call" | custom-call | tf_op jit(solution)/shard_map/pallas_call | solution.py:754
  3.4 8.2 %collective-permute-start = (f32[4,8,16,128]{3,2,1,0:T(8,128)}, f32[4,8,16,128]{3,2,1,0:T(8,128)S(1)}, u32[]{:S(2)}, u32[]{:S(2)}) collective-permute-start(f32[4,8,16,128]{3,2,1,0:T(8,128)} %shard_map.86.own), channel_id=1, source_target_pairs={{0,64},{128,192},{256,320},{384,448},{512,576},{640,704},{64,0},{1... | collective-permute-start | bytes 786440 | tf_op jit(solution)/shard_map/ppermute | solution.py:711
  12.6 2.9 %collective-permute-done.xfirst = f32[4,8,16,128]{3,2,1,0:T(8,128)S(1)} collective-permute-done((f32[4,8,16,128]{3,2,1,0:T(8,128)}, f32[4,8,16,128]{3,2,1,0:T(8,128)S(1)}, u32[]{:S(2)}, u32[]{:S(2)}) %collective-permute-start) | collective-permute-done | bytes 262176 | tf_op jit(solution)/shard_map/ppermute | solution.py:711
  15.6 6.5 %collective-permute-start.2 = (f32[4,24,8,128]{3,2,1,0:T(8,128)S(1)}, f32[4,24,8,128]{3,2,1,0:T(8,128)S(1)}, u32[]{:S(2)}, u32[]{:S(2)}) collective-permute-start(f32[4,24,8,128]{3,2,1,0:T(8,128)S(1)} %pad_maximum_fusion), channel_id=1, source_target_pairs={{1,2},{3,4},{5,6},{7,8},{9,10},{11,12},{13,14},{15,16},{17,18},{19... | collective-permute-start | bytes 1179656 | tf_op jit(solution)/shard_map/ppermute | solution.py:711
  22.1 3.1 %collective-permute-start.3 = (f32[4,24,8,128]{3,2,1,0:T(8,128)S(1)}, f32[4,24,8,128]{3,2,1,0:T(8,128)S(1)}, u32[]{:S(2)}, u32[]{:S(2)}) collective-permute-start(f32[4,24,8,128]{3,2,1,0:T(8,128)S(1)} %pad_maximum_fusion.1), channel_id=1, source_target_pairs={{0,1},{2,3},{4,5},{6,7},{8,9},{10,11},{12,13},{14,15},{16,17},{18,... | collective-permute-start | bytes 1179656 | tf_op jit(solution)/shard_map/ppermute | solution.py:711
  25.2 2.3 %collective-permute-done.2.yfirst = f32[4,24,8,128]{3,2,1,0:T(8,128)S(1)} collective-permute-done((f32[4,24,8,128]{3,2,1,0:T(8,128)S(1)}, f32[4,24,8,128]{3,2,1,0:T(8,128)S(1)}, u32[]{:S(2)}, u32[]{:S(2)}) %collective-permute-start.2) | collective-permute-done | bytes 393248 | tf_op jit(solution)/shard_map/ppermute | solution.py:711
  27.5 3.0 %shard_map.87 = (f32[26,32,128]{2,1,0:T(8,128)S(1)}, f32[26,32,128]{2,1,0:T(8,128)S(1)}, f32[26,32,128]{2,1,0:T(8,128)S(1)}, f32[26,32,128]{2,1,0:T(8,128)S(1)},...) custom-call(f32[4,8,16,128]{3,2,1,0:T(8,128)S(1)} %collective-permut, ...), custom_call_target="tpu_custom_call" | custom-call | flops 22528000 | bytes 9011200 | tf_op jit(solution)/shard_map/pallas_call | solution.py:691
  30.5 26.0 %all_to_all.20 = f32[24,6,2,128]{3,2,1,0:T(2,128)S(1)} all-to-all(f32[24,6,2,128]{3,2,1,0:T(2,128)S(1)} %get-tuple-element.44), channel_id=1, replica_groups={{0,1,64,65,128,129,192,193,256,257,320,321,384,385,448,449,512,513,576,..., dimensions={0} | all-to-all | bytes 294912 | tf_op jit(solution)/shard_map/all_to_all | solution.py:741
  57.3 6.1 %collective-permute-start.5 = (f32[12,6,2,128]{3,2,1,0:T(2,128)S(1)}, f32[12,6,2,128]{3,2,1,0:T(2,128)S(1)}, u32[]{:S(2)}, u32[]{:S(2)}) collective-permute-start(f32[12,6,2,128]{3,2,1,0:T(2,128)S(1)} %get-tuple-element.46), channel_id=1, source_target_pairs={{0,2},{1,3},{4,6},{5,7},{8,10},{9,11},{12,14},{13,15},{16,18},{17,... | collective-permute-start | bytes 221192 | tf_op jit(solution)/shard_map/ppermute | solution.py:711
  63.4 1.7 %collective-permute-done.5.second = f32[12,6,2,128]{3,2,1,0:T(2,128)S(1)} collective-permute-done((f32[12,6,2,128]{3,2,1,0:T(2,128)S(1)}, f32[12,6,2,128]{3,2,1,0:T(2,128)S(1)}, u32[]{:S(2)}, u32[]{:S(2)}) %collective-permute-start.5) | collective-permute-done | bytes 73760 | tf_op jit(solution)/shard_map/ppermute | solution.py:711
  65.1 3.2 %shard_map.89 = (f32[24,16,128]{2,1,0:T(8,128)S(1)}, f32[24,16,128]{2,1,0:T(8,128)S(1)}, f32[24,16,128]{2,1,0:T(8,128)S(1)}, f32[24,16,128]{2,1,0:T(8,128)S(1)},...) custom-call(f32[12,6,2,128]{3,2,1,0:T(2,128)S(1)} %collective-permut, ...), custom_call_target="tpu_custom_call" | custom-call | flops 11223040 | bytes 4489216 | tf_op jit(solution)/shard_map/pallas_call | solution.py:691
  68.3 25.6 %all_to_all.21 = f32[64,4,1,128]{3,2,1,0:T(1,128)S(1)} all-to-all(f32[64,4,1,128]{3,2,1,0:T(1,128)S(1)} %get-tuple-element.47), channel_id=1, replica_groups=mesh['tile'=12,'group'=64] {'group'}, dimensions={0} | all-to-all | bytes 262144 | tf_op jit(solution)/shard_map/all_to_all | solution.py:732
  93.9 1.4 shard_map.90
  96.0 3.8 %collective-permute-start.6 = (f32[8,16,128]{2,1,0:T(8,128)S(1)}, f32[8,16,128]{2,1,0:T(8,128)S(1)}, u32[]{:S(2)}, u32[]{:S(2)}) collective-permute-start(f32[8,16,128]{2,1,0:T(8,128)S(1)} %get-tuple-element.68.own), channel_id=1, source_target_pairs={{0,64},{128,192},{256,320},{384,448},{512,576},{640,704},{64,0},{1... | collective-permute-start | bytes 196616 | tf_op jit(solution)/shard_map/ppermute | solution.py:711
  99.8 1.6 %collective-permute-done.6.xfirst = f32[8,16,128]{2,1,0:T(8,128)S(1)} collective-permute-done((f32[8,16,128]{2,1,0:T(8,128)S(1)}, f32[8,16,128]{2,1,0:T(8,128)S(1)}, u32[]{:S(2)}, u32[]{:S(2)}) %collective-permute-start.6) | collective-permute-done | bytes 65568 | tf_op jit(solution)/shard_map/ppermute | solution.py:711
  101.5 3.5 %collective-permute-start.8 = (f32[24,8,128]{2,1,0:T(8,128)S(1)}, f32[24,8,128]{2,1,0:T(8,128)S(1)}, u32[]{:S(2)}, u32[]{:S(2)}) collective-permute-start(f32[24,8,128]{2,1,0:T(8,128)S(1)} %pad_maximum_fusion.2), channel_id=1, source_target_pairs={{1,2},{3,4},{5,6},{7,8},{9,10},{11,12},{13,14},{15,16},{17,18},{19... | collective-permute-start | bytes 294920 | tf_op jit(solution)/shard_map/ppermute | solution.py:711
  105.0 1.9 %collective-permute-start.9 = (f32[24,8,128]{2,1,0:T(8,128)S(1)}, f32[24,8,128]{2,1,0:T(8,128)S(1)}, u32[]{:S(2)}, u32[]{:S(2)}) collective-permute-start(f32[24,8,128]{2,1,0:T(8,128)S(1)} %pad_maximum_fusion.3), channel_id=1, source_target_pairs={{0,1},{2,3},{4,5},{6,7},{8,9},{10,11},{12,13},{14,15},{16,17},{18,... | collective-permute-start | bytes 294920 | tf_op jit(solution)/shard_map/ppermute | solution.py:711
  108.2 2.3 %shard_map.91 = (f32[26,32,128]{2,1,0:T(8,128)S(1)}, f32[26,32,128]{2,1,0:T(8,128)S(1)}, f32[26,32,128]{2,1,0:T(8,128)S(1)}, f32[12,32,128]{2,1,0:T(8,128)S(1)},...) custom-call(f32[8,16,128]{2,1,0:T(8,128)S(1)} %collective-permute-done.6.xfirst, ...), custom_call_target="tpu_custom_call" | custom-call | flops 8555520 | bytes 3422208 | tf_op jit(solution)/shard_map/pallas_call | solution.py:691
  110.6 15.0 %all_to_all.22 = f32[12,3,2,128]{3,2,1,0:T(2,128)S(1)} all-to-all(f32[12,3,2,128]{3,2,1,0:T(2,128)S(1)} %get-tuple-element.75), channel_id=1, replica_groups=mesh['tile'=12,'group'=64] {'tile'}, dimensions={0} | all-to-all | bytes 73728 | tf_op jit(solution)/shard_map/all_to_all | solution.py:732
  125.5 4.2 %collective-permute-start.11 = (f32[13,3,2,128]{3,2,1,0:T(2,128)S(1)}, f32[13,3,2,128]{3,2,1,0:T(2,128)S(1)}, u32[]{:S(2)}, u32[]{:S(2)}) collective-permute-start(f32[13,3,2,128]{3,2,1,0:T(2,128)S(1)} %constant_dynamic-update-slice_fusion.own), channel_id=1, source_target_pairs={{1,2},{3,4},{5,6},{7,8},{9,10},{11,12},{13,14},{15,16},{17,18},{19... | collective-permute-start | bytes 119816 | tf_op jit(solution)/shard_map/ppermute | solution.py:711
  129.7 1.9 %collective-permute-start.10 = (f32[13,3,2,128]{3,2,1,0:T(2,128)S(1)}, f32[13,3,2,128]{3,2,1,0:T(2,128)S(1)}, u32[]{:S(2)}, u32[]{:S(2)}) collective-permute-start(f32[13,3,2,128]{3,2,1,0:T(2,128)S(1)} %constant_dynamic-update-slice_fusion.own), channel_id=1, source_target_pairs={{0,1},{2,3},{4,5},{6,7},{8,9},{10,11},{12,13},{14,15},{16,17},{18,... | collective-permute-start | bytes 119816 | tf_op jit(solution)/shard_map/ppermute | solution.py:711
  131.7 1.2 collective-permute-done.10.first
  133.7 20.2 %all_to_all.23 = f32[64,3,1,128]{3,2,1,0:T(1,128)S(1)} all-to-all(f32[64,3,1,128]{3,2,1,0:T(1,128)S(1)} %get-tuple-element.77), channel_id=1, replica_groups=mesh['tile'=12,'group'=64] {'group'}, dimensions={0} | all-to-all | bytes 196608 | tf_op jit(solution)/shard_map/all_to_all | solution.py:732
  153.9 2.3 %shard_map.93 = (f32[8,16,128]{2,1,0:T(8,128)}, f32[8,16,128]{2,1,0:T(8,128)}) custom-call(f32[192,128]{1,0:T(8,128)S(1)} %bitcast.6, f32[12,1,128]{2,1,0:T(1,128)S(1)} %get-tuple-element.78.below_ref, f32[12,24,128]{2,1,0:T(8,128)S(1)} %get-tuple-element.48.s3_ref, f32[12,24,128]{2,1,0:T(8,128)S(1)} %get-tuple-element.49.di3_ref, ...), custom_call_target="tpu_custom_call" | custom-call | flops 655360 | bytes 262144 | tf_op jit(solution)/shard_map/pallas_call | solution.py:691
  (26 shorter events, 5.3 us)
Async XLA Ops:
  2.7 9.9 %collective-permute-start.1 = (f32[4,8,16,128]{3,2,1,0:T(8,128)}, f32[4,8,16,128]{3,2,1,0:T(8,128)S(1)}, u32[]{:S(2)}, u32[]{:S(2)}) collective-permute-start(f32[4,8,16,128]{3,2,1,0:T(8,128)} %shard_map.86.own), channel_id=1, source_target_pairs={{64,128},{192,256},{320,384},{448,512},{576,640},{128,64},{256,192... | collective-permute-start | bytes 786440 | tf_op jit(solution)/shard_map/ppermute | solution.py:711
  3.4 12.1 %collective-permute-start = (f32[4,8,16,128]{3,2,1,0:T(8,128)}, f32[4,8,16,128]{3,2,1,0:T(8,128)S(1)}, u32[]{:S(2)}, u32[]{:S(2)}) collective-permute-start(f32[4,8,16,128]{3,2,1,0:T(8,128)} %shard_map.86.own), channel_id=1, source_target_pairs={{0,64},{128,192},{256,320},{384,448},{512,576},{640,704},{64,0},{1... | collective-permute-start | bytes 786440 | tf_op jit(solution)/shard_map/ppermute | solution.py:711
  15.6 12.0 %collective-permute-start.2 = (f32[4,24,8,128]{3,2,1,0:T(8,128)S(1)}, f32[4,24,8,128]{3,2,1,0:T(8,128)S(1)}, u32[]{:S(2)}, u32[]{:S(2)}) collective-permute-start(f32[4,24,8,128]{3,2,1,0:T(8,128)S(1)} %pad_maximum_fusion), channel_id=1, source_target_pairs={{1,2},{3,4},{5,6},{7,8},{9,10},{11,12},{13,14},{15,16},{17,18},{19... | collective-permute-start | bytes 1179656 | tf_op jit(solution)/shard_map/ppermute | solution.py:711
  22.1 5.5 %copy-start = (f32[4,8,16,128]{3,2,1,0:T(8,128)S(1)}, f32[4,8,16,128]{3,2,1,0:T(8,128)}, u32[]{:S(2)}) copy-start(f32[4,8,16,128]{3,2,1,0:T(8,128)} %shard_map.86.own) | copy-start | bytes 786436
  22.1 5.4 %collective-permute-start.3 = (f32[4,24,8,128]{3,2,1,0:T(8,128)S(1)}, f32[4,24,8,128]{3,2,1,0:T(8,128)S(1)}, u32[]{:S(2)}, u32[]{:S(2)}) collective-permute-start(f32[4,24,8,128]{3,2,1,0:T(8,128)S(1)} %pad_maximum_fusion.1), channel_id=1, source_target_pairs={{0,1},{2,3},{4,5},{6,7},{8,9},{10,11},{12,13},{14,15},{16,17},{18,... | collective-permute-start | bytes 1179656 | tf_op jit(solution)/shard_map/ppermute | solution.py:711
  56.6 6.8 %collective-permute-start.4 = (f32[12,6,2,128]{3,2,1,0:T(2,128)S(1)}, f32[12,6,2,128]{3,2,1,0:T(2,128)S(1)}, u32[]{:S(2)}, u32[]{:S(2)}) collective-permute-start(f32[12,6,2,128]{3,2,1,0:T(2,128)S(1)} %get-tuple-element.45), channel_id=1, source_target_pairs={{2,4},{3,5},{6,8},{7,9},{10,12},{11,13},{14,16},{15,17},{18,20},{1... | collective-permute-start | bytes 221192 | tf_op jit(solution)/shard_map/ppermute | solution.py:711
  57.3 7.8 %collective-permute-start.5 = (f32[12,6,2,128]{3,2,1,0:T(2,128)S(1)}, f32[12,6,2,128]{3,2,1,0:T(2,128)S(1)}, u32[]{:S(2)}, u32[]{:S(2)}) collective-permute-start(f32[12,6,2,128]{3,2,1,0:T(2,128)S(1)} %get-tuple-element.46), channel_id=1, source_target_pairs={{0,2},{1,3},{4,6},{5,7},{8,10},{9,11},{12,14},{13,15},{16,18},{17,... | collective-permute-start | bytes 221192 | tf_op jit(solution)/shard_map/ppermute | solution.py:711
  95.3 4.5 %collective-permute-start.7 = (f32[8,16,128]{2,1,0:T(8,128)S(1)}, f32[8,16,128]{2,1,0:T(8,128)S(1)}, u32[]{:S(2)}, u32[]{:S(2)}) collective-permute-start(f32[8,16,128]{2,1,0:T(8,128)S(1)} %get-tuple-element.68.own), channel_id=1, source_target_pairs={{64,128},{192,256},{320,384},{448,512},{576,640},{128,64},{256,192... | collective-permute-start | bytes 196616 | tf_op jit(solution)/shard_map/ppermute | solution.py:711
  96.0 5.5 %collective-permute-start.6 = (f32[8,16,128]{2,1,0:T(8,128)S(1)}, f32[8,16,128]{2,1,0:T(8,128)S(1)}, u32[]{:S(2)}, u32[]{:S(2)}) collective-permute-start(f32[8,16,128]{2,1,0:T(8,128)S(1)} %get-tuple-element.68.own), channel_id=1, source_target_pairs={{0,64},{128,192},{256,320},{384,448},{512,576},{640,704},{64,0},{1... | collective-permute-start | bytes 196616 | tf_op jit(solution)/shard_map/ppermute | solution.py:711
  101.5 5.9 %collective-permute-start.8 = (f32[24,8,128]{2,1,0:T(8,128)S(1)}, f32[24,8,128]{2,1,0:T(8,128)S(1)}, u32[]{:S(2)}, u32[]{:S(2)}) collective-permute-start(f32[24,8,128]{2,1,0:T(8,128)S(1)} %pad_maximum_fusion.2), channel_id=1, source_target_pairs={{1,2},{3,4},{5,6},{7,8},{9,10},{11,12},{13,14},{15,16},{17,18},{19... | collective-permute-start | bytes 294920 | tf_op jit(solution)/shard_map/ppermute | solution.py:711
  105.0 3.2 %collective-permute-start.9 = (f32[24,8,128]{2,1,0:T(8,128)S(1)}, f32[24,8,128]{2,1,0:T(8,128)S(1)}, u32[]{:S(2)}, u32[]{:S(2)}) collective-permute-start(f32[24,8,128]{2,1,0:T(8,128)S(1)} %pad_maximum_fusion.3), channel_id=1, source_target_pairs={{0,1},{2,3},{4,5},{6,7},{8,9},{10,11},{12,13},{14,15},{16,17},{18,... | collective-permute-start | bytes 294920 | tf_op jit(solution)/shard_map/ppermute | solution.py:711
  125.5 6.1 %collective-permute-start.11 = (f32[13,3,2,128]{3,2,1,0:T(2,128)S(1)}, f32[13,3,2,128]{3,2,1,0:T(2,128)S(1)}, u32[]{:S(2)}, u32[]{:S(2)}) collective-permute-start(f32[13,3,2,128]{3,2,1,0:T(2,128)S(1)} %constant_dynamic-update-slice_fusion.own), channel_id=1, source_target_pairs={{1,2},{3,4},{5,6},{7,8},{9,10},{11,12},{13,14},{15,16},{17,18},{19... | collective-permute-start | bytes 119816 | tf_op jit(solution)/shard_map/ppermute | solution.py:711
  129.7 3.1 %collective-permute-start.10 = (f32[13,3,2,128]{3,2,1,0:T(2,128)S(1)}, f32[13,3,2,128]{3,2,1,0:T(2,128)S(1)}, u32[]{:S(2)}, u32[]{:S(2)}) collective-permute-start(f32[13,3,2,128]{3,2,1,0:T(2,128)S(1)} %constant_dynamic-update-slice_fusion.own), channel_id=1, source_target_pairs={{0,1},{2,3},{4,5},{6,7},{8,9},{10,11},{12,13},{14,15},{16,17},{18,... | collective-permute-start | bytes 119816 | tf_op jit(solution)/shard_map/ppermute | solution.py:711

commit v12 on v11

--- a/solution.py
+++ b/solution.py
@@ -161,7 +161,7 @@
         e2_ref[pl.ds(at, 2)] = v + di_ref[pl.ds(at, 2)] * (r_ref[pl.ds(at, 2)] - av)
         return carry
 
-    lax.fori_loop(1, WX // 2 - 1, second, 0, unroll=5)
+    lax.fori_loop(1, WX // 2 - 1, second, 0, unroll=True)
 
     def third(i, carry):
         at = 1 + 2 * i
@@ -169,7 +169,7 @@
         r1_ref[pl.ds(i, 1)] = restrict(r_ref[pl.ds(at, 2)] - av, 1, 1)
         return carry
 
-    lax.fori_loop(2, WX // 2 - 2, third, 0, unroll=4)
+    lax.fori_loop(2, WX // 2 - 2, third, 0, unroll=True)
 
 
 def descend_second(r1, s1, wx1, wy1, wz1, di1):
@@ -221,7 +221,7 @@
         out_ref[3, row] = span * (saturation - old_saturation) + STORAGE * (head - old)
         return carry
 
-    lax.fori_loop(0, BX, cells, 0, unroll=4)
+    lax.fori_loop(0, BX, cells, 0, unroll=True)
 
 
 def is_even(axis, step=1, lead=0):
@@ -268,7 +268,7 @@
         wz_ref[pl.ds(at, 2)] = jnp.where(iota(wz.shape, 2) == 0, 0.0, wz)
         return carry
 
-    lax.fori_loop(0, WX // 2, faces, 0, unroll=4)
+    lax.fori_loop(0, WX // 2, faces, 0, unroll=True)
 
     def right_side(i, carry):
         at = 1 + 2 * i
@@ -287,7 +287,7 @@
         e1_ref[rows] = rhs * di
         return carry
 
-    lax.fori_loop(0, WX // 2, right_side, 0, unroll=4)
+    lax.fori_loop(0, WX // 2, right_side, 0, unroll=True)
 
     def bands(i, carry):
         rows = pl.ds(1 + 2 * i, 2)
@@ -296,7 +296,7 @@
         s1_ref[row], wx1_ref[row], wy1_ref[row], wz1_ref[row] = s1, wx1, wy1, wz1
         return carry
 
-    lax.fori_loop(1, WX // 2 - 1, bands, 0, unroll=5)
+    lax.fori_loop(1, WX // 2 - 1, bands, 0, unroll=True)
     for ref in (s1_ref, wx1_ref, wy1_ref, wz1_ref):
         blank_level1(ref, 1)
     blank_level1(r1_ref, 2)
@@ -329,7 +329,7 @@
         u_ref[rows] = v + di_ref[rows] * (rhs_ref[rows] - av)
         return carry
 
-    lax.fori_loop(0, WX // 2, post, 0, unroll=4)
+    lax.fori_loop(0, WX // 2, post, 0, unroll=True)
 
     def remain(i, carry):
         at = 1 + 2 * i
@@ -340,7 +340,7 @@
         e1_ref[rows] = left * di_ref[rows]
         return carry
 
-    lax.fori_loop(1, WX // 2 - 1, remain, 0, unroll=5)
+    lax.fori_loop(1, WX // 2 - 1, remain, 0, unroll=True)
     descend_top(r_ref, e1_ref, e2_ref, s_ref, wx_ref, wy_ref, wz_ref, di_ref, r1_ref)
     blank_level1(r1_ref, 2)
     e21, r2 = descend_second(

time: 157 us -> 159 us (1.013)
  Pallas kernels: 15.2 us -> 17 us
    pallas_call x7, Pallas kernels: 13.1 us -> 15 us  [call(): pl.pallas_call(body, out_shape=[jax.ShapeDtypeStruct(shape, F32) for shap...]
where the time goes in v12:
time: 159 us; the launch traced here: 158 us
  blocking collectives  86.7 us (55%)
  starting transfers between devices  41.2 us (26%)
  Pallas kernels  17 us (11%)
  waiting for transfers between devices  11 us (7%)
    all_to_all x3, blocking collectives, everyone(): return lax.all_to_all(blocks, axis, 0, 0, tiled=True)  60.7 us
    ppermute x12, starting transfers between devices, swap(): return lax.ppermute(cells, axis, ups + [(j, i) for i, j in ups])  41.2 us
    all_to_all x1, blocking collectives, pairs_of_tiles(): lax.all_to_all(block, ('tile', 'group'), 0, 0, axis_index_groups=members,...  26 us
    pallas_call x7, Pallas kernels, call(): pl.pallas_call(body, out_shape=[jax.ShapeDtypeStruct(shape, F32) for shap...  15 us
    ppermute x12, waiting for transfers between devices, swap(): return lax.ppermute(cells, axis, ups + [(j, i) for i, j in ups])  11 us
  transfers between devices with their start and end apart: 12, of which 7 were waited for; matrix products, arithmetic and copies ran while one was open for 1% of the time, Pallas kernels for 0%

profile of v12, /device:TPU:1, one launch (start us, length us, event | category | flops | bytes accessed | tf_op | source)
XLA Modules:
  0.0 158.1 jit_solution(14274597238655867249)
XLA Ops:
  0.6 2.1 %shard_map.86.own = f32[4,8,16,128]{3,2,1,0:T(8,128)} custom-call(f32[8,16,128]{2,1,0:T(8,128)} %head_in.1, f32[8,16,128]{2,1,0:T(8,128)} %old_in.1, s32[8,16,128]{2,1,0:T(8,128)} %soil_in.1, f32[12]{0:T(128)} %ks_in.1, f32[12]{0:T(128)} %alpha_in.1, f32[12]{0:T(128)} %shape_in.1, f32[12]{0:T(128)} %span_in.1), custom_call_target="tpu_custom_call" | custom-call | tf_op jit(solution)/shard_map/pallas_call | solution.py:754
  3.4 8.2 %collective-permute-start = (f32[4,8,16,128]{3,2,1,0:T(8,128)}, f32[4,8,16,128]{3,2,1,0:T(8,128)S(1)}, u32[]{:S(2)}, u32[]{:S(2)}) collective-permute-start(f32[4,8,16,128]{3,2,1,0:T(8,128)} %shard_map.86.own), channel_id=1, source_target_pairs={{0,64},{128,192},{256,320},{384,448},{512,576},{640,704},{64,0},{1... | collective-permute-start | bytes 786440 | tf_op jit(solution)/shard_map/ppermute | solution.py:711
  12.6 2.9 %collective-permute-done.xfirst = f32[4,8,16,128]{3,2,1,0:T(8,128)S(1)} collective-permute-done((f32[4,8,16,128]{3,2,1,0:T(8,128)}, f32[4,8,16,128]{3,2,1,0:T(8,128)S(1)}, u32[]{:S(2)}, u32[]{:S(2)}) %collective-permute-start) | collective-permute-done | bytes 262176 | tf_op jit(solution)/shard_map/ppermute | solution.py:711
  15.6 6.5 %collective-permute-start.2 = (f32[4,24,8,128]{3,2,1,0:T(8,128)S(1)}, f32[4,24,8,128]{3,2,1,0:T(8,128)S(1)}, u32[]{:S(2)}, u32[]{:S(2)}) collective-permute-start(f32[4,24,8,128]{3,2,1,0:T(8,128)S(1)} %pad_maximum_fusion), channel_id=1, source_target_pairs={{1,2},{3,4},{5,6},{7,8},{9,10},{11,12},{13,14},{15,16},{17,18},{19... | collective-permute-start | bytes 1179656 | tf_op jit(solution)/shard_map/ppermute | solution.py:711
  22.1 3.1 %collective-permute-start.3 = (f32[4,24,8,128]{3,2,1,0:T(8,128)S(1)}, f32[4,24,8,128]{3,2,1,0:T(8,128)S(1)}, u32[]{:S(2)}, u32[]{:S(2)}) collective-permute-start(f32[4,24,8,128]{3,2,1,0:T(8,128)S(1)} %pad_maximum_fusion.1), channel_id=1, source_target_pairs={{0,1},{2,3},{4,5},{6,7},{8,9},{10,11},{12,13},{14,15},{16,17},{18,... | collective-permute-start | bytes 1179656 | tf_op jit(solution)/shard_map/ppermute | solution.py:711
  25.2 2.3 %collective-permute-done.2.yfirst = f32[4,24,8,128]{3,2,1,0:T(8,128)S(1)} collective-permute-done((f32[4,24,8,128]{3,2,1,0:T(8,128)S(1)}, f32[4,24,8,128]{3,2,1,0:T(8,128)S(1)}, u32[]{:S(2)}, u32[]{:S(2)}) %collective-permute-start.2) | collective-permute-done | bytes 393248 | tf_op jit(solution)/shard_map/ppermute | solution.py:711
  27.5 4.2 %shard_map.87 = (f32[26,32,128]{2,1,0:T(8,128)S(1)}, f32[26,32,128]{2,1,0:T(8,128)S(1)}, f32[26,32,128]{2,1,0:T(8,128)S(1)}, f32[26,32,128]{2,1,0:T(8,128)S(1)},...) custom-call(f32[4,8,16,128]{3,2,1,0:T(8,128)S(1)} %collective-permut, ...), custom_call_target="tpu_custom_call" | custom-call | flops 22528000 | bytes 9011200 | tf_op jit(solution)/shard_map/pallas_call | solution.py:691
  31.7 26.0 %all_to_all.20 = f32[24,6,2,128]{3,2,1,0:T(2,128)S(1)} all-to-all(f32[24,6,2,128]{3,2,1,0:T(2,128)S(1)} %get-tuple-element.44), channel_id=1, replica_groups={{0,1,64,65,128,129,192,193,256,257,320,321,384,385,448,449,512,513,576,..., dimensions={0} | all-to-all | bytes 294912 | tf_op jit(solution)/shard_map/all_to_all | solution.py:741
  58.5 6.1 %collective-permute-start.5 = (f32[12,6,2,128]{3,2,1,0:T(2,128)S(1)}, f32[12,6,2,128]{3,2,1,0:T(2,128)S(1)}, u32[]{:S(2)}, u32[]{:S(2)}) collective-permute-start(f32[12,6,2,128]{3,2,1,0:T(2,128)S(1)} %get-tuple-element.46), channel_id=1, source_target_pairs={{0,2},{1,3},{4,6},{5,7},{8,10},{9,11},{12,14},{13,15},{16,18},{17,... | collective-permute-start | bytes 221192 | tf_op jit(solution)/shard_map/ppermute | solution.py:711
  64.6 1.7 %collective-permute-done.5.second = f32[12,6,2,128]{3,2,1,0:T(2,128)S(1)} collective-permute-done((f32[12,6,2,128]{3,2,1,0:T(2,128)S(1)}, f32[12,6,2,128]{3,2,1,0:T(2,128)S(1)}, u32[]{:S(2)}, u32[]{:S(2)}) %collective-permute-start.5) | collective-permute-done | bytes 73760 | tf_op jit(solution)/shard_map/ppermute | solution.py:711
  66.3 3.2 %shard_map.89 = (f32[24,16,128]{2,1,0:T(8,128)S(1)}, f32[24,16,128]{2,1,0:T(8,128)S(1)}, f32[24,16,128]{2,1,0:T(8,128)S(1)}, f32[24,16,128]{2,1,0:T(8,128)S(1)},...) custom-call(f32[12,6,2,128]{3,2,1,0:T(2,128)S(1)} %collective-permut, ...), custom_call_target="tpu_custom_call" | custom-call | flops 11223040 | bytes 4489216 | tf_op jit(solution)/shard_map/pallas_call | solution.py:691
  69.5 25.6 %all_to_all.21 = f32[64,4,1,128]{3,2,1,0:T(1,128)S(1)} all-to-all(f32[64,4,1,128]{3,2,1,0:T(1,128)S(1)} %get-tuple-element.47), channel_id=1, replica_groups=mesh['tile'=12,'group'=64] {'group'}, dimensions={0} | all-to-all | bytes 262144 | tf_op jit(solution)/shard_map/all_to_all | solution.py:732
  95.1 1.4 shard_map.90
  97.2 3.8 %collective-permute-start.6 = (f32[8,16,128]{2,1,0:T(8,128)S(1)}, f32[8,16,128]{2,1,0:T(8,128)S(1)}, u32[]{:S(2)}, u32[]{:S(2)}) collective-permute-start(f32[8,16,128]{2,1,0:T(8,128)S(1)} %get-tuple-element.68.own), channel_id=1, source_target_pairs={{0,64},{128,192},{256,320},{384,448},{512,576},{640,704},{64,0},{1... | collective-permute-start | bytes 196616 | tf_op jit(solution)/shard_map/ppermute | solution.py:711
  101.1 1.6 %collective-permute-done.6.xfirst = f32[8,16,128]{2,1,0:T(8,128)S(1)} collective-permute-done((f32[8,16,128]{2,1,0:T(8,128)S(1)}, f32[8,16,128]{2,1,0:T(8,128)S(1)}, u32[]{:S(2)}, u32[]{:S(2)}) %collective-permute-start.6) | collective-permute-done | bytes 65568 | tf_op jit(solution)/shard_map/ppermute | solution.py:711
  102.7 3.5 %collective-permute-start.8 = (f32[24,8,128]{2,1,0:T(8,128)S(1)}, f32[24,8,128]{2,1,0:T(8,128)S(1)}, u32[]{:S(2)}, u32[]{:S(2)}) collective-permute-start(f32[24,8,128]{2,1,0:T(8,128)S(1)} %pad_maximum_fusion.2), channel_id=1, source_target_pairs={{1,2},{3,4},{5,6},{7,8},{9,10},{11,12},{13,14},{15,16},{17,18},{19... | collective-permute-start | bytes 294920 | tf_op jit(solution)/shard_map/ppermute | solution.py:711
  106.3 1.9 %collective-permute-start.9 = (f32[24,8,128]{2,1,0:T(8,128)S(1)}, f32[24,8,128]{2,1,0:T(8,128)S(1)}, u32[]{:S(2)}, u32[]{:S(2)}) collective-permute-start(f32[24,8,128]{2,1,0:T(8,128)S(1)} %pad_maximum_fusion.3), channel_id=1, source_target_pairs={{0,1},{2,3},{4,5},{6,7},{8,9},{10,11},{12,13},{14,15},{16,17},{18,... | collective-permute-start | bytes 294920 | tf_op jit(solution)/shard_map/ppermute | solution.py:711
  109.5 2.9 %shard_map.91 = (f32[26,32,128]{2,1,0:T(8,128)S(1)}, f32[26,32,128]{2,1,0:T(8,128)S(1)}, f32[26,32,128]{2,1,0:T(8,128)S(1)}, f32[12,32,128]{2,1,0:T(8,128)S(1)},...) custom-call(f32[8,16,128]{2,1,0:T(8,128)S(1)} %collective-permute-done.6.xfirst, ...), custom_call_target="tpu_custom_call" | custom-call | flops 8555520 | bytes 3422208 | tf_op jit(solution)/shard_map/pallas_call | solution.py:691
  112.4 15.0 %all_to_all.22 = f32[12,3,2,128]{3,2,1,0:T(2,128)S(1)} all-to-all(f32[12,3,2,128]{3,2,1,0:T(2,128)S(1)} %get-tuple-element.75), channel_id=1, replica_groups=mesh['tile'=12,'group'=64] {'tile'}, dimensions={0} | all-to-all | bytes 73728 | tf_op jit(solution)/shard_map/all_to_all | solution.py:732
  127.4 4.2 %collective-permute-start.11 = (f32[13,3,2,128]{3,2,1,0:T(2,128)S(1)}, f32[13,3,2,128]{3,2,1,0:T(2,128)S(1)}, u32[]{:S(2)}, u32[]{:S(2)}) collective-permute-start(f32[13,3,2,128]{3,2,1,0:T(2,128)S(1)} %constant_dynamic-update-slice_fusion.own), channel_id=1, source_target_pairs={{1,2},{3,4},{5,6},{7,8},{9,10},{11,12},{13,14},{15,16},{17,18},{19... | collective-permute-start | bytes 119816 | tf_op jit(solution)/shard_map/ppermute | solution.py:711
  131.6 1.9 %collective-permute-start.10 = (f32[13,3,2,128]{3,2,1,0:T(2,128)S(1)}, f32[13,3,2,128]{3,2,1,0:T(2,128)S(1)}, u32[]{:S(2)}, u32[]{:S(2)}) collective-permute-start(f32[13,3,2,128]{3,2,1,0:T(2,128)S(1)} %constant_dynamic-update-slice_fusion.own), channel_id=1, source_target_pairs={{0,1},{2,3},{4,5},{6,7},{8,9},{10,11},{12,13},{14,15},{16,17},{18,... | collective-permute-start | bytes 119816 | tf_op jit(solution)/shard_map/ppermute | solution.py:711
  133.5 1.2 collective-permute-done.10.first
  135.5 20.2 %all_to_all.23 = f32[64,3,1,128]{3,2,1,0:T(1,128)S(1)} all-to-all(f32[64,3,1,128]{3,2,1,0:T(1,128)S(1)} %get-tuple-element.77), channel_id=1, replica_groups=mesh['tile'=12,'group'=64] {'group'}, dimensions={0} | all-to-all | bytes 196608 | tf_op jit(solution)/shard_map/all_to_all | solution.py:732
  155.7 2.3 %shard_map.93 = (f32[8,16,128]{2,1,0:T(8,128)}, f32[8,16,128]{2,1,0:T(8,128)}) custom-call(f32[192,128]{1,0:T(8,128)S(1)} %bitcast.6, f32[12,1,128]{2,1,0:T(1,128)S(1)} %get-tuple-element.78.below_ref, f32[12,24,128]{2,1,0:T(8,128)S(1)} %get-tuple-element.48.s3_ref, f32[12,24,128]{2,1,0:T(8,128)S(1)} %get-tuple-element.49.di3_ref, ...), custom_call_target="tpu_custom_call" | custom-call | flops 655360 | bytes 262144 | tf_op jit(solution)/shard_map/pallas_call | solution.py:691
  (26 shorter events, 5.3 us)
Async XLA Ops:
  2.7 9.9 %collective-permute-start.1 = (f32[4,8,16,128]{3,2,1,0:T(8,128)}, f32[4,8,16,128]{3,2,1,0:T(8,128)S(1)}, u32[]{:S(2)}, u32[]{:S(2)}) collective-permute-start(f32[4,8,16,128]{3,2,1,0:T(8,128)} %shard_map.86.own), channel_id=1, source_target_pairs={{64,128},{192,256},{320,384},{448,512},{576,640},{128,64},{256,192... | collective-permute-start | bytes 786440 | tf_op jit(solution)/shard_map/ppermute | solution.py:711
  3.4 12.1 %collective-permute-start = (f32[4,8,16,128]{3,2,1,0:T(8,128)}, f32[4,8,16,128]{3,2,1,0:T(8,128)S(1)}, u32[]{:S(2)}, u32[]{:S(2)}) collective-permute-start(f32[4,8,16,128]{3,2,1,0:T(8,128)} %shard_map.86.own), channel_id=1, source_target_pairs={{0,64},{128,192},{256,320},{384,448},{512,576},{640,704},{64,0},{1... | collective-permute-start | bytes 786440 | tf_op jit(solution)/shard_map/ppermute | solution.py:711
  15.6 12.0 %collective-permute-start.2 = (f32[4,24,8,128]{3,2,1,0:T(8,128)S(1)}, f32[4,24,8,128]{3,2,1,0:T(8,128)S(1)}, u32[]{:S(2)}, u32[]{:S(2)}) collective-permute-start(f32[4,24,8,128]{3,2,1,0:T(8,128)S(1)} %pad_maximum_fusion), channel_id=1, source_target_pairs={{1,2},{3,4},{5,6},{7,8},{9,10},{11,12},{13,14},{15,16},{17,18},{19... | collective-permute-start | bytes 1179656 | tf_op jit(solution)/shard_map/ppermute | solution.py:711
  22.1 5.5 %copy-start = (f32[4,8,16,128]{3,2,1,0:T(8,128)S(1)}, f32[4,8,16,128]{3,2,1,0:T(8,128)}, u32[]{:S(2)}) copy-start(f32[4,8,16,128]{3,2,1,0:T(8,128)} %shard_map.86.own) | copy-start | bytes 786436
  22.1 5.4 %collective-permute-start.3 = (f32[4,24,8,128]{3,2,1,0:T(8,128)S(1)}, f32[4,24,8,128]{3,2,1,0:T(8,128)S(1)}, u32[]{:S(2)}, u32[]{:S(2)}) collective-permute-start(f32[4,24,8,128]{3,2,1,0:T(8,128)S(1)} %pad_maximum_fusion.1), channel_id=1, source_target_pairs={{0,1},{2,3},{4,5},{6,7},{8,9},{10,11},{12,13},{14,15},{16,17},{18,... | collective-permute-start | bytes 1179656 | tf_op jit(solution)/shard_map/ppermute | solution.py:711
  57.8 6.8 %collective-permute-start.4 = (f32[12,6,2,128]{3,2,1,0:T(2,128)S(1)}, f32[12,6,2,128]{3,2,1,0:T(2,128)S(1)}, u32[]{:S(2)}, u32[]{:S(2)}) collective-permute-start(f32[12,6,2,128]{3,2,1,0:T(2,128)S(1)} %get-tuple-element.45), channel_id=1, source_target_pairs={{2,4},{3,5},{6,8},{7,9},{10,12},{11,13},{14,16},{15,17},{18,20},{1... | collective-permute-start | bytes 221192 | tf_op jit(solution)/shard_map/ppermute | solution.py:711
  58.5 7.8 %collective-permute-start.5 = (f32[12,6,2,128]{3,2,1,0:T(2,128)S(1)}, f32[12,6,2,128]{3,2,1,0:T(2,128)S(1)}, u32[]{:S(2)}, u32[]{:S(2)}) collective-permute-start(f32[12,6,2,128]{3,2,1,0:T(2,128)S(1)} %get-tuple-element.46), channel_id=1, source_target_pairs={{0,2},{1,3},{4,6},{5,7},{8,10},{9,11},{12,14},{13,15},{16,18},{17,... | collective-permute-start | bytes 221192 | tf_op jit(solution)/shard_map/ppermute | solution.py:711
  96.5 4.5 %collective-permute-start.7 = (f32[8,16,128]{2,1,0:T(8,128)S(1)}, f32[8,16,128]{2,1,0:T(8,128)S(1)}, u32[]{:S(2)}, u32[]{:S(2)}) collective-permute-start(f32[8,16,128]{2,1,0:T(8,128)S(1)} %get-tuple-element.68.own), channel_id=1, source_target_pairs={{64,128},{192,256},{320,384},{448,512},{576,640},{128,64},{256,192... | collective-permute-start | bytes 196616 | tf_op jit(solution)/shard_map/ppermute | solution.py:711
  97.2 5.5 %collective-permute-start.6 = (f32[8,16,128]{2,1,0:T(8,128)S(1)}, f32[8,16,128]{2,1,0:T(8,128)S(1)}, u32[]{:S(2)}, u32[]{:S(2)}) collective-permute-start(f32[8,16,128]{2,1,0:T(8,128)S(1)} %get-tuple-element.68.own), channel_id=1, source_target_pairs={{0,64},{128,192},{256,320},{384,448},{512,576},{640,704},{64,0},{1... | collective-permute-start | bytes 196616 | tf_op jit(solution)/shard_map/ppermute | solution.py:711
  102.7 5.9 %collective-permute-start.8 = (f32[24,8,128]{2,1,0:T(8,128)S(1)}, f32[24,8,128]{2,1,0:T(8,128)S(1)}, u32[]{:S(2)}, u32[]{:S(2)}) collective-permute-start(f32[24,8,128]{2,1,0:T(8,128)S(1)} %pad_maximum_fusion.2), channel_id=1, source_target_pairs={{1,2},{3,4},{5,6},{7,8},{9,10},{11,12},{13,14},{15,16},{17,18},{19... | collective-permute-start | bytes 294920 | tf_op jit(solution)/shard_map/ppermute | solution.py:711
  106.3 3.2 %collective-permute-start.9 = (f32[24,8,128]{2,1,0:T(8,128)S(1)}, f32[24,8,128]{2,1,0:T(8,128)S(1)}, u32[]{:S(2)}, u32[]{:S(2)}) collective-permute-start(f32[24,8,128]{2,1,0:T(8,128)S(1)} %pad_maximum_fusion.3), channel_id=1, source_target_pairs={{0,1},{2,3},{4,5},{6,7},{8,9},{10,11},{12,13},{14,15},{16,17},{18,... | collective-permute-start | bytes 294920 | tf_op jit(solution)/shard_map/ppermute | solution.py:711
  127.4 6.1 %collective-permute-start.11 = (f32[13,3,2,128]{3,2,1,0:T(2,128)S(1)}, f32[13,3,2,128]{3,2,1,0:T(2,128)S(1)}, u32[]{:S(2)}, u32[]{:S(2)}) collective-permute-start(f32[13,3,2,128]{3,2,1,0:T(2,128)S(1)} %constant_dynamic-update-slice_fusion.own), channel_id=1, source_target_pairs={{1,2},{3,4},{5,6},{7,8},{9,10},{11,12},{13,14},{15,16},{17,18},{19... | collective-permute-start | bytes 119816 | tf_op jit(solution)/shard_map/ppermute | solution.py:711
  131.6 3.1 %collective-permute-start.10 = (f32[13,3,2,128]{3,2,1,0:T(2,128)S(1)}, f32[13,3,2,128]{3,2,1,0:T(2,128)S(1)}, u32[]{:S(2)}, u32[]{:S(2)}) collective-permute-start(f32[13,3,2,128]{3,2,1,0:T(2,128)S(1)} %constant_dynamic-update-slice_fusion.own), channel_id=1, source_target_pairs={{0,1},{2,3},{4,5},{6,7},{8,9},{10,11},{12,13},{14,15},{16,17},{18,... | collective-permute-start | bytes 119816 | tf_op jit(solution)/shard_map/ppermute | solution.py:711
